TPU v7x, 512 devices: a whole 4x4x16 slice. The times are simulated.
512 devices in a mesh: face: 8 (over x_hi, y), tile: 64 (over x_lo, z, core).
Axes of the slice: x: 4 (x_hi: 2, x_lo: 2; x = x_hi * 2 + x_lo), y: 4, z: 16, core: 2. Of those that a mesh axis runs over, the one named last changes fastest.
Arguments:
- saved_input: bfloat16 [1, 32, 64, 64, 256], P(None, 'face', 'tile'), may hold values from -16 to 16
- saved_pre: bfloat16 [1, 32, 64, 64, 256], P(None, 'face', 'tile'), may hold values from -8 to 8
- cotangent: bfloat16 [1, 32, 64, 64, 256], P(None, 'face', 'tile'), may hold values from -16 to 16
- first_weight: bfloat16 [3, 3, 256, 256], replicated, may hold values from -0.125 to 0.125
- second_weight: bfloat16 [3, 3, 256, 256], replicated, may hold values from -0.125 to 0.125
- seams: int32 [32, 4], P('face'), may hold values from 0 to 31, as said below
- corners: int32 [32, 4], P('face'), may hold values from 0 to 31, as said below
Outputs:
- grad_input: bfloat16 [1, 32, 64, 64, 256], P(None, 'face', 'tile')
- grad_first: float32 [3, 3, 256, 256], P(None, None, 'tile', 'face')
Inputs may be any that keep to these rules, and one draw needn't show every extreme that they name: seams[f, s] names the face glued to side s of face f (0 top, 1 right, 2 bottom, 3 left). A top side meets the bottom side of the face named there and a right side the left side, pixel for pixel in the same order along the side; the gluing holds both ways (seams[seams[f, 1], 3] = f and seams[seams[f, 0], 2] = f), and crossing a side seam then a top or bottom seam reaches the same face as the other order. corners[f, c] names the face reached from f by crossing the two seams that meet at corner c (0 top left, 1 top right, 2 bottom left, 3 bottom right).
All inputs are finite; a program needn't handle non-finite values.
Results may differ from a plain program's by a relative error of at most 0.0033.
Values may be sent and summed in bfloat16 or wider, within the bound.
No kernel may reach another device: no remote copies, remote signals or barrier semaphores. Data moves between devices by JAX's collectives and lax.ppermute only.
A program may use at most 64 MiB of HBM per device.

v0:
```python
import math

import jax
import jax.numpy as jnp
from jax import lax
from jax.sharding import PartitionSpec as P


def with_halo(array, sides, width):
    for axis, dim in sides:
        devices, length = (lax.axis_size(axis), array.shape[dim])
        up = [(i, (i + 1) % devices) for i in range(devices)]
        down = [(j, i) for i, j in up]
        last = lax.slice_in_dim(array, length - width, length, axis=dim)
        leading = lax.slice_in_dim(array, 0, width, axis=dim)
        before = lax.ppermute(last, axis, up)
        after = lax.ppermute(leading, axis, down)
        array = jnp.concatenate([before, array, after], axis=dim)
    return array


def broadcast(array, axis, root):
    mine = lax.axis_index(axis) == root
    return lax.psum(jnp.where(mine, array, jnp.zeros_like(array)), axis)


def select_rows(source_table, wanted):
    entries = source_table.shape[0]
    onehot = (wanted[:, None] == jnp.arange(entries, dtype=jnp.int32)[None, :]).astype(
        source_table.dtype
    )
    flat_table = source_table.reshape(entries, -1)
    picked = jnp.dot(onehot, flat_table, preferred_element_type=jnp.float32)
    return picked.astype(source_table.dtype).reshape((wanted.shape[0],) + source_table.shape[1:])


def glue_faces(fields, seam_rows_table, corner_table):
    tile_count = lax.axis_size("tile")
    tile_pos = lax.axis_index("tile")
    local_faces = fields.shape[2]
    strip_rows = fields.shape[3]
    side_cells = fields.shape[4]
    row_halo = with_halo(fields, (("tile", 3),), 1)
    end_rows = broadcast(jnp.stack([row_halo[:, :, :, 1], row_halo[:, :, :, 0]], 0), "tile", 0)
    first_row = end_rows[0]
    last_row = end_rows[1]
    begin_cell = tile_pos * strip_rows
    seam_pieces = jnp.stack(
        [
            lax.dynamic_slice_in_dim(first_row, begin_cell, strip_rows, 3),
            lax.dynamic_slice_in_dim(last_row, begin_cell, strip_rows, 3),
        ],
        0,
    )
    seam_pieces = jnp.transpose(seam_pieces, (3, 0, 1, 2, 4, 5))
    side_edges = jnp.stack([row_halo[:, :, :, :, 0], row_halo[:, :, :, :, side_cells - 1]], 0)
    side_edges = jnp.transpose(side_edges, (3, 0, 1, 2, 4, 5))
    corner_points = jnp.stack(
        [
            first_row[:, :, :, 0],
            first_row[:, :, :, side_cells - 1],
            last_row[:, :, :, 0],
            last_row[:, :, :, side_cells - 1],
        ],
        0,
    )
    corner_points = jnp.transpose(corner_points, (3, 0, 1, 2, 4))
    all_edges, all_pieces, all_points = (
        lax.all_gather(side_edges, "face", axis=0, tiled=True),
        lax.all_gather(seam_pieces, "face", axis=0, tiled=True),
        lax.all_gather(corner_points, "face", axis=0, tiled=True),
    )
    all_edges = all_edges.reshape((-1,) + all_edges.shape[2:])
    all_pieces = all_pieces.reshape((-1,) + all_pieces.shape[2:])
    all_points = all_points.reshape((-1,) + all_points.shape[2:])
    above_face = seam_rows_table[:, 0]
    right_face = seam_rows_table[:, 1]
    below_face = seam_rows_table[:, 2]
    left_face = seam_rows_table[:, 3]
    side_columns = select_rows(
        all_edges, jnp.stack([left_face * 2 + 1, right_face * 2], 1).reshape(-1)
    )
    side_columns = side_columns.reshape((local_faces, 2) + side_columns.shape[1:])
    glued_pieces = select_rows(
        all_pieces, jnp.stack([above_face * 2 + 1, below_face * 2], 1).reshape(-1)
    )
    glued_pieces = glued_pieces.reshape((local_faces, 2) + glued_pieces.shape[1:])
    corner_cells = select_rows(
        all_points,
        jnp.stack(
            [
                corner_table[:, 0] * 4 + 3,
                corner_table[:, 1] * 4 + 2,
                corner_table[:, 2] * 4 + 1,
                corner_table[:, 3] * 4,
            ],
            1,
        ).reshape(-1),
    )
    corner_cells = corner_cells.reshape((local_faces, 4) + corner_cells.shape[1:])
    corner_cells = jnp.transpose(corner_cells, (1, 2, 3, 0, 4))
    seam_lines = lax.all_gather(glued_pieces, "tile", axis=4, tiled=True)
    seam_lines = jnp.transpose(seam_lines, (1, 2, 3, 0, 4, 5))
    at_first = tile_pos == 0
    at_last = tile_pos == tile_count - 1
    top_line = jnp.where(at_first, seam_lines[0], row_halo[:, :, :, 0])
    low_line = jnp.where(at_last, seam_lines[1], row_halo[:, :, :, strip_rows + 1])
    middle = jnp.concatenate(
        [top_line[:, :, :, None], row_halo[:, :, :, 1 : strip_rows + 1], low_line[:, :, :, None]], 3
    )
    left_edge = jnp.transpose(side_columns[:, 0], (1, 2, 0, 3, 4))
    right_edge = jnp.transpose(side_columns[:, 1], (1, 2, 0, 3, 4))
    left_edge = left_edge.at[:, :, :, 0].set(
        jnp.where(at_first, corner_cells[0], left_edge[:, :, :, 0])
    )
    left_edge = left_edge.at[:, :, :, strip_rows + 1].set(
        jnp.where(at_last, corner_cells[2], left_edge[:, :, :, strip_rows + 1])
    )
    right_edge = right_edge.at[:, :, :, 0].set(
        jnp.where(at_first, corner_cells[1], right_edge[:, :, :, 0])
    )
    right_edge = right_edge.at[:, :, :, strip_rows + 1].set(
        jnp.where(at_last, corner_cells[3], right_edge[:, :, :, strip_rows + 1])
    )
    return jnp.concatenate([left_edge[:, :, :, :, None], middle, right_edge[:, :, :, :, None]], 4)


def correlate(padded, kernel):
    return lax.conv_general_dilated(
        padded,
        kernel,
        (1, 1),
        "VALID",
        dimension_numbers=("NHWC", "HWIO", "NHWC"),
        preferred_element_type=jnp.float32,
    )


def tap_stack(padded, strip_rows, side_cells):
    return jnp.stack(
        [
            padded[:, tap_row : tap_row + strip_rows, tap_col : tap_col + side_cells]
            for tap_row in range(3)
            for tap_col in range(3)
        ],
        0,
    )


def flatten_pairs(values):
    return values.reshape((values.shape[0] * values.shape[1],) + values.shape[2:])


def on_device(saved_input, saved_pre, cotangent, first_weight, second_weight, seams, corners):
    samples = saved_input.shape[0]
    local_faces = saved_input.shape[1]
    strip_rows = saved_input.shape[2]
    side_cells = saved_input.shape[3]
    channels = saved_input.shape[4]
    grad_out = flatten_pairs(cotangent)
    pre_wide = flatten_pairs(saved_pre).astype(jnp.float32)
    back_one = jnp.transpose(first_weight[::-1, ::-1], (0, 1, 3, 2))
    back_two = jnp.transpose(second_weight[::-1, ::-1], (0, 1, 3, 2))
    padded = glue_faces(jnp.stack([saved_input, cotangent], 0), seams, corners)
    padded_input = flatten_pairs(padded[0])
    padded_grad = flatten_pairs(padded[1])
    grad_hidden = correlate(padded_grad, back_two)
    logistic = jax.nn.sigmoid(pre_wide)
    grad_pre = (grad_hidden * (logistic * (1.0 + pre_wide * (1.0 - logistic)))).astype(jnp.bfloat16)
    shaped_pre = grad_pre.reshape(saved_input.shape)
    padded_pre = flatten_pairs(glue_faces(shaped_pre[None], seams, corners)[0])
    grad_input = (grad_out.astype(jnp.float32) + correlate(padded_pre, back_one)).astype(
        jnp.bfloat16
    )
    grad_first = jnp.einsum(
        "kbrnc,brnd->kcd",
        tap_stack(padded_input, strip_rows, side_cells),
        grad_pre,
        preferred_element_type=jnp.float32,
    )
    tile_count = lax.axis_size("tile")
    face_count = lax.axis_size("face")
    scale_factor = 1.0 / math.sqrt(samples * face_count * local_faces * side_cells * side_cells)
    grad_first = (grad_first * scale_factor).reshape(3, 3, channels, channels)
    in_block = channels // tile_count
    out_block = channels // face_count
    shaped = grad_first.reshape(3, 3, tile_count, in_block, face_count, out_block)
    arranged = jnp.transpose(shaped, (4, 2, 0, 1, 3, 5)).reshape(
        face_count * tile_count, 3, 3, in_block, out_block
    )
    summed = lax.psum_scatter(arranged, ("face", "tile"), scatter_dimension=0, tiled=True)
    first_out = summed.reshape(3, 3, in_block, out_block)
    return (grad_input.reshape(saved_input.shape), first_out)


def solution(mesh):
    in_specs = (
        P(None, "face", "tile", None, None),
        P(None, "face", "tile", None, None),
        P(None, "face", "tile", None, None),
        P(),
        P(),
        P("face", None),
        P("face", None),
    )
    out_specs = (P(None, "face", "tile", None, None), P(None, None, "tile", "face"))
    return jax.shard_map(
        on_device, mesh=mesh, in_specs=in_specs, out_specs=out_specs, check_vma=False
    )
```

profile of v0, /device:TPU:6, one launch (start us, length us, event | category | flops | bytes accessed | tf_op | source)
XLA Modules:
  0.0 1498.2 jit_solution(13260086857045921069)
XLA Ops:
  7.2 1.1 fusion.44
  8.4 11.1 collective-permute-start.1
  19.5 1.9 collective-permute-start
  21.4 0.9 multiply_add_fusion
  22.3 0.9 multiply_add_fusion.3
  23.7 5.6 collective-permute-done
  29.4 0.9 maximum_select_fusion
  30.4 34.3 %all_gather.24 = bf16[32,2,2,1,3,256]{5,2,4,3,1,0:T(2,128)(2,1)S(1)} all-gather(bf16[4,2,2,1,3,256]{5,2,4,3,1,0:T(2,128)(2,1)S(1)} %copy.491), channel_id=1, replica_groups=mesh['face'=8,'tile'=64] {'face'}, dimensions={0}, use_global_device_ids=true | all-gather | bytes 221184 | tf_op jit(solution)/shard_map/all_gather | solution.py:69
  64.8 0.2 reshape_reshape.39
  65.0 0.2 convolution_convert_fusion
  65.3 387.5 %all-reduce.5.cloned.1.call-done = bf16[2,2,1,4,64,256]{5,4,3,1,2,0:T(8,128)(2,1)} async-done(((bf16[2,2,1,4,64,256]{5,4,3,1,2,0:T(8,128)(2,1)}), bf16[2,2,1,4,64,256]{5,4,3,1,2,0:T(8,128)(2,1)}) %all-reduce.5.cloned.1.call-update) | async-done | bytes 524304 | tf_op jit(solution)/shard_map/psum | solution.py:24
  452.8 1.1 fusion.46
  454.0 34.2 %all_gather.25 = bf16[32,4,2,1,256]{4,1,3,2,0:T(4,128)(2,1)S(1)} all-gather(bf16[4,4,2,1,256]{4,1,3,2,0:T(4,128)(2,1)S(1)} %copy.496), channel_id=1, replica_groups=mesh['face'=8,'tile'=64] {'face'}, dimensions={0}, use_global_device_ids=true | all-gather | bytes 147456 | tf_op jit(solution)/shard_map/all_gather | solution.py:71
  488.8 34.2 %all_gather.26 = bf16[32,2,2,1,1,256]{5,4,0,2,3,1:T(2,128)(2,1)S(1)} all-gather(bf16[4,2,2,1,1,256]{5,4,0,2,3,1:T(2,128)(2,1)S(1)} %maximum_bitcast_fusion.3), channel_id=1, replica_groups=mesh['face'=8,'tile'=64] {'face'}, dimensions={0}, use_global_device_ids=true | all-gather | bytes 73728 | tf_op jit(solution)/shard_map/all_gather | solution.py:70
  523.3 63.4 %all_gather.27 = bf16[4,2,2,1,64,256]{5,0,3,2,1,4:T(4,128)(2,1)S(1)} all-gather(bf16[4,2,2,1,1,256]{5,0,3,2,1,4:T(4,128)(2,1)S(1)} %copy.506), channel_id=1, replica_groups=mesh['face'=8,'tile'=64] {'tile'}, dimensions={4}, use_global_device_ids=true | all-gather | bytes 532480 | tf_op jit(solution)/shard_map/all_gather | solution.py:102
  587.1 0.5 pad_maximum_fusion
  588.1 0.2 fusion.3
  588.3 0.2 copy-done.10
  588.6 0.5 convolution_select_fusion.1
  589.1 0.3 copy.518
  589.5 0.8 fusion.12
  590.3 0.7 copy.650
  591.0 1.9 collective-permute-start.3
  592.9 2.4 collective-permute-start.2
  595.6 5.9 collective-permute-done.2
  601.5 0.7 copy-done.3
  602.2 1.7 maximum_select_fusion.1
  603.9 1.8 bitcast_multiply_fusion
  605.7 4.8 reshape_reshape.51
  610.5 9.8 copy.563
  620.3 0.9 copy-done.4
  621.2 0.8 pad_maximum_fusion.8
  622.0 34.2 %all_gather.28 = bf16[32,2,1,1,3,256]{5,1,4,3,2,0:T(2,128)(2,1)S(1)} all-gather(bf16[4,2,1,1,3,256]{5,1,4,3,2,0:T(2,128)(2,1)S(1)} %copy.520), channel_id=1, replica_groups=mesh['face'=8,'tile'=64] {'face'}, dimensions={0}, use_global_device_ids=true | all-gather | bytes 110592 | tf_op jit(solution)/shard_map/all_gather | solution.py:69
  656.6 327.2 %all-reduce.7.cloned.1.call-done = bf16[2,1,1,4,64,256]{5,4,3,2,1,0:T(8,128)(2,1)} async-done(((bf16[2,1,1,4,64,256]{5,4,3,2,1,0:T(8,128)(2,1)}), bf16[2,1,1,4,64,256]{5,4,3,2,1,0:T(8,128)(2,1)}) %all-reduce.7.cloned.1.call-update) | async-done | bytes 262160 | tf_op jit(solution)/shard_map/psum | solution.py:24
  983.8 1.0 fusion.47
  984.9 34.3 %all_gather.29 = bf16[32,4,1,1,256]{4,1,3,2,0:T(4,128)(2,1)S(1)} all-gather(bf16[4,4,1,1,256]{4,1,3,2,0:T(4,128)(2,1)S(1)} %copy.525), channel_id=1, replica_groups=mesh['face'=8,'tile'=64] {'face'}, dimensions={0}, use_global_device_ids=true | all-gather | bytes 73728 | tf_op jit(solution)/shard_map/all_gather | solution.py:71
  1019.6 34.4 %all_gather.30 = bf16[32,2,1,1,1,256]{5,4,0,3,2,1:T(2,128)(2,1)S(1)} all-gather(bf16[4,2,1,1,1,256]{5,4,0,3,2,1:T(2,128)(2,1)S(1)} %maximum_bitcast_fusion.6), channel_id=1, replica_groups=mesh['face'=8,'tile'=64] {'face'}, dimensions={0}, use_global_device_ids=true | all-gather | bytes 36864 | tf_op jit(solution)/shard_map/all_gather | solution.py:70
  1054.3 62.2 %all_gather.31 = bf16[4,2,1,1,64,256]{5,0,3,2,1,4:T(4,128)(2,1)S(1)} all-gather(bf16[4,2,1,1,1,256]{5,0,3,2,1,4:T(4,128)(2,1)S(1)} %copy.533), channel_id=1, replica_groups=mesh['face'=8,'tile'=64] {'tile'}, dimensions={4}, use_global_device_ids=true | all-gather | bytes 266240 | tf_op jit(solution)/shard_map/all_gather | solution.py:102
  1116.6 0.9 fusion.31
  1117.6 1.1 maximum_bitcast_fusion
  1119.1 0.2 fusion.4
  1119.3 0.8 copy-done.9
  1120.1 0.5 convolution_select_fusion
  1120.7 0.3 copy.542
  1121.0 0.3 fusion.10
  1121.3 0.7 copy.635
  1122.0 368.4 %all-reduce.9.cloned.1.call-done = f32[512,3,3,4,32]{4,3,2,1,0:T(4,128)} async-done(((f32[512,3,3,4,32]{4,3,2,1,0:T(4,128)}), f32[512,3,3,4,32]{4,3,2,1,0:T(4,128)}) %all-reduce.9.cloned.1.call-update) | async-done | bytes 2359312
  1490.4 1.3 dynamic-slice_bitcast_fusion
  (129 shorter events, 4.5 us)
Async XLA Ops:
  7.2 581.2 %copy-start = (bf16[3,3,256,256]{3,2,1,0:T(8,128)(2,1)S(1)}, bf16[3,3,256,256]{3,2,1,0:T(8,128)(2,1)}, u32[]{:S(2)}) copy-start(bf16[3,3,256,256]{3,2,1,0:T(8,128)(2,1)} %param.27) | copy-start | bytes 3538948
  7.2 22.1 %copy-start.1 = (bf16[1,4,1,64,256]{4,3,2,1,0:T(8,128)(2,1)S(1)}, bf16[1,4,1,64,256]{4,3,2,1,0:T(8,128)(2,1)}, u32[]{:S(2)}) copy-start(bf16[1,4,1,64,256]{4,3,2,1,0:T(8,128)(2,1)} %param.25) | copy-start | bytes 393220
  7.2 22.1 %copy-start.5 = (bf16[1,4,1,64,256]{4,3,2,1,0:T(8,128)(2,1)S(1)}, bf16[1,4,1,64,256]{4,3,2,1,0:T(8,128)(2,1)}, u32[]{:S(2)}) copy-start(bf16[1,4,1,64,256]{4,3,2,1,0:T(8,128)(2,1)} %param.23) | copy-start | bytes 393220
  7.2 445.6 %all-reduce.5.cloned.1.call-start = ((), (), s32[]{:S(2)}) async-start(), calls=%async_computation | async-start | bytes 1048576 | tf_op jit(solution)/shard_map/psum | solution.py:24
  8.4 15.3 %collective-permute-start.1 = (bf16[2,1,4,1,64,256]{5,4,2,3,1,0:T(8,128)(2,1)S(1)}, bf16[2,1,4,1,64,256]{5,4,2,3,1,0:T(8,128)(2,1)S(1)}, u32[]{:S(2)}, u32[]{:S(2)}) collective-permute-start(bf16[2,1,4,1,64,256]{5,4,2,3,1,0:T(8,128)(2,1)S(1)} %get-tuple-element.140), channel_id=1, source_target_pairs={{1,0},{2,1},{3,2},{4,3},{5,4},{6,5},{7,6},{8,7},{9,8},{10,9},{11,1... | collective-permute-start | bytes 786440 | tf_op jit(solution)/shard_map/ppermute | solution.py:17
  19.5 9.8 collective-permute-start
  30.3 953.5 %all-reduce.7.cloned.1.call-start = ((), (), s32[]{:S(2)}) async-start(), calls=%async_computation.1 | async-start | bytes 524288 | tf_op jit(solution)/shard_map/psum | solution.py:24
  587.9 0.7 copy-start.10
  588.6 0.9 copy-start.7
  590.2 5.3 copy-start.6
  591.0 29.3 %collective-permute-start.3 = (bf16[1,1,4,1,64,256]{5,4,2,3,1,0:T(8,128)(2,1)}, bf16[1,1,4,1,64,256]{5,4,2,3,1,0:T(8,128)(2,1)}, u32[]{:S(2)}, u32[]{:S(2)}) collective-permute-start(bf16[1,1,4,1,64,256]{5,4,2,3,1,0:T(8,128)(2,1)} %bitcast.257.clone.2), channel_id=1, source_target_pairs={{1,0},{2,1},{3,2},{4,3},{5,4},{6,5},{7,6},{8,7},{9,8},{10,9},{11,1... | collective-permute-start | bytes 393224 | tf_op jit(solution)/shard_map/ppermute | solution.py:17
  592.9 8.6 collective-permute-start.2
  595.6 5.9 copy-start.8
  601.5 0.7 copy-start.3
  603.8 886.5 %all-reduce.9.cloned.1.call-start = ((), (), s32[]{:S(2)}) async-start(), calls=%async_computation.2 | async-start | bytes 18874368
  620.3 0.9 copy-start.4
  1118.8 1.3 copy-start.9
  1120.1 0.9 copy-start.2
Sparse Core Ops, SparseCore 0:
  30.4 422.2 all-reduce.4
  604.0 379.7 all-reduce.6
  989.2 501.1 all-reduce.8
where the time goes:
time: 1500 us
  waiting for transfers between devices  1090 us (73%)
  blocking collectives  331 us (22%)
  local copies, waits for them, and re-layouts  25.6 us (2%)
  starting transfers between devices  17.5 us (1%)
    psum x2, waiting for transfers between devices, broadcast(): return lax.psum(jnp.where(mine, array, jnp.zeros_like(array)), axis)  715 us
    unnamed x4, waiting for transfers between devices  368 us
    all_gather x2, blocking collectives, glue_faces(): seam_lines = lax.all_gather(glued_pieces, 'tile', axis=4, tiled=True)  126 us
    all_gather x2, blocking collectives, glue_faces(): lax.all_gather(seam_pieces, 'face', axis=0, tiled=True)  68.6 us
    all_gather x2, blocking collectives, glue_faces(): lax.all_gather(side_edges, 'face', axis=0, tiled=True)  68.5 us
    all_gather x2, blocking collectives, glue_faces(): lax.all_gather(corner_points, 'face', axis=0, tiled=True)  68.5 us
  transfers between devices with their start and end apart: 7, of which 5 were waited for; matrix products, arithmetic and copies ran while one was open for 2% of the time, Pallas kernels for 0%

commit v1 on v0

v1 whole, which is shorter than its diff:
```python
import functools
import math

import jax
import jax.numpy as jnp
import numpy as np
from jax import lax
from jax.experimental import pallas as pl
from jax.experimental.pallas import tpu as pltpu
from jax.sharding import Mesh
from jax.sharding import PartitionSpec as P

FACE = ("xh", "y")
TILE = ("xl", "z", "c")
CHIP = ("xl", "z")
GAP = 16
SIDE = 32
SEAM_AT = 26
VMEM = 40 * 2**20


def params():
    return pltpu.CompilerParams(vmem_limit_bytes=VMEM)


def whole(n):
    return [pl.BlockSpec(memory_space=pltpu.VMEM)] * n


SMEM = pl.BlockSpec(memory_space=pltpu.SMEM)


def pick_kernel(faces, want_ref, table_ref, out_ref):
    for i in range(faces):
        out_ref[i] = table_ref[want_ref[i]]


def one_hot(index, width):
    rows = index.shape[0]
    return jnp.where(lax.broadcasted_iota(jnp.int32, (rows, width), 1) == index, 1.0, 0.0).astype(jnp.bfloat16)


def grad_pre_kernel(
    local, side, blocks, flags_ref, index_ref, place_ref, table_ref, gfar_ref, near_ref, own_ref, part_ref,
    gb_ref, wrap_ref, weight_ref, out_ref, g_pad, p_pad, tails,
):
    pitch = side + 2 * GAP
    row = local * pitch
    px_blocks, ch_blocks = blocks
    px, ch = side // px_blocks, out_ref.shape[-1] // ch_blocks
    core, wrap_a, wrap_b = flags_ref[0], flags_ref[1], flags_ref[2]
    cells = jnp.dot(one_hot(index_ref[...], table_ref.shape[0]), table_ref[...], preferred_element_type=jnp.float32)
    cells = cells.astype(jnp.bfloat16)
    tails[...] = jnp.dot(
        one_hot(place_ref[...], cells.shape[0]), cells, preferred_element_type=jnp.float32
    ).astype(jnp.bfloat16)

    def put(pad, slot, source, face, tail_at):
        at = pl.multiple_of(slot * row + face * pitch, 16)
        pad[pl.ds(at + GAP, side), :] = source[face]
        tail = pl.multiple_of((tail_at + slot * local + face) * 2 * GAP, 16)
        pad[pl.ds(at, GAP), :] = tails[pl.ds(tail, GAP), :]
        pad[pl.ds(at + GAP + side, GAP), :] = tails[pl.ds(tail + GAP, GAP), :]

    def put_wrap(pad, slot, which, face):
        at = pl.multiple_of(slot * row + face * pitch + GAP, 16)
        for b in range(px_blocks * ch_blocks):
            i, j = divmod(b, ch_blocks)
            pad[pl.ds(at + i * px, px), j * ch : (j + 1) * ch] = wrap_ref[b, face, which]

    g_sources = (gfar_ref, near_ref.at[0], own_ref.at[0], part_ref.at[0], gb_ref)
    p_sources = (near_ref.at[1], own_ref.at[1], part_ref.at[1])
    slot_of = lambda role, last: jnp.where(core == 0, role, last - role)
    for face in range(local):
        for role, source in enumerate(g_sources):
            put(g_pad, slot_of(role, 4), source, face, 0)
        for role, source in enumerate(p_sources):
            put(p_pad, slot_of(role, 2), source, face, 5 * local)

    @pl.when(wrap_a == 1)
    def _():
        for face in range(local):
            put_wrap(g_pad, slot_of(0, 4), 0, face)
            put_wrap(g_pad, slot_of(1, 4), 1, face)
            put_wrap(p_pad, slot_of(0, 2), 2, face)

    @pl.when(wrap_b == 1)
    def _():
        for face in range(local):
            put_wrap(g_pad, slot_of(4, 4), 0, face)

    for slot in range(3):
        grad = conv_rows(g_pad, slot * row, row, weight_ref)
        pre = p_pad[slot * row : (slot + 1) * row, :].astype(jnp.float32)
        logistic = jax.nn.sigmoid(pre)
        slope = logistic * (1.0 + pre * (1.0 - logistic))
        out_ref[slot * row : (slot + 1) * row, :] = (grad * slope).astype(jnp.bfloat16)


def conv_rows(pad, start, row, weight_ref):
    sums = []
    for c in range(3):
        total = None
        for r in range(3):
            rows = pad[start + (2 - r) * row : start + (3 - r) * row, :]
            term = lax.dot_general(
                rows, weight_ref[r, c], (((1,), (1,)), ((), ())), preferred_element_type=jnp.float32
            )
            total = term if total is None else total + term
        sums.append(total)
    return pltpu.roll(sums[2], 1, 0) + sums[1] + pltpu.roll(sums[0], row - 1, 0)


def grad_input_kernel(local, side, pre_ref, own_ref, weight_ref, out_ref):
    pitch = side + 2 * GAP
    grad = conv_rows(pre_ref, 0, local * pitch, weight_ref)
    for face in range(local):
        at = face * pitch + GAP
        own = own_ref[face].astype(jnp.float32)
        out_ref[face] = (own + grad[at : at + side, :]).astype(jnp.bfloat16)


def grad_first_kernel(row, flags_ref, x_ref, pre_ref, swapped_ref, out_ref, rows4):
    core = flags_ref[0]
    rows4[pl.ds(pl.multiple_of(core * row, 16), 3 * row), :] = pre_ref[...]
    rows4[pl.ds(pl.multiple_of((1 - core) * 3 * row, 16), row), :] = swapped_ref[...]
    dests, _, width, half = out_ref.shape
    for r in range(3):
        lines = rows4[(2 - r) * row : (4 - r) * row, :]
        terms = jnp.dot(x_ref[...], lines, preferred_element_type=jnp.float32)
        for c in range(3):
            turned = terms[c * half : (c + 1) * half, :].T.astype(jnp.bfloat16)
            for d in range(dests):
                out_ref[d, 3 * r + c] = turned[d * width : (d + 1) * width, :]


def on_device(sizes, saved_input, saved_pre, cotangent, first_weight, second_weight, seams, corners):
    nxh, ny, nxl, nz, nc = sizes
    nface, ntile, nchip = nxh * ny, nxl * nz * nc, nxl * nz
    x, p, g = saved_input[0, :, 0], saved_pre[0, :, 0], cotangent[0, :, 0]
    local, side, channels = x.shape
    faces = nface * local
    pitch = side + 2 * GAP
    row = local * pitch
    bf = jnp.bfloat16
    core = lax.axis_index("c")
    chip = lax.axis_index(CHIP)

    t_all = range(ntile)
    out = lambda t: t + 1 if t % 2 else t - 1
    far = lambda t: t + 2 if t % 2 else t - 2
    back = lambda t: t - 2 if t % 2 else t + 2
    pairs = lambda source: [(source(t) % ntile, t) for t in t_all]
    gp = jnp.stack([g, p], 0)
    part = lax.ppermute(jnp.stack([g, p, x], 0), "c", [(0, 1), (1, 0)])
    near = lax.ppermute(gp, TILE, pairs(out))
    gfar = lax.ppermute(g, TILE, pairs(far))
    gb = lax.ppermute(g, TILE, pairs(back))

    top = chip < nchip // 2
    wrap_a = jnp.where(core == 0, chip == 0, chip == nchip - 1)
    wrap_b = jnp.where(core == 0, chip == nchip - 1, chip == 0)
    flags = jnp.stack([core, wrap_a.astype(jnp.int32), wrap_b.astype(jnp.int32)])

    ends = lambda a: [a[:, 0:2], a[:, side - 2 : side]]
    tips = lambda a: [a[:, 0:1], a[:, side - 1 : side]]
    seam_cell = jnp.pad(seams.astype(bf)[:, None, :], ((0, 0), (0, SIDE - SEAM_AT - 1), (0, channels - 4)))
    cells = jnp.concatenate(
        [*ends(gfar), *ends(near[0]), *ends(g), *ends(part[0]), *ends(gb), *tips(near[1]), *tips(p), *tips(part[1]), seam_cell],
        1,
    )
    px_blocks = 4
    ch_blocks = nface // px_blocks
    px, ch = side // px_blocks, channels // ch_blocks
    holds_a = (core == 0) == top
    rows3 = jnp.where(holds_a, jnp.stack([gfar, near[0], near[1]], 0), gb[None])
    pieces = jnp.transpose(
        rows3.reshape(3, local, px_blocks, px, ch_blocks, ch), (2, 4, 1, 0, 3, 5)
    )
    halves = pieces.reshape(nface, local, ch_blocks, 3 * px // ch_blocks, ch)
    pieces = jnp.concatenate([halves[:, :, i] for i in range(ch_blocks)], -1)
    sent = jnp.concatenate([jnp.broadcast_to(cells[None], (nface,) + cells.shape), pieces], 2)
    table = lax.all_to_all(sent, FACE, 0, 0, tiled=True).reshape(faces, -1, channels)

    all_seams = table[:, SEAM_AT, :4].astype(jnp.int32)
    want = jnp.where(top, all_seams[:, 0], all_seams[:, 2])
    count = table.shape[1] - SIDE
    picked = pl.pallas_call(
        functools.partial(pick_kernel, faces),
        out_shape=jax.ShapeDtypeStruct((faces, count, channels), bf),
        in_specs=[SMEM, *whole(1)],
        out_specs=whole(1)[0],
        compiler_params=params(),
        name="pick",
    )(want, table[:, SIDE:])
    wrapped = lax.all_to_all(picked.reshape(nface, local, count, channels), FACE, 0, 0, tiled=True)
    wrapped = jnp.concatenate(
        [wrapped[..., i * ch : (i + 1) * ch] for i in range(ch_blocks)], 2
    ).reshape(nface, local, 3, px, ch)

    first = jnp.where(top, 0, 2)
    turn = lambda n: jnp.where(core == 0, np.arange(n), n - 1 - np.arange(n))
    inner = jnp.stack([seams[:, 3], seams[:, 1]], 1)
    outer = lax.dynamic_slice_in_dim(corners, first, 2, 1)
    beyond = lambda flag: jnp.where(flag, outer, inner)
    by_role = jnp.stack([beyond(wrap_a), beyond(wrap_a), inner, inner, beyond(wrap_b)], 0)
    g_role, p_role = turn(5), turn(3)
    g_face = jnp.where(core == 0, by_role, by_role[::-1])
    p_by_role = by_role[1:4]
    p_face = jnp.where(core == 0, p_by_role, p_by_role[::-1])
    g_index = (
        g_face[..., None] * SIDE + g_role[:, None, None, None] * 4 + np.array([[2, 3], [0, 1]], np.int32)
    ).reshape(-1)
    p_index = (
        p_face * SIDE + 20 + p_role[:, None, None] * 2 + np.array([1, 0], np.int32)
    ).reshape(-1)
    cells_held = 128
    index = jnp.concatenate([g_index, p_index])
    index = jnp.pad(index, (0, cells_held - index.shape[0]))[:, None].astype(jnp.int32)
    place = np.full((8 * local, 2, GAP), -1, np.int32)
    for i in range(5 * local):
        place[i, 0, GAP - 2 :] = (4 * i, 4 * i + 1)
        place[i, 1, :2] = (4 * i + 2, 4 * i + 3)
    for i in range(3 * local):
        at = 20 * local + 2 * i
        place[5 * local + i, 0, GAP - 1] = at
        place[5 * local + i, 1, 0] = at + 1
    place = jnp.asarray(place.reshape(-1, 1))

    grad_pre = pl.pallas_call(
        functools.partial(grad_pre_kernel, local, side, (px_blocks, ch_blocks)),
        out_shape=jax.ShapeDtypeStruct((3 * row, channels), bf),
        in_specs=[SMEM, *whole(10)],
        out_specs=whole(1)[0],
        scratch_shapes=[
            pltpu.VMEM((5 * row, channels), bf),
            pltpu.VMEM((3 * row, channels), bf),
            pltpu.VMEM((8 * local * 2 * GAP, channels), bf),
        ],
        compiler_params=params(),
        cost_estimate=pl.CostEstimate(flops=2 * 27 * row * channels**2, bytes_accessed=4 * 2**20, transcendentals=3 * row * channels),
        name="grad_pre",
    )(flags, index, place, table[:, :SIDE].reshape(faces * SIDE, channels), gfar, near, gp, part, gb, wrapped, second_weight)

    lacking = jnp.where(core == 0, grad_pre[:row], grad_pre[2 * row :])
    swapped = lax.ppermute(lacking, "c", [(0, 1), (1, 0)])

    grad_input = pl.pallas_call(
        functools.partial(grad_input_kernel, local, side),
        out_shape=jax.ShapeDtypeStruct((local, side, channels), bf),
        in_specs=whole(3),
        out_specs=whole(1)[0],
        compiler_params=params(),
        cost_estimate=pl.CostEstimate(flops=2 * 9 * row * channels**2, bytes_accessed=2 * 2**20, transcendentals=0),
        name="grad_input",
    )(grad_pre, g, first_weight)

    half = channels // nc
    per_tile = channels // ntile
    both = jnp.where(core == 0, jnp.stack([x, part[2]], 0), jnp.stack([part[2], x], 0))
    shifted = jnp.stack(
        [jnp.pad(both, ((0, 0), (0, 0), (GAP + 1 - c, GAP - 1 + c), (0, 0))) for c in range(3)], 0
    ).reshape(3, 2 * row, channels)
    kept = np.arange(half)
    chosen = (kept // per_tile) * (nc * per_tile) + kept % per_tile
    choose = (chosen[:, None] + core * per_tile == np.arange(channels)[None, :]).astype(bf)
    x_turned = lax.dot_general(
        choose, shifted, (((1,), (2,)), ((), ())), preferred_element_type=jnp.float32
    ).astype(bf)
    x_turned = jnp.transpose(x_turned, (1, 0, 2)).reshape(3 * half, 2 * row)

    width = channels // nface
    parts = pl.pallas_call(
        functools.partial(grad_first_kernel, row),
        out_shape=jax.ShapeDtypeStruct((nface, 9, width, half), bf),
        in_specs=[SMEM, *whole(3)],
        out_specs=whole(1)[0],
        scratch_shapes=[pltpu.VMEM((4 * row, channels), bf)],
        compiler_params=params(),
        cost_estimate=pl.CostEstimate(flops=2 * 9 * half * 2 * row * channels, bytes_accessed=2**20, transcendentals=0),
        name="grad_first",
    )(flags, x_turned, grad_pre, swapped)
    scale_factor = 1.0 / math.sqrt(faces * ntile * side)
    got = lax.all_to_all(parts, FACE, 0, 0, tiled=True)
    total = jnp.sum(got.astype(jnp.float32), 0) * scale_factor
    total = jnp.transpose(total.reshape(9 * width, half)).reshape(nchip, per_tile, 9 * width)
    got = lax.all_to_all(total, CHIP, 0, 0, tiled=True)
    total = jnp.sum(got, 0).reshape(per_tile, 9, width)
    first_out = jnp.transpose(total, (1, 0, 2)).reshape(3, 3, per_tile, width)
    return grad_input.reshape(saved_input.shape), first_out


def solution(mesh, sizes=(2, 4, 2, 16, 2)):
    fine = Mesh(mesh.devices.reshape(sizes), FACE + TILE)
    field = P(None, FACE, TILE, None, None)
    return jax.shard_map(
        functools.partial(on_device, sizes),
        mesh=fine,
        in_specs=(field, field, field, P(), P(), P(FACE, None), P(FACE, None)),
        out_specs=(field, P(None, None, TILE, FACE)),
        check_vma=False,
    )
```

time: 1500 us -> 115 us (0.08)
  waiting for transfers between devices: 1090 us -> 35.7 us
  blocking collectives: 331 us -> 15.2 us
  starting transfers between devices: 17.5 us -> 43.1 us
  local copies, waits for them, and re-layouts: 25.6 us -> 6.35 us
    psum x2 -> x0, waiting for transfers between devices: 715 us -> none  [broadcast(): return lax.psum(jnp.where(mine, array, jnp.zeros_like(array)), axis)]
    unnamed x4 -> x0, waiting for transfers between devices: 368 us -> none
    all_gather x8 -> x0, blocking collectives: 331 us -> none  [the longest x2 126 us: glue_faces(): seam_lines = lax.all_gather(glued_pieces, 'tile', axis=4, tiled=True)]
    all_to_all x0 -> x3, waiting for transfers between devices: none -> 34.5 us  [the longest x1 16 us: on_device(): got = lax.all_to_all(total, CHIP, 0, 0, tiled=True)]
    all_to_all x0 -> x3, starting transfers between devices: none -> 20.6 us  [the longest x1 7.57 us: on_device(): lax.all_to_all(sent, FACE, 0, 0, tiled=True).reshape(faces, -1, channels)]
    all_to_all x0 -> x1, blocking collectives: none -> 15.2 us  [on_device(): got = lax.all_to_all(parts, FACE, 0, 0, tiled=True)]
  transfers between devices with their start and end apart: 7 -> 8, of which waited for: 5 -> 5; matrix products, arithmetic and copies ran while one was open for 2% -> 5% of each run, Pallas kernels for 0% -> 1%
where the time goes in v1:
time: 115 us; the launch traced here: 113 us
  starting transfers between devices  43.1 us (37%)
  waiting for transfers between devices  35.7 us (31%)
  blocking collectives  15.2 us (13%)
  Pallas kernels  6.94 us (6%)
  local copies, waits for them, and re-layouts  6.35 us (6%)
  other arithmetic  3.86 us (3%)
  between operations  1.21 us (1%)
    all_to_all x1, waiting for transfers between devices, on_device(): got = lax.all_to_all(total, CHIP, 0, 0, tiled=True)  16 us
    all_to_all x1, blocking collectives, on_device(): got = lax.all_to_all(parts, FACE, 0, 0, tiled=True)  15.2 us
    all_to_all x1, waiting for transfers between devices, on_device(): lax.all_to_all(sent, FACE, 0, 0, tiled=True).reshape(faces, -1, channels)  12.5 us
    ppermute x1, starting transfers between devices, on_device(): gb = lax.ppermute(g, TILE, pairs(back))  9.76 us
    all_to_all x1, starting transfers between devices, on_device(): lax.all_to_all(sent, FACE, 0, 0, tiled=True).reshape(faces, -1, channels)  7.57 us
    all_to_all x1, starting transfers between devices, on_device(): got = lax.all_to_all(total, CHIP, 0, 0, tiled=True)  7.36 us
    all_to_all x1, waiting for transfers between devices, on_device(): lax.all_to_all(picked.reshape(nface, local, count, channels), FACE, 0, 0,...  6.04 us
    all_to_all x1, starting transfers between devices, on_device(): lax.all_to_all(picked.reshape(nface, local, count, channels), FACE, 0, 0,...  5.7 us
  transfers between devices with their start and end apart: 8, of which 5 were waited for; matrix products, arithmetic and copies ran while one was open for 5% of the time, Pallas kernels for 1%

profile of v1, /device:TPU:6, one launch (start us, length us, event | category | flops | bytes accessed | tf_op | source)
XLA Modules:
  0.0 112.9 jit_solution(13926439669921260254)
XLA Ops:
  0.7 4.0 %collective-permute-start = (bf16[4,64,256]{2,1,0:T(8,128)(2,1)}, bf16[4,64,256]{2,1,0:T(8,128)(2,1)S(1)}, u32[]{:S(2)}, u32[]{:S(2)}) collective-permute-start(bf16[4,64,256]{2,1,0:T(8,128)(2,1)} %bitcast.63), channel_id=1, source_target_pairs={{62,0},{3,1},{0,2},{5,3},{2,4},{7,5},{4,6},{9,7},{6,8},{11,9},{8,1... | collective-permute-start | bytes 393224 | tf_op jit(solution)/shard_map/ppermute | solution.py:157
  4.7 9.8 %collective-permute-start.3 = (bf16[4,64,256]{2,1,0:T(8,128)(2,1)}, bf16[4,64,256]{2,1,0:T(8,128)(2,1)S(1)}, u32[]{:S(2)}, u32[]{:S(2)}) collective-permute-start(bf16[4,64,256]{2,1,0:T(8,128)(2,1)} %bitcast.64), channel_id=1, source_target_pairs={{2,0},{63,1},{4,2},{1,3},{6,4},{3,5},{8,6},{5,7},{10,8},{7,9},{12,... | collective-permute-start | bytes 393224 | tf_op jit(solution)/shard_map/ppermute | solution.py:158
  14.4 1.0 pad_maximum_fusion.2.own_ref
  15.4 4.9 %collective-permute-start.1 = (bf16[2,4,64,256]{3,2,1,0:T(8,128)(2,1)S(1)}, bf16[2,4,64,256]{3,2,1,0:T(8,128)(2,1)S(1)}, u32[]{:S(2)}, u32[]{:S(2)}) collective-permute-start(bf16[2,4,64,256]{3,2,1,0:T(8,128)(2,1)S(1)} %pad_maximum_fusion.2.own_ref), channel_id=1, source_target_pairs={{63,0},{2,1},{1,2},{4,3},{3,4},{6,5},{5,6},{8,7},{7,8},{10,9},{9,1... | collective-permute-start | bytes 786440 | tf_op jit(solution)/shard_map/ppermute | solution.py:156
  20.4 1.1 pad_maximum_fusion
  21.4 1.9 %collective-permute-start.2 = (bf16[3,4,64,256]{3,2,1,0:T(8,128)(2,1)S(1)}, bf16[3,4,64,256]{3,2,1,0:T(8,128)(2,1)S(1)}, u32[]{:S(2)}, u32[]{:S(2)}) collective-permute-start(bf16[3,4,64,256]{3,2,1,0:T(8,128)(2,1)S(1)} %pad_maximum_fusion), channel_id=1, source_target_pairs={{0,1},{1,0},{2,3},{3,2},{4,5},{5,4},{6,7},{7,6},{8,9},{9,8},{10,11... | collective-permute-start | bytes 1179656 | tf_op jit(solution)/shard_map/ppermute | solution.py:155
  23.4 0.1 copy.154
  23.6 0.1 select_bitcast_fusion
  23.7 0.1 copy.102
  23.8 0.1 copy.101
  23.9 0.1 copy.104
  24.0 0.1 copy.106
  24.1 0.1 copy.108
  24.2 0.1 stack.80
  24.3 0.1 rev.6
  24.4 0.1 copy.109
  24.6 0.1 broadcast_add_fusion
  24.9 0.4 collective-permute-done.1.near_ref
  25.9 1.0 maximum_maximum_fusion
  26.9 7.6 %all-to-all-start = ((bf16[8,4,56,256]{3,2,1,0:T(8,128)(2,1)}), bf16[8,4,56,256]{3,2,1,0:T(8,128)(2,1)S(1)}, u32[]{:S(2)}, u32[]{:S(2)}) async-start(bf16[8,4,56,256]{3,2,1,0:T(8,128)(2,1)} %maximum_maximum_fusion), calls=%async_computation | async-start | bytes 1835008 | tf_op jit(solution)/shard_map/all_to_all | solution.py:183
  34.5 0.1 add.71
  34.6 0.1 fusion.11
  34.7 0.1 copy.110
  34.8 0.1 reshape.75
  34.9 0.1 pad_add_fusion.3
  35.0 0.1 copy.132.index_ref
  35.1 12.5 %all-to-all-done = bf16[8,4,56,256]{3,2,1,0:T(8,128)(2,1)S(1)} async-done(((bf16[8,4,56,256]{3,2,1,0:T(8,128)(2,1)}), bf16[8,4,56,256]{3,2,1,0:T(8,128)(2,1)S(1)}, u32[]{:S(2)}, u32[]{:S(2)}) %all-to-all-start) | async-done | bytes 917536 | tf_op jit(solution)/shard_map/all_to_all | solution.py:183
  47.7 0.1 copy.131
  47.8 1.3 %pick.1 = bf16[32,24,256]{2,1,0:T(8,128)(2,1)} custom-call(s32[32]{0:T(128)S(1)} %fusion.14.want_ref, bf16[32,24,256]{2,1,0:T(8,128)(2,1)S(1)} %slice.166.table_ref), custom_call_target="tpu_custom_call" | custom-call | tf_op jit(solution)/shard_map/pick/pallas_call | solution.py:188
  49.1 5.7 %all-to-all-start.1 = ((bf16[8,4,24,256]{3,2,1,0:T(8,128)(2,1)}), bf16[8,4,24,256]{3,2,1,0:T(8,128)(2,1)S(1)}, u32[]{:S(2)}, u32[]{:S(2)}) async-start(bf16[8,4,24,256]{3,2,1,0:T(8,128)(2,1)} %bitcast.26), calls=%async_computation.1 | async-start | bytes 786432 | tf_op jit(solution)/shard_map/all_to_all | solution.py:196
  54.8 0.1 pad_add_fusion.2.flags_ref
  54.9 1.1 %fusion.18 = (bf16[2,4,96,256]{3,2,1,0:T(8,128)(2,1)}, bf16[2,4,96,256]{3,2,1,0:T(8,128)(2,1)}, bf16[2,4,96,256]{3,2,1,0:T(8,128)(2,1)}) fusion(bf16[2,4,64,256]{3,2,1,0:T(8,128)(2,1)S(1)} %maximum_select_fusion.1), kind=kLoop, calls=%fused_computation.68 | loop fusion | bytes 1441792 | tf_op jit(solution)/shard_map/jit(_pad)/pad | solution.py:262
  56.2 6.0 %all-to-all-done.1 = bf16[8,4,24,256]{3,2,1,0:T(8,128)(2,1)S(1)} async-done(((bf16[8,4,24,256]{3,2,1,0:T(8,128)(2,1)}), bf16[8,4,24,256]{3,2,1,0:T(8,128)(2,1)S(1)}, u32[]{:S(2)}, u32[]{:S(2)}) %all-to-all-start.1) | async-done | bytes 393248 | tf_op jit(solution)/shard_map/all_to_all | solution.py:196
  62.4 1.3 %copy-done.2 = bf16[3,3,256,256]{3,2,1,0:T(8,128)(2,1)S(1)} copy-done((bf16[3,3,256,256]{3,2,1,0:T(8,128)(2,1)S(1)}, bf16[3,3,256,256]{3,2,1,0:T(8,128)(2,1)}, u32[]{:S(2)}) %copy-start.2) | copy-done | bytes 1179672
  63.6 3.0 %grad_pre.1.pre_ref = bf16[1152,256]{1,0:T(8,128)(2,1)S(1)} custom-call(s32[3]{0:T(128)S(1)} %pad_add_fusion.2.flags_ref, s32[128,1]{1,0:T(8,128)S(1)} %copy.132.index_ref, s32[1024,1]{1,0:T(8,128)S(1)} %copy-done.3, bf16[1024,256]{1,0:T(8,128)(2,1)S(1)} %bitcast.70, bf16[4,64,256]{2,1,0:T(8,128)(2,1)S(1)} %collective-permute-done.gfar_ref, ...), custom_call_target="tpu_custom_call" | custom-call | flops 1358954496 | bytes 4194304 | tf_op jit(solution)/shard_map/grad_pre/pallas_call | solution.py:230
  66.6 1.9 %collective-permute-start.4 = (bf16[384,256]{1,0:T(8,128)(2,1)S(1)}, bf16[384,256]{1,0:T(8,128)(2,1)S(1)}, u32[]{:S(2)}, u32[]{:S(2)}) collective-permute-start(bf16[384,256]{1,0:T(8,128)(2,1)S(1)} %slice_select_fusion), channel_id=1, source_target_pairs={{0,1},{1,0},{2,3},{3,2},{4,5},{5,4},{6,7},{7,6},{8,9},{9,8},{10,11... | collective-permute-start | bytes 589832 | tf_op jit(solution)/shard_map/ppermute | solution.py:246
  68.6 0.5 convolution_convert_fusion
  69.1 0.8 collective-permute-done.4.swapped_ref
  70.0 1.3 %grad_first.1 = bf16[8,9,32,128]{3,2,1,0:T(8,128)(2,1)S(1)} custom-call(s32[3]{0:T(128)S(1)} %pad_add_fusion.2.flags_ref, bf16[384,768]{1,0:T(8,128)(2,1)S(1)} %bitcast.69, bf16[1152,256]{1,0:T(8,128)(2,1)S(1)} %grad_pre.1.pre_ref, bf16[384,256]{1,0:T(8,128)(2,1)S(1)} %collective-permute-done.4.swapped_ref), custom_call_target="tpu_custom_call" | custom-call | flops 452984832 | bytes 1048576 | tf_op jit(solution)/shard_map/grad_first/pallas_call | solution.py:273
  71.3 15.2 %all_to_all.20 = bf16[8,9,32,128]{3,2,1,0:T(8,128)(2,1)S(1)} all-to-all(bf16[8,9,32,128]{3,2,1,0:T(8,128)(2,1)S(1)} %grad_first.1), channel_id=1, replica_groups=mesh['xh'=2,'y'=4,'xl'=2,'z'=16,'c'=2] {'xh','y'}, dimensions={0} | all-to-all | bytes 1179648 | tf_op jit(solution)/shard_map/all_to_all | solution.py:284
  86.5 0.1 convert_reduce_fusion
  86.7 0.1 copy.133
  86.8 0.7 reshape.83
  87.5 7.4 %all-to-all-start.3 = ((f32[32,4,288]{2,1,0:T(4,128)}), f32[32,4,288]{2,1,0:T(4,128)S(1)}, u32[]{:S(2)}, u32[]{:S(2)}) async-start(f32[32,4,288]{2,1,0:T(4,128)} %reshape.83), calls=%async_computation.3 | async-start | bytes 393216 | tf_op jit(solution)/shard_map/all_to_all | solution.py:287
  94.9 1.3 %grad_input.1 = bf16[4,64,256]{2,1,0:T(8,128)(2,1)} custom-call(bf16[1152,256]{1,0:T(8,128)(2,1)S(1)} %grad_pre.1.pre_ref, bf16[4,64,256]{2,1,0:T(8,128)(2,1)S(1)} %bitcast.68, bf16[3,3,256,256]{3,2,1,0:T(8,128)(2,1)S(1)} %copy-done.1), custom_call_target="tpu_custom_call" | custom-call | flops 452984832 | bytes 2097152 | tf_op jit(solution)/shard_map/grad_input/pallas_call | solution.py:248
  96.2 16.0 %all-to-all-done.3 = f32[32,4,288]{2,1,0:T(4,128)S(1)} async-done(((f32[32,4,288]{2,1,0:T(4,128)}), f32[32,4,288]{2,1,0:T(4,128)S(1)}, u32[]{:S(2)}, u32[]{:S(2)}) %all-to-all-start.3) | async-done | bytes 147488 | tf_op jit(solution)/shard_map/all_to_all | solution.py:287
  112.2 0.1 reshape.84
  112.3 0.6 copy.134
  (93 shorter events, 1.3 us)
Async XLA Ops:
  0.6 23.8 %copy-start.17 = (s32[5]{0:T(128)S(1)}, s32[5]{0:T(128)}, u32[]{:S(2)}) copy-start(s32[5]{0:T(128)} %constant.54.clone) | copy-start | bytes 64
  0.6 23.9 %copy-start.13 = (s32[2,2]{1,0:T(2,128)S(1)}, s32[2,2]{1,0:T(2,128)}, u32[]{:S(2)}) copy-start(s32[2,2]{1,0:T(2,128)} %constant.56.clone) | copy-start | bytes 52
  0.7 22.7 %copy-start = (bf16[1,4,1,64,256]{4,3,2,1,0:T(8,128)(2,1)S(1)}, bf16[1,4,1,64,256]{4,3,2,1,0:T(8,128)(2,1)}, u32[]{:S(2)}) copy-start(bf16[1,4,1,64,256]{4,3,2,1,0:T(8,128)(2,1)} %param.18) | copy-start | bytes 393220
  0.7 22.7 %copy-start.6 = (bf16[1,4,1,64,256]{4,3,2,1,0:T(8,128)(2,1)S(1)}, bf16[1,4,1,64,256]{4,3,2,1,0:T(8,128)(2,1)}, u32[]{:S(2)}) copy-start(bf16[1,4,1,64,256]{4,3,2,1,0:T(8,128)(2,1)} %param.17) | copy-start | bytes 393220
  0.7 22.9 %copy-start.11 = (s32[4,4]{1,0:T(4,128)S(1)}, s32[4,4]{1,0:T(4,128)}, u32[]{:S(2)}) copy-start(s32[4,4]{1,0:T(4,128)} %param.21) | copy-start | bytes 196
  0.7 22.9 %copy-start.12 = (s32[4,4]{1,0:T(4,128)S(1)}, s32[4,4]{1,0:T(4,128)}, u32[]{:S(2)}) copy-start(s32[4,4]{1,0:T(4,128)} %param.22) | copy-start | bytes 196
  0.7 24.0 %collective-permute-start = (bf16[4,64,256]{2,1,0:T(8,128)(2,1)}, bf16[4,64,256]{2,1,0:T(8,128)(2,1)S(1)}, u32[]{:S(2)}, u32[]{:S(2)}) collective-permute-start(bf16[4,64,256]{2,1,0:T(8,128)(2,1)} %bitcast.63), channel_id=1, source_target_pairs={{62,0},{3,1},{0,2},{5,3},{2,4},{7,5},{4,6},{9,7},{6,8},{11,9},{8,1... | collective-permute-start | bytes 393224 | tf_op jit(solution)/shard_map/ppermute | solution.py:157
  4.7 20.1 %collective-permute-start.3 = (bf16[4,64,256]{2,1,0:T(8,128)(2,1)}, bf16[4,64,256]{2,1,0:T(8,128)(2,1)S(1)}, u32[]{:S(2)}, u32[]{:S(2)}) collective-permute-start(bf16[4,64,256]{2,1,0:T(8,128)(2,1)} %bitcast.64), channel_id=1, source_target_pairs={{2,0},{63,1},{4,2},{1,3},{6,4},{3,5},{8,6},{5,7},{10,8},{7,9},{12,... | collective-permute-start | bytes 393224 | tf_op jit(solution)/shard_map/ppermute | solution.py:158
  15.4 9.8 %collective-permute-start.1 = (bf16[2,4,64,256]{3,2,1,0:T(8,128)(2,1)S(1)}, bf16[2,4,64,256]{3,2,1,0:T(8,128)(2,1)S(1)}, u32[]{:S(2)}, u32[]{:S(2)}) collective-permute-start(bf16[2,4,64,256]{3,2,1,0:T(8,128)(2,1)S(1)} %pad_maximum_fusion.2.own_ref), channel_id=1, source_target_pairs={{63,0},{2,1},{1,2},{4,3},{3,4},{6,5},{5,6},{8,7},{7,8},{10,9},{9,1... | collective-permute-start | bytes 786440 | tf_op jit(solution)/shard_map/ppermute | solution.py:156
  21.4 4.1 %collective-permute-start.2 = (bf16[3,4,64,256]{3,2,1,0:T(8,128)(2,1)S(1)}, bf16[3,4,64,256]{3,2,1,0:T(8,128)(2,1)S(1)}, u32[]{:S(2)}, u32[]{:S(2)}) collective-permute-start(bf16[3,4,64,256]{3,2,1,0:T(8,128)(2,1)S(1)} %pad_maximum_fusion), channel_id=1, source_target_pairs={{0,1},{1,0},{2,3},{3,2},{4,5},{5,4},{6,7},{7,6},{8,9},{9,8},{10,11... | collective-permute-start | bytes 1179656 | tf_op jit(solution)/shard_map/ppermute | solution.py:155
  26.9 7.6 %copy-start.16 = (s32[3]{0:T(128)S(1)}, s32[3]{0:T(128)}, u32[]{:S(2)}) copy-start(s32[3]{0:T(128)} %constant.55.clone) | copy-start | bytes 40
  26.9 7.7 %copy-start.14 = (s32[2]{0:T(128)S(1)}, s32[2]{0:T(128)}, u32[]{:S(2)}) copy-start(s32[2]{0:T(128)} %constant.57.clone) | copy-start | bytes 28
  26.9 8.2 %copy-start.15 = (s32[128,1]{0,1:T(1,128)S(1)}, s32[128,1]{0,1:T(1,128)}, u32[]{:S(2)}) copy-start(s32[128,1]{0,1:T(1,128)} %constant.59.clone) | copy-start | bytes 1540
  26.9 20.7 %all-to-all-start = ((bf16[8,4,56,256]{3,2,1,0:T(8,128)(2,1)}), bf16[8,4,56,256]{3,2,1,0:T(8,128)(2,1)S(1)}, u32[]{:S(2)}, u32[]{:S(2)}) async-start(bf16[8,4,56,256]{3,2,1,0:T(8,128)(2,1)} %maximum_maximum_fusion), calls=%async_computation | async-start | bytes 1835008 | tf_op jit(solution)/shard_map/all_to_all | solution.py:183
  47.6 1.5 %copy-start.4 = (bf16[8,4,56,256]{3,2,1,0:T(8,128)(2,1)}, bf16[8,4,56,256]{3,2,1,0:T(8,128)(2,1)S(1)}, u32[]{:S(2)}) copy-start(bf16[8,4,56,256]{3,2,1,0:T(8,128)(2,1)S(1)} %all-to-all-done) | copy-start | bytes 2752516
  47.7 7.2 %copy-start.7 = (bf16[1,4,1,64,256]{4,3,2,1,0:T(8,128)(2,1)S(1)}, bf16[1,4,1,64,256]{4,3,2,1,0:T(8,128)(2,1)}, u32[]{:S(2)}) copy-start(bf16[1,4,1,64,256]{4,3,2,1,0:T(8,128)(2,1)} %param.16) | copy-start | bytes 393220
  49.1 13.1 %all-to-all-start.1 = ((bf16[8,4,24,256]{3,2,1,0:T(8,128)(2,1)}), bf16[8,4,24,256]{3,2,1,0:T(8,128)(2,1)S(1)}, u32[]{:S(2)}, u32[]{:S(2)}) async-start(bf16[8,4,24,256]{3,2,1,0:T(8,128)(2,1)} %bitcast.26), calls=%async_computation.1 | async-start | bytes 786432 | tf_op jit(solution)/shard_map/all_to_all | solution.py:196
  54.8 1.3 %copy-start.5 = (bf16[8,4,56,256]{3,2,1,0:T(8,128)(2,1)S(1)}, bf16[8,4,56,256]{3,2,1,0:T(8,128)(2,1)}, u32[]{:S(2)}) copy-start(bf16[8,4,56,256]{3,2,1,0:T(8,128)(2,1)} %copy-done.4) | copy-start | bytes 2752516
  56.1 6.2 %copy-start.3 = (s32[1024,1]{1,0:T(8,128)S(1)}, s32[1024,1]{1,0:T(8,128)}, u32[]{:S(2)}) copy-start(s32[1024,1]{1,0:T(8,128)} %constant.58.clone.place_ref) | copy-start | bytes 12292
  62.4 1.3 %copy-start.2 = (bf16[3,3,256,256]{3,2,1,0:T(8,128)(2,1)S(1)}, bf16[3,3,256,256]{3,2,1,0:T(8,128)(2,1)}, u32[]{:S(2)}) copy-start(bf16[3,3,256,256]{3,2,1,0:T(8,128)(2,1)} %weight_ref.2) | copy-start | bytes 3538948
  63.6 4.9 %copy-start.8 = (bf16[2,4,96,256]{3,2,1,0:T(8,128)(2,1)S(1)}, bf16[2,4,96,256]{3,2,1,0:T(8,128)(2,1)}, u32[]{:S(2)}) copy-start(bf16[2,4,96,256]{3,2,1,0:T(8,128)(2,1)} %get-tuple-element.19) | copy-start | bytes 1179652
  63.6 4.9 %copy-start.9 = (bf16[2,4,96,256]{3,2,1,0:T(8,128)(2,1)S(1)}, bf16[2,4,96,256]{3,2,1,0:T(8,128)(2,1)}, u32[]{:S(2)}) copy-start(bf16[2,4,96,256]{3,2,1,0:T(8,128)(2,1)} %get-tuple-element.20) | copy-start | bytes 1179652
  63.6 5.0 %copy-start.10 = (bf16[2,4,96,256]{3,2,1,0:T(8,128)(2,1)S(1)}, bf16[2,4,96,256]{3,2,1,0:T(8,128)(2,1)}, u32[]{:S(2)}) copy-start(bf16[2,4,96,256]{3,2,1,0:T(8,128)(2,1)} %get-tuple-element.21) | copy-start | bytes 1179652
  66.6 3.3 %collective-permute-start.4 = (bf16[384,256]{1,0:T(8,128)(2,1)S(1)}, bf16[384,256]{1,0:T(8,128)(2,1)S(1)}, u32[]{:S(2)}, u32[]{:S(2)}) collective-permute-start(bf16[384,256]{1,0:T(8,128)(2,1)S(1)} %slice_select_fusion), channel_id=1, source_target_pairs={{0,1},{1,0},{2,3},{3,2},{4,5},{5,4},{6,7},{7,6},{8,9},{9,8},{10,11... | collective-permute-start | bytes 589832 | tf_op jit(solution)/shard_map/ppermute | solution.py:246
  86.5 8.3 %copy-start.1 = (bf16[3,3,256,256]{3,2,1,0:T(8,128)(2,1)S(1)}, bf16[3,3,256,256]{3,2,1,0:T(8,128)(2,1)}, u32[]{:S(2)}) copy-start(bf16[3,3,256,256]{3,2,1,0:T(8,128)(2,1)} %weight_ref.3) | copy-start | bytes 3538948
  87.5 24.7 %all-to-all-start.3 = ((f32[32,4,288]{2,1,0:T(4,128)}), f32[32,4,288]{2,1,0:T(4,128)S(1)}, u32[]{:S(2)}, u32[]{:S(2)}) async-start(f32[32,4,288]{2,1,0:T(4,128)} %reshape.83), calls=%async_computation.3 | async-start | bytes 393216 | tf_op jit(solution)/shard_map/all_to_all | solution.py:287

commit v2 on v1

v2 whole, which is shorter than its diff:
```python
import functools
import math

import jax
import jax.numpy as jnp
import numpy as np
from jax import lax
from jax.experimental import pallas as pl
from jax.experimental.pallas import tpu as pltpu
from jax.sharding import Mesh
from jax.sharding import PartitionSpec as P

FACE = ("xh", "y")
TILE = ("xl", "z", "c")
CHIP = ("xl", "z")
GAP = 16
CELLS = 8
SEAM_AT = 6
VMEM = 40 * 2**20


def whole(n):
    return [pl.BlockSpec(memory_space=pltpu.VMEM)] * n


def pick_kernel(faces, count, want_ref, table_ref, out_ref):
    for i in range(faces):
        out_ref[i] = table_ref[want_ref[i], :count]


def border_kernel(local, side, index_ref, cells_ref, g_ref, p_ref, own_ref, wrap_ref):
    rows, width = index_ref.shape[0], cells_ref.shape[0]
    where = lax.broadcasted_iota(jnp.int32, (rows, width), 1) == index_ref[...]
    tails = jnp.dot(
        jnp.where(where, 1.0, 0.0).astype(jnp.bfloat16), cells_ref[...], preferred_element_type=jnp.float32
    ).astype(jnp.bfloat16)
    for which, source in enumerate((g_ref, p_ref)):
        for face in range(local):
            at = (which * local + face) * GAP
            own_ref[which, face, :side] = source[face]
            own_ref[which, face, side:] = tails[at : at + GAP]
            at += 2 * local * GAP
            wrap_ref[which, face] = tails[at : at + GAP]


def send_kernel(local, side, blocks, flags_ref, own_ref, tails_ref, pieces_ref, near_ref, far_ref):
    px_blocks, ch_blocks = blocks
    px = side // px_blocks
    channels = own_ref.shape[-1]
    ch = channels // ch_blocks
    near, far = flags_ref[1], flags_ref[2]

    def put_wrap(out, which, face):
        for b in range(px_blocks * ch_blocks):
            i, j = divmod(b, ch_blocks)
            piece = pieces_ref[b, face]
            if ch_blocks == 1:
                part = piece[which * px : (which + 1) * px]
            else:
                part = piece[:, which * ch : (which + 1) * ch]
            out[i * px : (i + 1) * px, j * ch : (j + 1) * ch] = part
        out[side:, :] = tails_ref[which, face]

    @pl.when(near == 1)
    def _():
        for face in range(local):
            put_wrap(near_ref.at[0, face], 0, face)
            put_wrap(near_ref.at[1, face], 1, face)

    @pl.when(near == 0)
    def _():
        near_ref[...] = own_ref[...]

    @pl.when(far == 1)
    def _():
        for face in range(local):
            put_wrap(far_ref.at[face], 0, face)

    @pl.when(far == 0)
    def _():
        far_ref[...] = own_ref[0]


def grad_pre_kernel(local, side, flags_ref, own_ref, part_ref, near_ref, far_ref, weight_ref, out_ref, g_pad, p_pad):
    pitch = side + 2 * GAP
    row = local * pitch
    core = flags_ref[0]

    def put(pad, slot, source, face):
        at = pl.multiple_of(slot * row + face * pitch, 16)
        border = source[face, side:]
        pad[pl.ds(at, GAP), :] = border
        pad[pl.ds(at + GAP, side), :] = source[face, :side]
        pad[pl.ds(at + GAP + side, GAP), :] = border

    for face in range(local):
        for role, source in enumerate((far_ref, near_ref.at[0], own_ref.at[0], part_ref)):
            put(g_pad, jnp.where(core == 0, role, 3 - role), source, face)
        for role, source in enumerate((near_ref.at[1], own_ref.at[1])):
            put(p_pad, jnp.where(core == 0, role, 1 - role), source, face)
    for slot in range(2):
        grad = conv_rows(g_pad, slot * row, row, weight_ref)
        pre = p_pad[slot * row : (slot + 1) * row, :].astype(jnp.float32)
        logistic = jax.nn.sigmoid(pre)
        slope = logistic * (1.0 + pre * (1.0 - logistic))
        out_ref[slot * row : (slot + 1) * row, :] = (grad * slope).astype(jnp.bfloat16)


def conv_rows(pad, start, row, weight_ref):
    sums = []
    for c in range(3):
        total = None
        for r in range(3):
            at = start + (2 - r) * row
            rows = pad[pl.ds(at if isinstance(at, int) else pl.multiple_of(at, 16), row), :]
            term = lax.dot_general(
                rows, weight_ref[r, c], (((1,), (1,)), ((), ())), preferred_element_type=jnp.float32
            )
            total = term if total is None else total + term
        sums.append(total)
    return pltpu.roll(sums[2], 1, 0) + sums[1] + pltpu.roll(sums[0], row - 1, 0)


def four_rows(rows4, core, row, pre_ref, swapped_ref):
    rows4[pl.ds(pl.multiple_of(core * 2 * row, 16), 2 * row), :] = pre_ref[...]
    rows4[pl.ds(pl.multiple_of((1 - core) * 2 * row, 16), 2 * row), :] = swapped_ref[...]


def grad_input_kernel(local, side, flags_ref, pre_ref, swapped_ref, own_ref, weight_ref, out_ref, rows4):
    pitch = side + 2 * GAP
    row = local * pitch
    core = flags_ref[0]
    four_rows(rows4, core, row, pre_ref, swapped_ref)
    grad = conv_rows(rows4, core * row, row, weight_ref)
    for face in range(local):
        at = face * pitch + GAP
        own = own_ref[face].astype(jnp.float32)
        out_ref[face] = (own + grad[at : at + side, :]).astype(jnp.bfloat16)


def grad_first_kernel(row, nxl, flags_ref, x_ref, pre_ref, swapped_ref, out_ref, rows4):
    four_rows(rows4, flags_ref[0], row, pre_ref, swapped_ref)
    dests, _, lines, half = out_ref.shape
    for r in range(3):
        terms = jnp.dot(x_ref[...], rows4[(2 - r) * row : (4 - r) * row, :], preferred_element_type=jnp.float32)
        for c in range(3):
            turned = terms[c * half : (c + 1) * half, :].T
            if nxl == 1:
                for d in range(dests):
                    out_ref[d, 3 * r + c] = turned[d * lines : (d + 1) * lines, :].astype(jnp.bfloat16)
                continue
            split = turned.reshape(dests // 2, 2, lines, half)
            left = split[:, 0].reshape(-1, half)
            right = split[:, 1].reshape(-1, half)
            low = lax.broadcasted_iota(jnp.int32, left.shape, 1) < half // 2
            ones = (
                jnp.where(low, left, pltpu.roll(right, half // 2, 1)),
                jnp.where(low, pltpu.roll(left, half // 2, 1), right),
            )
            for xl, one in enumerate(ones):
                for d in range(dests // 2):
                    out_ref[2 * d + xl, 3 * r + c] = one[d * lines : (d + 1) * lines, :].astype(jnp.bfloat16)


def kernel(body, out_shape, inputs, smem=0, scratch=(), name=None, flops=0, nbytes=2**20, exps=0):
    many = isinstance(out_shape, tuple)
    return pl.pallas_call(
        body,
        out_shape=out_shape,
        in_specs=[pl.BlockSpec(memory_space=pltpu.SMEM)] * smem + whole(len(inputs) - smem),
        out_specs=tuple(whole(len(out_shape))) if many else whole(1)[0],
        scratch_shapes=scratch,
        compiler_params=pltpu.CompilerParams(vmem_limit_bytes=VMEM),
        cost_estimate=pl.CostEstimate(flops=flops, bytes_accessed=nbytes, transcendentals=exps),
        name=name,
    )(*inputs)


def on_device(sizes, saved_input, saved_pre, cotangent, first_weight, second_weight, seams, corners):
    nxh, ny, nxl, nz, nc = sizes
    nface, ntile, nchip = nxh * ny, nxl * nz * nc, nxl * nz
    x, p, g = saved_input[0, :, 0], saved_pre[0, :, 0], cotangent[0, :, 0]
    local, side, channels = x.shape
    faces = nface * local
    row = local * (side + 2 * GAP)
    bf = jnp.bfloat16
    shape = jax.ShapeDtypeStruct
    core = lax.axis_index("c")
    tile = lax.axis_index(TILE)
    top = tile >= ntile // 2
    near_wraps = (tile == 0) | (tile == ntile - 1)
    far_wraps = (tile == 1) | (tile == ntile - 2)
    flags = jnp.stack([core, near_wraps.astype(jnp.int32), far_wraps.astype(jnp.int32)])

    px_blocks = 4
    ch_blocks = nface // px_blocks
    px, ch = side // px_blocks, channels // ch_blocks
    cut = lambda a: jnp.transpose(a.reshape(local, px_blocks, px, ch_blocks, ch), (1, 3, 0, 2, 4)).reshape(
        nface, local, px, ch
    )
    pieces = jnp.concatenate([cut(g), cut(p)], 3 if ch_blocks > 1 else 2)
    count = pieces.shape[2]
    seam_cell = jnp.pad(seams.astype(bf)[:, None, :], ((0, 0), (0, 1), (0, channels - 4)))
    cells = jnp.concatenate([g[:, :2], g[:, side - 2 :], p[:, :1], p[:, side - 1 :], seam_cell], 1)
    sent = jnp.concatenate([pieces, jnp.broadcast_to(cells[None], (nface,) + cells.shape)], 2)
    table = lax.all_to_all(sent, FACE, 0, 0, tiled=True).reshape(faces, count + CELLS, channels)

    cells = table[:, count:]
    all_seams = cells[:, SEAM_AT, :4].astype(jnp.int32)
    want = jnp.where(top, all_seams[:, 0], all_seams[:, 2])
    picked = kernel(
        functools.partial(pick_kernel, faces, count), shape((faces, count, channels), bf), (want, table), 1, name="pick"
    )
    wrapped = lax.all_to_all(picked.reshape(nface, local, count, channels), FACE, 0, 0, tiled=True)

    outer = jnp.where(top, corners[:, 0:2], corners[:, 2:4])
    sides = jnp.stack([jnp.stack([seams[:, 3], seams[:, 1]], 1), outer], 0)
    spots = np.full((2, GAP), -1, np.int32)
    spots[0, [0, 1, GAP - 2, GAP - 1]] = (0, 1, 2, 3)
    spots[1, [0, GAP - 1]] = (4, 5)
    on_left = np.arange(GAP) >= GAP // 2
    face_at = jnp.where(on_left, sides[:, None, :, 0:1], sides[:, None, :, 1:2])
    index = jnp.where(spots[None, :, None] >= 0, face_at * CELLS + spots[None, :, None], -1)
    index = index.reshape(-1, 1).astype(jnp.int32)
    own, tails = kernel(
        functools.partial(border_kernel, local, side),
        (shape((2, local, side + GAP, channels), bf), shape((2, local, GAP, channels), bf)),
        (index, cells.reshape(faces * CELLS, channels), g, p),
        name="border",
    )
    near, far = kernel(
        functools.partial(send_kernel, local, side, (px_blocks, ch_blocks)),
        (shape(own.shape, bf), shape(own.shape[1:], bf)),
        (flags, own, tails, wrapped),
        1,
        name="send",
    )

    pairs = lambda step: [((t + step if t % 2 else t - step) % ntile, t) for t in range(ntile)]
    swap = lambda a: lax.ppermute(a, "c", [(0, 1), (1, 0)])
    part = swap(own[0])
    near = lax.ppermute(near, TILE, pairs(1))
    far = lax.ppermute(far, TILE, pairs(2))
    grad_pre = kernel(
        functools.partial(grad_pre_kernel, local, side),
        shape((2 * row, channels), bf),
        (flags, own, part, near, far, second_weight),
        1,
        (pltpu.VMEM((4 * row, channels), bf), pltpu.VMEM((2 * row, channels), bf)),
        "grad_pre",
        2 * 18 * row * channels**2,
        4 * 2**20,
        2 * row * channels,
    )
    swapped = swap(grad_pre)

    half = channels // nc
    per_tile = channels // ntile
    other = swap(x)
    both = jnp.where(core == 0, jnp.stack([x, other], 0), jnp.stack([other, x], 0))
    shifted = jnp.stack(
        [jnp.pad(both, ((0, 0), (0, 0), (GAP + 1 - c, GAP - 1 + c), (0, 0))) for c in range(3)], 0
    ).reshape(3, 2 * row, channels)
    kept = np.arange(half)
    chosen = (kept // per_tile) * (nc * per_tile) + kept % per_tile
    choose = (chosen[:, None] + core * per_tile == np.arange(channels)[None, :]).astype(bf)
    x_turned = lax.dot_general(
        choose, shifted, (((1,), (2,)), ((), ())), preferred_element_type=jnp.float32
    ).astype(bf)
    x_turned = jnp.transpose(x_turned, (1, 0, 2)).reshape(3 * half, 2 * row)

    rows4 = (pltpu.VMEM((4 * row, channels), bf),)
    width = channels // nface
    lines = width // nxl
    parts = kernel(
        functools.partial(grad_first_kernel, row, nxl),
        shape((nface * nxl, 9, lines, half), bf),
        (flags, x_turned, grad_pre, swapped),
        1,
        rows4,
        "grad_first",
        2 * 18 * half * row * channels,
    )
    grad_input = kernel(
        functools.partial(grad_input_kernel, local, side),
        shape((local, side, channels), bf),
        (flags, grad_pre, swapped, g, first_weight),
        1,
        rows4,
        "grad_input",
        2 * 9 * row * channels**2,
        2 * 2**20,
    )
    scale_factor = 1.0 / math.sqrt(faces * ntile * side)
    got = lax.all_to_all(parts, FACE + ("xl",), 0, 0, tiled=True)
    total = jnp.sum(got.astype(jnp.float32), 0) * scale_factor
    total = jnp.transpose(total.reshape(9 * lines, half)).reshape(nxl, nz, per_tile, 9 * lines)
    total = jnp.transpose(total, (1, 0, 2, 3)).reshape(nz, nxl * per_tile, 9 * lines)
    got = lax.all_to_all(total, "z", 0, 0, tiled=True)
    total = jnp.sum(got, 0).reshape(nxl, per_tile, 9, lines)
    first_out = jnp.transpose(total, (2, 1, 0, 3)).reshape(3, 3, per_tile, width)
    return grad_input.reshape(saved_input.shape), first_out


def solution(mesh, sizes=(2, 4, 2, 16, 2)):
    fine = Mesh(mesh.devices.reshape(sizes), FACE + TILE)
    field = P(None, FACE, TILE, None, None)
    return jax.shard_map(
        functools.partial(on_device, sizes),
        mesh=fine,
        in_specs=(field, field, field, P(), P(), P(FACE, None), P(FACE, None)),
        out_specs=(field, P(None, None, TILE, FACE)),
        check_vma=False,
    )
```

time: 115 us -> 104 us (0.904)
  waiting for transfers between devices: 35.7 us -> 30.5 us
  starting transfers between devices: 43.1 us -> 38.2 us
  other arithmetic: 3.86 us -> 1.98 us
  blocking collectives: 15.2 us -> 16.8 us
    all_to_all x2, waiting for transfers between devices: 28.5 us -> 16.6 us  [the longest x1 12 us: on_device(): got = lax.all_to_all(total, 'z', 0, 0, tiled=True)]
    ppermute x5, waiting for transfers between devices: 1.2 us -> 8.31 us  [the longest x1 7.35 us: on_device(): far = lax.ppermute(far, TILE, pairs(2))]
    ppermute x5, starting transfers between devices: 22.5 us -> 16.8 us  [the longest x1 9.15 us: on_device(): near = lax.ppermute(near, TILE, pairs(1))]
    another operation x5 -> x3, other arithmetic: 2.23 us -> 0.16 us  [the longest x2 0.08 us: on_device(): sides = jnp.stack([jnp.stack([seams[:, 3], seams[:, 1]], 1), outer], 0)]
    unnamed x53 -> x22, local copies, waits for them, and re-layouts: 1.65 us -> 0.05 us
    all_to_all x1, blocking collectives: 15.2 us -> 16.8 us  [on_device(): got = lax.all_to_all(parts, FACE + ('xl',), 0, 0, tiled=True)]
    another operation x9 -> x3, local copies, waits for them, and re-layouts: 0.66 us -> 1.98 us  [the longest x2 1.88 us: on_device(): a.reshape(local, px_blocks, px, ch_blocks, ch)]
    slice x12 -> x3, local copies, waits for them, and re-layouts: 0.33 us -> 1.63 us  [the longest x1 0.8 us: on_device(): p[:, side - 1:]]
  transfers between devices with their start and end apart: 8 -> 8, of which waited for: 5 -> 5; matrix products, arithmetic and copies ran while one was open for 5% -> 2% of each run, Pallas kernels for 1% -> 5%
where the time goes in v2:
time: 104 us; the launch traced here: 102 us
  starting transfers between devices  38.2 us (37%)
  waiting for transfers between devices  30.5 us (29%)
  blocking collectives  16.8 us (16%)
  Pallas kernels  7.24 us (7%)
  local copies, waits for them, and re-layouts  5.91 us (6%)
  other arithmetic  1.98 us (2%)
    all_to_all x1, blocking collectives, on_device(): got = lax.all_to_all(parts, FACE + ('xl',), 0, 0, tiled=True)  16.8 us
    all_to_all x1, waiting for transfers between devices, on_device(): got = lax.all_to_all(total, 'z', 0, 0, tiled=True)  12 us
    ppermute x1, starting transfers between devices, on_device(): near = lax.ppermute(near, TILE, pairs(1))  9.15 us
    all_to_all x1, starting transfers between devices, on_device(): got = lax.all_to_all(total, 'z', 0, 0, tiled=True)  7.6 us
    all_to_all x1, starting transfers between devices, on_device(): lax.all_to_all(sent, FACE, 0, 0, tiled=True)  7.57 us
    ppermute x1, waiting for transfers between devices, on_device(): far = lax.ppermute(far, TILE, pairs(2))  7.35 us
    pallas_call x6, Pallas kernels, kernel(): pl.pallas_call(body, out_shape=out_shape, in_specs=[pl.BlockSpec(memory_s...  7.24 us
    all_to_all x1, starting transfers between devices, on_device(): lax.all_to_all(picked.reshape(nface, local, count, channels), FACE, 0, 0,...  6.19 us
  transfers between devices with their start and end apart: 8, of which 5 were waited for; matrix products, arithmetic and copies ran while one was open for 2% of the time, Pallas kernels for 5%

profile of v2, /device:TPU:6, one launch (start us, length us, event | category | flops | bytes accessed | tf_op | source)
XLA Modules:
  0.0 102.1 jit_solution(9741902882072001509)
XLA Ops:
  0.6 0.9 reshape_squeeze.6
  1.6 0.7 fusion.13
  2.3 0.9 reshape_squeeze.7
  3.3 0.0 copy-start.4
  3.3 0.0 copy-start.5
  3.3 0.0 copy-start.6
  3.3 0.8 fusion.12
  4.1 0.7 convert_bitcast_fusion
  4.8 0.0 copy-start.8
  5.0 0.8 pad_maximum_fusion
  5.8 7.6 %all-to-all-start = ((bf16[8,4,24,256]{3,2,1,0:T(8,128)(2,1)}), bf16[8,4,24,256]{3,2,1,0:T(8,128)(2,1)S(1)}, u32[]{:S(2)}, u32[]{:S(2)}) async-start(bf16[8,4,24,256]{3,2,1,0:T(8,128)(2,1)} %pad_maximum_fusion), calls=%async_computation | async-start | bytes 786432 | tf_op jit(solution)/shard_map/all_to_all | solution.py:206
  13.3 1.9 %collective-permute-start.4 = (bf16[4,64,256]{2,1,0:T(8,128)(2,1)S(1)}, bf16[4,64,256]{2,1,0:T(8,128)(2,1)S(1)}, u32[]{:S(2)}, u32[]{:S(2)}) collective-permute-start(bf16[4,64,256]{2,1,0:T(8,128)(2,1)S(1)} %bitcast.71), channel_id=1, source_target_pairs={{0,1},{1,0},{2,3},{3,2},{4,5},{5,4},{6,7},{7,6},{8,9},{9,8},{10,11... | collective-permute-start | bytes 393224 | tf_op jit(solution)/shard_map/ppermute | solution.py:240
  15.3 0.1 fusion.14
  15.3 0.1 slice_select_fusion
  15.4 0.1 copy.54
  15.5 0.1 pad_add_fusion
  15.6 0.1 copy.53
  15.7 0.1 select_multiply_fusion
  15.8 0.1 select_n.59.index_ref
  15.9 0.1 pad_add_fusion.2.flags_ref
  16.0 4.6 %all-to-all-done = bf16[8,4,24,256]{3,2,1,0:T(8,128)(2,1)S(1)} async-done(((bf16[8,4,24,256]{3,2,1,0:T(8,128)(2,1)}), bf16[8,4,24,256]{3,2,1,0:T(8,128)(2,1)S(1)}, u32[]{:S(2)}, u32[]{:S(2)}) %all-to-all-start) | async-done | bytes 393248 | tf_op jit(solution)/shard_map/all_to_all | solution.py:206
  20.6 0.1 copy.59
  20.7 1.3 %pick.1 = bf16[32,16,256]{2,1,0:T(8,128)(2,1)} custom-call(s32[32]{0:T(128)S(1)} %fusion.9.want_ref, bf16[32,24,256]{2,1,0:T(8,128)(2,1)S(1)} %bitcast.52), custom_call_target="tpu_custom_call" | custom-call | bytes 1048576 | tf_op jit(solution)/shard_map/pick/pallas_call | solution.py:167
  21.9 6.2 %all-to-all-start.1 = ((bf16[8,4,16,256]{3,2,1,0:T(8,128)(2,1)}), bf16[8,4,16,256]{3,2,1,0:T(8,128)(2,1)S(1)}, u32[]{:S(2)}, u32[]{:S(2)}) async-start(bf16[8,4,16,256]{3,2,1,0:T(8,128)(2,1)} %bitcast.19), calls=%async_computation.1 | async-start | bytes 524288 | tf_op jit(solution)/shard_map/all_to_all | solution.py:214
  28.2 0.2 border.1
  28.4 5.6 %all-to-all-done.1.pieces_ref = bf16[8,4,16,256]{3,2,1,0:T(8,128)(2,1)S(1)} async-done(((bf16[8,4,16,256]{3,2,1,0:T(8,128)(2,1)}), bf16[8,4,16,256]{3,2,1,0:T(8,128)(2,1)S(1)}, u32[]{:S(2)}, u32[]{:S(2)}) %all-to-all-start.1) | async-done | bytes 262176 | tf_op jit(solution)/shard_map/all_to_all | solution.py:214
  34.0 0.6 send.1
  34.6 9.2 %collective-permute-start.1 = (bf16[2,4,80,256]{3,2,1,0:T(8,128)(2,1)S(1)}, bf16[2,4,80,256]{3,2,1,0:T(8,128)(2,1)S(1)}, u32[]{:S(2)}, u32[]{:S(2)}) collective-permute-start(bf16[2,4,80,256]{3,2,1,0:T(8,128)(2,1)S(1)} %get-tuple-element.8), channel_id=1, source_target_pairs={{63,0},{2,1},{1,2},{4,3},{3,4},{6,5},{5,6},{8,7},{7,8},{10,9},{9,1... | collective-permute-start | bytes 983048 | tf_op jit(solution)/shard_map/ppermute | solution.py:242
  43.8 1.9 %collective-permute-start = (bf16[4,80,256]{2,1,0:T(8,128)(2,1)S(1)}, bf16[4,80,256]{2,1,0:T(8,128)(2,1)S(1)}, u32[]{:S(2)}, u32[]{:S(2)}) collective-permute-start(bf16[4,80,256]{2,1,0:T(8,128)(2,1)S(1)} %slice_bitcast_fusion), channel_id=1, source_target_pairs={{0,1},{1,0},{2,3},{3,2},{4,5},{5,4},{6,7},{7,6},{8,9},{9,8},{10,11... | collective-permute-start | bytes 491528 | tf_op jit(solution)/shard_map/ppermute | solution.py:240
  45.7 1.9 %collective-permute-start.2 = (bf16[4,80,256]{2,1,0:T(8,128)(2,1)S(1)}, bf16[4,80,256]{2,1,0:T(8,128)(2,1)S(1)}, u32[]{:S(2)}, u32[]{:S(2)}) collective-permute-start(bf16[4,80,256]{2,1,0:T(8,128)(2,1)S(1)} %get-tuple-element.9), channel_id=1, source_target_pairs={{62,0},{3,1},{0,2},{5,3},{2,4},{7,5},{4,6},{9,7},{6,8},{11,9},{8,1... | collective-permute-start | bytes 491528 | tf_op jit(solution)/shard_map/ppermute | solution.py:243
  47.6 7.4 %collective-permute-done.2.far_ref = bf16[4,80,256]{2,1,0:T(8,128)(2,1)S(1)} collective-permute-done((bf16[4,80,256]{2,1,0:T(8,128)(2,1)S(1)}, bf16[4,80,256]{2,1,0:T(8,128)(2,1)S(1)}, u32[]{:S(2)}, u32[]{:S(2)}) %collective-permute-start.2) | collective-permute-done | bytes 163872 | tf_op jit(solution)/shard_map/ppermute | solution.py:243
  55.0 0.0 collective-permute-done.1.near_ref
  55.0 1.8 %grad_pre.1.pre_ref = bf16[768,256]{1,0:T(8,128)(2,1)S(1)} custom-call(s32[3]{0:T(128)S(1)} %pad_add_fusion.2.flags_ref, bf16[2,4,80,256]{3,2,1,0:T(8,128)(2,1)S(1)} %get-tuple-element.6.own_ref, bf16[4,80,256]{2,1,0:T(8,128)(2,1)S(1)} %collective-permute-done.part_ref, bf16[2,4,80,256]{3,2,1,0:T(8,128)(2,1)S(1)} %collective-permute-done.1.near_ref, ...), custom_call_target="tpu_custom_call" | custom-call | flops 905969664 | bytes 4194304 | tf_op jit(solution)/shard_map/grad_pre/pallas_call | solution.py:167
  56.8 1.9 %collective-permute-start.3 = (bf16[768,256]{1,0:T(8,128)(2,1)S(1)}, bf16[768,256]{1,0:T(8,128)(2,1)S(1)}, u32[]{:S(2)}, u32[]{:S(2)}) collective-permute-start(bf16[768,256]{1,0:T(8,128)(2,1)S(1)} %grad_pre.1.pre_ref), channel_id=1, source_target_pairs={{0,1},{1,0},{2,3},{3,2},{4,5},{5,4},{6,7},{7,6},{8,9},{9,8},{10,11... | collective-permute-start | bytes 1179656 | tf_op jit(solution)/shard_map/ppermute | solution.py:240
  58.7 0.0 collective-permute-done.4
  58.8 0.1 fusion.11
  58.9 0.5 convolution_convert_fusion
  59.5 0.9 collective-permute-done.3.swapped_ref
  60.4 1.5 %grad_first.1 = bf16[16,9,16,128]{3,2,1,0:T(8,128)(2,1)S(1)} custom-call(s32[3]{0:T(128)S(1)} %pad_add_fusion.2.flags_ref, bf16[384,768]{1,0:T(8,128)(2,1)S(1)} %bitcast.57, bf16[768,256]{1,0:T(8,128)(2,1)S(1)} %grad_pre.1.pre_ref, bf16[768,256]{1,0:T(8,128)(2,1)S(1)} %collective-permute-done.3.swapped_ref), custom_call_target="tpu_custom_call" | custom-call | flops 452984832 | bytes 1048576 | tf_op jit(solution)/shard_map/grad_first/pallas_call | solution.py:167
  61.9 16.8 %all_to_all.20 = bf16[16,9,16,128]{3,2,1,0:T(8,128)(2,1)S(1)} all-to-all(bf16[16,9,16,128]{3,2,1,0:T(8,128)(2,1)S(1)} %grad_first.1), channel_id=1, replica_groups=mesh['xh'=2,'y'=4,'xl'=2,'z'=16,'c'=2] {'xh','y','xl'}, dimensions={0} | all-to-all | bytes 1179648 | tf_op jit(solution)/shard_map/all_to_all | solution.py:295
  78.7 0.1 convert_reduce_fusion
  78.8 0.1 copy.60
  79.0 0.7 copy.62
  79.7 7.6 %all-to-all-start.3 = ((f32[16,8,144]{2,1,0:T(8,128)}), f32[16,8,144]{2,1,0:T(8,128)S(1)}, u32[]{:S(2)}, u32[]{:S(2)}) async-start(f32[16,8,144]{2,1,0:T(8,128)} %copy.62), calls=%async_computation.3 | async-start | bytes 262144 | tf_op jit(solution)/shard_map/all_to_all | solution.py:299
  87.3 1.9 %grad_input.1 = bf16[4,64,256]{2,1,0:T(8,128)(2,1)} custom-call(s32[3]{0:T(128)S(1)} %pad_add_fusion.2.flags_ref, bf16[768,256]{1,0:T(8,128)(2,1)S(1)} %grad_pre.1.pre_ref, bf16[768,256]{1,0:T(8,128)(2,1)S(1)} %collective-permute-done.3.swapped_ref, bf16[4,64,256]{2,1,0:T(8,128)(2,1)S(1)} %bitcast.56, bf16[3,3,256,256]{3,2,1,0:T(8,128)(2,1)S(1)} %copy-done.1), custom_call_target="tpu_custom_call" | custom-call | flops 452984832 | bytes 2097152 | tf_op jit(solution)/shard_map/grad_input/pallas_call | solution.py:167
  89.2 12.0 %all-to-all-done.3 = f32[16,8,144]{2,1,0:T(8,128)S(1)} async-done(((f32[16,8,144]{2,1,0:T(8,128)}), f32[16,8,144]{2,1,0:T(8,128)S(1)}, u32[]{:S(2)}, u32[]{:S(2)}) %all-to-all-start.3) | async-done | bytes 73760 | tf_op jit(solution)/shard_map/all_to_all | solution.py:299
  101.2 0.1 reshape.109
  101.4 0.7 reshape.110
  (38 shorter events, 0.4 us)
Async XLA Ops:
  3.3 10.1 %copy-start.4 = (bf16[1,4,1,64,256]{4,3,2,1,0:T(8,128)(2,1)S(1)}, bf16[1,4,1,64,256]{4,3,2,1,0:T(8,128)(2,1)}, u32[]{:S(2)}) copy-start(bf16[1,4,1,64,256]{4,3,2,1,0:T(8,128)(2,1)} %param.12) | copy-start | bytes 393220
  3.3 12.0 %copy-start.5 = (s32[4,4]{1,0:T(4,128)S(1)}, s32[4,4]{1,0:T(4,128)}, u32[]{:S(2)}) copy-start(s32[4,4]{1,0:T(4,128)} %param.17) | copy-start | bytes 196
  3.3 12.0 %copy-start.6 = (s32[4,4]{1,0:T(4,128)S(1)}, s32[4,4]{1,0:T(4,128)}, u32[]{:S(2)}) copy-start(s32[4,4]{1,0:T(4,128)} %param.18) | copy-start | bytes 196
  4.8 10.9 %copy-start.9 = (pred[16]{0:T(512)(128)(4,1)S(1)}, pred[16]{0:T(512)(128)(4,1)}, u32[]{:S(2)}) copy-start(pred[16]{0:T(512)(128)(4,1)} %constant.46.clone) | copy-start | bytes 52
  4.8 10.9 %copy-start.7 = (s32[2,16]{1,0:T(2,128)S(1)}, s32[2,16]{1,0:T(2,128)}, u32[]{:S(2)}) copy-start(s32[2,16]{1,0:T(2,128)} %constant.65) | copy-start | bytes 388
  4.8 10.9 %copy-start.8 = (pred[2,16]{1,0:T(4,128)(4,1)S(1)}, pred[2,16]{1,0:T(4,128)(4,1)}, u32[]{:S(2)}) copy-start(pred[2,16]{1,0:T(4,128)(4,1)} %constant.64) | copy-start | bytes 100
  5.8 22.4 %copy-start = (bf16[1,4,1,64,256]{4,3,2,1,0:T(8,128)(2,1)S(1)}, bf16[1,4,1,64,256]{4,3,2,1,0:T(8,128)(2,1)}, u32[]{:S(2)}) copy-start(bf16[1,4,1,64,256]{4,3,2,1,0:T(8,128)(2,1)} %param.14) | copy-start | bytes 393220
  5.8 22.4 %copy-start.2 = (bf16[1,4,1,64,256]{4,3,2,1,0:T(8,128)(2,1)S(1)}, bf16[1,4,1,64,256]{4,3,2,1,0:T(8,128)(2,1)}, u32[]{:S(2)}) copy-start(bf16[1,4,1,64,256]{4,3,2,1,0:T(8,128)(2,1)} %param.13) | copy-start | bytes 393220
  5.8 14.8 %all-to-all-start = ((bf16[8,4,24,256]{3,2,1,0:T(8,128)(2,1)}), bf16[8,4,24,256]{3,2,1,0:T(8,128)(2,1)S(1)}, u32[]{:S(2)}, u32[]{:S(2)}) async-start(bf16[8,4,24,256]{3,2,1,0:T(8,128)(2,1)} %pad_maximum_fusion), calls=%async_computation | async-start | bytes 786432 | tf_op jit(solution)/shard_map/all_to_all | solution.py:206
  13.3 45.4 %collective-permute-start.4 = (bf16[4,64,256]{2,1,0:T(8,128)(2,1)S(1)}, bf16[4,64,256]{2,1,0:T(8,128)(2,1)S(1)}, u32[]{:S(2)}, u32[]{:S(2)}) collective-permute-start(bf16[4,64,256]{2,1,0:T(8,128)(2,1)S(1)} %bitcast.71), channel_id=1, source_target_pairs={{0,1},{1,0},{2,3},{3,2},{4,5},{5,4},{6,7},{7,6},{8,9},{9,8},{10,11... | collective-permute-start | bytes 393224 | tf_op jit(solution)/shard_map/ppermute | solution.py:240
  21.9 25.7 %copy-start.10 = (s32[128,1]{0,1:T(1,128)S(1)}, s32[128,1]{0,1:T(1,128)}, u32[]{:S(2)}) copy-start(s32[128,1]{0,1:T(1,128)} %constant.49.clone) | copy-start | bytes 1540
  21.9 33.1 %copy-start.3 = (bf16[3,3,256,256]{3,2,1,0:T(8,128)(2,1)S(1)}, bf16[3,3,256,256]{3,2,1,0:T(8,128)(2,1)}, u32[]{:S(2)}) copy-start(bf16[3,3,256,256]{3,2,1,0:T(8,128)(2,1)} %weight_ref.2) | copy-start | bytes 3538948
  21.9 12.0 %all-to-all-start.1 = ((bf16[8,4,16,256]{3,2,1,0:T(8,128)(2,1)}), bf16[8,4,16,256]{3,2,1,0:T(8,128)(2,1)S(1)}, u32[]{:S(2)}, u32[]{:S(2)}) async-start(bf16[8,4,16,256]{3,2,1,0:T(8,128)(2,1)} %bitcast.19), calls=%async_computation.1 | async-start | bytes 524288 | tf_op jit(solution)/shard_map/all_to_all | solution.py:214
  34.6 20.4 %collective-permute-start.1 = (bf16[2,4,80,256]{3,2,1,0:T(8,128)(2,1)S(1)}, bf16[2,4,80,256]{3,2,1,0:T(8,128)(2,1)S(1)}, u32[]{:S(2)}, u32[]{:S(2)}) collective-permute-start(bf16[2,4,80,256]{3,2,1,0:T(8,128)(2,1)S(1)} %get-tuple-element.8), channel_id=1, source_target_pairs={{63,0},{2,1},{1,2},{4,3},{3,4},{6,5},{5,6},{8,7},{7,8},{10,9},{9,1... | collective-permute-start | bytes 983048 | tf_op jit(solution)/shard_map/ppermute | solution.py:242
  43.8 3.9 %collective-permute-start = (bf16[4,80,256]{2,1,0:T(8,128)(2,1)S(1)}, bf16[4,80,256]{2,1,0:T(8,128)(2,1)S(1)}, u32[]{:S(2)}, u32[]{:S(2)}) collective-permute-start(bf16[4,80,256]{2,1,0:T(8,128)(2,1)S(1)} %slice_bitcast_fusion), channel_id=1, source_target_pairs={{0,1},{1,0},{2,3},{3,2},{4,5},{5,4},{6,7},{7,6},{8,9},{9,8},{10,11... | collective-permute-start | bytes 491528 | tf_op jit(solution)/shard_map/ppermute | solution.py:240
  45.7 9.3 %collective-permute-start.2 = (bf16[4,80,256]{2,1,0:T(8,128)(2,1)S(1)}, bf16[4,80,256]{2,1,0:T(8,128)(2,1)S(1)}, u32[]{:S(2)}, u32[]{:S(2)}) collective-permute-start(bf16[4,80,256]{2,1,0:T(8,128)(2,1)S(1)} %get-tuple-element.9), channel_id=1, source_target_pairs={{62,0},{3,1},{0,2},{5,3},{2,4},{7,5},{4,6},{9,7},{6,8},{11,9},{8,1... | collective-permute-start | bytes 491528 | tf_op jit(solution)/shard_map/ppermute | solution.py:243
  56.8 3.6 %collective-permute-start.3 = (bf16[768,256]{1,0:T(8,128)(2,1)S(1)}, bf16[768,256]{1,0:T(8,128)(2,1)S(1)}, u32[]{:S(2)}, u32[]{:S(2)}) collective-permute-start(bf16[768,256]{1,0:T(8,128)(2,1)S(1)} %grad_pre.1.pre_ref), channel_id=1, source_target_pairs={{0,1},{1,0},{2,3},{3,2},{4,5},{5,4},{6,7},{7,6},{8,9},{9,8},{10,11... | collective-permute-start | bytes 1179656 | tf_op jit(solution)/shard_map/ppermute | solution.py:240
  78.7 8.6 %copy-start.1 = (bf16[3,3,256,256]{3,2,1,0:T(8,128)(2,1)S(1)}, bf16[3,3,256,256]{3,2,1,0:T(8,128)(2,1)}, u32[]{:S(2)}) copy-start(bf16[3,3,256,256]{3,2,1,0:T(8,128)(2,1)} %weight_ref.3) | copy-start | bytes 3538948
  79.7 21.5 %all-to-all-start.3 = ((f32[16,8,144]{2,1,0:T(8,128)}), f32[16,8,144]{2,1,0:T(8,128)S(1)}, u32[]{:S(2)}, u32[]{:S(2)}) async-start(f32[16,8,144]{2,1,0:T(8,128)} %copy.62), calls=%async_computation.3 | async-start | bytes 262144 | tf_op jit(solution)/shard_map/all_to_all | solution.py:299

commit v3 on v2

--- a/solution.py
+++ b/solution.py
@@ -23,9 +23,48 @@
     return [pl.BlockSpec(memory_space=pltpu.VMEM)] * n
 
 
-def pick_kernel(faces, count, want_ref, table_ref, out_ref):
+def pack_kernel(local, side, blocks, seams_ref, g_ref, p_ref, out_ref):
+    px_blocks, ch_blocks = blocks
+    channels = g_ref.shape[-1]
+    px, ch = side // px_blocks, channels // ch_blocks
+    count = px * 2 // ch_blocks
+    shape = (local * CELLS, local * side)
+    line = lax.broadcasted_iota(jnp.int32, shape, 0)
+    pixel = lax.broadcasted_iota(jnp.int32, shape, 1)
+    cell, base = line % CELLS, line // CELLS * side
+    of_g = jnp.where(cell < 2, base + cell, jnp.where(cell < 4, base + side - 4 + cell, -1))
+    of_p = jnp.where(cell == 4, base, jnp.where(cell == 5, base + side - 1, -1))
+    take = lambda at, ref: jnp.dot(
+        jnp.where(at == pixel, 1.0, 0.0).astype(jnp.bfloat16),
+        ref[...].reshape(local * side, channels),
+        preferred_element_type=jnp.float32,
+    )
+    cells = take(of_g, g_ref) + take(of_p, p_ref)
+    line = lax.broadcasted_iota(jnp.int32, cells.shape, 0)
+    lane = lax.broadcasted_iota(jnp.int32, cells.shape, 1)
+    for face in range(local):
+        for i in range(4):
+            here = (line == face * CELLS + SEAM_AT) & (lane == i)
+            cells = jnp.where(here, seams_ref[face, i].astype(jnp.float32), cells)
+    cells = cells.astype(jnp.bfloat16)
+    for b in range(px_blocks * ch_blocks):
+        i, j = divmod(b, ch_blocks)
+        for face in range(local):
+            at = face * count
+            for which, source in enumerate((g_ref, p_ref)):
+                piece = source[face, i * px : (i + 1) * px, j * ch : (j + 1) * ch]
+                if ch_blocks == 1:
+                    out_ref[b, at + which * px : at + (which + 1) * px] = piece
+                else:
+                    out_ref[b, at : at + px, which * ch : (which + 1) * ch] = piece
+        out_ref[b, local * count :] = cells
+
+
+def pick_kernel(faces, local, count, want_ref, table_ref, out_ref):
     for i in range(faces):
-        out_ref[i] = table_ref[want_ref[i], :count]
+        face = want_ref[i]
+        at = pl.multiple_of(lax.rem(face, local) * count, 16)
+        out_ref[i] = table_ref[lax.div(face, local), pl.ds(at, count)]
 
 
 def border_kernel(local, side, index_ref, cells_ref, g_ref, p_ref, own_ref, wrap_ref):
@@ -194,22 +233,23 @@
 
     px_blocks = 4
     ch_blocks = nface // px_blocks
-    px, ch = side // px_blocks, channels // ch_blocks
-    cut = lambda a: jnp.transpose(a.reshape(local, px_blocks, px, ch_blocks, ch), (1, 3, 0, 2, 4)).reshape(
-        nface, local, px, ch
-    )
-    pieces = jnp.concatenate([cut(g), cut(p)], 3 if ch_blocks > 1 else 2)
-    count = pieces.shape[2]
-    seam_cell = jnp.pad(seams.astype(bf)[:, None, :], ((0, 0), (0, 1), (0, channels - 4)))
-    cells = jnp.concatenate([g[:, :2], g[:, side - 2 :], p[:, :1], p[:, side - 1 :], seam_cell], 1)
-    sent = jnp.concatenate([pieces, jnp.broadcast_to(cells[None], (nface,) + cells.shape)], 2)
-    table = lax.all_to_all(sent, FACE, 0, 0, tiled=True).reshape(faces, count + CELLS, channels)
-
-    cells = table[:, count:]
+    px = side // px_blocks
+    count = px * 2 // ch_blocks
+    sent = kernel(
+        functools.partial(pack_kernel, local, side, (px_blocks, ch_blocks)),
+        shape((nface, local * (count + CELLS), channels), bf),
+        (seams, g, p),
+        1,
+        name="pack",
+    )
+    swap = lambda a: lax.ppermute(a, "c", [(0, 1), (1, 0)])
+    table, other = lax.optimization_barrier((lax.all_to_all(sent, FACE, 0, 0, tiled=True), swap(x)))
+
+    cells = table[:, local * count :].reshape(faces, CELLS, channels)
     all_seams = cells[:, SEAM_AT, :4].astype(jnp.int32)
     want = jnp.where(top, all_seams[:, 0], all_seams[:, 2])
     picked = kernel(
-        functools.partial(pick_kernel, faces, count), shape((faces, count, channels), bf), (want, table), 1, name="pick"
+        functools.partial(pick_kernel, faces, local, count), shape((faces, count, channels), bf), (want, table), 1, name="pick"
     )
     wrapped = lax.all_to_all(picked.reshape(nface, local, count, channels), FACE, 0, 0, tiled=True)
 
@@ -228,6 +268,7 @@
         (index, cells.reshape(faces * CELLS, channels), g, p),
         name="border",
     )
+    wrapped, part = lax.optimization_barrier((wrapped, swap(own[0])))
     near, far = kernel(
         functools.partial(send_kernel, local, side, (px_blocks, ch_blocks)),
         (shape(own.shape, bf), shape(own.shape[1:], bf)),
@@ -237,8 +278,6 @@
     )
 
     pairs = lambda step: [((t + step if t % 2 else t - step) % ntile, t) for t in range(ntile)]
-    swap = lambda a: lax.ppermute(a, "c", [(0, 1), (1, 0)])
-    part = swap(own[0])
     near = lax.ppermute(near, TILE, pairs(1))
     far = lax.ppermute(far, TILE, pairs(2))
     grad_pre = kernel(
@@ -256,7 +295,6 @@
 
     half = channels // nc
     per_tile = channels // ntile
-    other = swap(x)
     both = jnp.where(core == 0, jnp.stack([x, other], 0), jnp.stack([other, x], 0))
     shifted = jnp.stack(
         [jnp.pad(both, ((0, 0), (0, 0), (GAP + 1 - c, GAP - 1 + c), (0, 0))) for c in range(3)], 0
@@ -295,9 +333,9 @@
     got = lax.all_to_all(parts, FACE + ("xl",), 0, 0, tiled=True)
     total = jnp.sum(got.astype(jnp.float32), 0) * scale_factor
     total = jnp.transpose(total.reshape(9 * lines, half)).reshape(nxl, nz, per_tile, 9 * lines)
-    total = jnp.transpose(total, (1, 0, 2, 3)).reshape(nz, nxl * per_tile, 9 * lines)
+    total = jnp.transpose(total, (1, 0, 2, 3)).reshape(nz, nxl * per_tile, 9 * lines).astype(bf)
     got = lax.all_to_all(total, "z", 0, 0, tiled=True)
-    total = jnp.sum(got, 0).reshape(nxl, per_tile, 9, lines)
+    total = jnp.sum(got.astype(jnp.float32), 0).reshape(nxl, per_tile, 9, lines)
     first_out = jnp.transpose(total, (2, 1, 0, 3)).reshape(3, 3, per_tile, width)
     return grad_input.reshape(saved_input.shape), first_out
 

time: 104 us -> 99.4 us (0.956)
  waiting for transfers between devices: 30.5 us -> 27.5 us
  Pallas kernels: 7.24 us -> 8.85 us
  other arithmetic: 1.98 us -> 0.47 us
  starting transfers between devices: 38.2 us -> 36.9 us
  blocking collectives: 16.8 us -> 18.1 us
  local copies, waits for them, and re-layouts: 5.91 us -> 4.83 us
    all_to_all x1, waiting for transfers between devices: 5.57 us -> 2.29 us  [on_device(): lax.all_to_all(picked.reshape(nface, local, count, channels), FACE, 0, 0,...]
    unnamed x22 -> x29, local copies, waits for them, and re-layouts: 0.05 us -> 2.64 us
    ppermute x3, waiting for transfers between devices: 0.95 us -> 2.87 us  [on_device(): swap = lambda a: lax.ppermute(a, 'c', [(0, 1), (1, 0)])]
    another operation x2 -> x0, local copies, waits for them, and re-layouts: 1.88 us -> none  [on_device(): a.reshape(local, px_blocks, px, ch_blocks, ch)]
    pallas_call x6 -> x7, Pallas kernels: 7.24 us -> 8.85 us  [kernel(): pl.pallas_call(body, out_shape=out_shape, in_specs=[pl.BlockSpec(memory_s...]
    slice x2, local copies, waits for them, and re-layouts: 1.55 us -> 0.03 us  [the longest x1 0.02 us: on_device(): all_seams = cells[:, SEAM_AT, :4].astype(jnp.int32)]
    all_to_all x1, blocking collectives: 16.8 us -> 18.1 us  [on_device(): got = lax.all_to_all(parts, FACE + ('xl',), 0, 0, tiled=True)]
    all_to_all x1, starting transfers between devices: 7.6 us -> 6.28 us  [on_device(): got = lax.all_to_all(total, 'z', 0, 0, tiled=True)]
  transfers between devices with their start and end apart: 8 -> 8, of which waited for: 5 -> 7; matrix products, arithmetic and copies ran while one was open for 2% -> 1% of each run, Pallas kernels for 5% -> 2%
where the time goes in v3:
time: 99.4 us; the launch traced here: 98.1 us
  starting transfers between devices  36.9 us (37%)
  waiting for transfers between devices  27.5 us (28%)
  blocking collectives  18.1 us (18%)
  Pallas kernels  8.85 us (9%)
  local copies, waits for them, and re-layouts  4.83 us (5%)
    all_to_all x1, blocking collectives, on_device(): got = lax.all_to_all(parts, FACE + ('xl',), 0, 0, tiled=True)  18.1 us
    all_to_all x1, waiting for transfers between devices, on_device(): got = lax.all_to_all(total, 'z', 0, 0, tiled=True)  11 us
    ppermute x1, starting transfers between devices, on_device(): near = lax.ppermute(near, TILE, pairs(1))  9.15 us
    pallas_call x7, Pallas kernels, kernel(): pl.pallas_call(body, out_shape=out_shape, in_specs=[pl.BlockSpec(memory_s...  8.85 us
    all_to_all x1, starting transfers between devices, on_device(): lax.all_to_all(sent, FACE, 0, 0, tiled=True)  7.57 us
    ppermute x1, waiting for transfers between devices, on_device(): far = lax.ppermute(far, TILE, pairs(2))  7.37 us
    all_to_all x1, starting transfers between devices, on_device(): got = lax.all_to_all(total, 'z', 0, 0, tiled=True)  6.28 us
    all_to_all x1, starting transfers between devices, on_device(): lax.all_to_all(picked.reshape(nface, local, count, channels), FACE, 0, 0,...  6.19 us
  transfers between devices with their start and end apart: 8, of which 7 were waited for; matrix products, arithmetic and copies ran while one was open for 1% of the time, Pallas kernels for 2%

profile of v3, /device:TPU:6, one launch (start us, length us, event | category | flops | bytes accessed | tf_op | source)
XLA Modules:
  0.0 98.1 jit_solution(4488851702303957073)
XLA Ops:
  0.6 0.0 copy-start.12
  0.6 0.0 copy-start.11
  0.7 0.0 copy-start.10
  0.7 0.0 copy-start.1
  0.7 0.9 copy-done.1
  1.6 0.9 copy-done.3
  2.5 0.7 copy-done.5
  3.2 1.5 %pack.1 = bf16[8,96,256]{2,1,0:T(8,128)(2,1)} custom-call(s32[4,4]{1,0:T(4,128)S(1)} %copy-done.5, bf16[4,64,256]{2,1,0:T(8,128)(2,1)S(1)} %bitcast.42, bf16[4,64,256]{2,1,0:T(8,128)(2,1)S(1)} %bitcast.48), custom_call_target="tpu_custom_call" | custom-call | bytes 1048576 | tf_op jit(solution)/shard_map/pack/pallas_call | solution.py:206
  4.7 7.6 %all-to-all-start = ((bf16[8,96,256]{2,1,0:T(8,128)(2,1)}), bf16[8,96,256]{2,1,0:T(8,128)(2,1)S(1)}, u32[]{:S(2)}, u32[]{:S(2)}) async-start(bf16[8,96,256]{2,1,0:T(8,128)(2,1)} %pack.1), calls=%async_computation | async-start | bytes 786432 | tf_op jit(solution)/shard_map/all_to_all | solution.py:246
  12.2 1.9 %collective-permute-start = (bf16[4,64,256]{2,1,0:T(8,128)(2,1)S(1)}, bf16[4,64,256]{2,1,0:T(8,128)(2,1)S(1)}, u32[]{:S(2)}, u32[]{:S(2)}) collective-permute-start(bf16[4,64,256]{2,1,0:T(8,128)(2,1)S(1)} %bitcast.57), channel_id=1, source_target_pairs={{0,1},{1,0},{2,3},{3,2},{4,5},{5,4},{6,7},{7,6},{8,9},{9,8},{10,11... | collective-permute-start | bytes 393224 | tf_op jit(solution)/shard_map/ppermute | solution.py:245
  14.2 0.1 fusion.12
  14.3 0.1 slice_select_fusion
  14.3 0.1 copy.33
  14.4 0.1 pad_add_fusion
  14.5 0.1 copy.32
  14.6 0.1 select_multiply_fusion
  14.7 0.1 select_n.59.index_ref
  14.8 0.7 collective-permute-done
  15.5 4.0 %all-to-all-done.table_ref = bf16[8,96,256]{2,1,0:T(8,128)(2,1)S(1)} async-done(((bf16[8,96,256]{2,1,0:T(8,128)(2,1)}), bf16[8,96,256]{2,1,0:T(8,128)(2,1)S(1)}, u32[]{:S(2)}, u32[]{:S(2)}) %all-to-all-start) | async-done | bytes 393248 | tf_op jit(solution)/shard_map/all_to_all | solution.py:246
  19.5 0.1 copy.41
  19.6 1.4 %pick.1 = bf16[32,16,256]{2,1,0:T(8,128)(2,1)} custom-call(s32[32]{0:T(128)S(1)} %fusion.9.want_ref, bf16[8,96,256]{2,1,0:T(8,128)(2,1)S(1)} %all-to-all-done.table_ref), custom_call_target="tpu_custom_call" | custom-call | bytes 1048576 | tf_op jit(solution)/shard_map/pick/pallas_call | solution.py:206
  21.0 6.2 %all-to-all-start.1 = ((bf16[8,4,16,256]{3,2,1,0:T(8,128)(2,1)}), bf16[8,4,16,256]{3,2,1,0:T(8,128)(2,1)S(1)}, u32[]{:S(2)}, u32[]{:S(2)}) async-start(bf16[8,4,16,256]{3,2,1,0:T(8,128)(2,1)} %bitcast.15), calls=%async_computation.1 | async-start | bytes 524288 | tf_op jit(solution)/shard_map/all_to_all | solution.py:254
  27.2 0.2 border.1
  27.5 1.9 %collective-permute-start.1 = (bf16[4,80,256]{2,1,0:T(8,128)(2,1)S(1)}, bf16[4,80,256]{2,1,0:T(8,128)(2,1)S(1)}, u32[]{:S(2)}, u32[]{:S(2)}) collective-permute-start(bf16[4,80,256]{2,1,0:T(8,128)(2,1)S(1)} %slice_bitcast_fusion), channel_id=1, source_target_pairs={{0,1},{1,0},{2,3},{3,2},{4,5},{5,4},{6,7},{7,6},{8,9},{9,8},{10,11... | collective-permute-start | bytes 491528 | tf_op jit(solution)/shard_map/ppermute | solution.py:245
  29.4 0.1 pad_add_fusion.2.flags_ref
  29.5 1.3 %collective-permute-done.1.part_ref = bf16[4,80,256]{2,1,0:T(8,128)(2,1)S(1)} collective-permute-done((bf16[4,80,256]{2,1,0:T(8,128)(2,1)S(1)}, bf16[4,80,256]{2,1,0:T(8,128)(2,1)S(1)}, u32[]{:S(2)}, u32[]{:S(2)}) %collective-permute-start.1) | collective-permute-done | bytes 163872 | tf_op jit(solution)/shard_map/ppermute | solution.py:245
  30.8 2.3 %all-to-all-done.1.pieces_ref = bf16[8,4,16,256]{3,2,1,0:T(8,128)(2,1)S(1)} async-done(((bf16[8,4,16,256]{3,2,1,0:T(8,128)(2,1)}), bf16[8,4,16,256]{3,2,1,0:T(8,128)(2,1)S(1)}, u32[]{:S(2)}, u32[]{:S(2)}) %all-to-all-start.1) | async-done | bytes 262176 | tf_op jit(solution)/shard_map/all_to_all | solution.py:254
  33.1 0.6 send.1
  33.7 9.2 %collective-permute-start.2 = (bf16[2,4,80,256]{3,2,1,0:T(8,128)(2,1)S(1)}, bf16[2,4,80,256]{3,2,1,0:T(8,128)(2,1)S(1)}, u32[]{:S(2)}, u32[]{:S(2)}) collective-permute-start(bf16[2,4,80,256]{3,2,1,0:T(8,128)(2,1)S(1)} %get-tuple-element.15), channel_id=1, source_target_pairs={{63,0},{2,1},{1,2},{4,3},{3,4},{6,5},{5,6},{8,7},{7,8},{10,9},{9,1... | collective-permute-start | bytes 983048 | tf_op jit(solution)/shard_map/ppermute | solution.py:281
  42.8 1.9 %collective-permute-start.3 = (bf16[4,80,256]{2,1,0:T(8,128)(2,1)S(1)}, bf16[4,80,256]{2,1,0:T(8,128)(2,1)S(1)}, u32[]{:S(2)}, u32[]{:S(2)}) collective-permute-start(bf16[4,80,256]{2,1,0:T(8,128)(2,1)S(1)} %get-tuple-element.16), channel_id=1, source_target_pairs={{62,0},{3,1},{0,2},{5,3},{2,4},{7,5},{4,6},{9,7},{6,8},{11,9},{8,1... | collective-permute-start | bytes 491528 | tf_op jit(solution)/shard_map/ppermute | solution.py:282
  44.8 7.4 %collective-permute-done.3.far_ref = bf16[4,80,256]{2,1,0:T(8,128)(2,1)S(1)} collective-permute-done((bf16[4,80,256]{2,1,0:T(8,128)(2,1)S(1)}, bf16[4,80,256]{2,1,0:T(8,128)(2,1)S(1)}, u32[]{:S(2)}, u32[]{:S(2)}) %collective-permute-start.3) | collective-permute-done | bytes 163872 | tf_op jit(solution)/shard_map/ppermute | solution.py:282
  52.1 0.0 collective-permute-done.2.near_ref
  52.1 1.8 %grad_pre.1.pre_ref = bf16[768,256]{1,0:T(8,128)(2,1)S(1)} custom-call(s32[3]{0:T(128)S(1)} %pad_add_fusion.2.flags_ref, bf16[2,4,80,256]{3,2,1,0:T(8,128)(2,1)S(1)} %get-tuple-element.11.own_ref, bf16[4,80,256]{2,1,0:T(8,128)(2,1)S(1)} %collective-permute-done.1.part_ref, bf16[2,4,80,256]{3,2,1,0:T(8,128)(2,1)S(1)} %collective-permute-done.2.near_ref, ...), custom_call_target="tpu_custom_call" | custom-call | flops 905969664 | bytes 4194304 | tf_op jit(solution)/shard_map/grad_pre/pallas_call | solution.py:206
  53.9 1.9 %collective-permute-start.4 = (bf16[768,256]{1,0:T(8,128)(2,1)S(1)}, bf16[768,256]{1,0:T(8,128)(2,1)S(1)}, u32[]{:S(2)}, u32[]{:S(2)}) collective-permute-start(bf16[768,256]{1,0:T(8,128)(2,1)S(1)} %grad_pre.1.pre_ref), channel_id=1, source_target_pairs={{0,1},{1,0},{2,3},{3,2},{4,5},{5,4},{6,7},{7,6},{8,9},{9,8},{10,11... | collective-permute-start | bytes 1179656 | tf_op jit(solution)/shard_map/ppermute | solution.py:245
  55.9 0.2 fusion.11
  56.1 0.5 convolution_convert_fusion
  56.6 0.9 collective-permute-done.4.swapped_ref
  57.5 1.5 %grad_first.1 = bf16[16,9,16,128]{3,2,1,0:T(8,128)(2,1)S(1)} custom-call(s32[3]{0:T(128)S(1)} %pad_add_fusion.2.flags_ref, bf16[384,768]{1,0:T(8,128)(2,1)S(1)} %bitcast.47, bf16[768,256]{1,0:T(8,128)(2,1)S(1)} %grad_pre.1.pre_ref, bf16[768,256]{1,0:T(8,128)(2,1)S(1)} %collective-permute-done.4.swapped_ref), custom_call_target="tpu_custom_call" | custom-call | flops 452984832 | bytes 1048576 | tf_op jit(solution)/shard_map/grad_first/pallas_call | solution.py:206
  59.1 0.0 copy-start
  59.1 18.1 %all_to_all.20 = bf16[16,9,16,128]{3,2,1,0:T(8,128)(2,1)S(1)} all-to-all(bf16[16,9,16,128]{3,2,1,0:T(8,128)(2,1)S(1)} %grad_first.1), channel_id=1, replica_groups=mesh['xh'=2,'y'=4,'xl'=2,'z'=16,'c'=2] {'xh','y','xl'}, dimensions={0} | all-to-all | bytes 1179648 | tf_op jit(solution)/shard_map/all_to_all | solution.py:333
  77.2 0.1 convert_reduce_fusion
  77.3 0.1 copy.36
  77.4 0.6 copy.38
  78.1 6.3 %all-to-all-start.3 = ((bf16[16,8,144]{2,1,0:T(8,128)(2,1)}), bf16[16,8,144]{2,1,0:T(8,128)(2,1)S(1)}, u32[]{:S(2)}, u32[]{:S(2)}) async-start(bf16[16,8,144]{2,1,0:T(8,128)(2,1)} %copy.38), calls=%async_computation.3 | async-start | bytes 131072 | tf_op jit(solution)/shard_map/all_to_all | solution.py:337
  84.4 1.9 %grad_input.1 = bf16[4,64,256]{2,1,0:T(8,128)(2,1)} custom-call(s32[3]{0:T(128)S(1)} %pad_add_fusion.2.flags_ref, bf16[768,256]{1,0:T(8,128)(2,1)S(1)} %grad_pre.1.pre_ref, bf16[768,256]{1,0:T(8,128)(2,1)S(1)} %collective-permute-done.4.swapped_ref, bf16[4,64,256]{2,1,0:T(8,128)(2,1)S(1)} %bitcast.44, bf16[3,3,256,256]{3,2,1,0:T(8,128)(2,1)S(1)} %copy-done), custom_call_target="tpu_custom_call" | custom-call | flops 452984832 | bytes 2097152 | tf_op jit(solution)/shard_map/grad_input/pallas_call | solution.py:206
  86.3 11.0 %all-to-all-done.3 = bf16[16,8,144]{2,1,0:T(8,128)(2,1)S(1)} async-done(((bf16[16,8,144]{2,1,0:T(8,128)(2,1)}), bf16[16,8,144]{2,1,0:T(8,128)(2,1)S(1)}, u32[]{:S(2)}, u32[]{:S(2)}) %all-to-all-start.3) | async-done | bytes 36896 | tf_op jit(solution)/shard_map/all_to_all | solution.py:337
  97.3 0.1 reshape.93
  97.4 0.7 reshape.94
  (34 shorter events, 0.2 us)
Async XLA Ops:
  0.6 14.0 %copy-start.12 = (pred[16]{0:T(512)(128)(4,1)S(1)}, pred[16]{0:T(512)(128)(4,1)}, u32[]{:S(2)}) copy-start(pred[16]{0:T(512)(128)(4,1)} %constant.46.clone) | copy-start | bytes 52
  0.6 14.0 %copy-start.11 = (pred[2,16]{1,0:T(4,128)(4,1)S(1)}, pred[2,16]{1,0:T(4,128)(4,1)}, u32[]{:S(2)}) copy-start(pred[2,16]{1,0:T(4,128)(4,1)} %constant.62) | copy-start | bytes 100
  0.7 14.0 %copy-start.10 = (s32[2,16]{1,0:T(2,128)S(1)}, s32[2,16]{1,0:T(2,128)}, u32[]{:S(2)}) copy-start(s32[2,16]{1,0:T(2,128)} %constant.63) | copy-start | bytes 388
  0.7 13.5 %copy-start.6 = (s32[4,4]{1,0:T(4,128)S(1)}, s32[4,4]{1,0:T(4,128)}, u32[]{:S(2)}) copy-start(s32[4,4]{1,0:T(4,128)} %seams_ref.1) | copy-start | bytes 196
  0.7 0.9 copy-start.1
  1.6 0.9 copy-start.3
  2.5 0.7 copy-start.5
  3.2 9.1 %copy-start.8 = (bf16[1,4,1,64,256]{4,3,2,1,0:T(8,128)(2,1)S(1)}, bf16[1,4,1,64,256]{4,3,2,1,0:T(8,128)(2,1)}, u32[]{:S(2)}) copy-start(bf16[1,4,1,64,256]{4,3,2,1,0:T(8,128)(2,1)} %param.12) | copy-start | bytes 393220
  3.2 11.1 %copy-start.9 = (s32[4,4]{1,0:T(4,128)S(1)}, s32[4,4]{1,0:T(4,128)}, u32[]{:S(2)}) copy-start(s32[4,4]{1,0:T(4,128)} %param.18) | copy-start | bytes 196
  4.7 22.5 %copy-start.2 = (bf16[1,4,1,64,256]{4,3,2,1,0:T(8,128)(2,1)S(1)}, bf16[1,4,1,64,256]{4,3,2,1,0:T(8,128)(2,1)}, u32[]{:S(2)}) copy-start(bf16[1,4,1,64,256]{4,3,2,1,0:T(8,128)(2,1)} %param.14) | copy-start | bytes 393220
  4.7 22.5 %copy-start.4 = (bf16[1,4,1,64,256]{4,3,2,1,0:T(8,128)(2,1)S(1)}, bf16[1,4,1,64,256]{4,3,2,1,0:T(8,128)(2,1)}, u32[]{:S(2)}) copy-start(bf16[1,4,1,64,256]{4,3,2,1,0:T(8,128)(2,1)} %param.13) | copy-start | bytes 393220
  4.7 14.8 %all-to-all-start = ((bf16[8,96,256]{2,1,0:T(8,128)(2,1)}), bf16[8,96,256]{2,1,0:T(8,128)(2,1)S(1)}, u32[]{:S(2)}, u32[]{:S(2)}) async-start(bf16[8,96,256]{2,1,0:T(8,128)(2,1)} %pack.1), calls=%async_computation | async-start | bytes 786432 | tf_op jit(solution)/shard_map/all_to_all | solution.py:246
  12.2 3.2 %collective-permute-start = (bf16[4,64,256]{2,1,0:T(8,128)(2,1)S(1)}, bf16[4,64,256]{2,1,0:T(8,128)(2,1)S(1)}, u32[]{:S(2)}, u32[]{:S(2)}) collective-permute-start(bf16[4,64,256]{2,1,0:T(8,128)(2,1)S(1)} %bitcast.57), channel_id=1, source_target_pairs={{0,1},{1,0},{2,3},{3,2},{4,5},{5,4},{6,7},{7,6},{8,9},{9,8},{10,11... | collective-permute-start | bytes 393224 | tf_op jit(solution)/shard_map/ppermute | solution.py:245
  21.0 23.7 %copy-start.13 = (s32[128,1]{0,1:T(1,128)S(1)}, s32[128,1]{0,1:T(1,128)}, u32[]{:S(2)}) copy-start(s32[128,1]{0,1:T(1,128)} %constant.49.clone) | copy-start | bytes 1540
  21.0 31.1 %copy-start.7 = (bf16[3,3,256,256]{3,2,1,0:T(8,128)(2,1)S(1)}, bf16[3,3,256,256]{3,2,1,0:T(8,128)(2,1)}, u32[]{:S(2)}) copy-start(bf16[3,3,256,256]{3,2,1,0:T(8,128)(2,1)} %weight_ref.2) | copy-start | bytes 3538948
  21.0 12.0 %all-to-all-start.1 = ((bf16[8,4,16,256]{3,2,1,0:T(8,128)(2,1)}), bf16[8,4,16,256]{3,2,1,0:T(8,128)(2,1)S(1)}, u32[]{:S(2)}, u32[]{:S(2)}) async-start(bf16[8,4,16,256]{3,2,1,0:T(8,128)(2,1)} %bitcast.15), calls=%async_computation.1 | async-start | bytes 524288 | tf_op jit(solution)/shard_map/all_to_all | solution.py:254
  27.5 3.3 %collective-permute-start.1 = (bf16[4,80,256]{2,1,0:T(8,128)(2,1)S(1)}, bf16[4,80,256]{2,1,0:T(8,128)(2,1)S(1)}, u32[]{:S(2)}, u32[]{:S(2)}) collective-permute-start(bf16[4,80,256]{2,1,0:T(8,128)(2,1)S(1)} %slice_bitcast_fusion), channel_id=1, source_target_pairs={{0,1},{1,0},{2,3},{3,2},{4,5},{5,4},{6,7},{7,6},{8,9},{9,8},{10,11... | collective-permute-start | bytes 491528 | tf_op jit(solution)/shard_map/ppermute | solution.py:245
  33.7 18.5 %collective-permute-start.2 = (bf16[2,4,80,256]{3,2,1,0:T(8,128)(2,1)S(1)}, bf16[2,4,80,256]{3,2,1,0:T(8,128)(2,1)S(1)}, u32[]{:S(2)}, u32[]{:S(2)}) collective-permute-start(bf16[2,4,80,256]{3,2,1,0:T(8,128)(2,1)S(1)} %get-tuple-element.15), channel_id=1, source_target_pairs={{63,0},{2,1},{1,2},{4,3},{3,4},{6,5},{5,6},{8,7},{7,8},{10,9},{9,1... | collective-permute-start | bytes 983048 | tf_op jit(solution)/shard_map/ppermute | solution.py:281
  42.8 9.3 %collective-permute-start.3 = (bf16[4,80,256]{2,1,0:T(8,128)(2,1)S(1)}, bf16[4,80,256]{2,1,0:T(8,128)(2,1)S(1)}, u32[]{:S(2)}, u32[]{:S(2)}) collective-permute-start(bf16[4,80,256]{2,1,0:T(8,128)(2,1)S(1)} %get-tuple-element.16), channel_id=1, source_target_pairs={{62,0},{3,1},{0,2},{5,3},{2,4},{7,5},{4,6},{9,7},{6,8},{11,9},{8,1... | collective-permute-start | bytes 491528 | tf_op jit(solution)/shard_map/ppermute | solution.py:282
  53.9 3.6 %collective-permute-start.4 = (bf16[768,256]{1,0:T(8,128)(2,1)S(1)}, bf16[768,256]{1,0:T(8,128)(2,1)S(1)}, u32[]{:S(2)}, u32[]{:S(2)}) collective-permute-start(bf16[768,256]{1,0:T(8,128)(2,1)S(1)} %grad_pre.1.pre_ref), channel_id=1, source_target_pairs={{0,1},{1,0},{2,3},{3,2},{4,5},{5,4},{6,7},{7,6},{8,9},{9,8},{10,11... | collective-permute-start | bytes 1179656 | tf_op jit(solution)/shard_map/ppermute | solution.py:245
  59.1 25.3 %copy-start = (bf16[3,3,256,256]{3,2,1,0:T(8,128)(2,1)S(1)}, bf16[3,3,256,256]{3,2,1,0:T(8,128)(2,1)}, u32[]{:S(2)}) copy-start(bf16[3,3,256,256]{3,2,1,0:T(8,128)(2,1)} %weight_ref.3) | copy-start | bytes 3538948
  78.1 19.2 %all-to-all-start.3 = ((bf16[16,8,144]{2,1,0:T(8,128)(2,1)}), bf16[16,8,144]{2,1,0:T(8,128)(2,1)S(1)}, u32[]{:S(2)}, u32[]{:S(2)}) async-start(bf16[16,8,144]{2,1,0:T(8,128)(2,1)} %copy.38), calls=%async_computation.3 | async-start | bytes 131072 | tf_op jit(solution)/shard_map/all_to_all | solution.py:337

commit v4 on v3

--- a/solution.py
+++ b/solution.py
@@ -23,48 +23,92 @@
     return [pl.BlockSpec(memory_space=pltpu.VMEM)] * n
 
 
-def pack_kernel(local, side, blocks, seams_ref, g_ref, p_ref, out_ref):
+def pack_kernel(local, side, blocks, seams_ref, g_ref, p_ref, out_ref, ends, cells_held, end_sems, sems):
     px_blocks, ch_blocks = blocks
     channels = g_ref.shape[-1]
     px, ch = side // px_blocks, channels // ch_blocks
     count = px * 2 // ch_blocks
-    shape = (local * CELLS, local * side)
-    line = lax.broadcasted_iota(jnp.int32, shape, 0)
-    pixel = lax.broadcasted_iota(jnp.int32, shape, 1)
-    cell, base = line % CELLS, line // CELLS * side
-    of_g = jnp.where(cell < 2, base + cell, jnp.where(cell < 4, base + side - 4 + cell, -1))
-    of_p = jnp.where(cell == 4, base, jnp.where(cell == 5, base + side - 1, -1))
-    take = lambda at, ref: jnp.dot(
-        jnp.where(at == pixel, 1.0, 0.0).astype(jnp.bfloat16),
-        ref[...].reshape(local * side, channels),
-        preferred_element_type=jnp.float32,
-    )
-    cells = take(of_g, g_ref) + take(of_p, p_ref)
-    line = lax.broadcasted_iota(jnp.int32, cells.shape, 0)
-    lane = lax.broadcasted_iota(jnp.int32, cells.shape, 1)
-    for face in range(local):
-        for i in range(4):
-            here = (line == face * CELLS + SEAM_AT) & (lane == i)
-            cells = jnp.where(here, seams_ref[face, i].astype(jnp.float32), cells)
-    cells = cells.astype(jnp.bfloat16)
+    fetches = [
+        pltpu.make_async_copy(source.at[:, at : at + GAP], ends.at[which, end], end_sems.at[which, end])
+        for which, source in enumerate((g_ref, p_ref))
+        for end, at in enumerate((0, side - GAP))
+    ]
+    for fetch in fetches:
+        fetch.start()
+    moves = []
     for b in range(px_blocks * ch_blocks):
         i, j = divmod(b, ch_blocks)
         for face in range(local):
             at = face * count
             for which, source in enumerate((g_ref, p_ref)):
-                piece = source[face, i * px : (i + 1) * px, j * ch : (j + 1) * ch]
+                piece = source.at[face, i * px : (i + 1) * px, j * ch : (j + 1) * ch]
                 if ch_blocks == 1:
-                    out_ref[b, at + which * px : at + (which + 1) * px] = piece
+                    into = out_ref.at[b, at + which * px : at + (which + 1) * px]
                 else:
-                    out_ref[b, at : at + px, which * ch : (which + 1) * ch] = piece
-        out_ref[b, local * count :] = cells
-
-
-def pick_kernel(faces, local, count, want_ref, table_ref, out_ref):
+                    into = out_ref.at[b, at : at + px, which * ch : (which + 1) * ch]
+                moves.append(pltpu.make_async_copy(piece, into, sems.at[len(moves)]))
+    for move in moves:
+        move.start()
+    held = 4 * local * GAP
+    line = lax.broadcasted_iota(jnp.int32, (local * CELLS, held), 0)
+    pixel = lax.broadcasted_iota(jnp.int32, (local * CELLS, held), 1)
+    cell, face_at = line % CELLS, line // CELLS * GAP
+    block = local * GAP
+    at = jnp.where(cell < 2, face_at + cell, block + face_at + GAP - 4 + cell)
+    at = jnp.where(cell == 4, 2 * block + face_at, at)
+    at = jnp.where(cell == 5, 3 * block + face_at + GAP - 1, at)
+    take = jnp.where((at == pixel) & (cell < SEAM_AT), 1.0, 0.0).astype(jnp.bfloat16)
+    line = lax.broadcasted_iota(jnp.int32, (local * CELLS, channels), 0)
+    lane = lax.broadcasted_iota(jnp.int32, (local * CELLS, channels), 1)
+    seams = jnp.zeros((local * CELLS, channels), jnp.float32)
+    for face in range(local):
+        for i in range(4):
+            here = (line == face * CELLS + SEAM_AT) & (lane == i)
+            seams = jnp.where(here, seams_ref[face, i].astype(jnp.float32), seams)
+    for fetch in fetches:
+        fetch.wait()
+    cells = jnp.dot(take, ends[...].reshape(held, channels), preferred_element_type=jnp.float32)
+    cells_held[...] = (cells + seams).astype(jnp.bfloat16)
+    for b in range(px_blocks * ch_blocks):
+        into = out_ref.at[b, local * count : local * (count + CELLS)]
+        moves.append(pltpu.make_async_copy(cells_held, into, sems.at[len(moves)]))
+        moves[-1].start()
+    for move in moves:
+        move.wait()
+
+
+def pick_kernel(faces, local, count, want_ref, table_ref, out_ref, sems):
+    moves = []
     for i in range(faces):
         face = want_ref[i]
         at = pl.multiple_of(lax.rem(face, local) * count, 16)
-        out_ref[i] = table_ref[lax.div(face, local), pl.ds(at, count)]
+        source = table_ref.at[lax.div(face, local), pl.ds(at, count)]
+        moves.append(pltpu.make_async_copy(source, out_ref.at[i], sems.at[i]))
+        moves[-1].start()
+    for move in moves:
+        move.wait()
+
+
+def first_sum_kernel(scale, got_ref, out_ref):
+    total = got_ref[0].astype(jnp.float32)
+    for i in range(1, got_ref.shape[0]):
+        total = total + got_ref[i].astype(jnp.float32)
+    turned = (total * scale).reshape(-1, total.shape[-1]).T
+    out_ref[...] = turned.reshape(out_ref.shape).astype(jnp.bfloat16)
+
+
+def second_sum_kernel(got_ref, out_ref):
+    total = got_ref[0].astype(jnp.float32)
+    for i in range(1, got_ref.shape[0]):
+        total = total + got_ref[i].astype(jnp.float32)
+    _, _, per_tile, width = out_ref.shape
+    lines = total.shape[1] // 9
+    for tap in range(9):
+        r, c = divmod(tap, 3)
+        for h in range(width // lines):
+            out_ref[r, c, :, h * lines : (h + 1) * lines] = total[
+                h * per_tile : (h + 1) * per_tile, tap * lines : (tap + 1) * lines
+            ]
 
 
 def border_kernel(local, side, index_ref, cells_ref, g_ref, p_ref, own_ref, wrap_ref):
@@ -177,7 +221,7 @@
         out_ref[face] = (own + grad[at : at + side, :]).astype(jnp.bfloat16)
 
 
-def grad_first_kernel(row, nxl, flags_ref, x_ref, pre_ref, swapped_ref, out_ref, rows4):
+def grad_first_kernel(row, nxl, per_tile, flags_ref, x_ref, pre_ref, swapped_ref, out_ref, rows4):
     four_rows(rows4, flags_ref[0], row, pre_ref, swapped_ref)
     dests, _, lines, half = out_ref.shape
     for r in range(3):
@@ -191,25 +235,26 @@
             split = turned.reshape(dests // 2, 2, lines, half)
             left = split[:, 0].reshape(-1, half)
             right = split[:, 1].reshape(-1, half)
-            low = lax.broadcasted_iota(jnp.int32, left.shape, 1) < half // 2
+            low = lax.broadcasted_iota(jnp.int32, left.shape, 1) % (2 * per_tile) < per_tile
             ones = (
-                jnp.where(low, left, pltpu.roll(right, half // 2, 1)),
-                jnp.where(low, pltpu.roll(left, half // 2, 1), right),
+                jnp.where(low, left, pltpu.roll(right, per_tile, 1)),
+                jnp.where(low, pltpu.roll(left, half - per_tile, 1), right),
             )
             for xl, one in enumerate(ones):
                 for d in range(dests // 2):
                     out_ref[2 * d + xl, 3 * r + c] = one[d * lines : (d + 1) * lines, :].astype(jnp.bfloat16)
 
 
-def kernel(body, out_shape, inputs, smem=0, scratch=(), name=None, flops=0, nbytes=2**20, exps=0):
+def kernel(body, out_shape, inputs, smem=0, scratch=(), name=None, flops=0, nbytes=2**20, exps=0, hbm=(0, 0), vmem=VMEM):
     many = isinstance(out_shape, tuple)
+    spots = [pl.BlockSpec(memory_space=pltpu.HBM)] * hbm[0] + whole(len(inputs) - smem - hbm[0])
     return pl.pallas_call(
         body,
         out_shape=out_shape,
-        in_specs=[pl.BlockSpec(memory_space=pltpu.SMEM)] * smem + whole(len(inputs) - smem),
-        out_specs=tuple(whole(len(out_shape))) if many else whole(1)[0],
+        in_specs=[pl.BlockSpec(memory_space=pltpu.SMEM)] * smem + spots,
+        out_specs=tuple(whole(len(out_shape))) if many else pl.BlockSpec(memory_space=pltpu.HBM) if hbm[1] else whole(1)[0],
         scratch_shapes=scratch,
-        compiler_params=pltpu.CompilerParams(vmem_limit_bytes=VMEM),
+        compiler_params=pltpu.CompilerParams(vmem_limit_bytes=vmem),
         cost_estimate=pl.CostEstimate(flops=flops, bytes_accessed=nbytes, transcendentals=exps),
         name=name,
     )(*inputs)
@@ -240,7 +285,15 @@
         shape((nface, local * (count + CELLS), channels), bf),
         (seams, g, p),
         1,
-        name="pack",
+        (
+            pltpu.VMEM((2, 2, local, GAP, channels), bf),
+            pltpu.VMEM((local * CELLS, channels), bf),
+            pltpu.SemaphoreType.DMA((2, 2)),
+            pltpu.SemaphoreType.DMA((nface * (2 * local + 1),)),
+        ),
+        "pack",
+        hbm=(2, 1),
+        vmem=None,
     )
     swap = lambda a: lax.ppermute(a, "c", [(0, 1), (1, 0)])
     table, other = lax.optimization_barrier((lax.all_to_all(sent, FACE, 0, 0, tiled=True), swap(x)))
@@ -249,7 +302,8 @@
     all_seams = cells[:, SEAM_AT, :4].astype(jnp.int32)
     want = jnp.where(top, all_seams[:, 0], all_seams[:, 2])
     picked = kernel(
-        functools.partial(pick_kernel, faces, local, count), shape((faces, count, channels), bf), (want, table), 1, name="pick"
+        functools.partial(pick_kernel, faces, local, count), shape((faces, count, channels), bf), (want, table), 1,
+        (pltpu.SemaphoreType.DMA((faces,)),), "pick", hbm=(0, 1),
     )
     wrapped = lax.all_to_all(picked.reshape(nface, local, count, channels), FACE, 0, 0, tiled=True)
 
@@ -299,8 +353,8 @@
     shifted = jnp.stack(
         [jnp.pad(both, ((0, 0), (0, 0), (GAP + 1 - c, GAP - 1 + c), (0, 0))) for c in range(3)], 0
     ).reshape(3, 2 * row, channels)
-    kept = np.arange(half)
-    chosen = (kept // per_tile) * (nc * per_tile) + kept % per_tile
+    kept = np.arange(channels).reshape(nxl, nz, nc, per_tile)[:, :, 0]
+    chosen = np.transpose(kept, (1, 0, 2)).reshape(half)
     choose = (chosen[:, None] + core * per_tile == np.arange(channels)[None, :]).astype(bf)
     x_turned = lax.dot_general(
         choose, shifted, (((1,), (2,)), ((), ())), preferred_element_type=jnp.float32
@@ -311,7 +365,7 @@
     width = channels // nface
     lines = width // nxl
     parts = kernel(
-        functools.partial(grad_first_kernel, row, nxl),
+        functools.partial(grad_first_kernel, row, nxl, per_tile),
         shape((nface * nxl, 9, lines, half), bf),
         (flags, x_turned, grad_pre, swapped),
         1,
@@ -331,12 +385,14 @@
     )
     scale_factor = 1.0 / math.sqrt(faces * ntile * side)
     got = lax.all_to_all(parts, FACE + ("xl",), 0, 0, tiled=True)
-    total = jnp.sum(got.astype(jnp.float32), 0) * scale_factor
-    total = jnp.transpose(total.reshape(9 * lines, half)).reshape(nxl, nz, per_tile, 9 * lines)
-    total = jnp.transpose(total, (1, 0, 2, 3)).reshape(nz, nxl * per_tile, 9 * lines).astype(bf)
+    total = kernel(
+        functools.partial(first_sum_kernel, scale_factor),
+        shape((nz, nxl * per_tile, 9 * lines), bf),
+        (got,),
+        name="first_sum",
+    )
     got = lax.all_to_all(total, "z", 0, 0, tiled=True)
-    total = jnp.sum(got.astype(jnp.float32), 0).reshape(nxl, per_tile, 9, lines)
-    first_out = jnp.transpose(total, (2, 1, 0, 3)).reshape(3, 3, per_tile, width)
+    first_out = kernel(second_sum_kernel, shape((3, 3, per_tile, width), jnp.float32), (got,), name="second_sum")
     return grad_input.reshape(saved_input.shape), first_out
 
 

time: 99.4 us -> 106 us (1.066)
  Pallas kernels: 8.85 us -> 19.7 us
  local copies, waits for them, and re-layouts: 4.83 us -> 0.72 us
    pallas_call x7 -> x9, Pallas kernels: 8.85 us -> 19.7 us  [kernel(): pl.pallas_call(body, out_shape=out_shape, in_specs=[pl.BlockSpec(memory_s...]
    unnamed x29 -> x23, local copies, waits for them, and re-layouts: 2.64 us -> 0.16 us
where the time goes in v4:
time: 106 us; the launch traced here: 105 us
  starting transfers between devices  36.9 us (35%)
  waiting for transfers between devices  27.5 us (26%)
  Pallas kernels  19.7 us (19%)
  blocking collectives  18.1 us (17%)
    pallas_call x9, Pallas kernels, kernel(): pl.pallas_call(body, out_shape=out_shape, in_specs=[pl.BlockSpec(memory_s...  19.7 us
    all_to_all x1, blocking collectives, on_device(): got = lax.all_to_all(parts, FACE + ('xl',), 0, 0, tiled=True)  18.1 us
    all_to_all x1, waiting for transfers between devices, on_device(): got = lax.all_to_all(total, 'z', 0, 0, tiled=True)  11 us
    ppermute x1, starting transfers between devices, on_device(): near = lax.ppermute(near, TILE, pairs(1))  9.15 us
    all_to_all x1, starting transfers between devices, on_device(): lax.all_to_all(sent, FACE, 0, 0, tiled=True)  7.58 us
    ppermute x1, waiting for transfers between devices, on_device(): far = lax.ppermute(far, TILE, pairs(2))  7.37 us
    all_to_all x1, starting transfers between devices, on_device(): got = lax.all_to_all(total, 'z', 0, 0, tiled=True)  6.28 us
    all_to_all x1, starting transfers between devices, on_device(): lax.all_to_all(picked.reshape(nface, local, count, channels), FACE, 0, 0,...  6.21 us
  transfers between devices with their start and end apart: 8, of which 7 were waited for; matrix products, arithmetic and copies ran while one was open for 1% of the time, Pallas kernels for 2%

profile of v4, /device:TPU:6, one launch (start us, length us, event | category | flops | bytes accessed | tf_op | source)
XLA Modules:
  0.0 104.7 jit_solution(1496723295841562769)
XLA Ops:
  0.6 0.0 copy-start.9
  0.6 0.0 copy-start.8
  0.7 0.0 copy-start.7
  0.7 0.0 copy-start.5
  0.7 10.6 %pack.1 = bf16[8,96,256]{2,1,0:T(8,128)(2,1)} custom-call(s32[4,4]{1,0:T(4,128)} %seams_ref.1, bf16[4,64,256]{2,1,0:T(8,128)(2,1)} %bitcast.36, bf16[4,64,256]{2,1,0:T(8,128)(2,1)} %bitcast.42), custom_call_target="tpu_custom_call" | custom-call | bytes 1048576 | tf_op jit(solution)/shard_map/pack/pallas_call | solution.py:251
  11.3 0.0 copy-start.1
  11.4 0.0 copy-start.2
  11.4 7.6 %all-to-all-start = ((bf16[8,96,256]{2,1,0:T(8,128)(2,1)}), bf16[8,96,256]{2,1,0:T(8,128)(2,1)S(1)}, u32[]{:S(2)}, u32[]{:S(2)}) async-start(bf16[8,96,256]{2,1,0:T(8,128)(2,1)} %pack.1), calls=%async_computation | async-start | bytes 786432 | tf_op jit(solution)/shard_map/all_to_all | solution.py:299
  18.9 1.9 %collective-permute-start = (bf16[4,64,256]{2,1,0:T(8,128)(2,1)S(1)}, bf16[4,64,256]{2,1,0:T(8,128)(2,1)S(1)}, u32[]{:S(2)}, u32[]{:S(2)}) collective-permute-start(bf16[4,64,256]{2,1,0:T(8,128)(2,1)S(1)} %bitcast.47), channel_id=1, source_target_pairs={{0,1},{1,0},{2,3},{3,2},{4,5},{5,4},{6,7},{7,6},{8,9},{9,8},{10,11... | collective-permute-start | bytes 393224 | tf_op jit(solution)/shard_map/ppermute | solution.py:298
  20.9 0.0 copy-done.5
  20.9 0.1 fusion.12
  21.0 0.1 slice_select_fusion
  21.0 0.1 copy.19
  21.1 0.1 pad_add_fusion
  21.2 0.1 copy.18
  21.3 0.1 select_multiply_fusion
  21.4 0.0 copy-done.8
  21.4 0.1 select_n.59.index_ref
  21.5 0.7 collective-permute-done
  22.2 4.0 %all-to-all-done.table_ref = bf16[8,96,256]{2,1,0:T(8,128)(2,1)S(1)} async-done(((bf16[8,96,256]{2,1,0:T(8,128)(2,1)}), bf16[8,96,256]{2,1,0:T(8,128)(2,1)S(1)}, u32[]{:S(2)}, u32[]{:S(2)}) %all-to-all-start) | async-done | bytes 393248 | tf_op jit(solution)/shard_map/all_to_all | solution.py:299
  26.2 0.1 copy.23
  26.3 1.6 %pick.1 = bf16[32,16,256]{2,1,0:T(8,128)(2,1)} custom-call(s32[32]{0:T(128)S(1)} %fusion.9.want_ref, bf16[8,96,256]{2,1,0:T(8,128)(2,1)S(1)} %all-to-all-done.table_ref), custom_call_target="tpu_custom_call" | custom-call | bytes 1048576 | tf_op jit(solution)/shard_map/pick/pallas_call | solution.py:251
  27.9 0.0 copy-start.10
  27.9 0.0 copy-start.3
  27.9 6.2 %all-to-all-start.1 = ((bf16[8,4,16,256]{3,2,1,0:T(8,128)(2,1)}), bf16[8,4,16,256]{3,2,1,0:T(8,128)(2,1)S(1)}, u32[]{:S(2)}, u32[]{:S(2)}) async-start(bf16[8,4,16,256]{3,2,1,0:T(8,128)(2,1)} %bitcast.15), calls=%async_computation.1 | async-start | bytes 524288 | tf_op jit(solution)/shard_map/all_to_all | solution.py:308
  34.2 0.2 border.1
  34.4 1.9 %collective-permute-start.1 = (bf16[4,80,256]{2,1,0:T(8,128)(2,1)S(1)}, bf16[4,80,256]{2,1,0:T(8,128)(2,1)S(1)}, u32[]{:S(2)}, u32[]{:S(2)}) collective-permute-start(bf16[4,80,256]{2,1,0:T(8,128)(2,1)S(1)} %slice_bitcast_fusion), channel_id=1, source_target_pairs={{0,1},{1,0},{2,3},{3,2},{4,5},{5,4},{6,7},{7,6},{8,9},{9,8},{10,11... | collective-permute-start | bytes 491528 | tf_op jit(solution)/shard_map/ppermute | solution.py:298
  36.4 0.1 pad_add_fusion.2.flags_ref
  36.4 1.3 %collective-permute-done.1.part_ref = bf16[4,80,256]{2,1,0:T(8,128)(2,1)S(1)} collective-permute-done((bf16[4,80,256]{2,1,0:T(8,128)(2,1)S(1)}, bf16[4,80,256]{2,1,0:T(8,128)(2,1)S(1)}, u32[]{:S(2)}, u32[]{:S(2)}) %collective-permute-start.1) | collective-permute-done | bytes 163872 | tf_op jit(solution)/shard_map/ppermute | solution.py:298
  37.7 2.3 %all-to-all-done.1.pieces_ref = bf16[8,4,16,256]{3,2,1,0:T(8,128)(2,1)S(1)} async-done(((bf16[8,4,16,256]{3,2,1,0:T(8,128)(2,1)}), bf16[8,4,16,256]{3,2,1,0:T(8,128)(2,1)S(1)}, u32[]{:S(2)}, u32[]{:S(2)}) %all-to-all-start.1) | async-done | bytes 262176 | tf_op jit(solution)/shard_map/all_to_all | solution.py:308
  40.0 0.6 send.1
  40.6 9.2 %collective-permute-start.2 = (bf16[2,4,80,256]{3,2,1,0:T(8,128)(2,1)S(1)}, bf16[2,4,80,256]{3,2,1,0:T(8,128)(2,1)S(1)}, u32[]{:S(2)}, u32[]{:S(2)}) collective-permute-start(bf16[2,4,80,256]{3,2,1,0:T(8,128)(2,1)S(1)} %get-tuple-element.15), channel_id=1, source_target_pairs={{63,0},{2,1},{1,2},{4,3},{3,4},{6,5},{5,6},{8,7},{7,8},{10,9},{9,1... | collective-permute-start | bytes 983048 | tf_op jit(solution)/shard_map/ppermute | solution.py:335
  49.8 1.9 %collective-permute-start.3 = (bf16[4,80,256]{2,1,0:T(8,128)(2,1)S(1)}, bf16[4,80,256]{2,1,0:T(8,128)(2,1)S(1)}, u32[]{:S(2)}, u32[]{:S(2)}) collective-permute-start(bf16[4,80,256]{2,1,0:T(8,128)(2,1)S(1)} %get-tuple-element.16), channel_id=1, source_target_pairs={{62,0},{3,1},{0,2},{5,3},{2,4},{7,5},{4,6},{9,7},{6,8},{11,9},{8,1... | collective-permute-start | bytes 491528 | tf_op jit(solution)/shard_map/ppermute | solution.py:336
  51.7 7.4 %collective-permute-done.3.far_ref = bf16[4,80,256]{2,1,0:T(8,128)(2,1)S(1)} collective-permute-done((bf16[4,80,256]{2,1,0:T(8,128)(2,1)S(1)}, bf16[4,80,256]{2,1,0:T(8,128)(2,1)S(1)}, u32[]{:S(2)}, u32[]{:S(2)}) %collective-permute-start.3) | collective-permute-done | bytes 163872 | tf_op jit(solution)/shard_map/ppermute | solution.py:336
  59.1 0.0 collective-permute-done.2.near_ref
  59.1 1.8 %grad_pre.1.pre_ref = bf16[768,256]{1,0:T(8,128)(2,1)S(1)} custom-call(s32[3]{0:T(128)S(1)} %pad_add_fusion.2.flags_ref, bf16[2,4,80,256]{3,2,1,0:T(8,128)(2,1)S(1)} %get-tuple-element.11.own_ref, bf16[4,80,256]{2,1,0:T(8,128)(2,1)S(1)} %collective-permute-done.1.part_ref, bf16[2,4,80,256]{3,2,1,0:T(8,128)(2,1)S(1)} %collective-permute-done.2.near_ref, ...), custom_call_target="tpu_custom_call" | custom-call | flops 905969664 | bytes 4194304 | tf_op jit(solution)/shard_map/grad_pre/pallas_call | solution.py:251
  60.8 1.9 %collective-permute-start.4 = (bf16[768,256]{1,0:T(8,128)(2,1)S(1)}, bf16[768,256]{1,0:T(8,128)(2,1)S(1)}, u32[]{:S(2)}, u32[]{:S(2)}) collective-permute-start(bf16[768,256]{1,0:T(8,128)(2,1)S(1)} %grad_pre.1.pre_ref), channel_id=1, source_target_pairs={{0,1},{1,0},{2,3},{3,2},{4,5},{5,4},{6,7},{7,6},{8,9},{9,8},{10,11... | collective-permute-start | bytes 1179656 | tf_op jit(solution)/shard_map/ppermute | solution.py:298
  62.8 0.2 fusion.11
  63.0 0.5 convolution_convert_fusion
  63.5 1.0 collective-permute-done.4.swapped_ref
  64.5 1.5 %grad_first.1 = bf16[16,9,16,128]{3,2,1,0:T(8,128)(2,1)S(1)} custom-call(s32[3]{0:T(128)S(1)} %pad_add_fusion.2.flags_ref, bf16[384,768]{1,0:T(8,128)(2,1)S(1)} %bitcast.41, bf16[768,256]{1,0:T(8,128)(2,1)S(1)} %grad_pre.1.pre_ref, bf16[768,256]{1,0:T(8,128)(2,1)S(1)} %collective-permute-done.4.swapped_ref), custom_call_target="tpu_custom_call" | custom-call | flops 452984832 | bytes 1048576 | tf_op jit(solution)/shard_map/grad_first/pallas_call | solution.py:251
  66.0 0.0 copy-start
  66.0 18.1 %all_to_all.20.got_ref = bf16[16,9,16,128]{3,2,1,0:T(8,128)(2,1)S(1)} all-to-all(bf16[16,9,16,128]{3,2,1,0:T(8,128)(2,1)S(1)} %grad_first.1), channel_id=1, replica_groups=mesh['xh'=2,'y'=4,'xl'=2,'z'=16,'c'=2] {'xh','y','xl'}, dimensions={0} | all-to-all | bytes 1179648 | tf_op jit(solution)/shard_map/all_to_all | solution.py:387
  84.1 0.8 first_sum.1
  84.9 6.3 %all-to-all-start.3 = ((bf16[16,8,144]{2,1,0:T(8,128)(2,1)}), bf16[16,8,144]{2,1,0:T(8,128)(2,1)S(1)}, u32[]{:S(2)}, u32[]{:S(2)}) async-start(bf16[16,8,144]{2,1,0:T(8,128)(2,1)} %first_sum.1), calls=%async_computation.3 | async-start | bytes 131072 | tf_op jit(solution)/shard_map/all_to_all | solution.py:394
  91.2 1.9 %grad_input.1 = bf16[4,64,256]{2,1,0:T(8,128)(2,1)} custom-call(s32[3]{0:T(128)S(1)} %pad_add_fusion.2.flags_ref, bf16[768,256]{1,0:T(8,128)(2,1)S(1)} %grad_pre.1.pre_ref, bf16[768,256]{1,0:T(8,128)(2,1)S(1)} %collective-permute-done.4.swapped_ref, bf16[4,64,256]{2,1,0:T(8,128)(2,1)S(1)} %bitcast.38, bf16[3,3,256,256]{3,2,1,0:T(8,128)(2,1)S(1)} %copy-done), custom_call_target="tpu_custom_call" | custom-call | flops 452984832 | bytes 2097152 | tf_op jit(solution)/shard_map/grad_input/pallas_call | solution.py:251
  93.0 11.0 %all-to-all-done.3.got_ref = bf16[16,8,144]{2,1,0:T(8,128)(2,1)S(1)} async-done(((bf16[16,8,144]{2,1,0:T(8,128)(2,1)}), bf16[16,8,144]{2,1,0:T(8,128)(2,1)S(1)}, u32[]{:S(2)}, u32[]{:S(2)}) %all-to-all-start.3) | async-done | bytes 36896 | tf_op jit(solution)/shard_map/all_to_all | solution.py:394
  104.0 0.7 second_sum.1
  (20 shorter events, 0.1 us)
Async XLA Ops:
  0.6 20.7 %copy-start.9 = (pred[16]{0:T(512)(128)(4,1)S(1)}, pred[16]{0:T(512)(128)(4,1)}, u32[]{:S(2)}) copy-start(pred[16]{0:T(512)(128)(4,1)} %constant.42.clone) | copy-start | bytes 52
  0.6 20.7 %copy-start.8 = (pred[2,16]{1,0:T(4,128)(4,1)S(1)}, pred[2,16]{1,0:T(4,128)(4,1)}, u32[]{:S(2)}) copy-start(pred[2,16]{1,0:T(4,128)(4,1)} %constant.58) | copy-start | bytes 100
  0.7 20.7 %copy-start.7 = (s32[2,16]{1,0:T(2,128)S(1)}, s32[2,16]{1,0:T(2,128)}, u32[]{:S(2)}) copy-start(s32[2,16]{1,0:T(2,128)} %constant.59) | copy-start | bytes 388
  0.7 20.2 %copy-start.5 = (s32[4,4]{1,0:T(4,128)S(1)}, s32[4,4]{1,0:T(4,128)}, u32[]{:S(2)}) copy-start(s32[4,4]{1,0:T(4,128)} %seams_ref.1) | copy-start | bytes 196
  0.7 18.3 %copy-start.4 = (bf16[1,4,1,64,256]{4,3,2,1,0:T(8,128)(2,1)S(1)}, bf16[1,4,1,64,256]{4,3,2,1,0:T(8,128)(2,1)}, u32[]{:S(2)}) copy-start(bf16[1,4,1,64,256]{4,3,2,1,0:T(8,128)(2,1)} %param.12) | copy-start | bytes 393220
  0.7 20.3 %copy-start.6 = (s32[4,4]{1,0:T(4,128)S(1)}, s32[4,4]{1,0:T(4,128)}, u32[]{:S(2)}) copy-start(s32[4,4]{1,0:T(4,128)} %param.18) | copy-start | bytes 196
  11.3 22.8 %copy-start.1 = (bf16[1,4,1,64,256]{4,3,2,1,0:T(8,128)(2,1)S(1)}, bf16[1,4,1,64,256]{4,3,2,1,0:T(8,128)(2,1)}, u32[]{:S(2)}) copy-start(bf16[1,4,1,64,256]{4,3,2,1,0:T(8,128)(2,1)} %param.14) | copy-start | bytes 393220
  11.4 22.8 %copy-start.2 = (bf16[1,4,1,64,256]{4,3,2,1,0:T(8,128)(2,1)S(1)}, bf16[1,4,1,64,256]{4,3,2,1,0:T(8,128)(2,1)}, u32[]{:S(2)}) copy-start(bf16[1,4,1,64,256]{4,3,2,1,0:T(8,128)(2,1)} %param.13) | copy-start | bytes 393220
  11.4 14.8 %all-to-all-start = ((bf16[8,96,256]{2,1,0:T(8,128)(2,1)}), bf16[8,96,256]{2,1,0:T(8,128)(2,1)S(1)}, u32[]{:S(2)}, u32[]{:S(2)}) async-start(bf16[8,96,256]{2,1,0:T(8,128)(2,1)} %pack.1), calls=%async_computation | async-start | bytes 786432 | tf_op jit(solution)/shard_map/all_to_all | solution.py:299
  18.9 3.2 %collective-permute-start = (bf16[4,64,256]{2,1,0:T(8,128)(2,1)S(1)}, bf16[4,64,256]{2,1,0:T(8,128)(2,1)S(1)}, u32[]{:S(2)}, u32[]{:S(2)}) collective-permute-start(bf16[4,64,256]{2,1,0:T(8,128)(2,1)S(1)} %bitcast.47), channel_id=1, source_target_pairs={{0,1},{1,0},{2,3},{3,2},{4,5},{5,4},{6,7},{7,6},{8,9},{9,8},{10,11... | collective-permute-start | bytes 393224 | tf_op jit(solution)/shard_map/ppermute | solution.py:298
  27.9 23.8 %copy-start.10 = (s32[128,1]{0,1:T(1,128)S(1)}, s32[128,1]{0,1:T(1,128)}, u32[]{:S(2)}) copy-start(s32[128,1]{0,1:T(1,128)} %constant.45.clone) | copy-start | bytes 1540
  27.9 31.2 %copy-start.3 = (bf16[3,3,256,256]{3,2,1,0:T(8,128)(2,1)S(1)}, bf16[3,3,256,256]{3,2,1,0:T(8,128)(2,1)}, u32[]{:S(2)}) copy-start(bf16[3,3,256,256]{3,2,1,0:T(8,128)(2,1)} %weight_ref.2) | copy-start | bytes 3538948
  27.9 12.1 %all-to-all-start.1 = ((bf16[8,4,16,256]{3,2,1,0:T(8,128)(2,1)}), bf16[8,4,16,256]{3,2,1,0:T(8,128)(2,1)S(1)}, u32[]{:S(2)}, u32[]{:S(2)}) async-start(bf16[8,4,16,256]{3,2,1,0:T(8,128)(2,1)} %bitcast.15), calls=%async_computation.1 | async-start | bytes 524288 | tf_op jit(solution)/shard_map/all_to_all | solution.py:308
  34.4 3.3 %collective-permute-start.1 = (bf16[4,80,256]{2,1,0:T(8,128)(2,1)S(1)}, bf16[4,80,256]{2,1,0:T(8,128)(2,1)S(1)}, u32[]{:S(2)}, u32[]{:S(2)}) collective-permute-start(bf16[4,80,256]{2,1,0:T(8,128)(2,1)S(1)} %slice_bitcast_fusion), channel_id=1, source_target_pairs={{0,1},{1,0},{2,3},{3,2},{4,5},{5,4},{6,7},{7,6},{8,9},{9,8},{10,11... | collective-permute-start | bytes 491528 | tf_op jit(solution)/shard_map/ppermute | solution.py:298
  40.6 18.5 %collective-permute-start.2 = (bf16[2,4,80,256]{3,2,1,0:T(8,128)(2,1)S(1)}, bf16[2,4,80,256]{3,2,1,0:T(8,128)(2,1)S(1)}, u32[]{:S(2)}, u32[]{:S(2)}) collective-permute-start(bf16[2,4,80,256]{3,2,1,0:T(8,128)(2,1)S(1)} %get-tuple-element.15), channel_id=1, source_target_pairs={{63,0},{2,1},{1,2},{4,3},{3,4},{6,5},{5,6},{8,7},{7,8},{10,9},{9,1... | collective-permute-start | bytes 983048 | tf_op jit(solution)/shard_map/ppermute | solution.py:335
  49.8 9.3 %collective-permute-start.3 = (bf16[4,80,256]{2,1,0:T(8,128)(2,1)S(1)}, bf16[4,80,256]{2,1,0:T(8,128)(2,1)S(1)}, u32[]{:S(2)}, u32[]{:S(2)}) collective-permute-start(bf16[4,80,256]{2,1,0:T(8,128)(2,1)S(1)} %get-tuple-element.16), channel_id=1, source_target_pairs={{62,0},{3,1},{0,2},{5,3},{2,4},{7,5},{4,6},{9,7},{6,8},{11,9},{8,1... | collective-permute-start | bytes 491528 | tf_op jit(solution)/shard_map/ppermute | solution.py:336
  60.8 3.6 %collective-permute-start.4 = (bf16[768,256]{1,0:T(8,128)(2,1)S(1)}, bf16[768,256]{1,0:T(8,128)(2,1)S(1)}, u32[]{:S(2)}, u32[]{:S(2)}) collective-permute-start(bf16[768,256]{1,0:T(8,128)(2,1)S(1)} %grad_pre.1.pre_ref), channel_id=1, source_target_pairs={{0,1},{1,0},{2,3},{3,2},{4,5},{5,4},{6,7},{7,6},{8,9},{9,8},{10,11... | collective-permute-start | bytes 1179656 | tf_op jit(solution)/shard_map/ppermute | solution.py:298
  66.0 25.2 %copy-start = (bf16[3,3,256,256]{3,2,1,0:T(8,128)(2,1)S(1)}, bf16[3,3,256,256]{3,2,1,0:T(8,128)(2,1)}, u32[]{:S(2)}) copy-start(bf16[3,3,256,256]{3,2,1,0:T(8,128)(2,1)} %weight_ref.3) | copy-start | bytes 3538948
  84.9 19.2 %all-to-all-start.3 = ((bf16[16,8,144]{2,1,0:T(8,128)(2,1)}), bf16[16,8,144]{2,1,0:T(8,128)(2,1)S(1)}, u32[]{:S(2)}, u32[]{:S(2)}) async-start(bf16[16,8,144]{2,1,0:T(8,128)(2,1)} %first_sum.1), calls=%async_computation.3 | async-start | bytes 131072 | tf_op jit(solution)/shard_map/all_to_all | solution.py:394

commit v5 on v3

--- a/solution.py
+++ b/solution.py
@@ -23,7 +23,13 @@
     return [pl.BlockSpec(memory_space=pltpu.VMEM)] * n
 
 
-def pack_kernel(local, side, blocks, seams_ref, g_ref, p_ref, out_ref):
+def pack_kernel(local, side, blocks, seams_ref, g_hbm, p_hbm, out_ref, g_ref, p_ref, sems):
+    fetches = [
+        pltpu.make_async_copy(g_hbm, g_ref, sems.at[0]),
+        pltpu.make_async_copy(p_hbm, p_ref, sems.at[1]),
+    ]
+    for fetch in fetches:
+        fetch.start()
     px_blocks, ch_blocks = blocks
     channels = g_ref.shape[-1]
     px, ch = side // px_blocks, channels // ch_blocks
@@ -34,19 +40,21 @@
     cell, base = line % CELLS, line // CELLS * side
     of_g = jnp.where(cell < 2, base + cell, jnp.where(cell < 4, base + side - 4 + cell, -1))
     of_p = jnp.where(cell == 4, base, jnp.where(cell == 5, base + side - 1, -1))
+    seams = jnp.zeros((local * CELLS, channels), jnp.float32)
+    line = lax.broadcasted_iota(jnp.int32, seams.shape, 0)
+    lane = lax.broadcasted_iota(jnp.int32, seams.shape, 1)
+    for face in range(local):
+        for i in range(4):
+            here = (line == face * CELLS + SEAM_AT) & (lane == i)
+            seams = jnp.where(here, seams_ref[face, i].astype(jnp.float32), seams)
     take = lambda at, ref: jnp.dot(
         jnp.where(at == pixel, 1.0, 0.0).astype(jnp.bfloat16),
         ref[...].reshape(local * side, channels),
         preferred_element_type=jnp.float32,
     )
-    cells = take(of_g, g_ref) + take(of_p, p_ref)
-    line = lax.broadcasted_iota(jnp.int32, cells.shape, 0)
-    lane = lax.broadcasted_iota(jnp.int32, cells.shape, 1)
-    for face in range(local):
-        for i in range(4):
-            here = (line == face * CELLS + SEAM_AT) & (lane == i)
-            cells = jnp.where(here, seams_ref[face, i].astype(jnp.float32), cells)
-    cells = cells.astype(jnp.bfloat16)
+    for fetch in fetches:
+        fetch.wait()
+    cells = (take(of_g, g_ref) + take(of_p, p_ref) + seams).astype(jnp.bfloat16)
     for b in range(px_blocks * ch_blocks):
         i, j = divmod(b, ch_blocks)
         for face in range(local):
@@ -64,7 +72,30 @@
     for i in range(faces):
         face = want_ref[i]
         at = pl.multiple_of(lax.rem(face, local) * count, 16)
-        out_ref[i] = table_ref[lax.div(face, local), pl.ds(at, count)]
+        into, row = divmod(i, local)
+        out_ref[into, row * count : (row + 1) * count] = table_ref[lax.div(face, local), pl.ds(at, count)]
+
+
+def first_sum_kernel(scale, got_ref, out_ref):
+    total = got_ref[0].astype(jnp.float32)
+    for i in range(1, got_ref.shape[0]):
+        total = total + got_ref[i].astype(jnp.float32)
+    turned = (total * scale).T
+    out_ref[...] = turned.reshape(out_ref.shape).astype(jnp.bfloat16)
+
+
+def second_sum_kernel(got_ref, out_ref):
+    total = got_ref[0].astype(jnp.float32)
+    for i in range(1, got_ref.shape[0]):
+        total = total + got_ref[i].astype(jnp.float32)
+    _, _, per_tile, width = out_ref.shape
+    lines = total.shape[1] // 9
+    for tap in range(9):
+        r, c = divmod(tap, 3)
+        for h in range(width // lines):
+            out_ref[r, c, :, h * lines : (h + 1) * lines] = total[
+                h * per_tile : (h + 1) * per_tile, tap * lines : (tap + 1) * lines
+            ]
 
 
 def border_kernel(local, side, index_ref, cells_ref, g_ref, p_ref, own_ref, wrap_ref):
@@ -87,12 +118,13 @@
     px = side // px_blocks
     channels = own_ref.shape[-1]
     ch = channels // ch_blocks
+    count = px * 2 // ch_blocks
     near, far = flags_ref[1], flags_ref[2]
 
     def put_wrap(out, which, face):
         for b in range(px_blocks * ch_blocks):
             i, j = divmod(b, ch_blocks)
-            piece = pieces_ref[b, face]
+            piece = pieces_ref[b, face * count : (face + 1) * count]
             if ch_blocks == 1:
                 part = piece[which * px : (which + 1) * px]
             else:
@@ -177,39 +209,41 @@
         out_ref[face] = (own + grad[at : at + side, :]).astype(jnp.bfloat16)
 
 
-def grad_first_kernel(row, nxl, flags_ref, x_ref, pre_ref, swapped_ref, out_ref, rows4):
+def grad_first_kernel(row, nxl, per_tile, flags_ref, x_ref, pre_ref, swapped_ref, out_ref, rows4):
     four_rows(rows4, flags_ref[0], row, pre_ref, swapped_ref)
-    dests, _, lines, half = out_ref.shape
+    dests, lines, half = out_ref.shape[0], out_ref.shape[1] // 9, out_ref.shape[2]
     for r in range(3):
         terms = jnp.dot(x_ref[...], rows4[(2 - r) * row : (4 - r) * row, :], preferred_element_type=jnp.float32)
         for c in range(3):
             turned = terms[c * half : (c + 1) * half, :].T
+            at = (3 * r + c) * lines
             if nxl == 1:
                 for d in range(dests):
-                    out_ref[d, 3 * r + c] = turned[d * lines : (d + 1) * lines, :].astype(jnp.bfloat16)
+                    out_ref[d, at : at + lines] = turned[d * lines : (d + 1) * lines, :].astype(jnp.bfloat16)
                 continue
             split = turned.reshape(dests // 2, 2, lines, half)
             left = split[:, 0].reshape(-1, half)
             right = split[:, 1].reshape(-1, half)
-            low = lax.broadcasted_iota(jnp.int32, left.shape, 1) < half // 2
+            low = lax.broadcasted_iota(jnp.int32, left.shape, 1) % (2 * per_tile) < per_tile
             ones = (
-                jnp.where(low, left, pltpu.roll(right, half // 2, 1)),
-                jnp.where(low, pltpu.roll(left, half // 2, 1), right),
+                jnp.where(low, left, pltpu.roll(right, per_tile, 1)),
+                jnp.where(low, pltpu.roll(left, half - per_tile, 1), right),
             )
             for xl, one in enumerate(ones):
                 for d in range(dests // 2):
-                    out_ref[2 * d + xl, 3 * r + c] = one[d * lines : (d + 1) * lines, :].astype(jnp.bfloat16)
-
-
-def kernel(body, out_shape, inputs, smem=0, scratch=(), name=None, flops=0, nbytes=2**20, exps=0):
+                    out_ref[2 * d + xl, at : at + lines] = one[d * lines : (d + 1) * lines, :].astype(jnp.bfloat16)
+
+
+def kernel(body, out_shape, inputs, smem=0, scratch=(), name=None, flops=0, nbytes=2**20, exps=0, hbm=0, vmem=VMEM):
     many = isinstance(out_shape, tuple)
+    spots = [pl.BlockSpec(memory_space=pltpu.HBM)] * hbm + whole(len(inputs) - smem - hbm)
     return pl.pallas_call(
         body,
         out_shape=out_shape,
-        in_specs=[pl.BlockSpec(memory_space=pltpu.SMEM)] * smem + whole(len(inputs) - smem),
+        in_specs=[pl.BlockSpec(memory_space=pltpu.SMEM)] * smem + spots,
         out_specs=tuple(whole(len(out_shape))) if many else whole(1)[0],
         scratch_shapes=scratch,
-        compiler_params=pltpu.CompilerParams(vmem_limit_bytes=VMEM),
+        compiler_params=pltpu.CompilerParams(vmem_limit_bytes=vmem),
         cost_estimate=pl.CostEstimate(flops=flops, bytes_accessed=nbytes, transcendentals=exps),
         name=name,
     )(*inputs)
@@ -240,7 +274,14 @@
         shape((nface, local * (count + CELLS), channels), bf),
         (seams, g, p),
         1,
-        name="pack",
+        (
+            pltpu.VMEM((local, side, channels), bf),
+            pltpu.VMEM((local, side, channels), bf),
+            pltpu.SemaphoreType.DMA((2,)),
+        ),
+        "pack",
+        hbm=2,
+        vmem=None,
     )
     swap = lambda a: lax.ppermute(a, "c", [(0, 1), (1, 0)])
     table, other = lax.optimization_barrier((lax.all_to_all(sent, FACE, 0, 0, tiled=True), swap(x)))
@@ -249,9 +290,13 @@
     all_seams = cells[:, SEAM_AT, :4].astype(jnp.int32)
     want = jnp.where(top, all_seams[:, 0], all_seams[:, 2])
     picked = kernel(
-        functools.partial(pick_kernel, faces, local, count), shape((faces, count, channels), bf), (want, table), 1, name="pick"
-    )
-    wrapped = lax.all_to_all(picked.reshape(nface, local, count, channels), FACE, 0, 0, tiled=True)
+        functools.partial(pick_kernel, faces, local, count),
+        shape((nface, local * count, channels), bf),
+        (want, table),
+        1,
+        name="pick",
+    )
+    wrapped = lax.all_to_all(picked, FACE, 0, 0, tiled=True)
 
     outer = jnp.where(top, corners[:, 0:2], corners[:, 2:4])
     sides = jnp.stack([jnp.stack([seams[:, 3], seams[:, 1]], 1), outer], 0)
@@ -299,8 +344,8 @@
     shifted = jnp.stack(
         [jnp.pad(both, ((0, 0), (0, 0), (GAP + 1 - c, GAP - 1 + c), (0, 0))) for c in range(3)], 0
     ).reshape(3, 2 * row, channels)
-    kept = np.arange(half)
-    chosen = (kept // per_tile) * (nc * per_tile) + kept % per_tile
+    kept = np.arange(channels).reshape(nxl, nz, nc, per_tile)[:, :, 0]
+    chosen = np.transpose(kept, (1, 0, 2)).reshape(half)
     choose = (chosen[:, None] + core * per_tile == np.arange(channels)[None, :]).astype(bf)
     x_turned = lax.dot_general(
         choose, shifted, (((1,), (2,)), ((), ())), preferred_element_type=jnp.float32
@@ -311,8 +356,8 @@
     width = channels // nface
     lines = width // nxl
     parts = kernel(
-        functools.partial(grad_first_kernel, row, nxl),
-        shape((nface * nxl, 9, lines, half), bf),
+        functools.partial(grad_first_kernel, row, nxl, per_tile),
+        shape((nface * nxl, 9 * lines, half), bf),
         (flags, x_turned, grad_pre, swapped),
         1,
         rows4,
@@ -331,12 +376,14 @@
     )
     scale_factor = 1.0 / math.sqrt(faces * ntile * side)
     got = lax.all_to_all(parts, FACE + ("xl",), 0, 0, tiled=True)
-    total = jnp.sum(got.astype(jnp.float32), 0) * scale_factor
-    total = jnp.transpose(total.reshape(9 * lines, half)).reshape(nxl, nz, per_tile, 9 * lines)
-    total = jnp.transpose(total, (1, 0, 2, 3)).reshape(nz, nxl * per_tile, 9 * lines).astype(bf)
+    total = kernel(
+        functools.partial(first_sum_kernel, scale_factor),
+        shape((nz, nxl * per_tile, 9 * lines), bf),
+        (got,),
+        name="first_sum",
+    )
     got = lax.all_to_all(total, "z", 0, 0, tiled=True)
-    total = jnp.sum(got.astype(jnp.float32), 0).reshape(nxl, per_tile, 9, lines)
-    first_out = jnp.transpose(total, (2, 1, 0, 3)).reshape(3, 3, per_tile, width)
+    first_out = kernel(second_sum_kernel, shape((3, 3, per_tile, width), jnp.float32), (got,), name="second_sum")
     return grad_input.reshape(saved_input.shape), first_out
 
 

time: 99.4 us -> 97.8 us (0.984)
  local copies, waits for them, and re-layouts: 4.83 us -> 0.71 us
  Pallas kernels: 8.85 us -> 11.5 us
    pallas_call x7 -> x9, Pallas kernels: 8.85 us -> 11.5 us  [kernel(): pl.pallas_call(body, out_shape=out_shape, in_specs=[pl.BlockSpec(memory_s...]
    unnamed x29 -> x23, local copies, waits for them, and re-layouts: 2.64 us -> 0.15 us
where the time goes in v5:
time: 97.8 us; the launch traced here: 96.6 us
  starting transfers between devices  36.9 us (38%)
  waiting for transfers between devices  27.5 us (28%)
  blocking collectives  18.1 us (19%)
  Pallas kernels  11.5 us (12%)
    all_to_all x1, blocking collectives, on_device(): got = lax.all_to_all(parts, FACE + ('xl',), 0, 0, tiled=True)  18.1 us
    pallas_call x9, Pallas kernels, kernel(): pl.pallas_call(body, out_shape=out_shape, in_specs=[pl.BlockSpec(memory_s...  11.5 us
    all_to_all x1, waiting for transfers between devices, on_device(): got = lax.all_to_all(total, 'z', 0, 0, tiled=True)  11 us
    ppermute x1, starting transfers between devices, on_device(): near = lax.ppermute(near, TILE, pairs(1))  9.15 us
    all_to_all x1, starting transfers between devices, on_device(): lax.all_to_all(sent, FACE, 0, 0, tiled=True)  7.58 us
    ppermute x1, waiting for transfers between devices, on_device(): far = lax.ppermute(far, TILE, pairs(2))  7.37 us
    all_to_all x1, starting transfers between devices, on_device(): got = lax.all_to_all(total, 'z', 0, 0, tiled=True)  6.29 us
    all_to_all x1, starting transfers between devices, on_device(): wrapped = lax.all_to_all(picked, FACE, 0, 0, tiled=True)  6.19 us
  transfers between devices with their start and end apart: 8, of which 7 were waited for; matrix products, arithmetic and copies ran while one was open for 1% of the time, Pallas kernels for 2%

profile of v5, /device:TPU:6, one launch (start us, length us, event | category | flops | bytes accessed | tf_op | source)
XLA Modules:
  0.0 96.6 jit_solution(11810910660964770749)
XLA Ops:
  0.6 0.0 copy-start.9
  0.6 0.0 copy-start.8
  0.7 0.0 copy-start.7
  0.7 0.0 copy-start.5
  0.7 0.0 copy-start.4
  0.7 0.0 copy-start.6
  0.7 2.7 %pack.1 = bf16[8,96,256]{2,1,0:T(8,128)(2,1)} custom-call(s32[4,4]{1,0:T(4,128)} %seams_ref.1, bf16[4,64,256]{2,1,0:T(8,128)(2,1)} %bitcast.35, bf16[4,64,256]{2,1,0:T(8,128)(2,1)} %bitcast.41), custom_call_target="tpu_custom_call" | custom-call | bytes 1048576 | tf_op jit(solution)/shard_map/pack/pallas_call | solution.py:240
  3.4 0.0 copy-start.1
  3.4 0.0 copy-start.2
  3.4 7.6 %all-to-all-start = ((bf16[8,96,256]{2,1,0:T(8,128)(2,1)}), bf16[8,96,256]{2,1,0:T(8,128)(2,1)S(1)}, u32[]{:S(2)}, u32[]{:S(2)}) async-start(bf16[8,96,256]{2,1,0:T(8,128)(2,1)} %pack.1), calls=%async_computation | async-start | bytes 786432 | tf_op jit(solution)/shard_map/all_to_all | solution.py:287
  11.0 0.0 copy-done.4
  11.0 1.9 %collective-permute-start = (bf16[4,64,256]{2,1,0:T(8,128)(2,1)S(1)}, bf16[4,64,256]{2,1,0:T(8,128)(2,1)S(1)}, u32[]{:S(2)}, u32[]{:S(2)}) collective-permute-start(bf16[4,64,256]{2,1,0:T(8,128)(2,1)S(1)} %bitcast.46), channel_id=1, source_target_pairs={{0,1},{1,0},{2,3},{3,2},{4,5},{5,4},{6,7},{7,6},{8,9},{9,8},{10,11... | collective-permute-start | bytes 393224 | tf_op jit(solution)/shard_map/ppermute | solution.py:286
  13.0 0.1 fusion.12
  13.0 0.1 slice_select_fusion
  13.1 0.1 copy.19
  13.2 0.1 pad_add_fusion
  13.3 0.1 copy.18
  13.4 0.1 select_multiply_fusion
  13.5 0.1 select_n.59.index_ref
  13.6 0.7 collective-permute-done
  14.3 4.0 %all-to-all-done.table_ref = bf16[8,96,256]{2,1,0:T(8,128)(2,1)S(1)} async-done(((bf16[8,96,256]{2,1,0:T(8,128)(2,1)}), bf16[8,96,256]{2,1,0:T(8,128)(2,1)S(1)}, u32[]{:S(2)}, u32[]{:S(2)}) %all-to-all-start) | async-done | bytes 393248 | tf_op jit(solution)/shard_map/all_to_all | solution.py:287
  18.3 0.1 copy.23
  18.4 1.4 %pick.1 = bf16[8,64,256]{2,1,0:T(8,128)(2,1)} custom-call(s32[32]{0:T(128)S(1)} %fusion.9.want_ref, bf16[8,96,256]{2,1,0:T(8,128)(2,1)S(1)} %all-to-all-done.table_ref), custom_call_target="tpu_custom_call" | custom-call | bytes 1048576 | tf_op jit(solution)/shard_map/pick/pallas_call | solution.py:240
  19.8 6.2 %all-to-all-start.1 = ((bf16[8,64,256]{2,1,0:T(8,128)(2,1)}), bf16[8,64,256]{2,1,0:T(8,128)(2,1)S(1)}, u32[]{:S(2)}, u32[]{:S(2)}) async-start(bf16[8,64,256]{2,1,0:T(8,128)(2,1)} %pick.1), calls=%async_computation.1 | async-start | bytes 524288 | tf_op jit(solution)/shard_map/all_to_all | solution.py:299
  26.0 0.2 border.1
  26.2 1.9 %collective-permute-start.1 = (bf16[4,80,256]{2,1,0:T(8,128)(2,1)S(1)}, bf16[4,80,256]{2,1,0:T(8,128)(2,1)S(1)}, u32[]{:S(2)}, u32[]{:S(2)}) collective-permute-start(bf16[4,80,256]{2,1,0:T(8,128)(2,1)S(1)} %slice_bitcast_fusion), channel_id=1, source_target_pairs={{0,1},{1,0},{2,3},{3,2},{4,5},{5,4},{6,7},{7,6},{8,9},{9,8},{10,11... | collective-permute-start | bytes 491528 | tf_op jit(solution)/shard_map/ppermute | solution.py:286
  28.2 0.1 pad_add_fusion.2.flags_ref
  28.3 1.3 %collective-permute-done.1.part_ref = bf16[4,80,256]{2,1,0:T(8,128)(2,1)S(1)} collective-permute-done((bf16[4,80,256]{2,1,0:T(8,128)(2,1)S(1)}, bf16[4,80,256]{2,1,0:T(8,128)(2,1)S(1)}, u32[]{:S(2)}, u32[]{:S(2)}) %collective-permute-start.1) | collective-permute-done | bytes 163872 | tf_op jit(solution)/shard_map/ppermute | solution.py:286
  29.5 2.3 %all-to-all-done.1.pieces_ref = bf16[8,64,256]{2,1,0:T(8,128)(2,1)S(1)} async-done(((bf16[8,64,256]{2,1,0:T(8,128)(2,1)}), bf16[8,64,256]{2,1,0:T(8,128)(2,1)S(1)}, u32[]{:S(2)}, u32[]{:S(2)}) %all-to-all-start.1) | async-done | bytes 262176 | tf_op jit(solution)/shard_map/all_to_all | solution.py:299
  31.8 0.6 send.1
  32.4 9.2 %collective-permute-start.2 = (bf16[2,4,80,256]{3,2,1,0:T(8,128)(2,1)S(1)}, bf16[2,4,80,256]{3,2,1,0:T(8,128)(2,1)S(1)}, u32[]{:S(2)}, u32[]{:S(2)}) collective-permute-start(bf16[2,4,80,256]{3,2,1,0:T(8,128)(2,1)S(1)} %get-tuple-element.15), channel_id=1, source_target_pairs={{63,0},{2,1},{1,2},{4,3},{3,4},{6,5},{5,6},{8,7},{7,8},{10,9},{9,1... | collective-permute-start | bytes 983048 | tf_op jit(solution)/shard_map/ppermute | solution.py:326
  41.6 1.9 %collective-permute-start.3 = (bf16[4,80,256]{2,1,0:T(8,128)(2,1)S(1)}, bf16[4,80,256]{2,1,0:T(8,128)(2,1)S(1)}, u32[]{:S(2)}, u32[]{:S(2)}) collective-permute-start(bf16[4,80,256]{2,1,0:T(8,128)(2,1)S(1)} %get-tuple-element.16), channel_id=1, source_target_pairs={{62,0},{3,1},{0,2},{5,3},{2,4},{7,5},{4,6},{9,7},{6,8},{11,9},{8,1... | collective-permute-start | bytes 491528 | tf_op jit(solution)/shard_map/ppermute | solution.py:327
  43.5 0.0 copy-done.10
  43.5 7.4 %collective-permute-done.3.far_ref = bf16[4,80,256]{2,1,0:T(8,128)(2,1)S(1)} collective-permute-done((bf16[4,80,256]{2,1,0:T(8,128)(2,1)S(1)}, bf16[4,80,256]{2,1,0:T(8,128)(2,1)S(1)}, u32[]{:S(2)}, u32[]{:S(2)}) %collective-permute-start.3) | collective-permute-done | bytes 163872 | tf_op jit(solution)/shard_map/ppermute | solution.py:327
  50.9 0.0 collective-permute-done.2.near_ref
  50.9 1.8 %grad_pre.1.pre_ref = bf16[768,256]{1,0:T(8,128)(2,1)S(1)} custom-call(s32[3]{0:T(128)S(1)} %pad_add_fusion.2.flags_ref, bf16[2,4,80,256]{3,2,1,0:T(8,128)(2,1)S(1)} %get-tuple-element.11.own_ref, bf16[4,80,256]{2,1,0:T(8,128)(2,1)S(1)} %collective-permute-done.1.part_ref, bf16[2,4,80,256]{3,2,1,0:T(8,128)(2,1)S(1)} %collective-permute-done.2.near_ref, ...), custom_call_target="tpu_custom_call" | custom-call | flops 905969664 | bytes 4194304 | tf_op jit(solution)/shard_map/grad_pre/pallas_call | solution.py:240
  52.7 1.9 %collective-permute-start.4 = (bf16[768,256]{1,0:T(8,128)(2,1)S(1)}, bf16[768,256]{1,0:T(8,128)(2,1)S(1)}, u32[]{:S(2)}, u32[]{:S(2)}) collective-permute-start(bf16[768,256]{1,0:T(8,128)(2,1)S(1)} %grad_pre.1.pre_ref), channel_id=1, source_target_pairs={{0,1},{1,0},{2,3},{3,2},{4,5},{5,4},{6,7},{7,6},{8,9},{9,8},{10,11... | collective-permute-start | bytes 1179656 | tf_op jit(solution)/shard_map/ppermute | solution.py:286
  54.6 0.2 fusion.11
  54.8 0.5 convolution_convert_fusion
  55.3 0.9 collective-permute-done.4.swapped_ref
  56.3 1.5 %grad_first.1 = bf16[16,144,128]{2,1,0:T(8,128)(2,1)S(1)} custom-call(s32[3]{0:T(128)S(1)} %pad_add_fusion.2.flags_ref, bf16[384,768]{1,0:T(8,128)(2,1)S(1)} %bitcast.40, bf16[768,256]{1,0:T(8,128)(2,1)S(1)} %grad_pre.1.pre_ref, bf16[768,256]{1,0:T(8,128)(2,1)S(1)} %collective-permute-done.4.swapped_ref), custom_call_target="tpu_custom_call" | custom-call | flops 452984832 | bytes 1048576 | tf_op jit(solution)/shard_map/grad_first/pallas_call | solution.py:240
  57.8 0.0 copy-start
  57.8 18.1 %all_to_all.20.got_ref = bf16[16,144,128]{2,1,0:T(8,128)(2,1)S(1)} all-to-all(bf16[16,144,128]{2,1,0:T(8,128)(2,1)S(1)} %grad_first.1), channel_id=1, replica_groups=mesh['xh'=2,'y'=4,'xl'=2,'z'=16,'c'=2] {'xh','y','xl'}, dimensions={0} | all-to-all | bytes 1179648 | tf_op jit(solution)/shard_map/all_to_all | solution.py:378
  75.9 0.8 first_sum.1
  76.7 6.3 %all-to-all-start.3 = ((bf16[16,8,144]{2,1,0:T(8,128)(2,1)}), bf16[16,8,144]{2,1,0:T(8,128)(2,1)S(1)}, u32[]{:S(2)}, u32[]{:S(2)}) async-start(bf16[16,8,144]{2,1,0:T(8,128)(2,1)} %first_sum.1), calls=%async_computation.3 | async-start | bytes 131072 | tf_op jit(solution)/shard_map/all_to_all | solution.py:385
  83.0 1.9 %grad_input.1 = bf16[4,64,256]{2,1,0:T(8,128)(2,1)} custom-call(s32[3]{0:T(128)S(1)} %pad_add_fusion.2.flags_ref, bf16[768,256]{1,0:T(8,128)(2,1)S(1)} %grad_pre.1.pre_ref, bf16[768,256]{1,0:T(8,128)(2,1)S(1)} %collective-permute-done.4.swapped_ref, bf16[4,64,256]{2,1,0:T(8,128)(2,1)S(1)} %bitcast.37, bf16[3,3,256,256]{3,2,1,0:T(8,128)(2,1)S(1)} %copy-done), custom_call_target="tpu_custom_call" | custom-call | flops 452984832 | bytes 2097152 | tf_op jit(solution)/shard_map/grad_input/pallas_call | solution.py:240
  84.9 11.0 %all-to-all-done.3.got_ref = bf16[16,8,144]{2,1,0:T(8,128)(2,1)S(1)} async-done(((bf16[16,8,144]{2,1,0:T(8,128)(2,1)}), bf16[16,8,144]{2,1,0:T(8,128)(2,1)S(1)}, u32[]{:S(2)}, u32[]{:S(2)}) %all-to-all-start.3) | async-done | bytes 36896 | tf_op jit(solution)/shard_map/all_to_all | solution.py:385
  95.9 0.7 second_sum.1
  (20 shorter events, 0.1 us)
Async XLA Ops:
  0.6 12.8 %copy-start.9 = (pred[16]{0:T(512)(128)(4,1)S(1)}, pred[16]{0:T(512)(128)(4,1)}, u32[]{:S(2)}) copy-start(pred[16]{0:T(512)(128)(4,1)} %constant.42.clone) | copy-start | bytes 52
  0.6 12.8 %copy-start.8 = (pred[2,16]{1,0:T(4,128)(4,1)S(1)}, pred[2,16]{1,0:T(4,128)(4,1)}, u32[]{:S(2)}) copy-start(pred[2,16]{1,0:T(4,128)(4,1)} %constant.58) | copy-start | bytes 100
  0.7 12.8 %copy-start.7 = (s32[2,16]{1,0:T(2,128)S(1)}, s32[2,16]{1,0:T(2,128)}, u32[]{:S(2)}) copy-start(s32[2,16]{1,0:T(2,128)} %constant.59) | copy-start | bytes 388
  0.7 12.3 %copy-start.5 = (s32[4,4]{1,0:T(4,128)S(1)}, s32[4,4]{1,0:T(4,128)}, u32[]{:S(2)}) copy-start(s32[4,4]{1,0:T(4,128)} %seams_ref.1) | copy-start | bytes 196
  0.7 10.3 %copy-start.4 = (bf16[1,4,1,64,256]{4,3,2,1,0:T(8,128)(2,1)S(1)}, bf16[1,4,1,64,256]{4,3,2,1,0:T(8,128)(2,1)}, u32[]{:S(2)}) copy-start(bf16[1,4,1,64,256]{4,3,2,1,0:T(8,128)(2,1)} %param.12) | copy-start | bytes 393220
  0.7 12.3 %copy-start.6 = (s32[4,4]{1,0:T(4,128)S(1)}, s32[4,4]{1,0:T(4,128)}, u32[]{:S(2)}) copy-start(s32[4,4]{1,0:T(4,128)} %param.18) | copy-start | bytes 196
  3.4 22.6 %copy-start.1 = (bf16[1,4,1,64,256]{4,3,2,1,0:T(8,128)(2,1)S(1)}, bf16[1,4,1,64,256]{4,3,2,1,0:T(8,128)(2,1)}, u32[]{:S(2)}) copy-start(bf16[1,4,1,64,256]{4,3,2,1,0:T(8,128)(2,1)} %param.14) | copy-start | bytes 393220
  3.4 22.6 %copy-start.2 = (bf16[1,4,1,64,256]{4,3,2,1,0:T(8,128)(2,1)S(1)}, bf16[1,4,1,64,256]{4,3,2,1,0:T(8,128)(2,1)}, u32[]{:S(2)}) copy-start(bf16[1,4,1,64,256]{4,3,2,1,0:T(8,128)(2,1)} %param.13) | copy-start | bytes 393220
  3.4 14.8 %all-to-all-start = ((bf16[8,96,256]{2,1,0:T(8,128)(2,1)}), bf16[8,96,256]{2,1,0:T(8,128)(2,1)S(1)}, u32[]{:S(2)}, u32[]{:S(2)}) async-start(bf16[8,96,256]{2,1,0:T(8,128)(2,1)} %pack.1), calls=%async_computation | async-start | bytes 786432 | tf_op jit(solution)/shard_map/all_to_all | solution.py:287
  11.0 3.2 %collective-permute-start = (bf16[4,64,256]{2,1,0:T(8,128)(2,1)S(1)}, bf16[4,64,256]{2,1,0:T(8,128)(2,1)S(1)}, u32[]{:S(2)}, u32[]{:S(2)}) collective-permute-start(bf16[4,64,256]{2,1,0:T(8,128)(2,1)S(1)} %bitcast.46), channel_id=1, source_target_pairs={{0,1},{1,0},{2,3},{3,2},{4,5},{5,4},{6,7},{7,6},{8,9},{9,8},{10,11... | collective-permute-start | bytes 393224 | tf_op jit(solution)/shard_map/ppermute | solution.py:286
  19.8 23.7 %copy-start.10 = (s32[128,1]{0,1:T(1,128)S(1)}, s32[128,1]{0,1:T(1,128)}, u32[]{:S(2)}) copy-start(s32[128,1]{0,1:T(1,128)} %constant.45.clone) | copy-start | bytes 1540
  19.8 31.1 %copy-start.3 = (bf16[3,3,256,256]{3,2,1,0:T(8,128)(2,1)S(1)}, bf16[3,3,256,256]{3,2,1,0:T(8,128)(2,1)}, u32[]{:S(2)}) copy-start(bf16[3,3,256,256]{3,2,1,0:T(8,128)(2,1)} %weight_ref.2) | copy-start | bytes 3538948
  19.8 12.0 %all-to-all-start.1 = ((bf16[8,64,256]{2,1,0:T(8,128)(2,1)}), bf16[8,64,256]{2,1,0:T(8,128)(2,1)S(1)}, u32[]{:S(2)}, u32[]{:S(2)}) async-start(bf16[8,64,256]{2,1,0:T(8,128)(2,1)} %pick.1), calls=%async_computation.1 | async-start | bytes 524288 | tf_op jit(solution)/shard_map/all_to_all | solution.py:299
  26.2 3.3 %collective-permute-start.1 = (bf16[4,80,256]{2,1,0:T(8,128)(2,1)S(1)}, bf16[4,80,256]{2,1,0:T(8,128)(2,1)S(1)}, u32[]{:S(2)}, u32[]{:S(2)}) collective-permute-start(bf16[4,80,256]{2,1,0:T(8,128)(2,1)S(1)} %slice_bitcast_fusion), channel_id=1, source_target_pairs={{0,1},{1,0},{2,3},{3,2},{4,5},{5,4},{6,7},{7,6},{8,9},{9,8},{10,11... | collective-permute-start | bytes 491528 | tf_op jit(solution)/shard_map/ppermute | solution.py:286
  32.4 18.5 %collective-permute-start.2 = (bf16[2,4,80,256]{3,2,1,0:T(8,128)(2,1)S(1)}, bf16[2,4,80,256]{3,2,1,0:T(8,128)(2,1)S(1)}, u32[]{:S(2)}, u32[]{:S(2)}) collective-permute-start(bf16[2,4,80,256]{3,2,1,0:T(8,128)(2,1)S(1)} %get-tuple-element.15), channel_id=1, source_target_pairs={{63,0},{2,1},{1,2},{4,3},{3,4},{6,5},{5,6},{8,7},{7,8},{10,9},{9,1... | collective-permute-start | bytes 983048 | tf_op jit(solution)/shard_map/ppermute | solution.py:326
  41.6 9.3 %collective-permute-start.3 = (bf16[4,80,256]{2,1,0:T(8,128)(2,1)S(1)}, bf16[4,80,256]{2,1,0:T(8,128)(2,1)S(1)}, u32[]{:S(2)}, u32[]{:S(2)}) collective-permute-start(bf16[4,80,256]{2,1,0:T(8,128)(2,1)S(1)} %get-tuple-element.16), channel_id=1, source_target_pairs={{62,0},{3,1},{0,2},{5,3},{2,4},{7,5},{4,6},{9,7},{6,8},{11,9},{8,1... | collective-permute-start | bytes 491528 | tf_op jit(solution)/shard_map/ppermute | solution.py:327
  52.7 3.6 %collective-permute-start.4 = (bf16[768,256]{1,0:T(8,128)(2,1)S(1)}, bf16[768,256]{1,0:T(8,128)(2,1)S(1)}, u32[]{:S(2)}, u32[]{:S(2)}) collective-permute-start(bf16[768,256]{1,0:T(8,128)(2,1)S(1)} %grad_pre.1.pre_ref), channel_id=1, source_target_pairs={{0,1},{1,0},{2,3},{3,2},{4,5},{5,4},{6,7},{7,6},{8,9},{9,8},{10,11... | collective-permute-start | bytes 1179656 | tf_op jit(solution)/shard_map/ppermute | solution.py:286
  57.8 25.2 %copy-start = (bf16[3,3,256,256]{3,2,1,0:T(8,128)(2,1)S(1)}, bf16[3,3,256,256]{3,2,1,0:T(8,128)(2,1)}, u32[]{:S(2)}) copy-start(bf16[3,3,256,256]{3,2,1,0:T(8,128)(2,1)} %weight_ref.3) | copy-start | bytes 3538948
  76.7 19.2 %all-to-all-start.3 = ((bf16[16,8,144]{2,1,0:T(8,128)(2,1)}), bf16[16,8,144]{2,1,0:T(8,128)(2,1)S(1)}, u32[]{:S(2)}, u32[]{:S(2)}) async-start(bf16[16,8,144]{2,1,0:T(8,128)(2,1)} %first_sum.1), calls=%async_computation.3 | async-start | bytes 131072 | tf_op jit(solution)/shard_map/all_to_all | solution.py:385

commit v6 on v5

--- a/solution.py
+++ b/solution.py
@@ -98,19 +98,76 @@
             ]
 
 
-def border_kernel(local, side, index_ref, cells_ref, g_ref, p_ref, own_ref, wrap_ref):
-    rows, width = index_ref.shape[0], cells_ref.shape[0]
-    where = lax.broadcasted_iota(jnp.int32, (rows, width), 1) == index_ref[...]
+def border_kernel(
+    local, side, tiles, flags_ref, seams_ref, corners_ref, table_ref, g_ref, p_ref, x_ref, own_ref, wrap_ref, mine_ref, kept_ref
+):
+    below = flags_ref[3]
+    held = local * CELLS
+    cells = table_ref[:, table_ref.shape[1] - held :].reshape(table_ref.shape[0] * held, -1)
+    rows, width = 4 * local * GAP, cells.shape[0]
+    row = lax.broadcasted_iota(jnp.int32, (rows, 1), 0)
+    spot, block = row % GAP, row // GAP
+    of_g = jnp.where(spot < 2, spot, jnp.where(spot >= GAP - 2, spot - (GAP - 4), -1))
+    of_p = jnp.where(spot == 0, 4, jnp.where(spot == GAP - 1, 5, -1))
+    cell = jnp.where(block % (2 * local) < local, of_g, of_p)
+    face_at = jnp.zeros((rows, 1), jnp.int32)
+    for face in range(local):
+        for beyond in range(2):
+            if beyond:
+                left, right = corners_ref[face, 2 * below], corners_ref[face, 2 * below + 1]
+            else:
+                left, right = seams_ref[face, 3], seams_ref[face, 1]
+            here = (block % local == face) & (block // (2 * local) == beyond)
+            face_at = jnp.where(here, jnp.where(spot < GAP // 2, right, left), face_at)
+    index = jnp.where(cell < 0, -1, face_at * CELLS + cell)
+    where = lax.broadcasted_iota(jnp.int32, (rows, width), 1) == index
     tails = jnp.dot(
-        jnp.where(where, 1.0, 0.0).astype(jnp.bfloat16), cells_ref[...], preferred_element_type=jnp.float32
+        jnp.where(where, 1.0, 0.0).astype(jnp.bfloat16), cells, preferred_element_type=jnp.float32
     ).astype(jnp.bfloat16)
     for which, source in enumerate((g_ref, p_ref)):
         for face in range(local):
             at = (which * local + face) * GAP
             own_ref[which, face, :side] = source[face]
             own_ref[which, face, side:] = tails[at : at + GAP]
+            if which == 0:
+                mine_ref[face, :side] = source[face]
+                mine_ref[face, side : side + GAP] = tails[at : at + GAP]
             at += 2 * local * GAP
             wrap_ref[which, face] = tails[at : at + GAP]
+    nxl, nz, nc, per_tile = tiles
+    channels, half = x_ref.shape[-1], kept_ref.shape[-1]
+    line = lax.broadcasted_iota(jnp.int32, (channels, nc * half), 0)
+    lane = lax.broadcasted_iota(jnp.int32, (channels, nc * half), 1)
+    of_core = jnp.where(lane < half, flags_ref[0], 1 - flags_ref[0])
+    place = lane % half
+    xl, z = place // per_tile % nxl, place // (per_tile * nxl)
+    wanted = ((xl * nz + z) * nc + of_core) * per_tile + place % per_tile
+    chosen = jnp.dot(
+        x_ref[...].reshape(local * side, channels),
+        jnp.where(line == wanted, 1.0, 0.0).astype(jnp.bfloat16),
+        preferred_element_type=jnp.float32,
+    ).astype(jnp.bfloat16)
+    kept_ref[...] = chosen[:, :half]
+    for face in range(local):
+        for part in range(2):
+            at = face * side + part * side // 2
+            mine_ref[face, side + GAP :, part * half : (part + 1) * half] = chosen[at : at + side // 2, half:]
+
+
+def turn_kernel(local, side, flags_ref, kept_ref, part_ref, out_ref, lines):
+    pitch = side + 2 * GAP
+    row = local * pitch
+    half = kept_ref.shape[-1]
+    lines[...] = jnp.zeros_like(lines)
+    for face in range(local):
+        at = pl.multiple_of(flags_ref[0] * row + face * pitch + GAP, 16)
+        lines[pl.ds(at, side), :] = kept_ref[face * side : (face + 1) * side].astype(jnp.float32)
+        for part in range(2):
+            at = pl.multiple_of((1 - flags_ref[0]) * row + face * pitch + GAP + part * side // 2, 16)
+            lines[pl.ds(at, side // 2), :] = part_ref[face, side + GAP :, part * half : (part + 1) * half].astype(jnp.float32)
+    for c in range(3):
+        moved = lines[...] if c == 1 else pltpu.roll(lines[...], (1 - c) % (2 * row), 0)
+        out_ref[c * half : (c + 1) * half, :] = moved.T.astype(jnp.bfloat16)
 
 
 def send_kernel(local, side, blocks, flags_ref, own_ref, tails_ref, pieces_ref, near_ref, far_ref):
@@ -159,7 +216,7 @@
 
     def put(pad, slot, source, face):
         at = pl.multiple_of(slot * row + face * pitch, 16)
-        border = source[face, side:]
+        border = source[face, side : side + GAP]
         pad[pl.ds(at, GAP), :] = border
         pad[pl.ds(at + GAP, side), :] = source[face, :side]
         pad[pl.ds(at + GAP + side, GAP), :] = border
@@ -263,7 +320,7 @@
     top = tile >= ntile // 2
     near_wraps = (tile == 0) | (tile == ntile - 1)
     far_wraps = (tile == 1) | (tile == ntile - 2)
-    flags = jnp.stack([core, near_wraps.astype(jnp.int32), far_wraps.astype(jnp.int32)])
+    flags = jnp.stack([core, *(flag.astype(jnp.int32) for flag in (near_wraps, far_wraps, ~top))])
 
     px_blocks = 4
     ch_blocks = nface // px_blocks
@@ -284,7 +341,8 @@
         vmem=None,
     )
     swap = lambda a: lax.ppermute(a, "c", [(0, 1), (1, 0)])
-    table, other = lax.optimization_barrier((lax.all_to_all(sent, FACE, 0, 0, tiled=True), swap(x)))
+    sent, flags, top = lax.optimization_barrier((sent, flags, top))
+    table = lax.all_to_all(sent, FACE, 0, 0, tiled=True)
 
     cells = table[:, local * count :].reshape(faces, CELLS, channels)
     all_seams = cells[:, SEAM_AT, :4].astype(jnp.int32)
@@ -296,24 +354,24 @@
         1,
         name="pick",
     )
+    picked, table = lax.optimization_barrier((picked, table))
     wrapped = lax.all_to_all(picked, FACE, 0, 0, tiled=True)
 
-    outer = jnp.where(top, corners[:, 0:2], corners[:, 2:4])
-    sides = jnp.stack([jnp.stack([seams[:, 3], seams[:, 1]], 1), outer], 0)
-    spots = np.full((2, GAP), -1, np.int32)
-    spots[0, [0, 1, GAP - 2, GAP - 1]] = (0, 1, 2, 3)
-    spots[1, [0, GAP - 1]] = (4, 5)
-    on_left = np.arange(GAP) >= GAP // 2
-    face_at = jnp.where(on_left, sides[:, None, :, 0:1], sides[:, None, :, 1:2])
-    index = jnp.where(spots[None, :, None] >= 0, face_at * CELLS + spots[None, :, None], -1)
-    index = index.reshape(-1, 1).astype(jnp.int32)
-    own, tails = kernel(
-        functools.partial(border_kernel, local, side),
-        (shape((2, local, side + GAP, channels), bf), shape((2, local, GAP, channels), bf)),
-        (index, cells.reshape(faces * CELLS, channels), g, p),
+    half = channels // nc
+    per_tile = channels // ntile
+    own, tails, mine, kept = kernel(
+        functools.partial(border_kernel, local, side, (nxl, nz, nc, per_tile)),
+        (
+            shape((2, local, side + GAP, channels), bf),
+            shape((2, local, GAP, channels), bf),
+            shape((local, side + GAP + side // 2, channels), bf),
+            shape((local * side, half), bf),
+        ),
+        (flags, seams, corners, table, g, p, x),
+        3,
         name="border",
     )
-    wrapped, part = lax.optimization_barrier((wrapped, swap(own[0])))
+    wrapped, part = lax.optimization_barrier((wrapped, swap(mine)))
     near, far = kernel(
         functools.partial(send_kernel, local, side, (px_blocks, ch_blocks)),
         (shape(own.shape, bf), shape(own.shape[1:], bf)),
@@ -338,19 +396,14 @@
     )
     swapped = swap(grad_pre)
 
-    half = channels // nc
-    per_tile = channels // ntile
-    both = jnp.where(core == 0, jnp.stack([x, other], 0), jnp.stack([other, x], 0))
-    shifted = jnp.stack(
-        [jnp.pad(both, ((0, 0), (0, 0), (GAP + 1 - c, GAP - 1 + c), (0, 0))) for c in range(3)], 0
-    ).reshape(3, 2 * row, channels)
-    kept = np.arange(channels).reshape(nxl, nz, nc, per_tile)[:, :, 0]
-    chosen = np.transpose(kept, (1, 0, 2)).reshape(half)
-    choose = (chosen[:, None] + core * per_tile == np.arange(channels)[None, :]).astype(bf)
-    x_turned = lax.dot_general(
-        choose, shifted, (((1,), (2,)), ((), ())), preferred_element_type=jnp.float32
-    ).astype(bf)
-    x_turned = jnp.transpose(x_turned, (1, 0, 2)).reshape(3 * half, 2 * row)
+    x_turned = kernel(
+        functools.partial(turn_kernel, local, side),
+        shape((3 * half, 2 * row), bf),
+        (flags, kept, part),
+        1,
+        (pltpu.VMEM((2 * row, half), jnp.float32),),
+        "turn",
+    )
 
     rows4 = (pltpu.VMEM((4 * row, channels), bf),)
     width = channels // nface

time: 97.8 us -> 97.8 us (level)
  blocking collectives: 18.1 us -> 33 us
  starting transfers between devices: 36.9 us -> 27.4 us
  waiting for transfers between devices: 27.5 us -> 22.3 us
  Pallas kernels: 11.5 us -> 12.9 us
    all_to_all x0 -> x1, blocking collectives: none -> 14.9 us  [on_device(): table = lax.all_to_all(sent, FACE, 0, 0, tiled=True)]
    all_to_all x1 -> x0, starting transfers between devices: 7.58 us -> none  [on_device(): lax.all_to_all(sent, FACE, 0, 0, tiled=True)]
    all_to_all x1 -> x0, waiting for transfers between devices: 3.99 us -> none  [on_device(): lax.all_to_all(sent, FACE, 0, 0, tiled=True)]
    ppermute x3 -> x2, waiting for transfers between devices: 2.89 us -> 0.87 us  [on_device(): swap = lambda a: lax.ppermute(a, 'c', [(0, 1), (1, 0)])]
    ppermute x3 -> x2, starting transfers between devices: 5.75 us -> 3.84 us  [on_device(): swap = lambda a: lax.ppermute(a, 'c', [(0, 1), (1, 0)])]
    pallas_call x9 -> x10, Pallas kernels: 11.5 us -> 12.9 us  [kernel(): pl.pallas_call(body, out_shape=out_shape, in_specs=[pl.BlockSpec(memory_s...]
  transfers between devices with their start and end apart: 8 -> 6, of which waited for: 7 -> 4; matrix products, arithmetic and copies ran while one was open for 1% -> 0% of each run, Pallas kernels for 2% -> 4%
where the time goes in v6:
time: 97.8 us; the launch traced here: 96.6 us
  blocking collectives  33 us (34%)
  starting transfers between devices  27.4 us (28%)
  waiting for transfers between devices  22.3 us (23%)
  Pallas kernels  12.9 us (13%)
    all_to_all x1, blocking collectives, on_device(): got = lax.all_to_all(parts, FACE + ('xl',), 0, 0, tiled=True)  18.1 us
    all_to_all x1, blocking collectives, on_device(): table = lax.all_to_all(sent, FACE, 0, 0, tiled=True)  14.9 us
    pallas_call x10, Pallas kernels, kernel(): pl.pallas_call(body, out_shape=out_shape, in_specs=[pl.BlockSpec(memory_s...  12.9 us
    all_to_all x1, waiting for transfers between devices, on_device(): got = lax.all_to_all(total, 'z', 0, 0, tiled=True)  11 us
    ppermute x1, starting transfers between devices, on_device(): near = lax.ppermute(near, TILE, pairs(1))  9.86 us
    ppermute x1, waiting for transfers between devices, on_device(): far = lax.ppermute(far, TILE, pairs(2))  7.39 us
    all_to_all x1, starting transfers between devices, on_device(): wrapped = lax.all_to_all(picked, FACE, 0, 0, tiled=True)  6.18 us
    all_to_all x1, starting transfers between devices, on_device(): got = lax.all_to_all(total, 'z', 0, 0, tiled=True)  5.55 us
  transfers between devices with their start and end apart: 6, of which 4 were waited for; matrix products, arithmetic and copies ran while one was open for 0% of the time, Pallas kernels for 4%

profile of v6, /device:TPU:6, one launch (start us, length us, event | category | flops | bytes accessed | tf_op | source)
XLA Modules:
  0.0 96.6 jit_solution(1724922140730198255)
XLA Ops:
  0.7 2.6 %pack.1 = bf16[8,96,256]{2,1,0:T(8,128)(2,1)} custom-call(s32[4,4]{1,0:T(4,128)} %seams_ref.3, bf16[4,64,256]{2,1,0:T(8,128)(2,1)} %bitcast.16, bf16[4,64,256]{2,1,0:T(8,128)(2,1)} %bitcast.19), custom_call_target="tpu_custom_call" | custom-call | bytes 1048576 | tf_op jit(solution)/shard_map/pack/pallas_call | solution.py:297
  3.3 0.0 copy-start.1
  3.3 0.0 copy-start.2
  3.3 0.0 copy-start.3
  3.3 0.0 copy-start.4
  3.3 0.0 copy-start.5
  3.3 0.1 pad_add_fusion.flags_ref
  3.4 14.9 %all_to_all.20.table_ref = bf16[8,96,256]{2,1,0:T(8,128)(2,1)S(1)} all-to-all(bf16[8,96,256]{2,1,0:T(8,128)(2,1)} %pack.1), channel_id=1, replica_groups=mesh['xh'=2,'y'=4,'xl'=2,'z'=16,'c'=2] {'xh','y'}, dimensions={0} | all-to-all | bytes 786432 | tf_op jit(solution)/shard_map/all_to_all | solution.py:345
  18.3 0.1 copy.11
  18.4 0.0 copy-start.6
  18.5 1.4 %pick.1 = bf16[8,64,256]{2,1,0:T(8,128)(2,1)} custom-call(s32[32]{0:T(128)S(1)} %fusion.want_ref, bf16[8,96,256]{2,1,0:T(8,128)(2,1)S(1)} %all_to_all.20.table_ref), custom_call_target="tpu_custom_call" | custom-call | bytes 1048576 | tf_op jit(solution)/shard_map/pick/pallas_call | solution.py:297
  19.8 6.2 %all-to-all-start.1 = ((bf16[8,64,256]{2,1,0:T(8,128)(2,1)}), bf16[8,64,256]{2,1,0:T(8,128)(2,1)S(1)}, u32[]{:S(2)}, u32[]{:S(2)}) async-start(bf16[8,64,256]{2,1,0:T(8,128)(2,1)} %pick.1), calls=%async_computation.1 | async-start | bytes 524288 | tf_op jit(solution)/shard_map/all_to_all | solution.py:358
  26.0 0.0 copy-done.1
  26.0 0.0 copy-done.2
  26.0 0.0 copy-done.3
  26.0 0.0 copy-done.4
  26.0 0.0 copy-done.5
  26.1 0.9 border.1
  26.9 1.9 %collective-permute-start = (bf16[4,112,256]{2,1,0:T(8,128)(2,1)S(1)}, bf16[4,112,256]{2,1,0:T(8,128)(2,1)S(1)}, u32[]{:S(2)}, u32[]{:S(2)}) collective-permute-start(bf16[4,112,256]{2,1,0:T(8,128)(2,1)S(1)} %get-tuple-element.21), channel_id=1, source_target_pairs={{0,1},{1,0},{2,3},{3,2},{4,5},{5,4},{6,7},{7,6},{8,9},{9,8},{10,11... | collective-permute-start | bytes 688136 | tf_op jit(solution)/shard_map/ppermute | solution.py:343
  28.9 3.0 %all-to-all-done.1.pieces_ref = bf16[8,64,256]{2,1,0:T(8,128)(2,1)S(1)} async-done(((bf16[8,64,256]{2,1,0:T(8,128)(2,1)}), bf16[8,64,256]{2,1,0:T(8,128)(2,1)S(1)}, u32[]{:S(2)}, u32[]{:S(2)}) %all-to-all-start.1) | async-done | bytes 262176 | tf_op jit(solution)/shard_map/all_to_all | solution.py:358
  31.9 0.0 collective-permute-done.part_ref
  31.9 0.6 send.1
  32.5 9.9 %collective-permute-start.1 = (bf16[2,4,80,256]{3,2,1,0:T(8,128)(2,1)S(1)}, bf16[2,4,80,256]{3,2,1,0:T(8,128)(2,1)S(1)}, u32[]{:S(2)}, u32[]{:S(2)}) collective-permute-start(bf16[2,4,80,256]{3,2,1,0:T(8,128)(2,1)S(1)} %get-tuple-element.25), channel_id=1, source_target_pairs={{63,0},{2,1},{1,2},{4,3},{3,4},{6,5},{5,6},{8,7},{7,8},{10,9},{9,1... | collective-permute-start | bytes 983048 | tf_op jit(solution)/shard_map/ppermute | solution.py:384
  42.3 1.9 %collective-permute-start.2 = (bf16[4,80,256]{2,1,0:T(8,128)(2,1)S(1)}, bf16[4,80,256]{2,1,0:T(8,128)(2,1)S(1)}, u32[]{:S(2)}, u32[]{:S(2)}) collective-permute-start(bf16[4,80,256]{2,1,0:T(8,128)(2,1)S(1)} %get-tuple-element.26), channel_id=1, source_target_pairs={{62,0},{3,1},{0,2},{5,3},{2,4},{7,5},{4,6},{9,7},{6,8},{11,9},{8,1... | collective-permute-start | bytes 491528 | tf_op jit(solution)/shard_map/ppermute | solution.py:385
  44.3 7.4 %collective-permute-done.2.far_ref = bf16[4,80,256]{2,1,0:T(8,128)(2,1)S(1)} collective-permute-done((bf16[4,80,256]{2,1,0:T(8,128)(2,1)S(1)}, bf16[4,80,256]{2,1,0:T(8,128)(2,1)S(1)}, u32[]{:S(2)}, u32[]{:S(2)}) %collective-permute-start.2) | collective-permute-done | bytes 163872 | tf_op jit(solution)/shard_map/ppermute | solution.py:385
  51.7 0.0 collective-permute-done.1.near_ref
  51.7 0.0 copy-done.6
  51.7 1.8 %grad_pre.1.pre_ref = bf16[768,256]{1,0:T(8,128)(2,1)S(1)} custom-call(s32[4]{0:T(128)S(1)} %pad_add_fusion.flags_ref, bf16[2,4,80,256]{3,2,1,0:T(8,128)(2,1)S(1)} %get-tuple-element.19.own_ref, bf16[4,112,256]{2,1,0:T(8,128)(2,1)S(1)} %collective-permute-done.part_ref, bf16[2,4,80,256]{3,2,1,0:T(8,128)(2,1)S(1)} %collective-permute-done.1.near_ref, ...), custom_call_target="tpu_custom_call" | custom-call | flops 905969664 | bytes 4194304 | tf_op jit(solution)/shard_map/grad_pre/pallas_call | solution.py:297
  53.4 1.9 %collective-permute-start.3 = (bf16[768,256]{1,0:T(8,128)(2,1)S(1)}, bf16[768,256]{1,0:T(8,128)(2,1)S(1)}, u32[]{:S(2)}, u32[]{:S(2)}) collective-permute-start(bf16[768,256]{1,0:T(8,128)(2,1)S(1)} %grad_pre.1.pre_ref), channel_id=1, source_target_pairs={{0,1},{1,0},{2,3},{3,2},{4,5},{5,4},{6,7},{7,6},{8,9},{9,8},{10,11... | collective-permute-start | bytes 1179656 | tf_op jit(solution)/shard_map/ppermute | solution.py:343
  55.4 0.8 turn.1.x_ref
  56.2 0.9 collective-permute-done.3.swapped_ref
  57.1 1.5 %grad_first.1 = bf16[16,144,128]{2,1,0:T(8,128)(2,1)S(1)} custom-call(s32[4]{0:T(128)S(1)} %pad_add_fusion.flags_ref, bf16[384,768]{1,0:T(8,128)(2,1)S(1)} %turn.1.x_ref, bf16[768,256]{1,0:T(8,128)(2,1)S(1)} %grad_pre.1.pre_ref, bf16[768,256]{1,0:T(8,128)(2,1)S(1)} %collective-permute-done.3.swapped_ref), custom_call_target="tpu_custom_call" | custom-call | flops 452984832 | bytes 1048576 | tf_op jit(solution)/shard_map/grad_first/pallas_call | solution.py:297
  58.6 0.0 copy-start
  58.6 18.1 %all_to_all.21.got_ref = bf16[16,144,128]{2,1,0:T(8,128)(2,1)S(1)} all-to-all(bf16[16,144,128]{2,1,0:T(8,128)(2,1)S(1)} %grad_first.1), channel_id=1, replica_groups=mesh['xh'=2,'y'=4,'xl'=2,'z'=16,'c'=2] {'xh','y','xl'}, dimensions={0} | all-to-all | bytes 1179648 | tf_op jit(solution)/shard_map/all_to_all | solution.py:431
  76.7 0.8 first_sum.1
  77.5 5.6 %all-to-all-start.3 = ((bf16[16,8,144]{2,1,0:T(8,128)(2,1)}), bf16[16,8,144]{2,1,0:T(8,128)(2,1)S(1)}, u32[]{:S(2)}, u32[]{:S(2)}) async-start(bf16[16,8,144]{2,1,0:T(8,128)(2,1)} %first_sum.1), calls=%async_computation.3 | async-start | bytes 131072 | tf_op jit(solution)/shard_map/all_to_all | solution.py:438
  83.0 0.0 copy-done
  83.0 1.9 %grad_input.1 = bf16[4,64,256]{2,1,0:T(8,128)(2,1)} custom-call(s32[4]{0:T(128)S(1)} %pad_add_fusion.flags_ref, bf16[768,256]{1,0:T(8,128)(2,1)S(1)} %grad_pre.1.pre_ref, bf16[768,256]{1,0:T(8,128)(2,1)S(1)} %collective-permute-done.3.swapped_ref, bf16[4,64,256]{2,1,0:T(8,128)(2,1)S(1)} %bitcast.18, bf16[3,3,256,256]{3,2,1,0:T(8,128)(2,1)S(1)} %copy-done), custom_call_target="tpu_custom_call" | custom-call | flops 452984832 | bytes 2097152 | tf_op jit(solution)/shard_map/grad_input/pallas_call | solution.py:297
  84.9 11.0 %all-to-all-done.3.got_ref = bf16[16,8,144]{2,1,0:T(8,128)(2,1)S(1)} async-done(((bf16[16,8,144]{2,1,0:T(8,128)(2,1)}), bf16[16,8,144]{2,1,0:T(8,128)(2,1)S(1)}, u32[]{:S(2)}, u32[]{:S(2)}) %all-to-all-start.3) | async-done | bytes 36896 | tf_op jit(solution)/shard_map/all_to_all | solution.py:438
  95.9 0.7 second_sum.1
  (4 shorter events, 0.0 us)
Async XLA Ops:
  3.3 22.8 %copy-start.1 = (bf16[1,4,1,64,256]{4,3,2,1,0:T(8,128)(2,1)S(1)}, bf16[1,4,1,64,256]{4,3,2,1,0:T(8,128)(2,1)}, u32[]{:S(2)}) copy-start(bf16[1,4,1,64,256]{4,3,2,1,0:T(8,128)(2,1)} %param.9) | copy-start | bytes 393220
  3.3 22.8 %copy-start.2 = (bf16[1,4,1,64,256]{4,3,2,1,0:T(8,128)(2,1)S(1)}, bf16[1,4,1,64,256]{4,3,2,1,0:T(8,128)(2,1)}, u32[]{:S(2)}) copy-start(bf16[1,4,1,64,256]{4,3,2,1,0:T(8,128)(2,1)} %param.8) | copy-start | bytes 393220
  3.3 22.7 %copy-start.3 = (bf16[1,4,1,64,256]{4,3,2,1,0:T(8,128)(2,1)S(1)}, bf16[1,4,1,64,256]{4,3,2,1,0:T(8,128)(2,1)}, u32[]{:S(2)}) copy-start(bf16[1,4,1,64,256]{4,3,2,1,0:T(8,128)(2,1)} %param.7) | copy-start | bytes 393220
  3.3 22.7 %copy-start.4 = (s32[4,4]{1,0:T(4,128)S(1)}, s32[4,4]{1,0:T(4,128)}, u32[]{:S(2)}) copy-start(s32[4,4]{1,0:T(4,128)} %seams_ref.3) | copy-start | bytes 196
  3.3 22.7 %copy-start.5 = (s32[4,4]{1,0:T(4,128)S(1)}, s32[4,4]{1,0:T(4,128)}, u32[]{:S(2)}) copy-start(s32[4,4]{1,0:T(4,128)} %corners_ref.1) | copy-start | bytes 196
  18.4 33.2 %copy-start.6 = (bf16[3,3,256,256]{3,2,1,0:T(8,128)(2,1)S(1)}, bf16[3,3,256,256]{3,2,1,0:T(8,128)(2,1)}, u32[]{:S(2)}) copy-start(bf16[3,3,256,256]{3,2,1,0:T(8,128)(2,1)} %weight_ref.2) | copy-start | bytes 3538948
  19.8 12.0 %all-to-all-start.1 = ((bf16[8,64,256]{2,1,0:T(8,128)(2,1)}), bf16[8,64,256]{2,1,0:T(8,128)(2,1)S(1)}, u32[]{:S(2)}, u32[]{:S(2)}) async-start(bf16[8,64,256]{2,1,0:T(8,128)(2,1)} %pick.1), calls=%async_computation.1 | async-start | bytes 524288 | tf_op jit(solution)/shard_map/all_to_all | solution.py:358
  26.9 4.9 %collective-permute-start = (bf16[4,112,256]{2,1,0:T(8,128)(2,1)S(1)}, bf16[4,112,256]{2,1,0:T(8,128)(2,1)S(1)}, u32[]{:S(2)}, u32[]{:S(2)}) collective-permute-start(bf16[4,112,256]{2,1,0:T(8,128)(2,1)S(1)} %get-tuple-element.21), channel_id=1, source_target_pairs={{0,1},{1,0},{2,3},{3,2},{4,5},{5,4},{6,7},{7,6},{8,9},{9,8},{10,11... | collective-permute-start | bytes 688136 | tf_op jit(solution)/shard_map/ppermute | solution.py:343
  32.5 19.2 %collective-permute-start.1 = (bf16[2,4,80,256]{3,2,1,0:T(8,128)(2,1)S(1)}, bf16[2,4,80,256]{3,2,1,0:T(8,128)(2,1)S(1)}, u32[]{:S(2)}, u32[]{:S(2)}) collective-permute-start(bf16[2,4,80,256]{3,2,1,0:T(8,128)(2,1)S(1)} %get-tuple-element.25), channel_id=1, source_target_pairs={{63,0},{2,1},{1,2},{4,3},{3,4},{6,5},{5,6},{8,7},{7,8},{10,9},{9,1... | collective-permute-start | bytes 983048 | tf_op jit(solution)/shard_map/ppermute | solution.py:384
  42.3 9.3 %collective-permute-start.2 = (bf16[4,80,256]{2,1,0:T(8,128)(2,1)S(1)}, bf16[4,80,256]{2,1,0:T(8,128)(2,1)S(1)}, u32[]{:S(2)}, u32[]{:S(2)}) collective-permute-start(bf16[4,80,256]{2,1,0:T(8,128)(2,1)S(1)} %get-tuple-element.26), channel_id=1, source_target_pairs={{62,0},{3,1},{0,2},{5,3},{2,4},{7,5},{4,6},{9,7},{6,8},{11,9},{8,1... | collective-permute-start | bytes 491528 | tf_op jit(solution)/shard_map/ppermute | solution.py:385
  53.4 3.6 %collective-permute-start.3 = (bf16[768,256]{1,0:T(8,128)(2,1)S(1)}, bf16[768,256]{1,0:T(8,128)(2,1)S(1)}, u32[]{:S(2)}, u32[]{:S(2)}) collective-permute-start(bf16[768,256]{1,0:T(8,128)(2,1)S(1)} %grad_pre.1.pre_ref), channel_id=1, source_target_pairs={{0,1},{1,0},{2,3},{3,2},{4,5},{5,4},{6,7},{7,6},{8,9},{9,8},{10,11... | collective-permute-start | bytes 1179656 | tf_op jit(solution)/shard_map/ppermute | solution.py:343
  58.6 24.5 %copy-start = (bf16[3,3,256,256]{3,2,1,0:T(8,128)(2,1)S(1)}, bf16[3,3,256,256]{3,2,1,0:T(8,128)(2,1)}, u32[]{:S(2)}) copy-start(bf16[3,3,256,256]{3,2,1,0:T(8,128)(2,1)} %weight_ref.3) | copy-start | bytes 3538948
  77.5 18.4 %all-to-all-start.3 = ((bf16[16,8,144]{2,1,0:T(8,128)(2,1)}), bf16[16,8,144]{2,1,0:T(8,128)(2,1)S(1)}, u32[]{:S(2)}, u32[]{:S(2)}) async-start(bf16[16,8,144]{2,1,0:T(8,128)(2,1)} %first_sum.1), calls=%async_computation.3 | async-start | bytes 131072 | tf_op jit(solution)/shard_map/all_to_all | solution.py:438

commit v7 on v6

--- a/solution.py
+++ b/solution.py
@@ -104,12 +104,14 @@
     below = flags_ref[3]
     held = local * CELLS
     cells = table_ref[:, table_ref.shape[1] - held :].reshape(table_ref.shape[0] * held, -1)
-    rows, width = 4 * local * GAP, cells.shape[0]
+    rows, width = 4 * GAP, cells.shape[0]
     row = lax.broadcasted_iota(jnp.int32, (rows, 1), 0)
     spot, block = row % GAP, row // GAP
-    of_g = jnp.where(spot < 2, spot, jnp.where(spot >= GAP - 2, spot - (GAP - 4), -1))
-    of_p = jnp.where(spot == 0, 4, jnp.where(spot == GAP - 1, 5, -1))
-    cell = jnp.where(block % (2 * local) < local, of_g, of_p)
+    of_g = block % 2 == 1
+    each = jnp.where(of_g, 4, 2)
+    k = spot % each
+    cell = jnp.where(of_g, k, jnp.where(spot < 2 * local, 4 + k, -1))
+    is_left = k * 2 >= each
     face_at = jnp.zeros((rows, 1), jnp.int32)
     for face in range(local):
         for beyond in range(2):
@@ -117,23 +119,21 @@
                 left, right = corners_ref[face, 2 * below], corners_ref[face, 2 * below + 1]
             else:
                 left, right = seams_ref[face, 3], seams_ref[face, 1]
-            here = (block % local == face) & (block // (2 * local) == beyond)
-            face_at = jnp.where(here, jnp.where(spot < GAP // 2, right, left), face_at)
+            here = (spot // each == face) & (block // 2 == beyond)
+            face_at = jnp.where(here, jnp.where(is_left, left, right), face_at)
     index = jnp.where(cell < 0, -1, face_at * CELLS + cell)
     where = lax.broadcasted_iota(jnp.int32, (rows, width), 1) == index
     tails = jnp.dot(
         jnp.where(where, 1.0, 0.0).astype(jnp.bfloat16), cells, preferred_element_type=jnp.float32
     ).astype(jnp.bfloat16)
-    for which, source in enumerate((g_ref, p_ref)):
-        for face in range(local):
-            at = (which * local + face) * GAP
-            own_ref[which, face, :side] = source[face]
-            own_ref[which, face, side:] = tails[at : at + GAP]
-            if which == 0:
-                mine_ref[face, :side] = source[face]
-                mine_ref[face, side : side + GAP] = tails[at : at + GAP]
-            at += 2 * local * GAP
-            wrap_ref[which, face] = tails[at : at + GAP]
+    full = local * side
+    for which, source in enumerate((p_ref, g_ref)):
+        at = which * (full + GAP)
+        own_ref[at : at + full] = source[...].reshape(full, -1)
+        own_ref[at + full : at + full + GAP] = tails[which * GAP : (which + 1) * GAP]
+    mine_ref[:full] = g_ref[...].reshape(full, -1)
+    mine_ref[full : full + GAP] = tails[GAP : 2 * GAP]
+    wrap_ref[...] = tails[2 * GAP :]
     nxl, nz, nc, per_tile = tiles
     channels, half = x_ref.shape[-1], kept_ref.shape[-1]
     line = lax.broadcasted_iota(jnp.int32, (channels, nc * half), 0)
@@ -151,20 +151,24 @@
     for face in range(local):
         for part in range(2):
             at = face * side + part * side // 2
-            mine_ref[face, side + GAP :, part * half : (part + 1) * half] = chosen[at : at + side // 2, half:]
+            into = full + GAP + face * side // 2
+            mine_ref[into : into + side // 2, part * half : (part + 1) * half] = chosen[at : at + side // 2, half:]
 
 
 def turn_kernel(local, side, flags_ref, kept_ref, part_ref, out_ref, lines):
     pitch = side + 2 * GAP
     row = local * pitch
     half = kept_ref.shape[-1]
+    start = local * side + GAP
     lines[...] = jnp.zeros_like(lines)
     for face in range(local):
         at = pl.multiple_of(flags_ref[0] * row + face * pitch + GAP, 16)
         lines[pl.ds(at, side), :] = kept_ref[face * side : (face + 1) * side].astype(jnp.float32)
         for part in range(2):
             at = pl.multiple_of((1 - flags_ref[0]) * row + face * pitch + GAP + part * side // 2, 16)
-            lines[pl.ds(at, side // 2), :] = part_ref[face, side + GAP :, part * half : (part + 1) * half].astype(jnp.float32)
+            lines[pl.ds(at, side // 2), :] = part_ref[
+                start + face * side // 2 : start + (face + 1) * side // 2, part * half : (part + 1) * half
+            ].astype(jnp.float32)
     for c in range(3):
         moved = lines[...] if c == 1 else pltpu.roll(lines[...], (1 - c) % (2 * row), 0)
         out_ref[c * half : (c + 1) * half, :] = moved.T.astype(jnp.bfloat16)
@@ -173,27 +177,30 @@
 def send_kernel(local, side, blocks, flags_ref, own_ref, tails_ref, pieces_ref, near_ref, far_ref):
     px_blocks, ch_blocks = blocks
     px = side // px_blocks
-    channels = own_ref.shape[-1]
-    ch = channels // ch_blocks
+    ch = own_ref.shape[-1] // ch_blocks
     count = px * 2 // ch_blocks
+    full = local * side
     near, far = flags_ref[1], flags_ref[2]
 
-    def put_wrap(out, which, face):
-        for b in range(px_blocks * ch_blocks):
-            i, j = divmod(b, ch_blocks)
-            piece = pieces_ref[b, face * count : (face + 1) * count]
-            if ch_blocks == 1:
-                part = piece[which * px : (which + 1) * px]
-            else:
-                part = piece[:, which * ch : (which + 1) * ch]
-            out[i * px : (i + 1) * px, j * ch : (j + 1) * ch] = part
-        out[side:, :] = tails_ref[which, face]
+    def put_wrap(out, start, of_g):
+        for face in range(local):
+            for b in range(px_blocks * ch_blocks):
+                i, j = divmod(b, ch_blocks)
+                piece = pieces_ref[b, face * count : (face + 1) * count]
+                which = 0 if of_g else 1
+                if ch_blocks == 1:
+                    part = piece[which * px : (which + 1) * px]
+                else:
+                    part = piece[:, which * ch : (which + 1) * ch]
+                at = start + face * side + i * px
+                out[at : at + px, j * ch : (j + 1) * ch] = part
+        tail = GAP if of_g else 0
+        out[start + full : start + full + GAP, :] = tails_ref[tail : tail + GAP]
 
     @pl.when(near == 1)
     def _():
-        for face in range(local):
-            put_wrap(near_ref.at[0, face], 0, face)
-            put_wrap(near_ref.at[1, face], 1, face)
+        put_wrap(near_ref, 0, False)
+        put_wrap(near_ref, full + GAP, True)
 
     @pl.when(near == 0)
     def _():
@@ -201,12 +208,11 @@
 
     @pl.when(far == 1)
     def _():
-        for face in range(local):
-            put_wrap(far_ref.at[face], 0, face)
+        put_wrap(far_ref, 0, True)
 
     @pl.when(far == 0)
     def _():
-        far_ref[...] = own_ref[0]
+        far_ref[...] = own_ref[full + GAP :]
 
 
 def grad_pre_kernel(local, side, flags_ref, own_ref, part_ref, near_ref, far_ref, weight_ref, out_ref, g_pad, p_pad):
@@ -214,18 +220,33 @@
     row = local * pitch
     core = flags_ref[0]
 
-    def put(pad, slot, source, face):
-        at = pl.multiple_of(slot * row + face * pitch, 16)
-        border = source[face, side : side + GAP]
-        pad[pl.ds(at, GAP), :] = border
-        pad[pl.ds(at + GAP, side), :] = source[face, :side]
-        pad[pl.ds(at + GAP + side, GAP), :] = border
-
-    for face in range(local):
-        for role, source in enumerate((far_ref, near_ref.at[0], own_ref.at[0], part_ref)):
-            put(g_pad, jnp.where(core == 0, role, 3 - role), source, face)
-        for role, source in enumerate((near_ref.at[1], own_ref.at[1])):
-            put(p_pad, jnp.where(core == 0, role, 1 - role), source, face)
+    full = local * side
+    line = lax.broadcasted_iota(jnp.int32, (local * GAP, GAP), 0)
+    lane = lax.broadcasted_iota(jnp.int32, (local * GAP, GAP), 1)
+    spot, at_face = line % GAP, line // GAP
+    last = spot - (GAP - 4)
+    of_g = jnp.where(spot < 2, spot, jnp.where(spot >= GAP - 2, last, -1)) + jnp.where(
+        (spot < 2) | (spot >= GAP - 2), 4 * at_face, 0
+    )
+    of_p = jnp.where(spot == 0, 2 * at_face, jnp.where(spot == GAP - 1, 2 * at_face + 1, -1))
+    spread_g = jnp.where(lane == of_g, 1.0, 0.0).astype(jnp.bfloat16)
+    spread_p = jnp.where(lane == of_p, 1.0, 0.0).astype(jnp.bfloat16)
+
+    def put(pad, slot, source, start, spread):
+        tails = source[start + full : start + full + GAP, :]
+        borders = jnp.dot(spread, tails, preferred_element_type=jnp.float32).astype(jnp.bfloat16)
+        for face in range(local):
+            at = pl.multiple_of(slot * row + face * pitch, 16)
+            border = borders[face * GAP : (face + 1) * GAP]
+            pad[pl.ds(at, GAP), :] = border
+            pad[pl.ds(at + GAP, side), :] = source[start + face * side : start + (face + 1) * side, :]
+            pad[pl.ds(at + GAP + side, GAP), :] = border
+
+    second = full + GAP
+    for role, (source, start) in enumerate(((far_ref, 0), (near_ref, second), (own_ref, second), (part_ref, 0))):
+        put(g_pad, jnp.where(core == 0, role, 3 - role), source, start, spread_g)
+    for role, source in enumerate((near_ref, own_ref)):
+        put(p_pad, jnp.where(core == 0, role, 1 - role), source, 0, spread_p)
     for slot in range(2):
         grad = conv_rows(g_pad, slot * row, row, weight_ref)
         pre = p_pad[slot * row : (slot + 1) * row, :].astype(jnp.float32)
@@ -362,9 +383,9 @@
     own, tails, mine, kept = kernel(
         functools.partial(border_kernel, local, side, (nxl, nz, nc, per_tile)),
         (
-            shape((2, local, side + GAP, channels), bf),
-            shape((2, local, GAP, channels), bf),
-            shape((local, side + GAP + side // 2, channels), bf),
+            shape((2 * (local * side + GAP), channels), bf),
+            shape((2 * GAP, channels), bf),
+            shape((local * side + GAP + local * side // 2, channels), bf),
             shape((local * side, half), bf),
         ),
         (flags, seams, corners, table, g, p, x),
@@ -374,7 +395,7 @@
     wrapped, part = lax.optimization_barrier((wrapped, swap(mine)))
     near, far = kernel(
         functools.partial(send_kernel, local, side, (px_blocks, ch_blocks)),
-        (shape(own.shape, bf), shape(own.shape[1:], bf)),
+        (shape(own.shape, bf), shape((own.shape[0] // 2, channels), bf)),
         (flags, own, tails, wrapped),
         1,
         name="send",

time: 97.8 us -> 97.2 us (level)
    all_to_all x1, waiting for transfers between devices: 3 us -> 1.33 us  [on_device(): wrapped = lax.all_to_all(picked, FACE, 0, 0, tiled=True)]
    ppermute x2, waiting for transfers between devices: 0.87 us -> 2.28 us  [on_device(): swap = lambda a: lax.ppermute(a, 'c', [(0, 1), (1, 0)])]
  transfers between devices with their start and end apart: 6 -> 6, of which waited for: 4 -> 5; matrix products, arithmetic and copies ran while one was open for 0% -> 0% of each run, Pallas kernels for 4% -> 4%
where the time goes in v7:
time: 97.2 us; the launch traced here: 95.9 us
  blocking collectives  33 us (34%)
  starting transfers between devices  26.9 us (28%)
  waiting for transfers between devices  21.7 us (22%)
  Pallas kernels  13.2 us (14%)
    all_to_all x1, blocking collectives, on_device(): got = lax.all_to_all(parts, FACE + ('xl',), 0, 0, tiled=True)  18.1 us
    all_to_all x1, blocking collectives, on_device(): table = lax.all_to_all(sent, FACE, 0, 0, tiled=True)  14.9 us
    pallas_call x10, Pallas kernels, kernel(): pl.pallas_call(body, out_shape=out_shape, in_specs=[pl.BlockSpec(memory_s...  13.2 us
    all_to_all x1, waiting for transfers between devices, on_device(): got = lax.all_to_all(total, 'z', 0, 0, tiled=True)  10.9 us
    ppermute x1, starting transfers between devices, on_device(): near = lax.ppermute(near, TILE, pairs(1))  10.1 us
    ppermute x1, waiting for transfers between devices, on_device(): far = lax.ppermute(far, TILE, pairs(2))  7.13 us
    all_to_all x1, starting transfers between devices, on_device(): wrapped = lax.all_to_all(picked, FACE, 0, 0, tiled=True)  6.18 us
    all_to_all x1, starting transfers between devices, on_device(): got = lax.all_to_all(total, 'z', 0, 0, tiled=True)  4.9 us
  transfers between devices with their start and end apart: 6, of which 5 were waited for; matrix products, arithmetic and copies ran while one was open for 0% of the time, Pallas kernels for 4%

profile of v7, /device:TPU:6, one launch (start us, length us, event | category | flops | bytes accessed | tf_op | source)
XLA Modules:
  0.0 95.9 jit_solution(25825021492988243)
XLA Ops:
  0.7 2.6 %pack.1 = bf16[8,96,256]{2,1,0:T(8,128)(2,1)} custom-call(s32[4,4]{1,0:T(4,128)} %seams_ref.3, bf16[4,64,256]{2,1,0:T(8,128)(2,1)} %bitcast.16, bf16[4,64,256]{2,1,0:T(8,128)(2,1)} %bitcast.19), custom_call_target="tpu_custom_call" | custom-call | bytes 1048576 | tf_op jit(solution)/shard_map/pack/pallas_call | solution.py:318
  3.3 0.0 copy-start.1
  3.3 0.0 copy-start.2
  3.3 0.0 copy-start.3
  3.3 0.0 copy-start.4
  3.3 0.0 copy-start.5
  3.3 0.1 pad_add_fusion.flags_ref
  3.4 14.9 %all_to_all.20.table_ref = bf16[8,96,256]{2,1,0:T(8,128)(2,1)S(1)} all-to-all(bf16[8,96,256]{2,1,0:T(8,128)(2,1)} %pack.1), channel_id=1, replica_groups=mesh['xh'=2,'y'=4,'xl'=2,'z'=16,'c'=2] {'xh','y'}, dimensions={0} | all-to-all | bytes 786432 | tf_op jit(solution)/shard_map/all_to_all | solution.py:366
  18.3 0.1 copy.11
  18.4 0.0 copy-start.6
  18.5 1.4 %pick.1 = bf16[8,64,256]{2,1,0:T(8,128)(2,1)} custom-call(s32[32]{0:T(128)S(1)} %fusion.want_ref, bf16[8,96,256]{2,1,0:T(8,128)(2,1)S(1)} %all_to_all.20.table_ref), custom_call_target="tpu_custom_call" | custom-call | bytes 1048576 | tf_op jit(solution)/shard_map/pick/pallas_call | solution.py:318
  19.8 6.2 %all-to-all-start.1 = ((bf16[8,64,256]{2,1,0:T(8,128)(2,1)}), bf16[8,64,256]{2,1,0:T(8,128)(2,1)S(1)}, u32[]{:S(2)}, u32[]{:S(2)}) async-start(bf16[8,64,256]{2,1,0:T(8,128)(2,1)} %pick.1), calls=%async_computation.1 | async-start | bytes 524288 | tf_op jit(solution)/shard_map/all_to_all | solution.py:379
  26.0 0.0 copy-done.1
  26.0 0.0 copy-done.2
  26.0 0.0 copy-done.3
  26.0 0.0 copy-done.4
  26.0 0.0 copy-done.5
  26.1 1.1 %border.1 = (bf16[544,256]{1,0:T(8,128)(2,1)S(1)}, bf16[32,256]{1,0:T(8,128)(2,1)S(1)}, bf16[400,256]{1,0:T(8,128)(2,1)S(1)}, bf16[256,128]{1,0:T(8,128)(2,1)S(1)}) custom-call(s32[4]{0:T(128)S(1)} %pad_add_fusion.flags_ref, s32[4,4]{1,0:T(4,128)S(1)} %copy-done.4, s32[4,4]{1,0:T(4,128)S(1)} %copy-done.5, bf16[8,96,256]{2,1,0:T(8,128)(2,1)S(1)} %all_to_all.20.table_ref, ...), custom_call_target="tpu_custom_call" | custom-call | bytes 1048576 | tf_op jit(solution)/shard_map/border/pallas_call | solution.py:318
  27.2 1.9 %collective-permute-start = (bf16[400,256]{1,0:T(8,128)(2,1)S(1)}, bf16[400,256]{1,0:T(8,128)(2,1)S(1)}, u32[]{:S(2)}, u32[]{:S(2)}) collective-permute-start(bf16[400,256]{1,0:T(8,128)(2,1)S(1)} %get-tuple-element.21), channel_id=1, source_target_pairs={{0,1},{1,0},{2,3},{3,2},{4,5},{5,4},{6,7},{7,6},{8,9},{9,8},{10,11... | collective-permute-start | bytes 614408 | tf_op jit(solution)/shard_map/ppermute | solution.py:364
  29.1 1.4 %collective-permute-done.part_ref = bf16[400,256]{1,0:T(8,128)(2,1)S(1)} collective-permute-done((bf16[400,256]{1,0:T(8,128)(2,1)S(1)}, bf16[400,256]{1,0:T(8,128)(2,1)S(1)}, u32[]{:S(2)}, u32[]{:S(2)}) %collective-permute-start) | collective-permute-done | bytes 204832 | tf_op jit(solution)/shard_map/ppermute | solution.py:364
  30.5 1.3 %all-to-all-done.1.pieces_ref = bf16[8,64,256]{2,1,0:T(8,128)(2,1)S(1)} async-done(((bf16[8,64,256]{2,1,0:T(8,128)(2,1)}), bf16[8,64,256]{2,1,0:T(8,128)(2,1)S(1)}, u32[]{:S(2)}, u32[]{:S(2)}) %all-to-all-start.1) | async-done | bytes 262176 | tf_op jit(solution)/shard_map/all_to_all | solution.py:379
  31.9 0.6 send.1
  32.5 10.1 %collective-permute-start.1 = (bf16[544,256]{1,0:T(8,128)(2,1)S(1)}, bf16[544,256]{1,0:T(8,128)(2,1)S(1)}, u32[]{:S(2)}, u32[]{:S(2)}) collective-permute-start(bf16[544,256]{1,0:T(8,128)(2,1)S(1)} %get-tuple-element.25), channel_id=1, source_target_pairs={{63,0},{2,1},{1,2},{4,3},{3,4},{6,5},{5,6},{8,7},{7,8},{10,9},{9,1... | collective-permute-start | bytes 835592 | tf_op jit(solution)/shard_map/ppermute | solution.py:405
  42.5 1.9 %collective-permute-start.2 = (bf16[272,256]{1,0:T(8,128)(2,1)S(1)}, bf16[272,256]{1,0:T(8,128)(2,1)S(1)}, u32[]{:S(2)}, u32[]{:S(2)}) collective-permute-start(bf16[272,256]{1,0:T(8,128)(2,1)S(1)} %get-tuple-element.26), channel_id=1, source_target_pairs={{62,0},{3,1},{0,2},{5,3},{2,4},{7,5},{4,6},{9,7},{6,8},{11,9},{8,1... | collective-permute-start | bytes 417800 | tf_op jit(solution)/shard_map/ppermute | solution.py:406
  44.5 7.1 %collective-permute-done.2.far_ref = bf16[272,256]{1,0:T(8,128)(2,1)S(1)} collective-permute-done((bf16[272,256]{1,0:T(8,128)(2,1)S(1)}, bf16[272,256]{1,0:T(8,128)(2,1)S(1)}, u32[]{:S(2)}, u32[]{:S(2)}) %collective-permute-start.2) | collective-permute-done | bytes 139296 | tf_op jit(solution)/shard_map/ppermute | solution.py:406
  51.6 0.0 collective-permute-done.1.near_ref
  51.6 0.0 copy-done.6
  51.6 1.9 %grad_pre.1.pre_ref = bf16[768,256]{1,0:T(8,128)(2,1)S(1)} custom-call(s32[4]{0:T(128)S(1)} %pad_add_fusion.flags_ref, bf16[544,256]{1,0:T(8,128)(2,1)S(1)} %get-tuple-element.19.own_ref, bf16[400,256]{1,0:T(8,128)(2,1)S(1)} %collective-permute-done.part_ref, bf16[544,256]{1,0:T(8,128)(2,1)S(1)} %collective-permute-done.1.near_ref, ...), custom_call_target="tpu_custom_call" | custom-call | flops 905969664 | bytes 4194304 | tf_op jit(solution)/shard_map/grad_pre/pallas_call | solution.py:318
  53.5 1.9 %collective-permute-start.3 = (bf16[768,256]{1,0:T(8,128)(2,1)S(1)}, bf16[768,256]{1,0:T(8,128)(2,1)S(1)}, u32[]{:S(2)}, u32[]{:S(2)}) collective-permute-start(bf16[768,256]{1,0:T(8,128)(2,1)S(1)} %grad_pre.1.pre_ref), channel_id=1, source_target_pairs={{0,1},{1,0},{2,3},{3,2},{4,5},{5,4},{6,7},{7,6},{8,9},{9,8},{10,11... | collective-permute-start | bytes 1179656 | tf_op jit(solution)/shard_map/ppermute | solution.py:364
  55.4 0.8 turn.1.x_ref
  56.2 0.9 collective-permute-done.3.swapped_ref
  57.1 1.5 %grad_first.1 = bf16[16,144,128]{2,1,0:T(8,128)(2,1)S(1)} custom-call(s32[4]{0:T(128)S(1)} %pad_add_fusion.flags_ref, bf16[384,768]{1,0:T(8,128)(2,1)S(1)} %turn.1.x_ref, bf16[768,256]{1,0:T(8,128)(2,1)S(1)} %grad_pre.1.pre_ref, bf16[768,256]{1,0:T(8,128)(2,1)S(1)} %collective-permute-done.3.swapped_ref), custom_call_target="tpu_custom_call" | custom-call | flops 452984832 | bytes 1048576 | tf_op jit(solution)/shard_map/grad_first/pallas_call | solution.py:318
  58.6 0.0 copy-start
  58.6 18.1 %all_to_all.21.got_ref = bf16[16,144,128]{2,1,0:T(8,128)(2,1)S(1)} all-to-all(bf16[16,144,128]{2,1,0:T(8,128)(2,1)S(1)} %grad_first.1), channel_id=1, replica_groups=mesh['xh'=2,'y'=4,'xl'=2,'z'=16,'c'=2] {'xh','y','xl'}, dimensions={0} | all-to-all | bytes 1179648 | tf_op jit(solution)/shard_map/all_to_all | solution.py:452
  76.7 0.8 first_sum.1
  77.5 4.9 %all-to-all-start.3 = ((bf16[16,8,144]{2,1,0:T(8,128)(2,1)}), bf16[16,8,144]{2,1,0:T(8,128)(2,1)S(1)}, u32[]{:S(2)}, u32[]{:S(2)}) async-start(bf16[16,8,144]{2,1,0:T(8,128)(2,1)} %first_sum.1), calls=%async_computation.3 | async-start | bytes 131072 | tf_op jit(solution)/shard_map/all_to_all | solution.py:459
  82.4 0.0 copy-done
  82.4 1.9 %grad_input.1 = bf16[4,64,256]{2,1,0:T(8,128)(2,1)} custom-call(s32[4]{0:T(128)S(1)} %pad_add_fusion.flags_ref, bf16[768,256]{1,0:T(8,128)(2,1)S(1)} %grad_pre.1.pre_ref, bf16[768,256]{1,0:T(8,128)(2,1)S(1)} %collective-permute-done.3.swapped_ref, bf16[4,64,256]{2,1,0:T(8,128)(2,1)S(1)} %bitcast.18, bf16[3,3,256,256]{3,2,1,0:T(8,128)(2,1)S(1)} %copy-done), custom_call_target="tpu_custom_call" | custom-call | flops 452984832 | bytes 2097152 | tf_op jit(solution)/shard_map/grad_input/pallas_call | solution.py:318
  84.3 10.9 %all-to-all-done.3.got_ref = bf16[16,8,144]{2,1,0:T(8,128)(2,1)S(1)} async-done(((bf16[16,8,144]{2,1,0:T(8,128)(2,1)}), bf16[16,8,144]{2,1,0:T(8,128)(2,1)S(1)}, u32[]{:S(2)}, u32[]{:S(2)}) %all-to-all-start.3) | async-done | bytes 36896 | tf_op jit(solution)/shard_map/all_to_all | solution.py:459
  95.2 0.7 second_sum.1
  (4 shorter events, 0.0 us)
Async XLA Ops:
  3.3 22.8 %copy-start.1 = (bf16[1,4,1,64,256]{4,3,2,1,0:T(8,128)(2,1)S(1)}, bf16[1,4,1,64,256]{4,3,2,1,0:T(8,128)(2,1)}, u32[]{:S(2)}) copy-start(bf16[1,4,1,64,256]{4,3,2,1,0:T(8,128)(2,1)} %param.9) | copy-start | bytes 393220
  3.3 22.8 %copy-start.2 = (bf16[1,4,1,64,256]{4,3,2,1,0:T(8,128)(2,1)S(1)}, bf16[1,4,1,64,256]{4,3,2,1,0:T(8,128)(2,1)}, u32[]{:S(2)}) copy-start(bf16[1,4,1,64,256]{4,3,2,1,0:T(8,128)(2,1)} %param.8) | copy-start | bytes 393220
  3.3 22.7 %copy-start.3 = (bf16[1,4,1,64,256]{4,3,2,1,0:T(8,128)(2,1)S(1)}, bf16[1,4,1,64,256]{4,3,2,1,0:T(8,128)(2,1)}, u32[]{:S(2)}) copy-start(bf16[1,4,1,64,256]{4,3,2,1,0:T(8,128)(2,1)} %param.7) | copy-start | bytes 393220
  3.3 22.7 %copy-start.4 = (s32[4,4]{1,0:T(4,128)S(1)}, s32[4,4]{1,0:T(4,128)}, u32[]{:S(2)}) copy-start(s32[4,4]{1,0:T(4,128)} %seams_ref.3) | copy-start | bytes 196
  3.3 22.7 %copy-start.5 = (s32[4,4]{1,0:T(4,128)S(1)}, s32[4,4]{1,0:T(4,128)}, u32[]{:S(2)}) copy-start(s32[4,4]{1,0:T(4,128)} %corners_ref.1) | copy-start | bytes 196
  18.4 33.2 %copy-start.6 = (bf16[3,3,256,256]{3,2,1,0:T(8,128)(2,1)S(1)}, bf16[3,3,256,256]{3,2,1,0:T(8,128)(2,1)}, u32[]{:S(2)}) copy-start(bf16[3,3,256,256]{3,2,1,0:T(8,128)(2,1)} %weight_ref.2) | copy-start | bytes 3538948
  19.8 12.0 %all-to-all-start.1 = ((bf16[8,64,256]{2,1,0:T(8,128)(2,1)}), bf16[8,64,256]{2,1,0:T(8,128)(2,1)S(1)}, u32[]{:S(2)}, u32[]{:S(2)}) async-start(bf16[8,64,256]{2,1,0:T(8,128)(2,1)} %pick.1), calls=%async_computation.1 | async-start | bytes 524288 | tf_op jit(solution)/shard_map/all_to_all | solution.py:379
  27.2 3.3 %collective-permute-start = (bf16[400,256]{1,0:T(8,128)(2,1)S(1)}, bf16[400,256]{1,0:T(8,128)(2,1)S(1)}, u32[]{:S(2)}, u32[]{:S(2)}) collective-permute-start(bf16[400,256]{1,0:T(8,128)(2,1)S(1)} %get-tuple-element.21), channel_id=1, source_target_pairs={{0,1},{1,0},{2,3},{3,2},{4,5},{5,4},{6,7},{7,6},{8,9},{9,8},{10,11... | collective-permute-start | bytes 614408 | tf_op jit(solution)/shard_map/ppermute | solution.py:364
  32.5 19.2 %collective-permute-start.1 = (bf16[544,256]{1,0:T(8,128)(2,1)S(1)}, bf16[544,256]{1,0:T(8,128)(2,1)S(1)}, u32[]{:S(2)}, u32[]{:S(2)}) collective-permute-start(bf16[544,256]{1,0:T(8,128)(2,1)S(1)} %get-tuple-element.25), channel_id=1, source_target_pairs={{63,0},{2,1},{1,2},{4,3},{3,4},{6,5},{5,6},{8,7},{7,8},{10,9},{9,1... | collective-permute-start | bytes 835592 | tf_op jit(solution)/shard_map/ppermute | solution.py:405
  42.5 9.1 %collective-permute-start.2 = (bf16[272,256]{1,0:T(8,128)(2,1)S(1)}, bf16[272,256]{1,0:T(8,128)(2,1)S(1)}, u32[]{:S(2)}, u32[]{:S(2)}) collective-permute-start(bf16[272,256]{1,0:T(8,128)(2,1)S(1)} %get-tuple-element.26), channel_id=1, source_target_pairs={{62,0},{3,1},{0,2},{5,3},{2,4},{7,5},{4,6},{9,7},{6,8},{11,9},{8,1... | collective-permute-start | bytes 417800 | tf_op jit(solution)/shard_map/ppermute | solution.py:406
  53.5 3.6 %collective-permute-start.3 = (bf16[768,256]{1,0:T(8,128)(2,1)S(1)}, bf16[768,256]{1,0:T(8,128)(2,1)S(1)}, u32[]{:S(2)}, u32[]{:S(2)}) collective-permute-start(bf16[768,256]{1,0:T(8,128)(2,1)S(1)} %grad_pre.1.pre_ref), channel_id=1, source_target_pairs={{0,1},{1,0},{2,3},{3,2},{4,5},{5,4},{6,7},{7,6},{8,9},{9,8},{10,11... | collective-permute-start | bytes 1179656 | tf_op jit(solution)/shard_map/ppermute | solution.py:364
  58.6 23.8 %copy-start = (bf16[3,3,256,256]{3,2,1,0:T(8,128)(2,1)S(1)}, bf16[3,3,256,256]{3,2,1,0:T(8,128)(2,1)}, u32[]{:S(2)}) copy-start(bf16[3,3,256,256]{3,2,1,0:T(8,128)(2,1)} %weight_ref.3) | copy-start | bytes 3538948
  77.5 17.7 %all-to-all-start.3 = ((bf16[16,8,144]{2,1,0:T(8,128)(2,1)}), bf16[16,8,144]{2,1,0:T(8,128)(2,1)S(1)}, u32[]{:S(2)}, u32[]{:S(2)}) async-start(bf16[16,8,144]{2,1,0:T(8,128)(2,1)} %first_sum.1), calls=%async_computation.3 | async-start | bytes 131072 | tf_op jit(solution)/shard_map/all_to_all | solution.py:459

commit v8 on v7

--- a/solution.py
+++ b/solution.py
@@ -215,44 +215,75 @@
         far_ref[...] = own_ref[full + GAP :]
 
 
-def grad_pre_kernel(local, side, flags_ref, own_ref, part_ref, near_ref, far_ref, weight_ref, out_ref, g_pad, p_pad):
+def put_row(pad, local, side, source, start, each):
     pitch = side + 2 * GAP
-    row = local * pitch
-    core = flags_ref[0]
-
     full = local * side
     line = lax.broadcasted_iota(jnp.int32, (local * GAP, GAP), 0)
     lane = lax.broadcasted_iota(jnp.int32, (local * GAP, GAP), 1)
     spot, at_face = line % GAP, line // GAP
-    last = spot - (GAP - 4)
-    of_g = jnp.where(spot < 2, spot, jnp.where(spot >= GAP - 2, last, -1)) + jnp.where(
-        (spot < 2) | (spot >= GAP - 2), 4 * at_face, 0
-    )
-    of_p = jnp.where(spot == 0, 2 * at_face, jnp.where(spot == GAP - 1, 2 * at_face + 1, -1))
-    spread_g = jnp.where(lane == of_g, 1.0, 0.0).astype(jnp.bfloat16)
-    spread_p = jnp.where(lane == of_p, 1.0, 0.0).astype(jnp.bfloat16)
-
-    def put(pad, slot, source, start, spread):
-        tails = source[start + full : start + full + GAP, :]
-        borders = jnp.dot(spread, tails, preferred_element_type=jnp.float32).astype(jnp.bfloat16)
-        for face in range(local):
-            at = pl.multiple_of(slot * row + face * pitch, 16)
-            border = borders[face * GAP : (face + 1) * GAP]
-            pad[pl.ds(at, GAP), :] = border
-            pad[pl.ds(at + GAP, side), :] = source[start + face * side : start + (face + 1) * side, :]
-            pad[pl.ds(at + GAP + side, GAP), :] = border
-
-    second = full + GAP
-    for role, (source, start) in enumerate(((far_ref, 0), (near_ref, second), (own_ref, second), (part_ref, 0))):
-        put(g_pad, jnp.where(core == 0, role, 3 - role), source, start, spread_g)
-    for role, source in enumerate((near_ref, own_ref)):
-        put(p_pad, jnp.where(core == 0, role, 1 - role), source, 0, spread_p)
-    for slot in range(2):
-        grad = conv_rows(g_pad, slot * row, row, weight_ref)
-        pre = p_pad[slot * row : (slot + 1) * row, :].astype(jnp.float32)
-        logistic = jax.nn.sigmoid(pre)
-        slope = logistic * (1.0 + pre * (1.0 - logistic))
-        out_ref[slot * row : (slot + 1) * row, :] = (grad * slope).astype(jnp.bfloat16)
+    n = each // 2
+    k = jnp.where(spot < n, spot, jnp.where(spot >= GAP - n, spot - (GAP - each), GAP))
+    spread = jnp.where(lane == k + each * at_face, 1.0, 0.0)
+    spread = jnp.where(k < each, spread, 0.0).astype(jnp.bfloat16)
+    tails = source[start + full : start + full + GAP, :]
+    borders = jnp.dot(spread, tails, preferred_element_type=jnp.float32).astype(jnp.bfloat16)
+    for face in range(local):
+        at = face * pitch
+        border = borders[face * GAP : (face + 1) * GAP]
+        pad[at : at + GAP, :] = border
+        pad[at + GAP : at + GAP + side, :] = source[start + face * side : start + (face + 1) * side, :]
+        pad[at + GAP + side : at + pitch, :] = border
+
+
+def row_taps(pairs, row):
+    sums = []
+    for c in range(3):
+        total = None
+        for rows, weight in pairs:
+            term = lax.dot_general(
+                rows, weight(c), (((1,), (1,)), ((), ())), preferred_element_type=jnp.float32
+            )
+            total = term if total is None else total + term
+        sums.append(total)
+    return pltpu.roll(sums[2], 1, 0) + sums[1] + pltpu.roll(sums[0], row - 1, 0)
+
+
+def silu_slope(pre):
+    pre = pre.astype(jnp.float32)
+    logistic = jax.nn.sigmoid(pre)
+    return logistic * (1.0 + pre * (1.0 - logistic))
+
+
+def near_half_kernel(local, side, flags_ref, own_ref, part_ref, weight_ref, hidden_ref, slope_ref, own_pad, part_pad, pre_pad):
+    row = own_pad.shape[0]
+    toward = 2 * flags_ref[0]
+    second = local * side + GAP
+    put_row(own_pad, local, side, own_ref, second, 4)
+    put_row(part_pad, local, side, part_ref, 0, 4)
+    put_row(pre_pad, local, side, own_ref, 0, 2)
+    own, part = own_pad[...], part_pad[...]
+    hidden_ref[:row] = row_taps([(own, lambda c: weight_ref[toward, c])], row)
+    hidden_ref[row:] = row_taps([(own, lambda c: weight_ref[1, c]), (part, lambda c: weight_ref[toward, c])], row)
+    slope_ref[...] = silu_slope(pre_pad[...])
+
+
+def grad_pre_kernel(local, side, flags_ref, near_ref, far_ref, hidden_ref, slope_ref, weight_ref, out_ref, near_pad, far_pad, pre_pad):
+    row = near_pad.shape[0]
+    core = flags_ref[0]
+    away = 2 - 2 * core
+    second = local * side + GAP
+    put_row(near_pad, local, side, near_ref, second, 4)
+    put_row(far_pad, local, side, far_ref, 0, 4)
+    put_row(pre_pad, local, side, near_ref, 0, 2)
+    near, far = near_pad[...], far_pad[...]
+    outer = hidden_ref[:row] + row_taps(
+        [(far, lambda c: weight_ref[away, c]), (near, lambda c: weight_ref[1, c])], row
+    )
+    inner = hidden_ref[row:] + row_taps([(near, lambda c: weight_ref[away, c])], row)
+    outer = (outer * silu_slope(pre_pad[...])).astype(jnp.bfloat16)
+    inner = (inner * slope_ref[...]).astype(jnp.bfloat16)
+    out_ref[pl.ds(pl.multiple_of(core * row, 16), row), :] = outer
+    out_ref[pl.ds(pl.multiple_of((1 - core) * row, 16), row), :] = inner
 
 
 def conv_rows(pad, start, row, weight_ref):
@@ -287,29 +318,54 @@
         out_ref[face] = (own + grad[at : at + side, :]).astype(jnp.bfloat16)
 
 
-def grad_first_kernel(row, nxl, per_tile, flags_ref, x_ref, pre_ref, swapped_ref, out_ref, rows4):
-    four_rows(rows4, flags_ref[0], row, pre_ref, swapped_ref)
-    dests, lines, half = out_ref.shape[0], out_ref.shape[1] // 9, out_ref.shape[2]
-    for r in range(3):
-        terms = jnp.dot(x_ref[...], rows4[(2 - r) * row : (4 - r) * row, :], preferred_element_type=jnp.float32)
-        for c in range(3):
-            turned = terms[c * half : (c + 1) * half, :].T
-            at = (3 * r + c) * lines
-            if nxl == 1:
-                for d in range(dests):
-                    out_ref[d, at : at + lines] = turned[d * lines : (d + 1) * lines, :].astype(jnp.bfloat16)
-                continue
-            split = turned.reshape(dests // 2, 2, lines, half)
-            left = split[:, 0].reshape(-1, half)
-            right = split[:, 1].reshape(-1, half)
-            low = lax.broadcasted_iota(jnp.int32, left.shape, 1) % (2 * per_tile) < per_tile
-            ones = (
-                jnp.where(low, left, pltpu.roll(right, per_tile, 1)),
-                jnp.where(low, pltpu.roll(left, half - per_tile, 1), right),
-            )
-            for xl, one in enumerate(ones):
-                for d in range(dests // 2):
-                    out_ref[2 * d + xl, at : at + lines] = one[d * lines : (d + 1) * lines, :].astype(jnp.bfloat16)
+def emit(out_ref, start, terms, nxl, per_tile):
+    dests, half = out_ref.shape[0], out_ref.shape[2]
+    lines = terms.shape[1] // dests
+    for c in range(3):
+        turned = terms[c * half : (c + 1) * half, :].T
+        at = pl.multiple_of(start + c * lines, 16)
+        if nxl == 1:
+            for d in range(dests):
+                out_ref[d, pl.ds(at, lines)] = turned[d * lines : (d + 1) * lines, :].astype(jnp.bfloat16)
+            continue
+        split = turned.reshape(dests // 2, 2, lines, half)
+        left = split[:, 0].reshape(-1, half)
+        right = split[:, 1].reshape(-1, half)
+        low = lax.broadcasted_iota(jnp.int32, left.shape, 1) % (2 * per_tile) < per_tile
+        ones = (
+            jnp.where(low, left, pltpu.roll(right, per_tile, 1)),
+            jnp.where(low, pltpu.roll(left, half - per_tile, 1), right),
+        )
+        for xl, one in enumerate(ones):
+            for d in range(dests // 2):
+                out_ref[2 * d + xl, pl.ds(at, lines)] = one[d * lines : (d + 1) * lines, :].astype(jnp.bfloat16)
+
+
+def first_half_kernel(row, nxl, per_tile, flags_ref, x_ref, pre_ref, out_ref, middle_ref):
+    core = flags_ref[0]
+    lanes = pl.ds(pl.multiple_of(core * row, 128), row)
+    rows = pl.ds(pl.multiple_of((1 - core) * row, 16), row)
+    middle_ref[...] = jnp.dot(x_ref[:, lanes], pre_ref[rows, :], preferred_element_type=jnp.float32)
+    emit(out_ref, 0, jnp.dot(x_ref[...], pre_ref[...], preferred_element_type=jnp.float32), nxl, per_tile)
+
+
+def grad_first_kernel(row, nxl, per_tile, flags_ref, x_ref, swapped_ref, done_ref, middle_ref, out_ref):
+    core = flags_ref[0]
+    lanes = pl.ds(pl.multiple_of((1 - core) * row, 128), row)
+    rows = pl.ds(pl.multiple_of(core * row, 16), row)
+    count = done_ref.shape[1]
+    emit(
+        out_ref,
+        count,
+        middle_ref[...] + jnp.dot(x_ref[:, lanes], swapped_ref[rows, :], preferred_element_type=jnp.float32),
+        nxl,
+        per_tile,
+    )
+    terms = jnp.dot(x_ref[...], swapped_ref[...], preferred_element_type=jnp.float32)
+    emit(out_ref, core * 2 * count, terms, nxl, per_tile)
+    at = pl.multiple_of((1 - core) * 2 * count, 16)
+    for d in range(done_ref.shape[0]):
+        out_ref[d, pl.ds(at, count)] = done_ref[d]
 
 
 def kernel(body, out_shape, inputs, smem=0, scratch=(), name=None, flops=0, nbytes=2**20, exps=0, hbm=0, vmem=VMEM):
@@ -404,19 +460,6 @@
     pairs = lambda step: [((t + step if t % 2 else t - step) % ntile, t) for t in range(ntile)]
     near = lax.ppermute(near, TILE, pairs(1))
     far = lax.ppermute(far, TILE, pairs(2))
-    grad_pre = kernel(
-        functools.partial(grad_pre_kernel, local, side),
-        shape((2 * row, channels), bf),
-        (flags, own, part, near, far, second_weight),
-        1,
-        (pltpu.VMEM((4 * row, channels), bf), pltpu.VMEM((2 * row, channels), bf)),
-        "grad_pre",
-        2 * 18 * row * channels**2,
-        4 * 2**20,
-        2 * row * channels,
-    )
-    swapped = swap(grad_pre)
-
     x_turned = kernel(
         functools.partial(turn_kernel, local, side),
         shape((3 * half, 2 * row), bf),
@@ -426,17 +469,50 @@
         "turn",
     )
 
+    pads = tuple(pltpu.VMEM((row, channels), bf) for _ in range(3))
+    hidden, slope = kernel(
+        functools.partial(near_half_kernel, local, side),
+        (shape((2 * row, channels), jnp.float32), shape((row, channels), jnp.float32)),
+        (flags, own, part, second_weight),
+        1,
+        pads,
+        "near_half",
+        2 * 9 * row * channels**2,
+        2 * 2**20,
+        row * channels,
+    )
+    near, far, x_turned, hidden, slope = lax.optimization_barrier((near, far, x_turned, hidden, slope))
+    grad_pre = kernel(
+        functools.partial(grad_pre_kernel, local, side),
+        shape((2 * row, channels), bf),
+        (flags, near, far, hidden, slope, second_weight),
+        1,
+        pads,
+        "grad_pre",
+        2 * 9 * row * channels**2,
+        4 * 2**20,
+        row * channels,
+    )
+    swapped = swap(grad_pre)
+
     rows4 = (pltpu.VMEM((4 * row, channels), bf),)
     width = channels // nface
     lines = width // nxl
+    done, middle = kernel(
+        functools.partial(first_half_kernel, row, nxl, per_tile),
+        (shape((nface * nxl, 3 * lines, half), bf), shape((3 * half, channels), jnp.float32)),
+        (flags, x_turned, grad_pre),
+        1,
+        name="first_half",
+    )
+    swapped, done, middle = lax.optimization_barrier((swapped, done, middle))
     parts = kernel(
         functools.partial(grad_first_kernel, row, nxl, per_tile),
         shape((nface * nxl, 9 * lines, half), bf),
-        (flags, x_turned, grad_pre, swapped),
-        1,
-        rows4,
-        "grad_first",
-        2 * 18 * half * row * channels,
+        (flags, x_turned, swapped, done, middle),
+        1,
+        name="grad_first",
+        flops=2 * 9 * half * row * channels,
     )
     grad_input = kernel(
         functools.partial(grad_input_kernel, local, side),

time: 97.2 us -> 96.4 us (level)
  waiting for transfers between devices: 21.7 us -> 19.1 us
  Pallas kernels: 13.2 us -> 15.1 us
    ppermute x1, waiting for transfers between devices: 7.13 us -> 4.93 us  [on_device(): far = lax.ppermute(far, TILE, pairs(2))]
    pallas_call x10 -> x12, Pallas kernels: 13.2 us -> 15.1 us  [kernel(): pl.pallas_call(body, out_shape=out_shape, in_specs=[pl.BlockSpec(memory_s...]
  transfers between devices with their start and end apart: 6 -> 6, of which waited for: 5 -> 5; matrix products, arithmetic and copies ran while one was open for 0% -> 0% of each run, Pallas kernels for 4% -> 7%
where the time goes in v8:
time: 96.4 us; the launch traced here: 95.2 us
  blocking collectives  33 us (34%)
  starting transfers between devices  26.9 us (28%)
  waiting for transfers between devices  19.1 us (20%)
  Pallas kernels  15.1 us (16%)
    all_to_all x1, blocking collectives, on_device(): got = lax.all_to_all(parts, FACE + ('xl',), 0, 0, tiled=True)  18.1 us
    pallas_call x12, Pallas kernels, kernel(): pl.pallas_call(body, out_shape=out_shape, in_specs=[pl.BlockSpec(memory_s...  15.1 us
    all_to_all x1, blocking collectives, on_device(): table = lax.all_to_all(sent, FACE, 0, 0, tiled=True)  14.9 us
    all_to_all x1, waiting for transfers between devices, on_device(): got = lax.all_to_all(total, 'z', 0, 0, tiled=True)  10.9 us
    ppermute x1, starting transfers between devices, on_device(): near = lax.ppermute(near, TILE, pairs(1))  10.1 us
    all_to_all x1, starting transfers between devices, on_device(): wrapped = lax.all_to_all(picked, FACE, 0, 0, tiled=True)  6.18 us
    ppermute x1, waiting for transfers between devices, on_device(): far = lax.ppermute(far, TILE, pairs(2))  4.93 us
    all_to_all x1, starting transfers between devices, on_device(): got = lax.all_to_all(total, 'z', 0, 0, tiled=True)  4.9 us
  transfers between devices with their start and end apart: 6, of which 5 were waited for; matrix products, arithmetic and copies ran while one was open for 0% of the time, Pallas kernels for 7%

profile of v8, /device:TPU:6, one launch (start us, length us, event | category | flops | bytes accessed | tf_op | source)
XLA Modules:
  0.0 95.2 jit_solution(1230594366574118827)
XLA Ops:
  0.7 2.6 %pack.1 = bf16[8,96,256]{2,1,0:T(8,128)(2,1)} custom-call(s32[4,4]{1,0:T(4,128)} %seams_ref.3, bf16[4,64,256]{2,1,0:T(8,128)(2,1)} %bitcast.16, bf16[4,64,256]{2,1,0:T(8,128)(2,1)} %bitcast.19), custom_call_target="tpu_custom_call" | custom-call | bytes 1048576 | tf_op jit(solution)/shard_map/pack/pallas_call | solution.py:374
  3.3 0.0 copy-start.1
  3.3 0.0 copy-start.3
  3.3 0.0 copy-start.4
  3.3 0.0 copy-start.5
  3.3 0.0 copy-start.6
  3.3 0.1 pad_add_fusion.flags_ref
  3.4 14.9 %all_to_all.20.table_ref = bf16[8,96,256]{2,1,0:T(8,128)(2,1)S(1)} all-to-all(bf16[8,96,256]{2,1,0:T(8,128)(2,1)} %pack.1), channel_id=1, replica_groups=mesh['xh'=2,'y'=4,'xl'=2,'z'=16,'c'=2] {'xh','y'}, dimensions={0} | all-to-all | bytes 786432 | tf_op jit(solution)/shard_map/all_to_all | solution.py:422
  18.3 0.1 copy.11
  18.4 1.4 %pick.1 = bf16[8,64,256]{2,1,0:T(8,128)(2,1)} custom-call(s32[32]{0:T(128)S(1)} %fusion.want_ref, bf16[8,96,256]{2,1,0:T(8,128)(2,1)S(1)} %all_to_all.20.table_ref), custom_call_target="tpu_custom_call" | custom-call | bytes 1048576 | tf_op jit(solution)/shard_map/pick/pallas_call | solution.py:374
  19.8 6.2 %all-to-all-start.1 = ((bf16[8,64,256]{2,1,0:T(8,128)(2,1)}), bf16[8,64,256]{2,1,0:T(8,128)(2,1)S(1)}, u32[]{:S(2)}, u32[]{:S(2)}) async-start(bf16[8,64,256]{2,1,0:T(8,128)(2,1)} %pick.1), calls=%async_computation.1 | async-start | bytes 524288 | tf_op jit(solution)/shard_map/all_to_all | solution.py:435
  26.0 0.0 copy-start.2
  26.0 0.0 copy-done.1
  26.0 0.0 copy-done.3
  26.0 0.0 copy-done.4
  26.0 0.0 copy-done.5
  26.1 0.0 copy-done.6
  26.1 1.1 %border.1 = (bf16[544,256]{1,0:T(8,128)(2,1)S(1)}, bf16[32,256]{1,0:T(8,128)(2,1)S(1)}, bf16[400,256]{1,0:T(8,128)(2,1)S(1)}, bf16[256,128]{1,0:T(8,128)(2,1)S(1)}) custom-call(s32[4]{0:T(128)S(1)} %pad_add_fusion.flags_ref, s32[4,4]{1,0:T(4,128)S(1)} %copy-done.5, s32[4,4]{1,0:T(4,128)S(1)} %copy-done.6, bf16[8,96,256]{2,1,0:T(8,128)(2,1)S(1)} %all_to_all.20.table_ref, ...), custom_call_target="tpu_custom_call" | custom-call | bytes 1048576 | tf_op jit(solution)/shard_map/border/pallas_call | solution.py:374
  27.2 1.9 %collective-permute-start = (bf16[400,256]{1,0:T(8,128)(2,1)S(1)}, bf16[400,256]{1,0:T(8,128)(2,1)S(1)}, u32[]{:S(2)}, u32[]{:S(2)}) collective-permute-start(bf16[400,256]{1,0:T(8,128)(2,1)S(1)} %get-tuple-element.34), channel_id=1, source_target_pairs={{0,1},{1,0},{2,3},{3,2},{4,5},{5,4},{6,7},{7,6},{8,9},{9,8},{10,11... | collective-permute-start | bytes 614408 | tf_op jit(solution)/shard_map/ppermute | solution.py:420
  29.1 1.4 %collective-permute-done.part_ref = bf16[400,256]{1,0:T(8,128)(2,1)S(1)} collective-permute-done((bf16[400,256]{1,0:T(8,128)(2,1)S(1)}, bf16[400,256]{1,0:T(8,128)(2,1)S(1)}, u32[]{:S(2)}, u32[]{:S(2)}) %collective-permute-start) | collective-permute-done | bytes 204832 | tf_op jit(solution)/shard_map/ppermute | solution.py:420
  30.5 1.3 %all-to-all-done.1.pieces_ref = bf16[8,64,256]{2,1,0:T(8,128)(2,1)S(1)} async-done(((bf16[8,64,256]{2,1,0:T(8,128)(2,1)}), bf16[8,64,256]{2,1,0:T(8,128)(2,1)S(1)}, u32[]{:S(2)}, u32[]{:S(2)}) %all-to-all-start.1) | async-done | bytes 262176 | tf_op jit(solution)/shard_map/all_to_all | solution.py:435
  31.9 0.6 send.1
  32.5 10.1 %collective-permute-start.1 = (bf16[544,256]{1,0:T(8,128)(2,1)S(1)}, bf16[544,256]{1,0:T(8,128)(2,1)S(1)}, u32[]{:S(2)}, u32[]{:S(2)}) collective-permute-start(bf16[544,256]{1,0:T(8,128)(2,1)S(1)} %get-tuple-element.36), channel_id=1, source_target_pairs={{63,0},{2,1},{1,2},{4,3},{3,4},{6,5},{5,6},{8,7},{7,8},{10,9},{9,1... | collective-permute-start | bytes 835592 | tf_op jit(solution)/shard_map/ppermute | solution.py:461
  42.5 1.9 %collective-permute-start.2 = (bf16[272,256]{1,0:T(8,128)(2,1)S(1)}, bf16[272,256]{1,0:T(8,128)(2,1)S(1)}, u32[]{:S(2)}, u32[]{:S(2)}) collective-permute-start(bf16[272,256]{1,0:T(8,128)(2,1)S(1)} %get-tuple-element.37), channel_id=1, source_target_pairs={{62,0},{3,1},{0,2},{5,3},{2,4},{7,5},{4,6},{9,7},{6,8},{11,9},{8,1... | collective-permute-start | bytes 417800 | tf_op jit(solution)/shard_map/ppermute | solution.py:462
  44.5 0.8 turn.1.x_ref
  45.3 0.0 copy-done.2
  45.3 1.4 %near_half.1 = (f32[768,256]{1,0:T(8,128)S(1)}, f32[384,256]{1,0:T(8,128)S(1)}) custom-call(s32[4]{0:T(128)S(1)} %pad_add_fusion.flags_ref, bf16[544,256]{1,0:T(8,128)(2,1)S(1)} %get-tuple-element.31.own_ref, bf16[400,256]{1,0:T(8,128)(2,1)S(1)} %collective-permute-done.part_ref, bf16[3,3,256,256]{3,2,1,0:T(8,128)(2,1)S(1)} %copy-done.2), custom_call_target="tpu_custom_call" | custom-call | flops 452984832 | bytes 2097152 | tf_op jit(solution)/shard_map/near_half/pallas_call | solution.py:374
  46.7 4.9 %collective-permute-done.2.far_ref = bf16[272,256]{1,0:T(8,128)(2,1)S(1)} collective-permute-done((bf16[272,256]{1,0:T(8,128)(2,1)S(1)}, bf16[272,256]{1,0:T(8,128)(2,1)S(1)}, u32[]{:S(2)}, u32[]{:S(2)}) %collective-permute-start.2) | collective-permute-done | bytes 139296 | tf_op jit(solution)/shard_map/ppermute | solution.py:462
  51.6 0.0 collective-permute-done.1.near_ref
  51.6 1.4 %grad_pre.1.pre_ref = bf16[768,256]{1,0:T(8,128)(2,1)S(1)} custom-call(s32[4]{0:T(128)S(1)} %pad_add_fusion.flags_ref, bf16[544,256]{1,0:T(8,128)(2,1)S(1)} %collective-permute-done.1.near_ref, bf16[272,256]{1,0:T(8,128)(2,1)S(1)} %collective-permute-done.2.far_ref, f32[768,256]{1,0:T(8,128)S(1)} %get-tuple-element.44.hidden_ref, ...), custom_call_target="tpu_custom_call" | custom-call | flops 452984832 | bytes 4194304 | tf_op jit(solution)/shard_map/grad_pre/pallas_call | solution.py:374
  53.0 1.9 %collective-permute-start.3 = (bf16[768,256]{1,0:T(8,128)(2,1)S(1)}, bf16[768,256]{1,0:T(8,128)(2,1)S(1)}, u32[]{:S(2)}, u32[]{:S(2)}) collective-permute-start(bf16[768,256]{1,0:T(8,128)(2,1)S(1)} %grad_pre.1.pre_ref), channel_id=1, source_target_pairs={{0,1},{1,0},{2,3},{3,2},{4,5},{5,4},{6,7},{7,6},{8,9},{9,8},{10,11... | collective-permute-start | bytes 1179656 | tf_op jit(solution)/shard_map/ppermute | solution.py:420
  54.9 1.2 %first_half.1 = (bf16[16,48,128]{2,1,0:T(8,128)(2,1)S(1)}, f32[384,256]{1,0:T(8,128)S(1)}) custom-call(s32[4]{0:T(128)S(1)} %pad_add_fusion.flags_ref, bf16[384,768]{1,0:T(8,128)(2,1)S(1)} %turn.1.x_ref, bf16[768,256]{1,0:T(8,128)(2,1)S(1)} %grad_pre.1.pre_ref), custom_call_target="tpu_custom_call" | custom-call | bytes 1048576 | tf_op jit(solution)/shard_map/first_half/pallas_call | solution.py:374
  56.2 0.5 collective-permute-done.3.swapped_ref
  56.6 1.2 %grad_first.1 = bf16[16,144,128]{2,1,0:T(8,128)(2,1)S(1)} custom-call(s32[4]{0:T(128)S(1)} %pad_add_fusion.flags_ref, bf16[384,768]{1,0:T(8,128)(2,1)S(1)} %turn.1.x_ref, bf16[768,256]{1,0:T(8,128)(2,1)S(1)} %collective-permute-done.3.swapped_ref, bf16[16,48,128]{2,1,0:T(8,128)(2,1)S(1)} %get-tuple-element.50.done_ref, ...), custom_call_target="tpu_custom_call" | custom-call | flops 226492416 | bytes 1048576 | tf_op jit(solution)/shard_map/grad_first/pallas_call | solution.py:374
  57.9 0.0 copy-start
  57.9 18.1 %all_to_all.21.got_ref = bf16[16,144,128]{2,1,0:T(8,128)(2,1)S(1)} all-to-all(bf16[16,144,128]{2,1,0:T(8,128)(2,1)S(1)} %grad_first.1), channel_id=1, replica_groups=mesh['xh'=2,'y'=4,'xl'=2,'z'=16,'c'=2] {'xh','y','xl'}, dimensions={0} | all-to-all | bytes 1179648 | tf_op jit(solution)/shard_map/all_to_all | solution.py:528
  76.0 0.8 first_sum.1
  76.8 4.9 %all-to-all-start.3 = ((bf16[16,8,144]{2,1,0:T(8,128)(2,1)}), bf16[16,8,144]{2,1,0:T(8,128)(2,1)S(1)}, u32[]{:S(2)}, u32[]{:S(2)}) async-start(bf16[16,8,144]{2,1,0:T(8,128)(2,1)} %first_sum.1), calls=%async_computation.3 | async-start | bytes 131072 | tf_op jit(solution)/shard_map/all_to_all | solution.py:535
  81.7 0.0 copy-done
  81.7 1.9 %grad_input.1 = bf16[4,64,256]{2,1,0:T(8,128)(2,1)} custom-call(s32[4]{0:T(128)S(1)} %pad_add_fusion.flags_ref, bf16[768,256]{1,0:T(8,128)(2,1)S(1)} %grad_pre.1.pre_ref, bf16[768,256]{1,0:T(8,128)(2,1)S(1)} %collective-permute-done.3.swapped_ref, bf16[4,64,256]{2,1,0:T(8,128)(2,1)S(1)} %bitcast.18, bf16[3,3,256,256]{3,2,1,0:T(8,128)(2,1)S(1)} %copy-done), custom_call_target="tpu_custom_call" | custom-call | flops 452984832 | bytes 2097152 | tf_op jit(solution)/shard_map/grad_input/pallas_call | solution.py:374
  83.6 10.9 %all-to-all-done.3.got_ref = bf16[16,8,144]{2,1,0:T(8,128)(2,1)S(1)} async-done(((bf16[16,8,144]{2,1,0:T(8,128)(2,1)}), bf16[16,8,144]{2,1,0:T(8,128)(2,1)S(1)}, u32[]{:S(2)}, u32[]{:S(2)}) %all-to-all-start.3) | async-done | bytes 36896 | tf_op jit(solution)/shard_map/all_to_all | solution.py:535
  94.5 0.7 second_sum.1
  (4 shorter events, 0.0 us)
Async XLA Ops:
  3.3 22.8 %copy-start.1 = (bf16[1,4,1,64,256]{4,3,2,1,0:T(8,128)(2,1)S(1)}, bf16[1,4,1,64,256]{4,3,2,1,0:T(8,128)(2,1)}, u32[]{:S(2)}) copy-start(bf16[1,4,1,64,256]{4,3,2,1,0:T(8,128)(2,1)} %param.9) | copy-start | bytes 393220
  3.3 22.8 %copy-start.3 = (bf16[1,4,1,64,256]{4,3,2,1,0:T(8,128)(2,1)S(1)}, bf16[1,4,1,64,256]{4,3,2,1,0:T(8,128)(2,1)}, u32[]{:S(2)}) copy-start(bf16[1,4,1,64,256]{4,3,2,1,0:T(8,128)(2,1)} %param.8) | copy-start | bytes 393220
  3.3 22.8 %copy-start.4 = (bf16[1,4,1,64,256]{4,3,2,1,0:T(8,128)(2,1)S(1)}, bf16[1,4,1,64,256]{4,3,2,1,0:T(8,128)(2,1)}, u32[]{:S(2)}) copy-start(bf16[1,4,1,64,256]{4,3,2,1,0:T(8,128)(2,1)} %param.7) | copy-start | bytes 393220
  3.3 22.8 %copy-start.5 = (s32[4,4]{1,0:T(4,128)S(1)}, s32[4,4]{1,0:T(4,128)}, u32[]{:S(2)}) copy-start(s32[4,4]{1,0:T(4,128)} %seams_ref.3) | copy-start | bytes 196
  3.3 22.8 %copy-start.6 = (s32[4,4]{1,0:T(4,128)S(1)}, s32[4,4]{1,0:T(4,128)}, u32[]{:S(2)}) copy-start(s32[4,4]{1,0:T(4,128)} %corners_ref.1) | copy-start | bytes 196
  19.8 12.0 %all-to-all-start.1 = ((bf16[8,64,256]{2,1,0:T(8,128)(2,1)}), bf16[8,64,256]{2,1,0:T(8,128)(2,1)S(1)}, u32[]{:S(2)}, u32[]{:S(2)}) async-start(bf16[8,64,256]{2,1,0:T(8,128)(2,1)} %pick.1), calls=%async_computation.1 | async-start | bytes 524288 | tf_op jit(solution)/shard_map/all_to_all | solution.py:435
  26.0 19.3 %copy-start.2 = (bf16[3,3,256,256]{3,2,1,0:T(8,128)(2,1)S(1)}, bf16[3,3,256,256]{3,2,1,0:T(8,128)(2,1)}, u32[]{:S(2)}) copy-start(bf16[3,3,256,256]{3,2,1,0:T(8,128)(2,1)} %weight_ref.4) | copy-start | bytes 3538948
  27.2 3.3 %collective-permute-start = (bf16[400,256]{1,0:T(8,128)(2,1)S(1)}, bf16[400,256]{1,0:T(8,128)(2,1)S(1)}, u32[]{:S(2)}, u32[]{:S(2)}) collective-permute-start(bf16[400,256]{1,0:T(8,128)(2,1)S(1)} %get-tuple-element.34), channel_id=1, source_target_pairs={{0,1},{1,0},{2,3},{3,2},{4,5},{5,4},{6,7},{7,6},{8,9},{9,8},{10,11... | collective-permute-start | bytes 614408 | tf_op jit(solution)/shard_map/ppermute | solution.py:420
  32.5 19.2 %collective-permute-start.1 = (bf16[544,256]{1,0:T(8,128)(2,1)S(1)}, bf16[544,256]{1,0:T(8,128)(2,1)S(1)}, u32[]{:S(2)}, u32[]{:S(2)}) collective-permute-start(bf16[544,256]{1,0:T(8,128)(2,1)S(1)} %get-tuple-element.36), channel_id=1, source_target_pairs={{63,0},{2,1},{1,2},{4,3},{3,4},{6,5},{5,6},{8,7},{7,8},{10,9},{9,1... | collective-permute-start | bytes 835592 | tf_op jit(solution)/shard_map/ppermute | solution.py:461
  42.5 9.1 %collective-permute-start.2 = (bf16[272,256]{1,0:T(8,128)(2,1)S(1)}, bf16[272,256]{1,0:T(8,128)(2,1)S(1)}, u32[]{:S(2)}, u32[]{:S(2)}) collective-permute-start(bf16[272,256]{1,0:T(8,128)(2,1)S(1)} %get-tuple-element.37), channel_id=1, source_target_pairs={{62,0},{3,1},{0,2},{5,3},{2,4},{7,5},{4,6},{9,7},{6,8},{11,9},{8,1... | collective-permute-start | bytes 417800 | tf_op jit(solution)/shard_map/ppermute | solution.py:462
  53.0 3.6 %collective-permute-start.3 = (bf16[768,256]{1,0:T(8,128)(2,1)S(1)}, bf16[768,256]{1,0:T(8,128)(2,1)S(1)}, u32[]{:S(2)}, u32[]{:S(2)}) collective-permute-start(bf16[768,256]{1,0:T(8,128)(2,1)S(1)} %grad_pre.1.pre_ref), channel_id=1, source_target_pairs={{0,1},{1,0},{2,3},{3,2},{4,5},{5,4},{6,7},{7,6},{8,9},{9,8},{10,11... | collective-permute-start | bytes 1179656 | tf_op jit(solution)/shard_map/ppermute | solution.py:420
  57.9 23.8 %copy-start = (bf16[3,3,256,256]{3,2,1,0:T(8,128)(2,1)S(1)}, bf16[3,3,256,256]{3,2,1,0:T(8,128)(2,1)}, u32[]{:S(2)}) copy-start(bf16[3,3,256,256]{3,2,1,0:T(8,128)(2,1)} %weight_ref.5) | copy-start | bytes 3538948
  76.8 17.7 %all-to-all-start.3 = ((bf16[16,8,144]{2,1,0:T(8,128)(2,1)}), bf16[16,8,144]{2,1,0:T(8,128)(2,1)S(1)}, u32[]{:S(2)}, u32[]{:S(2)}) async-start(bf16[16,8,144]{2,1,0:T(8,128)(2,1)} %first_sum.1), calls=%async_computation.3 | async-start | bytes 131072 | tf_op jit(solution)/shard_map/all_to_all | solution.py:535

commit v9 on v8

--- a/solution.py
+++ b/solution.py
@@ -23,7 +23,11 @@
     return [pl.BlockSpec(memory_space=pltpu.VMEM)] * n
 
 
-def pack_kernel(local, side, blocks, seams_ref, g_hbm, p_hbm, out_ref, g_ref, p_ref, sems):
+def leave(built, out_hbm, sems, b):
+    return pltpu.make_async_copy(built.at[b], out_hbm.at[b], sems.at[b])
+
+
+def pack_kernel(local, side, blocks, seams_ref, g_hbm, p_hbm, out_hbm, g_ref, p_ref, out_ref, sems, out_sems):
     fetches = [
         pltpu.make_async_copy(g_hbm, g_ref, sems.at[0]),
         pltpu.make_async_copy(p_hbm, p_ref, sems.at[1]),
@@ -66,14 +70,21 @@
                 else:
                     out_ref[b, at : at + px, which * ch : (which + 1) * ch] = piece
         out_ref[b, local * count :] = cells
-
-
-def pick_kernel(faces, local, count, want_ref, table_ref, out_ref):
+        leave(out_ref, out_hbm, out_sems, b).start()
+    for b in range(px_blocks * ch_blocks):
+        leave(out_ref, out_hbm, out_sems, b).wait()
+
+
+def pick_kernel(faces, local, count, want_ref, table_ref, out_hbm, out_ref, sems):
     for i in range(faces):
         face = want_ref[i]
         at = pl.multiple_of(lax.rem(face, local) * count, 16)
         into, row = divmod(i, local)
         out_ref[into, row * count : (row + 1) * count] = table_ref[lax.div(face, local), pl.ds(at, count)]
+        if row == local - 1:
+            leave(out_ref, out_hbm, sems, into).start()
+    for b in range(faces // local):
+        leave(out_ref, out_hbm, sems, b).wait()
 
 
 def first_sum_kernel(scale, got_ref, out_ref):
@@ -368,14 +379,14 @@
         out_ref[d, pl.ds(at, count)] = done_ref[d]
 
 
-def kernel(body, out_shape, inputs, smem=0, scratch=(), name=None, flops=0, nbytes=2**20, exps=0, hbm=0, vmem=VMEM):
+def kernel(body, out_shape, inputs, smem=0, scratch=(), name=None, flops=0, nbytes=2**20, exps=0, hbm=0, vmem=VMEM, out_hbm=False):
     many = isinstance(out_shape, tuple)
     spots = [pl.BlockSpec(memory_space=pltpu.HBM)] * hbm + whole(len(inputs) - smem - hbm)
     return pl.pallas_call(
         body,
         out_shape=out_shape,
         in_specs=[pl.BlockSpec(memory_space=pltpu.SMEM)] * smem + spots,
-        out_specs=tuple(whole(len(out_shape))) if many else whole(1)[0],
+        out_specs=tuple(whole(len(out_shape))) if many else pl.BlockSpec(memory_space=pltpu.HBM) if out_hbm else whole(1)[0],
         scratch_shapes=scratch,
         compiler_params=pltpu.CompilerParams(vmem_limit_bytes=vmem),
         cost_estimate=pl.CostEstimate(flops=flops, bytes_accessed=nbytes, transcendentals=exps),
@@ -411,11 +422,14 @@
         (
             pltpu.VMEM((local, side, channels), bf),
             pltpu.VMEM((local, side, channels), bf),
+            pltpu.VMEM((nface, local * (count + CELLS), channels), bf),
             pltpu.SemaphoreType.DMA((2,)),
+            pltpu.SemaphoreType.DMA((nface,)),
         ),
         "pack",
         hbm=2,
         vmem=None,
+        out_hbm=True,
     )
     swap = lambda a: lax.ppermute(a, "c", [(0, 1), (1, 0)])
     sent, flags, top = lax.optimization_barrier((sent, flags, top))
@@ -429,7 +443,9 @@
         shape((nface, local * count, channels), bf),
         (want, table),
         1,
-        name="pick",
+        (pltpu.VMEM((nface, local * count, channels), bf), pltpu.SemaphoreType.DMA((nface,))),
+        "pick",
+        out_hbm=True,
     )
     picked, table = lax.optimization_barrier((picked, table))
     wrapped = lax.all_to_all(picked, FACE, 0, 0, tiled=True)

time: 96.4 us -> 96.5 us (level)
  no operation moved by 1% of the time
where the time goes in v9:
time: 96.5 us; the launch traced here: 95.2 us
  blocking collectives  33 us (34%)
  starting transfers between devices  26.9 us (28%)
  waiting for transfers between devices  19.1 us (20%)
  Pallas kernels  15.1 us (16%)
    all_to_all x1, blocking collectives, on_device(): got = lax.all_to_all(parts, FACE + ('xl',), 0, 0, tiled=True)  18.1 us
    pallas_call x12, Pallas kernels, kernel(): pl.pallas_call(body, out_shape=out_shape, in_specs=[pl.BlockSpec(memory_s...  15.1 us
    all_to_all x1, blocking collectives, on_device(): table = lax.all_to_all(sent, FACE, 0, 0, tiled=True)  14.9 us
    all_to_all x1, waiting for transfers between devices, on_device(): got = lax.all_to_all(total, 'z', 0, 0, tiled=True)  10.9 us
    ppermute x1, starting transfers between devices, on_device(): near = lax.ppermute(near, TILE, pairs(1))  10.1 us
    all_to_all x1, starting transfers between devices, on_device(): wrapped = lax.all_to_all(picked, FACE, 0, 0, tiled=True)  6.19 us
    ppermute x1, waiting for transfers between devices, on_device(): far = lax.ppermute(far, TILE, pairs(2))  4.93 us
    all_to_all x1, starting transfers between devices, on_device(): got = lax.all_to_all(total, 'z', 0, 0, tiled=True)  4.9 us
  transfers between devices with their start and end apart: 6, of which 5 were waited for; matrix products, arithmetic and copies ran while one was open for 0% of the time, Pallas kernels for 7%

profile of v9, /device:TPU:6, one launch (start us, length us, event | category | flops | bytes accessed | tf_op | source)
XLA Modules:
  0.0 95.2 jit_solution(10164941929357999706)
XLA Ops:
  0.7 2.7 %pack.1 = bf16[8,96,256]{2,1,0:T(8,128)(2,1)} custom-call(s32[4,4]{1,0:T(4,128)} %seams_ref.3, bf16[4,64,256]{2,1,0:T(8,128)(2,1)} %bitcast.16, bf16[4,64,256]{2,1,0:T(8,128)(2,1)} %bitcast.19), custom_call_target="tpu_custom_call" | custom-call | bytes 1048576 | tf_op jit(solution)/shard_map/pack/pallas_call | solution.py:385
  3.3 0.0 copy-start.1
  3.3 0.0 copy-start.3
  3.3 0.0 copy-start.4
  3.4 0.0 copy-start.5
  3.4 0.0 copy-start.6
  3.4 0.1 pad_add_fusion.flags_ref
  3.5 14.9 %all_to_all.20.table_ref = bf16[8,96,256]{2,1,0:T(8,128)(2,1)S(1)} all-to-all(bf16[8,96,256]{2,1,0:T(8,128)(2,1)} %pack.1), channel_id=1, replica_groups=mesh['xh'=2,'y'=4,'xl'=2,'z'=16,'c'=2] {'xh','y'}, dimensions={0} | all-to-all | bytes 786432 | tf_op jit(solution)/shard_map/all_to_all | solution.py:436
  18.4 0.1 copy.11
  18.5 1.4 %pick.1 = bf16[8,64,256]{2,1,0:T(8,128)(2,1)} custom-call(s32[32]{0:T(128)S(1)} %fusion.want_ref, bf16[8,96,256]{2,1,0:T(8,128)(2,1)S(1)} %all_to_all.20.table_ref), custom_call_target="tpu_custom_call" | custom-call | bytes 1048576 | tf_op jit(solution)/shard_map/pick/pallas_call | solution.py:385
  19.9 6.2 %all-to-all-start.1 = ((bf16[8,64,256]{2,1,0:T(8,128)(2,1)}), bf16[8,64,256]{2,1,0:T(8,128)(2,1)S(1)}, u32[]{:S(2)}, u32[]{:S(2)}) async-start(bf16[8,64,256]{2,1,0:T(8,128)(2,1)} %pick.1), calls=%async_computation.1 | async-start | bytes 524288 | tf_op jit(solution)/shard_map/all_to_all | solution.py:451
  26.1 0.0 copy-start.2
  26.1 0.0 copy-done.1
  26.1 0.0 copy-done.3
  26.1 0.0 copy-done.4
  26.1 0.0 copy-done.5
  26.1 0.0 copy-done.6
  26.1 1.1 %border.1 = (bf16[544,256]{1,0:T(8,128)(2,1)S(1)}, bf16[32,256]{1,0:T(8,128)(2,1)S(1)}, bf16[400,256]{1,0:T(8,128)(2,1)S(1)}, bf16[256,128]{1,0:T(8,128)(2,1)S(1)}) custom-call(s32[4]{0:T(128)S(1)} %pad_add_fusion.flags_ref, s32[4,4]{1,0:T(4,128)S(1)} %copy-done.5, s32[4,4]{1,0:T(4,128)S(1)} %copy-done.6, bf16[8,96,256]{2,1,0:T(8,128)(2,1)S(1)} %all_to_all.20.table_ref, ...), custom_call_target="tpu_custom_call" | custom-call | bytes 1048576 | tf_op jit(solution)/shard_map/border/pallas_call | solution.py:385
  27.3 1.9 %collective-permute-start = (bf16[400,256]{1,0:T(8,128)(2,1)S(1)}, bf16[400,256]{1,0:T(8,128)(2,1)S(1)}, u32[]{:S(2)}, u32[]{:S(2)}) collective-permute-start(bf16[400,256]{1,0:T(8,128)(2,1)S(1)} %get-tuple-element.34), channel_id=1, source_target_pairs={{0,1},{1,0},{2,3},{3,2},{4,5},{5,4},{6,7},{7,6},{8,9},{9,8},{10,11... | collective-permute-start | bytes 614408 | tf_op jit(solution)/shard_map/ppermute | solution.py:434
  29.2 1.4 %collective-permute-done.part_ref = bf16[400,256]{1,0:T(8,128)(2,1)S(1)} collective-permute-done((bf16[400,256]{1,0:T(8,128)(2,1)S(1)}, bf16[400,256]{1,0:T(8,128)(2,1)S(1)}, u32[]{:S(2)}, u32[]{:S(2)}) %collective-permute-start) | collective-permute-done | bytes 204832 | tf_op jit(solution)/shard_map/ppermute | solution.py:434
  30.6 1.3 %all-to-all-done.1.pieces_ref = bf16[8,64,256]{2,1,0:T(8,128)(2,1)S(1)} async-done(((bf16[8,64,256]{2,1,0:T(8,128)(2,1)}), bf16[8,64,256]{2,1,0:T(8,128)(2,1)S(1)}, u32[]{:S(2)}, u32[]{:S(2)}) %all-to-all-start.1) | async-done | bytes 262176 | tf_op jit(solution)/shard_map/all_to_all | solution.py:451
  31.9 0.6 send.1
  32.5 10.1 %collective-permute-start.1 = (bf16[544,256]{1,0:T(8,128)(2,1)S(1)}, bf16[544,256]{1,0:T(8,128)(2,1)S(1)}, u32[]{:S(2)}, u32[]{:S(2)}) collective-permute-start(bf16[544,256]{1,0:T(8,128)(2,1)S(1)} %get-tuple-element.36), channel_id=1, source_target_pairs={{63,0},{2,1},{1,2},{4,3},{3,4},{6,5},{5,6},{8,7},{7,8},{10,9},{9,1... | collective-permute-start | bytes 835592 | tf_op jit(solution)/shard_map/ppermute | solution.py:477
  42.6 1.9 %collective-permute-start.2 = (bf16[272,256]{1,0:T(8,128)(2,1)S(1)}, bf16[272,256]{1,0:T(8,128)(2,1)S(1)}, u32[]{:S(2)}, u32[]{:S(2)}) collective-permute-start(bf16[272,256]{1,0:T(8,128)(2,1)S(1)} %get-tuple-element.37), channel_id=1, source_target_pairs={{62,0},{3,1},{0,2},{5,3},{2,4},{7,5},{4,6},{9,7},{6,8},{11,9},{8,1... | collective-permute-start | bytes 417800 | tf_op jit(solution)/shard_map/ppermute | solution.py:478
  44.5 0.8 turn.1.x_ref
  45.4 0.0 copy-done.2
  45.4 1.4 %near_half.1 = (f32[768,256]{1,0:T(8,128)S(1)}, f32[384,256]{1,0:T(8,128)S(1)}) custom-call(s32[4]{0:T(128)S(1)} %pad_add_fusion.flags_ref, bf16[544,256]{1,0:T(8,128)(2,1)S(1)} %get-tuple-element.31.own_ref, bf16[400,256]{1,0:T(8,128)(2,1)S(1)} %collective-permute-done.part_ref, bf16[3,3,256,256]{3,2,1,0:T(8,128)(2,1)S(1)} %copy-done.2), custom_call_target="tpu_custom_call" | custom-call | flops 452984832 | bytes 2097152 | tf_op jit(solution)/shard_map/near_half/pallas_call | solution.py:385
  46.7 4.9 %collective-permute-done.2.far_ref = bf16[272,256]{1,0:T(8,128)(2,1)S(1)} collective-permute-done((bf16[272,256]{1,0:T(8,128)(2,1)S(1)}, bf16[272,256]{1,0:T(8,128)(2,1)S(1)}, u32[]{:S(2)}, u32[]{:S(2)}) %collective-permute-start.2) | collective-permute-done | bytes 139296 | tf_op jit(solution)/shard_map/ppermute | solution.py:478
  51.7 0.0 collective-permute-done.1.near_ref
  51.7 1.4 %grad_pre.1.pre_ref = bf16[768,256]{1,0:T(8,128)(2,1)S(1)} custom-call(s32[4]{0:T(128)S(1)} %pad_add_fusion.flags_ref, bf16[544,256]{1,0:T(8,128)(2,1)S(1)} %collective-permute-done.1.near_ref, bf16[272,256]{1,0:T(8,128)(2,1)S(1)} %collective-permute-done.2.far_ref, f32[768,256]{1,0:T(8,128)S(1)} %get-tuple-element.44.hidden_ref, ...), custom_call_target="tpu_custom_call" | custom-call | flops 452984832 | bytes 4194304 | tf_op jit(solution)/shard_map/grad_pre/pallas_call | solution.py:385
  53.1 1.9 %collective-permute-start.3 = (bf16[768,256]{1,0:T(8,128)(2,1)S(1)}, bf16[768,256]{1,0:T(8,128)(2,1)S(1)}, u32[]{:S(2)}, u32[]{:S(2)}) collective-permute-start(bf16[768,256]{1,0:T(8,128)(2,1)S(1)} %grad_pre.1.pre_ref), channel_id=1, source_target_pairs={{0,1},{1,0},{2,3},{3,2},{4,5},{5,4},{6,7},{7,6},{8,9},{9,8},{10,11... | collective-permute-start | bytes 1179656 | tf_op jit(solution)/shard_map/ppermute | solution.py:434
  55.0 1.2 %first_half.1 = (bf16[16,48,128]{2,1,0:T(8,128)(2,1)S(1)}, f32[384,256]{1,0:T(8,128)S(1)}) custom-call(s32[4]{0:T(128)S(1)} %pad_add_fusion.flags_ref, bf16[384,768]{1,0:T(8,128)(2,1)S(1)} %turn.1.x_ref, bf16[768,256]{1,0:T(8,128)(2,1)S(1)} %grad_pre.1.pre_ref), custom_call_target="tpu_custom_call" | custom-call | bytes 1048576 | tf_op jit(solution)/shard_map/first_half/pallas_call | solution.py:385
  56.2 0.5 collective-permute-done.3.swapped_ref
  56.7 1.2 %grad_first.1 = bf16[16,144,128]{2,1,0:T(8,128)(2,1)S(1)} custom-call(s32[4]{0:T(128)S(1)} %pad_add_fusion.flags_ref, bf16[384,768]{1,0:T(8,128)(2,1)S(1)} %turn.1.x_ref, bf16[768,256]{1,0:T(8,128)(2,1)S(1)} %collective-permute-done.3.swapped_ref, bf16[16,48,128]{2,1,0:T(8,128)(2,1)S(1)} %get-tuple-element.50.done_ref, ...), custom_call_target="tpu_custom_call" | custom-call | flops 226492416 | bytes 1048576 | tf_op jit(solution)/shard_map/grad_first/pallas_call | solution.py:385
  57.9 0.0 copy-start
  57.9 18.1 %all_to_all.21.got_ref = bf16[16,144,128]{2,1,0:T(8,128)(2,1)S(1)} all-to-all(bf16[16,144,128]{2,1,0:T(8,128)(2,1)S(1)} %grad_first.1), channel_id=1, replica_groups=mesh['xh'=2,'y'=4,'xl'=2,'z'=16,'c'=2] {'xh','y','xl'}, dimensions={0} | all-to-all | bytes 1179648 | tf_op jit(solution)/shard_map/all_to_all | solution.py:544
  76.1 0.8 first_sum.1
  76.8 4.9 %all-to-all-start.3 = ((bf16[16,8,144]{2,1,0:T(8,128)(2,1)}), bf16[16,8,144]{2,1,0:T(8,128)(2,1)S(1)}, u32[]{:S(2)}, u32[]{:S(2)}) async-start(bf16[16,8,144]{2,1,0:T(8,128)(2,1)} %first_sum.1), calls=%async_computation.3 | async-start | bytes 131072 | tf_op jit(solution)/shard_map/all_to_all | solution.py:551
  81.8 0.0 copy-done
  81.8 1.9 %grad_input.1 = bf16[4,64,256]{2,1,0:T(8,128)(2,1)} custom-call(s32[4]{0:T(128)S(1)} %pad_add_fusion.flags_ref, bf16[768,256]{1,0:T(8,128)(2,1)S(1)} %grad_pre.1.pre_ref, bf16[768,256]{1,0:T(8,128)(2,1)S(1)} %collective-permute-done.3.swapped_ref, bf16[4,64,256]{2,1,0:T(8,128)(2,1)S(1)} %bitcast.18, bf16[3,3,256,256]{3,2,1,0:T(8,128)(2,1)S(1)} %copy-done), custom_call_target="tpu_custom_call" | custom-call | flops 452984832 | bytes 2097152 | tf_op jit(solution)/shard_map/grad_input/pallas_call | solution.py:385
  83.6 10.9 %all-to-all-done.3.got_ref = bf16[16,8,144]{2,1,0:T(8,128)(2,1)S(1)} async-done(((bf16[16,8,144]{2,1,0:T(8,128)(2,1)}), bf16[16,8,144]{2,1,0:T(8,128)(2,1)S(1)}, u32[]{:S(2)}, u32[]{:S(2)}) %all-to-all-start.3) | async-done | bytes 36896 | tf_op jit(solution)/shard_map/all_to_all | solution.py:551
  94.5 0.7 second_sum.1
  (4 shorter events, 0.0 us)
Async XLA Ops:
  3.3 22.8 %copy-start.1 = (bf16[1,4,1,64,256]{4,3,2,1,0:T(8,128)(2,1)S(1)}, bf16[1,4,1,64,256]{4,3,2,1,0:T(8,128)(2,1)}, u32[]{:S(2)}) copy-start(bf16[1,4,1,64,256]{4,3,2,1,0:T(8,128)(2,1)} %param.9) | copy-start | bytes 393220
  3.3 22.8 %copy-start.3 = (bf16[1,4,1,64,256]{4,3,2,1,0:T(8,128)(2,1)S(1)}, bf16[1,4,1,64,256]{4,3,2,1,0:T(8,128)(2,1)}, u32[]{:S(2)}) copy-start(bf16[1,4,1,64,256]{4,3,2,1,0:T(8,128)(2,1)} %param.8) | copy-start | bytes 393220
  3.3 22.8 %copy-start.4 = (bf16[1,4,1,64,256]{4,3,2,1,0:T(8,128)(2,1)S(1)}, bf16[1,4,1,64,256]{4,3,2,1,0:T(8,128)(2,1)}, u32[]{:S(2)}) copy-start(bf16[1,4,1,64,256]{4,3,2,1,0:T(8,128)(2,1)} %param.7) | copy-start | bytes 393220
  3.4 22.8 %copy-start.5 = (s32[4,4]{1,0:T(4,128)S(1)}, s32[4,4]{1,0:T(4,128)}, u32[]{:S(2)}) copy-start(s32[4,4]{1,0:T(4,128)} %seams_ref.3) | copy-start | bytes 196
  3.4 22.8 %copy-start.6 = (s32[4,4]{1,0:T(4,128)S(1)}, s32[4,4]{1,0:T(4,128)}, u32[]{:S(2)}) copy-start(s32[4,4]{1,0:T(4,128)} %corners_ref.1) | copy-start | bytes 196
  19.9 12.0 %all-to-all-start.1 = ((bf16[8,64,256]{2,1,0:T(8,128)(2,1)}), bf16[8,64,256]{2,1,0:T(8,128)(2,1)S(1)}, u32[]{:S(2)}, u32[]{:S(2)}) async-start(bf16[8,64,256]{2,1,0:T(8,128)(2,1)} %pick.1), calls=%async_computation.1 | async-start | bytes 524288 | tf_op jit(solution)/shard_map/all_to_all | solution.py:451
  26.1 19.3 %copy-start.2 = (bf16[3,3,256,256]{3,2,1,0:T(8,128)(2,1)S(1)}, bf16[3,3,256,256]{3,2,1,0:T(8,128)(2,1)}, u32[]{:S(2)}) copy-start(bf16[3,3,256,256]{3,2,1,0:T(8,128)(2,1)} %weight_ref.4) | copy-start | bytes 3538948
  27.3 3.3 %collective-permute-start = (bf16[400,256]{1,0:T(8,128)(2,1)S(1)}, bf16[400,256]{1,0:T(8,128)(2,1)S(1)}, u32[]{:S(2)}, u32[]{:S(2)}) collective-permute-start(bf16[400,256]{1,0:T(8,128)(2,1)S(1)} %get-tuple-element.34), channel_id=1, source_target_pairs={{0,1},{1,0},{2,3},{3,2},{4,5},{5,4},{6,7},{7,6},{8,9},{9,8},{10,11... | collective-permute-start | bytes 614408 | tf_op jit(solution)/shard_map/ppermute | solution.py:434
  32.5 19.2 %collective-permute-start.1 = (bf16[544,256]{1,0:T(8,128)(2,1)S(1)}, bf16[544,256]{1,0:T(8,128)(2,1)S(1)}, u32[]{:S(2)}, u32[]{:S(2)}) collective-permute-start(bf16[544,256]{1,0:T(8,128)(2,1)S(1)} %get-tuple-element.36), channel_id=1, source_target_pairs={{63,0},{2,1},{1,2},{4,3},{3,4},{6,5},{5,6},{8,7},{7,8},{10,9},{9,1... | collective-permute-start | bytes 835592 | tf_op jit(solution)/shard_map/ppermute | solution.py:477
  42.6 9.1 %collective-permute-start.2 = (bf16[272,256]{1,0:T(8,128)(2,1)S(1)}, bf16[272,256]{1,0:T(8,128)(2,1)S(1)}, u32[]{:S(2)}, u32[]{:S(2)}) collective-permute-start(bf16[272,256]{1,0:T(8,128)(2,1)S(1)} %get-tuple-element.37), channel_id=1, source_target_pairs={{62,0},{3,1},{0,2},{5,3},{2,4},{7,5},{4,6},{9,7},{6,8},{11,9},{8,1... | collective-permute-start | bytes 417800 | tf_op jit(solution)/shard_map/ppermute | solution.py:478
  53.1 3.6 %collective-permute-start.3 = (bf16[768,256]{1,0:T(8,128)(2,1)S(1)}, bf16[768,256]{1,0:T(8,128)(2,1)S(1)}, u32[]{:S(2)}, u32[]{:S(2)}) collective-permute-start(bf16[768,256]{1,0:T(8,128)(2,1)S(1)} %grad_pre.1.pre_ref), channel_id=1, source_target_pairs={{0,1},{1,0},{2,3},{3,2},{4,5},{5,4},{6,7},{7,6},{8,9},{9,8},{10,11... | collective-permute-start | bytes 1179656 | tf_op jit(solution)/shard_map/ppermute | solution.py:434
  57.9 23.8 %copy-start = (bf16[3,3,256,256]{3,2,1,0:T(8,128)(2,1)S(1)}, bf16[3,3,256,256]{3,2,1,0:T(8,128)(2,1)}, u32[]{:S(2)}) copy-start(bf16[3,3,256,256]{3,2,1,0:T(8,128)(2,1)} %weight_ref.5) | copy-start | bytes 3538948
  76.8 17.7 %all-to-all-start.3 = ((bf16[16,8,144]{2,1,0:T(8,128)(2,1)}), bf16[16,8,144]{2,1,0:T(8,128)(2,1)S(1)}, u32[]{:S(2)}, u32[]{:S(2)}) async-start(bf16[16,8,144]{2,1,0:T(8,128)(2,1)} %first_sum.1), calls=%async_computation.3 | async-start | bytes 131072 | tf_op jit(solution)/shard_map/all_to_all | solution.py:551

commit v10 on v8

--- a/solution.py
+++ b/solution.py
@@ -525,7 +525,7 @@
         2 * 2**20,
     )
     scale_factor = 1.0 / math.sqrt(faces * ntile * side)
-    got = lax.all_to_all(parts, FACE + ("xl",), 0, 0, tiled=True)
+    got, grad_input = lax.optimization_barrier((lax.all_to_all(parts, FACE + ("xl",), 0, 0, tiled=True), grad_input))
     total = kernel(
         functools.partial(first_sum_kernel, scale_factor),
         shape((nz, nxl * per_tile, 9 * lines), bf),

time: 96.4 us -> 97.2 us (level)
  starting transfers between devices: 26.9 us -> 29.6 us
  waiting for transfers between devices: 19.1 us -> 16.8 us
    all_to_all x1, starting transfers between devices: 4.9 us -> 7.6 us  [on_device(): lax.all_to_all(parts, FACE + ('xl',), 0, 0, tiled=True)]
    all_to_all x1, waiting for transfers between devices: 10.9 us -> 8.69 us  [on_device(): lax.all_to_all(parts, FACE + ('xl',), 0, 0, tiled=True)]
where the time goes in v10:
time: 97.2 us; the launch traced here: 96 us
  blocking collectives  33.2 us (34%)
  starting transfers between devices  29.6 us (30%)
  waiting for transfers between devices  16.8 us (17%)
  Pallas kernels  15.2 us (16%)
    all_to_all x1, blocking collectives, on_device(): got = lax.all_to_all(total, 'z', 0, 0, tiled=True)  18.3 us
    pallas_call x12, Pallas kernels, kernel(): pl.pallas_call(body, out_shape=out_shape, in_specs=[pl.BlockSpec(memory_s...  15.2 us
    all_to_all x1, blocking collectives, on_device(): table = lax.all_to_all(sent, FACE, 0, 0, tiled=True)  14.9 us
    ppermute x1, starting transfers between devices, on_device(): near = lax.ppermute(near, TILE, pairs(1))  10.1 us
    all_to_all x1, waiting for transfers between devices, on_device(): lax.all_to_all(parts, FACE + ('xl',), 0, 0, tiled=True)  8.69 us
    all_to_all x1, starting transfers between devices, on_device(): lax.all_to_all(parts, FACE + ('xl',), 0, 0, tiled=True)  7.6 us
    all_to_all x1, starting transfers between devices, on_device(): wrapped = lax.all_to_all(picked, FACE, 0, 0, tiled=True)  6.18 us
    ppermute x1, waiting for transfers between devices, on_device(): far = lax.ppermute(far, TILE, pairs(2))  4.93 us
  transfers between devices with their start and end apart: 6, of which 5 were waited for; matrix products, arithmetic and copies ran while one was open for 0% of the time, Pallas kernels for 7%

profile of v10, /device:TPU:6, one launch (start us, length us, event | category | flops | bytes accessed | tf_op | source)
XLA Modules:
  0.0 96.0 jit_solution(12509488527396582908)
XLA Ops:
  0.7 2.6 %pack.1 = bf16[8,96,256]{2,1,0:T(8,128)(2,1)} custom-call(s32[4,4]{1,0:T(4,128)} %seams_ref.3, bf16[4,64,256]{2,1,0:T(8,128)(2,1)} %bitcast.16, bf16[4,64,256]{2,1,0:T(8,128)(2,1)} %bitcast.19), custom_call_target="tpu_custom_call" | custom-call | bytes 1048576 | tf_op jit(solution)/shard_map/pack/pallas_call | solution.py:374
  3.3 0.0 copy-start.1
  3.3 0.0 copy-start.3
  3.3 0.0 copy-start.4
  3.3 0.0 copy-start.5
  3.3 0.0 copy-start.6
  3.3 0.1 pad_add_fusion.flags_ref
  3.4 14.9 %all_to_all.20.table_ref = bf16[8,96,256]{2,1,0:T(8,128)(2,1)S(1)} all-to-all(bf16[8,96,256]{2,1,0:T(8,128)(2,1)} %pack.1), channel_id=1, replica_groups=mesh['xh'=2,'y'=4,'xl'=2,'z'=16,'c'=2] {'xh','y'}, dimensions={0} | all-to-all | bytes 786432 | tf_op jit(solution)/shard_map/all_to_all | solution.py:422
  18.3 0.1 copy.11
  18.4 1.4 %pick.1 = bf16[8,64,256]{2,1,0:T(8,128)(2,1)} custom-call(s32[32]{0:T(128)S(1)} %fusion.want_ref, bf16[8,96,256]{2,1,0:T(8,128)(2,1)S(1)} %all_to_all.20.table_ref), custom_call_target="tpu_custom_call" | custom-call | bytes 1048576 | tf_op jit(solution)/shard_map/pick/pallas_call | solution.py:374
  19.8 6.2 %all-to-all-start.1 = ((bf16[8,64,256]{2,1,0:T(8,128)(2,1)}), bf16[8,64,256]{2,1,0:T(8,128)(2,1)S(1)}, u32[]{:S(2)}, u32[]{:S(2)}) async-start(bf16[8,64,256]{2,1,0:T(8,128)(2,1)} %pick.1), calls=%async_computation.1 | async-start | bytes 524288 | tf_op jit(solution)/shard_map/all_to_all | solution.py:435
  26.0 0.0 copy-start.2
  26.0 0.0 copy-done.1
  26.0 0.0 copy-done.3
  26.0 0.0 copy-done.4
  26.0 0.0 copy-done.5
  26.1 0.0 copy-done.6
  26.1 1.1 %border.1 = (bf16[544,256]{1,0:T(8,128)(2,1)S(1)}, bf16[32,256]{1,0:T(8,128)(2,1)S(1)}, bf16[400,256]{1,0:T(8,128)(2,1)S(1)}, bf16[256,128]{1,0:T(8,128)(2,1)S(1)}) custom-call(s32[4]{0:T(128)S(1)} %pad_add_fusion.flags_ref, s32[4,4]{1,0:T(4,128)S(1)} %copy-done.5, s32[4,4]{1,0:T(4,128)S(1)} %copy-done.6, bf16[8,96,256]{2,1,0:T(8,128)(2,1)S(1)} %all_to_all.20.table_ref, ...), custom_call_target="tpu_custom_call" | custom-call | bytes 1048576 | tf_op jit(solution)/shard_map/border/pallas_call | solution.py:374
  27.2 1.9 %collective-permute-start = (bf16[400,256]{1,0:T(8,128)(2,1)S(1)}, bf16[400,256]{1,0:T(8,128)(2,1)S(1)}, u32[]{:S(2)}, u32[]{:S(2)}) collective-permute-start(bf16[400,256]{1,0:T(8,128)(2,1)S(1)} %get-tuple-element.36), channel_id=1, source_target_pairs={{0,1},{1,0},{2,3},{3,2},{4,5},{5,4},{6,7},{7,6},{8,9},{9,8},{10,11... | collective-permute-start | bytes 614408 | tf_op jit(solution)/shard_map/ppermute | solution.py:420
  29.1 1.4 %collective-permute-done.part_ref = bf16[400,256]{1,0:T(8,128)(2,1)S(1)} collective-permute-done((bf16[400,256]{1,0:T(8,128)(2,1)S(1)}, bf16[400,256]{1,0:T(8,128)(2,1)S(1)}, u32[]{:S(2)}, u32[]{:S(2)}) %collective-permute-start) | collective-permute-done | bytes 204832 | tf_op jit(solution)/shard_map/ppermute | solution.py:420
  30.5 1.3 %all-to-all-done.1.pieces_ref = bf16[8,64,256]{2,1,0:T(8,128)(2,1)S(1)} async-done(((bf16[8,64,256]{2,1,0:T(8,128)(2,1)}), bf16[8,64,256]{2,1,0:T(8,128)(2,1)S(1)}, u32[]{:S(2)}, u32[]{:S(2)}) %all-to-all-start.1) | async-done | bytes 262176 | tf_op jit(solution)/shard_map/all_to_all | solution.py:435
  31.9 0.6 send.1
  32.5 10.1 %collective-permute-start.1 = (bf16[544,256]{1,0:T(8,128)(2,1)S(1)}, bf16[544,256]{1,0:T(8,128)(2,1)S(1)}, u32[]{:S(2)}, u32[]{:S(2)}) collective-permute-start(bf16[544,256]{1,0:T(8,128)(2,1)S(1)} %get-tuple-element.38), channel_id=1, source_target_pairs={{63,0},{2,1},{1,2},{4,3},{3,4},{6,5},{5,6},{8,7},{7,8},{10,9},{9,1... | collective-permute-start | bytes 835592 | tf_op jit(solution)/shard_map/ppermute | solution.py:461
  42.5 1.9 %collective-permute-start.2 = (bf16[272,256]{1,0:T(8,128)(2,1)S(1)}, bf16[272,256]{1,0:T(8,128)(2,1)S(1)}, u32[]{:S(2)}, u32[]{:S(2)}) collective-permute-start(bf16[272,256]{1,0:T(8,128)(2,1)S(1)} %get-tuple-element.39), channel_id=1, source_target_pairs={{62,0},{3,1},{0,2},{5,3},{2,4},{7,5},{4,6},{9,7},{6,8},{11,9},{8,1... | collective-permute-start | bytes 417800 | tf_op jit(solution)/shard_map/ppermute | solution.py:462
  44.5 0.8 turn.1.x_ref
  45.3 0.0 copy-done.2
  45.3 1.4 %near_half.1 = (f32[768,256]{1,0:T(8,128)S(1)}, f32[384,256]{1,0:T(8,128)S(1)}) custom-call(s32[4]{0:T(128)S(1)} %pad_add_fusion.flags_ref, bf16[544,256]{1,0:T(8,128)(2,1)S(1)} %get-tuple-element.33.own_ref, bf16[400,256]{1,0:T(8,128)(2,1)S(1)} %collective-permute-done.part_ref, bf16[3,3,256,256]{3,2,1,0:T(8,128)(2,1)S(1)} %copy-done.2), custom_call_target="tpu_custom_call" | custom-call | flops 452984832 | bytes 2097152 | tf_op jit(solution)/shard_map/near_half/pallas_call | solution.py:374
  46.7 4.9 %collective-permute-done.2.far_ref = bf16[272,256]{1,0:T(8,128)(2,1)S(1)} collective-permute-done((bf16[272,256]{1,0:T(8,128)(2,1)S(1)}, bf16[272,256]{1,0:T(8,128)(2,1)S(1)}, u32[]{:S(2)}, u32[]{:S(2)}) %collective-permute-start.2) | collective-permute-done | bytes 139296 | tf_op jit(solution)/shard_map/ppermute | solution.py:462
  51.6 0.0 collective-permute-done.1.near_ref
  51.6 1.4 %grad_pre.1.pre_ref = bf16[768,256]{1,0:T(8,128)(2,1)S(1)} custom-call(s32[4]{0:T(128)S(1)} %pad_add_fusion.flags_ref, bf16[544,256]{1,0:T(8,128)(2,1)S(1)} %collective-permute-done.1.near_ref, bf16[272,256]{1,0:T(8,128)(2,1)S(1)} %collective-permute-done.2.far_ref, f32[768,256]{1,0:T(8,128)S(1)} %get-tuple-element.47.hidden_ref, ...), custom_call_target="tpu_custom_call" | custom-call | flops 452984832 | bytes 4194304 | tf_op jit(solution)/shard_map/grad_pre/pallas_call | solution.py:374
  53.0 1.9 %collective-permute-start.3 = (bf16[768,256]{1,0:T(8,128)(2,1)S(1)}, bf16[768,256]{1,0:T(8,128)(2,1)S(1)}, u32[]{:S(2)}, u32[]{:S(2)}) collective-permute-start(bf16[768,256]{1,0:T(8,128)(2,1)S(1)} %grad_pre.1.pre_ref), channel_id=1, source_target_pairs={{0,1},{1,0},{2,3},{3,2},{4,5},{5,4},{6,7},{7,6},{8,9},{9,8},{10,11... | collective-permute-start | bytes 1179656 | tf_op jit(solution)/shard_map/ppermute | solution.py:420
  54.9 1.2 %first_half.1 = (bf16[16,48,128]{2,1,0:T(8,128)(2,1)S(1)}, f32[384,256]{1,0:T(8,128)S(1)}) custom-call(s32[4]{0:T(128)S(1)} %pad_add_fusion.flags_ref, bf16[384,768]{1,0:T(8,128)(2,1)S(1)} %turn.1.x_ref, bf16[768,256]{1,0:T(8,128)(2,1)S(1)} %grad_pre.1.pre_ref), custom_call_target="tpu_custom_call" | custom-call | bytes 1048576 | tf_op jit(solution)/shard_map/first_half/pallas_call | solution.py:374
  56.1 0.5 collective-permute-done.3.swapped_ref
  56.6 0.0 copy-start
  56.6 2.1 %grad_first.1 = bf16[16,144,128]{2,1,0:T(8,128)(2,1)} custom-call(s32[4]{0:T(128)S(1)} %pad_add_fusion.flags_ref, bf16[384,768]{1,0:T(8,128)(2,1)S(1)} %turn.1.x_ref, bf16[768,256]{1,0:T(8,128)(2,1)S(1)} %collective-permute-done.3.swapped_ref, bf16[16,48,128]{2,1,0:T(8,128)(2,1)S(1)} %get-tuple-element.52.done_ref, f32[384,256]{1,0:T(8,128)S(1)} %get-tuple-element.53.middle_ref), custom_call_target="tpu_custom_call" | custom-call | flops 226492416 | bytes 1048576 | tf_op jit(solution)/shard_map/grad_first/pallas_call | solution.py:374
  58.7 7.6 %all-to-all-start.2 = ((bf16[16,144,128]{2,1,0:T(8,128)(2,1)}), bf16[16,144,128]{2,1,0:T(8,128)(2,1)S(1)}, u32[]{:S(2)}, u32[]{:S(2)}) async-start(bf16[16,144,128]{2,1,0:T(8,128)(2,1)} %grad_first.1), calls=%async_computation.2 | async-start | bytes 1179648 | tf_op jit(solution)/shard_map/all_to_all | solution.py:528
  66.3 0.0 copy-done
  66.3 1.9 %grad_input.1 = bf16[4,64,256]{2,1,0:T(8,128)(2,1)} custom-call(s32[4]{0:T(128)S(1)} %pad_add_fusion.flags_ref, bf16[768,256]{1,0:T(8,128)(2,1)S(1)} %grad_pre.1.pre_ref, bf16[768,256]{1,0:T(8,128)(2,1)S(1)} %collective-permute-done.3.swapped_ref, bf16[4,64,256]{2,1,0:T(8,128)(2,1)S(1)} %bitcast.18, bf16[3,3,256,256]{3,2,1,0:T(8,128)(2,1)S(1)} %copy-done), custom_call_target="tpu_custom_call" | custom-call | flops 452984832 | bytes 2097152 | tf_op jit(solution)/shard_map/grad_input/pallas_call | solution.py:374
  68.1 8.7 %all-to-all-done.2.got_ref = bf16[16,144,128]{2,1,0:T(8,128)(2,1)S(1)} async-done(((bf16[16,144,128]{2,1,0:T(8,128)(2,1)}), bf16[16,144,128]{2,1,0:T(8,128)(2,1)S(1)}, u32[]{:S(2)}, u32[]{:S(2)}) %all-to-all-start.2) | async-done | bytes 589856 | tf_op jit(solution)/shard_map/all_to_all | solution.py:528
  76.8 0.1 first_sum.1
  77.0 18.3 %all_to_all.21.got_ref = bf16[16,8,144]{2,1,0:T(8,128)(2,1)S(1)} all-to-all(bf16[16,8,144]{2,1,0:T(8,128)(2,1)S(1)} %first_sum.1), channel_id=1, replica_groups=mesh['xh'=2,'y'=4,'xl'=2,'z'=16,'c'=2] {'z'}, dimensions={0} | all-to-all | bytes 73728 | tf_op jit(solution)/shard_map/all_to_all | solution.py:535
  95.3 0.7 second_sum.1
  (4 shorter events, 0.0 us)
Async XLA Ops:
  3.3 22.8 %copy-start.1 = (bf16[1,4,1,64,256]{4,3,2,1,0:T(8,128)(2,1)S(1)}, bf16[1,4,1,64,256]{4,3,2,1,0:T(8,128)(2,1)}, u32[]{:S(2)}) copy-start(bf16[1,4,1,64,256]{4,3,2,1,0:T(8,128)(2,1)} %param.9) | copy-start | bytes 393220
  3.3 22.8 %copy-start.3 = (bf16[1,4,1,64,256]{4,3,2,1,0:T(8,128)(2,1)S(1)}, bf16[1,4,1,64,256]{4,3,2,1,0:T(8,128)(2,1)}, u32[]{:S(2)}) copy-start(bf16[1,4,1,64,256]{4,3,2,1,0:T(8,128)(2,1)} %param.8) | copy-start | bytes 393220
  3.3 22.8 %copy-start.4 = (bf16[1,4,1,64,256]{4,3,2,1,0:T(8,128)(2,1)S(1)}, bf16[1,4,1,64,256]{4,3,2,1,0:T(8,128)(2,1)}, u32[]{:S(2)}) copy-start(bf16[1,4,1,64,256]{4,3,2,1,0:T(8,128)(2,1)} %param.7) | copy-start | bytes 393220
  3.3 22.8 %copy-start.5 = (s32[4,4]{1,0:T(4,128)S(1)}, s32[4,4]{1,0:T(4,128)}, u32[]{:S(2)}) copy-start(s32[4,4]{1,0:T(4,128)} %seams_ref.3) | copy-start | bytes 196
  3.3 22.8 %copy-start.6 = (s32[4,4]{1,0:T(4,128)S(1)}, s32[4,4]{1,0:T(4,128)}, u32[]{:S(2)}) copy-start(s32[4,4]{1,0:T(4,128)} %corners_ref.1) | copy-start | bytes 196
  19.8 12.0 %all-to-all-start.1 = ((bf16[8,64,256]{2,1,0:T(8,128)(2,1)}), bf16[8,64,256]{2,1,0:T(8,128)(2,1)S(1)}, u32[]{:S(2)}, u32[]{:S(2)}) async-start(bf16[8,64,256]{2,1,0:T(8,128)(2,1)} %pick.1), calls=%async_computation.1 | async-start | bytes 524288 | tf_op jit(solution)/shard_map/all_to_all | solution.py:435
  26.0 19.3 %copy-start.2 = (bf16[3,3,256,256]{3,2,1,0:T(8,128)(2,1)S(1)}, bf16[3,3,256,256]{3,2,1,0:T(8,128)(2,1)}, u32[]{:S(2)}) copy-start(bf16[3,3,256,256]{3,2,1,0:T(8,128)(2,1)} %weight_ref.4) | copy-start | bytes 3538948
  27.2 3.3 %collective-permute-start = (bf16[400,256]{1,0:T(8,128)(2,1)S(1)}, bf16[400,256]{1,0:T(8,128)(2,1)S(1)}, u32[]{:S(2)}, u32[]{:S(2)}) collective-permute-start(bf16[400,256]{1,0:T(8,128)(2,1)S(1)} %get-tuple-element.36), channel_id=1, source_target_pairs={{0,1},{1,0},{2,3},{3,2},{4,5},{5,4},{6,7},{7,6},{8,9},{9,8},{10,11... | collective-permute-start | bytes 614408 | tf_op jit(solution)/shard_map/ppermute | solution.py:420
  32.5 19.2 %collective-permute-start.1 = (bf16[544,256]{1,0:T(8,128)(2,1)S(1)}, bf16[544,256]{1,0:T(8,128)(2,1)S(1)}, u32[]{:S(2)}, u32[]{:S(2)}) collective-permute-start(bf16[544,256]{1,0:T(8,128)(2,1)S(1)} %get-tuple-element.38), channel_id=1, source_target_pairs={{63,0},{2,1},{1,2},{4,3},{3,4},{6,5},{5,6},{8,7},{7,8},{10,9},{9,1... | collective-permute-start | bytes 835592 | tf_op jit(solution)/shard_map/ppermute | solution.py:461
  42.5 9.1 %collective-permute-start.2 = (bf16[272,256]{1,0:T(8,128)(2,1)S(1)}, bf16[272,256]{1,0:T(8,128)(2,1)S(1)}, u32[]{:S(2)}, u32[]{:S(2)}) collective-permute-start(bf16[272,256]{1,0:T(8,128)(2,1)S(1)} %get-tuple-element.39), channel_id=1, source_target_pairs={{62,0},{3,1},{0,2},{5,3},{2,4},{7,5},{4,6},{9,7},{6,8},{11,9},{8,1... | collective-permute-start | bytes 417800 | tf_op jit(solution)/shard_map/ppermute | solution.py:462
  53.0 3.6 %collective-permute-start.3 = (bf16[768,256]{1,0:T(8,128)(2,1)S(1)}, bf16[768,256]{1,0:T(8,128)(2,1)S(1)}, u32[]{:S(2)}, u32[]{:S(2)}) collective-permute-start(bf16[768,256]{1,0:T(8,128)(2,1)S(1)} %grad_pre.1.pre_ref), channel_id=1, source_target_pairs={{0,1},{1,0},{2,3},{3,2},{4,5},{5,4},{6,7},{7,6},{8,9},{9,8},{10,11... | collective-permute-start | bytes 1179656 | tf_op jit(solution)/shard_map/ppermute | solution.py:420
  56.6 9.7 %copy-start = (bf16[3,3,256,256]{3,2,1,0:T(8,128)(2,1)S(1)}, bf16[3,3,256,256]{3,2,1,0:T(8,128)(2,1)}, u32[]{:S(2)}) copy-start(bf16[3,3,256,256]{3,2,1,0:T(8,128)(2,1)} %weight_ref.5) | copy-start | bytes 3538948
  58.7 18.2 %all-to-all-start.2 = ((bf16[16,144,128]{2,1,0:T(8,128)(2,1)}), bf16[16,144,128]{2,1,0:T(8,128)(2,1)S(1)}, u32[]{:S(2)}, u32[]{:S(2)}) async-start(bf16[16,144,128]{2,1,0:T(8,128)(2,1)} %grad_first.1), calls=%async_computation.2 | async-start | bytes 1179648 | tf_op jit(solution)/shard_map/all_to_all | solution.py:528

commit v11 on v9

--- a/solution.py
+++ b/solution.py
@@ -166,7 +166,7 @@
             mine_ref[into : into + side // 2, part * half : (part + 1) * half] = chosen[at : at + side // 2, half:]
 
 
-def turn_kernel(local, side, flags_ref, kept_ref, part_ref, out_ref, lines):
+def copies_kernel(local, side, flags_ref, kept_ref, part_ref, out_ref, lines):
     pitch = side + 2 * GAP
     row = local * pitch
     half = kept_ref.shape[-1]
@@ -182,7 +182,7 @@
             ].astype(jnp.float32)
     for c in range(3):
         moved = lines[...] if c == 1 else pltpu.roll(lines[...], (1 - c) % (2 * row), 0)
-        out_ref[c * half : (c + 1) * half, :] = moved.T.astype(jnp.bfloat16)
+        out_ref[:, c * half : (c + 1) * half] = moved.astype(jnp.bfloat16)
 
 
 def send_kernel(local, side, blocks, flags_ref, own_ref, tails_ref, pieces_ref, near_ref, far_ref):
@@ -329,11 +329,15 @@
         out_ref[face] = (own + grad[at : at + side, :]).astype(jnp.bfloat16)
 
 
+def over_pixels(left, right):
+    return lax.dot_general(left, right, (((0,), (0,)), ((), ())), preferred_element_type=jnp.float32)
+
+
 def emit(out_ref, start, terms, nxl, per_tile):
     dests, half = out_ref.shape[0], out_ref.shape[2]
-    lines = terms.shape[1] // dests
+    lines = terms.shape[0] // dests
     for c in range(3):
-        turned = terms[c * half : (c + 1) * half, :].T
+        turned = terms[:, c * half : (c + 1) * half]
         at = pl.multiple_of(start + c * lines, 16)
         if nxl == 1:
             for d in range(dests):
@@ -354,26 +358,25 @@
 
 def first_half_kernel(row, nxl, per_tile, flags_ref, x_ref, pre_ref, out_ref, middle_ref):
     core = flags_ref[0]
-    lanes = pl.ds(pl.multiple_of(core * row, 128), row)
+    x_rows = pl.ds(pl.multiple_of(core * row, 16), row)
     rows = pl.ds(pl.multiple_of((1 - core) * row, 16), row)
-    middle_ref[...] = jnp.dot(x_ref[:, lanes], pre_ref[rows, :], preferred_element_type=jnp.float32)
-    emit(out_ref, 0, jnp.dot(x_ref[...], pre_ref[...], preferred_element_type=jnp.float32), nxl, per_tile)
+    middle_ref[...] = over_pixels(pre_ref[rows, :], x_ref[x_rows, :])
+    emit(out_ref, 0, over_pixels(pre_ref[...], x_ref[...]), nxl, per_tile)
 
 
 def grad_first_kernel(row, nxl, per_tile, flags_ref, x_ref, swapped_ref, done_ref, middle_ref, out_ref):
     core = flags_ref[0]
-    lanes = pl.ds(pl.multiple_of((1 - core) * row, 128), row)
+    x_rows = pl.ds(pl.multiple_of((1 - core) * row, 16), row)
     rows = pl.ds(pl.multiple_of(core * row, 16), row)
     count = done_ref.shape[1]
     emit(
         out_ref,
         count,
-        middle_ref[...] + jnp.dot(x_ref[:, lanes], swapped_ref[rows, :], preferred_element_type=jnp.float32),
+        middle_ref[...] + over_pixels(swapped_ref[rows, :], x_ref[x_rows, :]),
         nxl,
         per_tile,
     )
-    terms = jnp.dot(x_ref[...], swapped_ref[...], preferred_element_type=jnp.float32)
-    emit(out_ref, core * 2 * count, terms, nxl, per_tile)
+    emit(out_ref, core * 2 * count, over_pixels(swapped_ref[...], x_ref[...]), nxl, per_tile)
     at = pl.multiple_of((1 - core) * 2 * count, 16)
     for d in range(done_ref.shape[0]):
         out_ref[d, pl.ds(at, count)] = done_ref[d]
@@ -476,13 +479,13 @@
     pairs = lambda step: [((t + step if t % 2 else t - step) % ntile, t) for t in range(ntile)]
     near = lax.ppermute(near, TILE, pairs(1))
     far = lax.ppermute(far, TILE, pairs(2))
-    x_turned = kernel(
-        functools.partial(turn_kernel, local, side),
-        shape((3 * half, 2 * row), bf),
+    x_copies = kernel(
+        functools.partial(copies_kernel, local, side),
+        shape((2 * row, 3 * half), bf),
         (flags, kept, part),
         1,
         (pltpu.VMEM((2 * row, half), jnp.float32),),
-        "turn",
+        "copies",
     )
 
     pads = tuple(pltpu.VMEM((row, channels), bf) for _ in range(3))
@@ -497,7 +500,7 @@
         2 * 2**20,
         row * channels,
     )
-    near, far, x_turned, hidden, slope = lax.optimization_barrier((near, far, x_turned, hidden, slope))
+    near, far, x_copies, hidden, slope = lax.optimization_barrier((near, far, x_copies, hidden, slope))
     grad_pre = kernel(
         functools.partial(grad_pre_kernel, local, side),
         shape((2 * row, channels), bf),
@@ -516,8 +519,8 @@
     lines = width // nxl
     done, middle = kernel(
         functools.partial(first_half_kernel, row, nxl, per_tile),
-        (shape((nface * nxl, 3 * lines, half), bf), shape((3 * half, channels), jnp.float32)),
-        (flags, x_turned, grad_pre),
+        (shape((nface * nxl, 3 * lines, half), bf), shape((channels, 3 * half), jnp.float32)),
+        (flags, x_copies, grad_pre),
         1,
         name="first_half",
     )
@@ -525,7 +528,7 @@
     parts = kernel(
         functools.partial(grad_first_kernel, row, nxl, per_tile),
         shape((nface * nxl, 9 * lines, half), bf),
-        (flags, x_turned, swapped, done, middle),
+        (flags, x_copies, swapped, done, middle),
         1,
         name="grad_first",
         flops=2 * 9 * half * row * channels,

time: 96.5 us -> 96.5 us (level)
  no operation moved by 1% of the time
where the time goes in v11:
time: 96.5 us; the launch traced here: 95.2 us
  blocking collectives  33 us (34%)
  starting transfers between devices  26.9 us (28%)
  waiting for transfers between devices  19.2 us (20%)
  Pallas kernels  14.9 us (15%)
    all_to_all x1, blocking collectives, on_device(): got = lax.all_to_all(parts, FACE + ('xl',), 0, 0, tiled=True)  18.1 us
    pallas_call x12, Pallas kernels, kernel(): pl.pallas_call(body, out_shape=out_shape, in_specs=[pl.BlockSpec(memory_s...  14.9 us
    all_to_all x1, blocking collectives, on_device(): table = lax.all_to_all(sent, FACE, 0, 0, tiled=True)  14.9 us
    all_to_all x1, waiting for transfers between devices, on_device(): got = lax.all_to_all(total, 'z', 0, 0, tiled=True)  10.9 us
    ppermute x1, starting transfers between devices, on_device(): near = lax.ppermute(near, TILE, pairs(1))  10.1 us
    all_to_all x1, starting transfers between devices, on_device(): wrapped = lax.all_to_all(picked, FACE, 0, 0, tiled=True)  6.19 us
    ppermute x1, waiting for transfers between devices, on_device(): far = lax.ppermute(far, TILE, pairs(2))  4.99 us
    all_to_all x1, starting transfers between devices, on_device(): got = lax.all_to_all(total, 'z', 0, 0, tiled=True)  4.9 us
  transfers between devices with their start and end apart: 6, of which 5 were waited for; matrix products, arithmetic and copies ran while one was open for 0% of the time, Pallas kernels for 7%

profile of v11, /device:TPU:6, one launch (start us, length us, event | category | flops | bytes accessed | tf_op | source)
XLA Modules:
  0.0 95.2 jit_solution(9789789159645750696)
XLA Ops:
  0.7 2.7 %pack.1 = bf16[8,96,256]{2,1,0:T(8,128)(2,1)} custom-call(s32[4,4]{1,0:T(4,128)} %seams_ref.3, bf16[4,64,256]{2,1,0:T(8,128)(2,1)} %bitcast.16, bf16[4,64,256]{2,1,0:T(8,128)(2,1)} %bitcast.19), custom_call_target="tpu_custom_call" | custom-call | bytes 1048576 | tf_op jit(solution)/shard_map/pack/pallas_call | solution.py:388
  3.3 0.0 copy-start.1
  3.3 0.0 copy-start.3
  3.3 0.0 copy-start.4
  3.4 0.0 copy-start.5
  3.4 0.0 copy-start.6
  3.4 0.1 pad_add_fusion.flags_ref
  3.5 14.9 %all_to_all.20.table_ref = bf16[8,96,256]{2,1,0:T(8,128)(2,1)S(1)} all-to-all(bf16[8,96,256]{2,1,0:T(8,128)(2,1)} %pack.1), channel_id=1, replica_groups=mesh['xh'=2,'y'=4,'xl'=2,'z'=16,'c'=2] {'xh','y'}, dimensions={0} | all-to-all | bytes 786432 | tf_op jit(solution)/shard_map/all_to_all | solution.py:439
  18.4 0.1 copy.11
  18.5 1.4 %pick.1 = bf16[8,64,256]{2,1,0:T(8,128)(2,1)} custom-call(s32[32]{0:T(128)S(1)} %fusion.want_ref, bf16[8,96,256]{2,1,0:T(8,128)(2,1)S(1)} %all_to_all.20.table_ref), custom_call_target="tpu_custom_call" | custom-call | bytes 1048576 | tf_op jit(solution)/shard_map/pick/pallas_call | solution.py:388
  19.9 6.2 %all-to-all-start.1 = ((bf16[8,64,256]{2,1,0:T(8,128)(2,1)}), bf16[8,64,256]{2,1,0:T(8,128)(2,1)S(1)}, u32[]{:S(2)}, u32[]{:S(2)}) async-start(bf16[8,64,256]{2,1,0:T(8,128)(2,1)} %pick.1), calls=%async_computation.1 | async-start | bytes 524288 | tf_op jit(solution)/shard_map/all_to_all | solution.py:454
  26.1 0.0 copy-start.2
  26.1 0.0 copy-done.1
  26.1 0.0 copy-done.3
  26.1 0.0 copy-done.4
  26.1 0.0 copy-done.5
  26.1 0.0 copy-done.6
  26.1 1.1 %border.1 = (bf16[544,256]{1,0:T(8,128)(2,1)S(1)}, bf16[32,256]{1,0:T(8,128)(2,1)S(1)}, bf16[400,256]{1,0:T(8,128)(2,1)S(1)}, bf16[256,128]{1,0:T(8,128)(2,1)S(1)}) custom-call(s32[4]{0:T(128)S(1)} %pad_add_fusion.flags_ref, s32[4,4]{1,0:T(4,128)S(1)} %copy-done.5, s32[4,4]{1,0:T(4,128)S(1)} %copy-done.6, bf16[8,96,256]{2,1,0:T(8,128)(2,1)S(1)} %all_to_all.20.table_ref, ...), custom_call_target="tpu_custom_call" | custom-call | bytes 1048576 | tf_op jit(solution)/shard_map/border/pallas_call | solution.py:388
  27.3 1.9 %collective-permute-start = (bf16[400,256]{1,0:T(8,128)(2,1)S(1)}, bf16[400,256]{1,0:T(8,128)(2,1)S(1)}, u32[]{:S(2)}, u32[]{:S(2)}) collective-permute-start(bf16[400,256]{1,0:T(8,128)(2,1)S(1)} %get-tuple-element.34), channel_id=1, source_target_pairs={{0,1},{1,0},{2,3},{3,2},{4,5},{5,4},{6,7},{7,6},{8,9},{9,8},{10,11... | collective-permute-start | bytes 614408 | tf_op jit(solution)/shard_map/ppermute | solution.py:437
  29.2 1.4 %collective-permute-done.part_ref = bf16[400,256]{1,0:T(8,128)(2,1)S(1)} collective-permute-done((bf16[400,256]{1,0:T(8,128)(2,1)S(1)}, bf16[400,256]{1,0:T(8,128)(2,1)S(1)}, u32[]{:S(2)}, u32[]{:S(2)}) %collective-permute-start) | collective-permute-done | bytes 204832 | tf_op jit(solution)/shard_map/ppermute | solution.py:437
  30.6 1.3 %all-to-all-done.1.pieces_ref = bf16[8,64,256]{2,1,0:T(8,128)(2,1)S(1)} async-done(((bf16[8,64,256]{2,1,0:T(8,128)(2,1)}), bf16[8,64,256]{2,1,0:T(8,128)(2,1)S(1)}, u32[]{:S(2)}, u32[]{:S(2)}) %all-to-all-start.1) | async-done | bytes 262176 | tf_op jit(solution)/shard_map/all_to_all | solution.py:454
  31.9 0.6 send.1
  32.5 10.1 %collective-permute-start.1 = (bf16[544,256]{1,0:T(8,128)(2,1)S(1)}, bf16[544,256]{1,0:T(8,128)(2,1)S(1)}, u32[]{:S(2)}, u32[]{:S(2)}) collective-permute-start(bf16[544,256]{1,0:T(8,128)(2,1)S(1)} %get-tuple-element.36), channel_id=1, source_target_pairs={{63,0},{2,1},{1,2},{4,3},{3,4},{6,5},{5,6},{8,7},{7,8},{10,9},{9,1... | collective-permute-start | bytes 835592 | tf_op jit(solution)/shard_map/ppermute | solution.py:480
  42.6 1.9 %collective-permute-start.2 = (bf16[272,256]{1,0:T(8,128)(2,1)S(1)}, bf16[272,256]{1,0:T(8,128)(2,1)S(1)}, u32[]{:S(2)}, u32[]{:S(2)}) collective-permute-start(bf16[272,256]{1,0:T(8,128)(2,1)S(1)} %get-tuple-element.37), channel_id=1, source_target_pairs={{62,0},{3,1},{0,2},{5,3},{2,4},{7,5},{4,6},{9,7},{6,8},{11,9},{8,1... | collective-permute-start | bytes 417800 | tf_op jit(solution)/shard_map/ppermute | solution.py:481
  44.5 0.8 copies.1.x_ref
  45.3 0.0 copy-done.2
  45.3 1.4 %near_half.1 = (f32[768,256]{1,0:T(8,128)S(1)}, f32[384,256]{1,0:T(8,128)S(1)}) custom-call(s32[4]{0:T(128)S(1)} %pad_add_fusion.flags_ref, bf16[544,256]{1,0:T(8,128)(2,1)S(1)} %get-tuple-element.31.own_ref, bf16[400,256]{1,0:T(8,128)(2,1)S(1)} %collective-permute-done.part_ref, bf16[3,3,256,256]{3,2,1,0:T(8,128)(2,1)S(1)} %copy-done.2), custom_call_target="tpu_custom_call" | custom-call | flops 452984832 | bytes 2097152 | tf_op jit(solution)/shard_map/near_half/pallas_call | solution.py:388
  46.7 5.0 %collective-permute-done.2.far_ref = bf16[272,256]{1,0:T(8,128)(2,1)S(1)} collective-permute-done((bf16[272,256]{1,0:T(8,128)(2,1)S(1)}, bf16[272,256]{1,0:T(8,128)(2,1)S(1)}, u32[]{:S(2)}, u32[]{:S(2)}) %collective-permute-start.2) | collective-permute-done | bytes 139296 | tf_op jit(solution)/shard_map/ppermute | solution.py:481
  51.7 0.0 collective-permute-done.1.near_ref
  51.7 1.4 %grad_pre.1.pre_ref = bf16[768,256]{1,0:T(8,128)(2,1)S(1)} custom-call(s32[4]{0:T(128)S(1)} %pad_add_fusion.flags_ref, bf16[544,256]{1,0:T(8,128)(2,1)S(1)} %collective-permute-done.1.near_ref, bf16[272,256]{1,0:T(8,128)(2,1)S(1)} %collective-permute-done.2.far_ref, f32[768,256]{1,0:T(8,128)S(1)} %get-tuple-element.44.hidden_ref, ...), custom_call_target="tpu_custom_call" | custom-call | flops 452984832 | bytes 4194304 | tf_op jit(solution)/shard_map/grad_pre/pallas_call | solution.py:388
  53.1 1.9 %collective-permute-start.3 = (bf16[768,256]{1,0:T(8,128)(2,1)S(1)}, bf16[768,256]{1,0:T(8,128)(2,1)S(1)}, u32[]{:S(2)}, u32[]{:S(2)}) collective-permute-start(bf16[768,256]{1,0:T(8,128)(2,1)S(1)} %grad_pre.1.pre_ref), channel_id=1, source_target_pairs={{0,1},{1,0},{2,3},{3,2},{4,5},{5,4},{6,7},{7,6},{8,9},{9,8},{10,11... | collective-permute-start | bytes 1179656 | tf_op jit(solution)/shard_map/ppermute | solution.py:437
  55.0 1.2 %first_half.1 = (bf16[16,48,128]{2,1,0:T(8,128)(2,1)S(1)}, f32[256,384]{1,0:T(8,128)S(1)}) custom-call(s32[4]{0:T(128)S(1)} %pad_add_fusion.flags_ref, bf16[768,384]{1,0:T(8,128)(2,1)S(1)} %copies.1.x_ref, bf16[768,256]{1,0:T(8,128)(2,1)S(1)} %grad_pre.1.pre_ref), custom_call_target="tpu_custom_call" | custom-call | bytes 1048576 | tf_op jit(solution)/shard_map/first_half/pallas_call | solution.py:388
  56.2 0.5 collective-permute-done.3.swapped_ref
  56.7 1.2 %grad_first.1 = bf16[16,144,128]{2,1,0:T(8,128)(2,1)S(1)} custom-call(s32[4]{0:T(128)S(1)} %pad_add_fusion.flags_ref, bf16[768,384]{1,0:T(8,128)(2,1)S(1)} %copies.1.x_ref, bf16[768,256]{1,0:T(8,128)(2,1)S(1)} %collective-permute-done.3.swapped_ref, bf16[16,48,128]{2,1,0:T(8,128)(2,1)S(1)} %get-tuple-element.50.done_ref, ...), custom_call_target="tpu_custom_call" | custom-call | flops 226492416 | bytes 1048576 | tf_op jit(solution)/shard_map/grad_first/pallas_call | solution.py:388
  57.9 0.0 copy-start
  57.9 18.1 %all_to_all.21.got_ref = bf16[16,144,128]{2,1,0:T(8,128)(2,1)S(1)} all-to-all(bf16[16,144,128]{2,1,0:T(8,128)(2,1)S(1)} %grad_first.1), channel_id=1, replica_groups=mesh['xh'=2,'y'=4,'xl'=2,'z'=16,'c'=2] {'xh','y','xl'}, dimensions={0} | all-to-all | bytes 1179648 | tf_op jit(solution)/shard_map/all_to_all | solution.py:547
  76.0 0.8 first_sum.1
  76.8 4.9 %all-to-all-start.3 = ((bf16[16,8,144]{2,1,0:T(8,128)(2,1)}), bf16[16,8,144]{2,1,0:T(8,128)(2,1)S(1)}, u32[]{:S(2)}, u32[]{:S(2)}) async-start(bf16[16,8,144]{2,1,0:T(8,128)(2,1)} %first_sum.1), calls=%async_computation.3 | async-start | bytes 131072 | tf_op jit(solution)/shard_map/all_to_all | solution.py:554
  81.7 0.0 copy-done
  81.7 1.9 %grad_input.1 = bf16[4,64,256]{2,1,0:T(8,128)(2,1)} custom-call(s32[4]{0:T(128)S(1)} %pad_add_fusion.flags_ref, bf16[768,256]{1,0:T(8,128)(2,1)S(1)} %grad_pre.1.pre_ref, bf16[768,256]{1,0:T(8,128)(2,1)S(1)} %collective-permute-done.3.swapped_ref, bf16[4,64,256]{2,1,0:T(8,128)(2,1)S(1)} %bitcast.18, bf16[3,3,256,256]{3,2,1,0:T(8,128)(2,1)S(1)} %copy-done), custom_call_target="tpu_custom_call" | custom-call | flops 452984832 | bytes 2097152 | tf_op jit(solution)/shard_map/grad_input/pallas_call | solution.py:388
  83.6 10.9 %all-to-all-done.3.got_ref = bf16[16,8,144]{2,1,0:T(8,128)(2,1)S(1)} async-done(((bf16[16,8,144]{2,1,0:T(8,128)(2,1)}), bf16[16,8,144]{2,1,0:T(8,128)(2,1)S(1)}, u32[]{:S(2)}, u32[]{:S(2)}) %all-to-all-start.3) | async-done | bytes 36896 | tf_op jit(solution)/shard_map/all_to_all | solution.py:554
  94.5 0.7 second_sum.1
  (4 shorter events, 0.0 us)
Async XLA Ops:
  3.3 22.8 %copy-start.1 = (bf16[1,4,1,64,256]{4,3,2,1,0:T(8,128)(2,1)S(1)}, bf16[1,4,1,64,256]{4,3,2,1,0:T(8,128)(2,1)}, u32[]{:S(2)}) copy-start(bf16[1,4,1,64,256]{4,3,2,1,0:T(8,128)(2,1)} %param.9) | copy-start | bytes 393220
  3.3 22.8 %copy-start.3 = (bf16[1,4,1,64,256]{4,3,2,1,0:T(8,128)(2,1)S(1)}, bf16[1,4,1,64,256]{4,3,2,1,0:T(8,128)(2,1)}, u32[]{:S(2)}) copy-start(bf16[1,4,1,64,256]{4,3,2,1,0:T(8,128)(2,1)} %param.8) | copy-start | bytes 393220
  3.3 22.8 %copy-start.4 = (bf16[1,4,1,64,256]{4,3,2,1,0:T(8,128)(2,1)S(1)}, bf16[1,4,1,64,256]{4,3,2,1,0:T(8,128)(2,1)}, u32[]{:S(2)}) copy-start(bf16[1,4,1,64,256]{4,3,2,1,0:T(8,128)(2,1)} %param.7) | copy-start | bytes 393220
  3.4 22.8 %copy-start.5 = (s32[4,4]{1,0:T(4,128)S(1)}, s32[4,4]{1,0:T(4,128)}, u32[]{:S(2)}) copy-start(s32[4,4]{1,0:T(4,128)} %seams_ref.3) | copy-start | bytes 196
  3.4 22.8 %copy-start.6 = (s32[4,4]{1,0:T(4,128)S(1)}, s32[4,4]{1,0:T(4,128)}, u32[]{:S(2)}) copy-start(s32[4,4]{1,0:T(4,128)} %corners_ref.1) | copy-start | bytes 196
  19.9 12.0 %all-to-all-start.1 = ((bf16[8,64,256]{2,1,0:T(8,128)(2,1)}), bf16[8,64,256]{2,1,0:T(8,128)(2,1)S(1)}, u32[]{:S(2)}, u32[]{:S(2)}) async-start(bf16[8,64,256]{2,1,0:T(8,128)(2,1)} %pick.1), calls=%async_computation.1 | async-start | bytes 524288 | tf_op jit(solution)/shard_map/all_to_all | solution.py:454
  26.1 19.2 %copy-start.2 = (bf16[3,3,256,256]{3,2,1,0:T(8,128)(2,1)S(1)}, bf16[3,3,256,256]{3,2,1,0:T(8,128)(2,1)}, u32[]{:S(2)}) copy-start(bf16[3,3,256,256]{3,2,1,0:T(8,128)(2,1)} %weight_ref.4) | copy-start | bytes 3538948
  27.3 3.3 %collective-permute-start = (bf16[400,256]{1,0:T(8,128)(2,1)S(1)}, bf16[400,256]{1,0:T(8,128)(2,1)S(1)}, u32[]{:S(2)}, u32[]{:S(2)}) collective-permute-start(bf16[400,256]{1,0:T(8,128)(2,1)S(1)} %get-tuple-element.34), channel_id=1, source_target_pairs={{0,1},{1,0},{2,3},{3,2},{4,5},{5,4},{6,7},{7,6},{8,9},{9,8},{10,11... | collective-permute-start | bytes 614408 | tf_op jit(solution)/shard_map/ppermute | solution.py:437
  32.5 19.2 %collective-permute-start.1 = (bf16[544,256]{1,0:T(8,128)(2,1)S(1)}, bf16[544,256]{1,0:T(8,128)(2,1)S(1)}, u32[]{:S(2)}, u32[]{:S(2)}) collective-permute-start(bf16[544,256]{1,0:T(8,128)(2,1)S(1)} %get-tuple-element.36), channel_id=1, source_target_pairs={{63,0},{2,1},{1,2},{4,3},{3,4},{6,5},{5,6},{8,7},{7,8},{10,9},{9,1... | collective-permute-start | bytes 835592 | tf_op jit(solution)/shard_map/ppermute | solution.py:480
  42.6 9.1 %collective-permute-start.2 = (bf16[272,256]{1,0:T(8,128)(2,1)S(1)}, bf16[272,256]{1,0:T(8,128)(2,1)S(1)}, u32[]{:S(2)}, u32[]{:S(2)}) collective-permute-start(bf16[272,256]{1,0:T(8,128)(2,1)S(1)} %get-tuple-element.37), channel_id=1, source_target_pairs={{62,0},{3,1},{0,2},{5,3},{2,4},{7,5},{4,6},{9,7},{6,8},{11,9},{8,1... | collective-permute-start | bytes 417800 | tf_op jit(solution)/shard_map/ppermute | solution.py:481
  53.1 3.6 %collective-permute-start.3 = (bf16[768,256]{1,0:T(8,128)(2,1)S(1)}, bf16[768,256]{1,0:T(8,128)(2,1)S(1)}, u32[]{:S(2)}, u32[]{:S(2)}) collective-permute-start(bf16[768,256]{1,0:T(8,128)(2,1)S(1)} %grad_pre.1.pre_ref), channel_id=1, source_target_pairs={{0,1},{1,0},{2,3},{3,2},{4,5},{5,4},{6,7},{7,6},{8,9},{9,8},{10,11... | collective-permute-start | bytes 1179656 | tf_op jit(solution)/shard_map/ppermute | solution.py:437
  57.9 23.8 %copy-start = (bf16[3,3,256,256]{3,2,1,0:T(8,128)(2,1)S(1)}, bf16[3,3,256,256]{3,2,1,0:T(8,128)(2,1)}, u32[]{:S(2)}) copy-start(bf16[3,3,256,256]{3,2,1,0:T(8,128)(2,1)} %weight_ref.5) | copy-start | bytes 3538948
  76.8 17.7 %all-to-all-start.3 = ((bf16[16,8,144]{2,1,0:T(8,128)(2,1)}), bf16[16,8,144]{2,1,0:T(8,128)(2,1)S(1)}, u32[]{:S(2)}, u32[]{:S(2)}) async-start(bf16[16,8,144]{2,1,0:T(8,128)(2,1)} %first_sum.1), calls=%async_computation.3 | async-start | bytes 131072 | tf_op jit(solution)/shard_map/all_to_all | solution.py:554

commit v12 on v11

--- a/solution.py
+++ b/solution.py
@@ -29,8 +29,9 @@
 
 def pack_kernel(local, side, blocks, seams_ref, g_hbm, p_hbm, out_hbm, g_ref, p_ref, out_ref, sems, out_sems):
     fetches = [
-        pltpu.make_async_copy(g_hbm, g_ref, sems.at[0]),
-        pltpu.make_async_copy(p_hbm, p_ref, sems.at[1]),
+        pltpu.make_async_copy(source.at[face], into.at[face], sems.at[which, face])
+        for face in range(local)
+        for which, (source, into) in enumerate(((g_hbm, g_ref), (p_hbm, p_ref)))
     ]
     for fetch in fetches:
         fetch.start()
@@ -426,7 +427,7 @@
             pltpu.VMEM((local, side, channels), bf),
             pltpu.VMEM((local, side, channels), bf),
             pltpu.VMEM((nface, local * (count + CELLS), channels), bf),
-            pltpu.SemaphoreType.DMA((2,)),
+            pltpu.SemaphoreType.DMA((2, local)),
             pltpu.SemaphoreType.DMA((nface,)),
         ),
         "pack",

time: 96.5 us -> 96.5 us (level)
  no operation moved by 1% of the time
where the time goes in v12:
time: 96.5 us; the launch traced here: 95.2 us
  blocking collectives  33 us (34%)
  starting transfers between devices  26.9 us (28%)
  waiting for transfers between devices  19.2 us (20%)
  Pallas kernels  14.9 us (15%)
    all_to_all x1, blocking collectives, on_device(): got = lax.all_to_all(parts, FACE + ('xl',), 0, 0, tiled=True)  18.1 us
    all_to_all x1, blocking collectives, on_device(): table = lax.all_to_all(sent, FACE, 0, 0, tiled=True)  14.9 us
    pallas_call x12, Pallas kernels, kernel(): pl.pallas_call(body, out_shape=out_shape, in_specs=[pl.BlockSpec(memory_s...  14.9 us
    all_to_all x1, waiting for transfers between devices, on_device(): got = lax.all_to_all(total, 'z', 0, 0, tiled=True)  10.9 us
    ppermute x1, starting transfers between devices, on_device(): near = lax.ppermute(near, TILE, pairs(1))  10.1 us
    all_to_all x1, starting transfers between devices, on_device(): wrapped = lax.all_to_all(picked, FACE, 0, 0, tiled=True)  6.19 us
    ppermute x1, waiting for transfers between devices, on_device(): far = lax.ppermute(far, TILE, pairs(2))  4.99 us
    all_to_all x1, starting transfers between devices, on_device(): got = lax.all_to_all(total, 'z', 0, 0, tiled=True)  4.9 us
  transfers between devices with their start and end apart: 6, of which 5 were waited for; matrix products, arithmetic and copies ran while one was open for 0% of the time, Pallas kernels for 7%

profile of v12, /device:TPU:6, one launch (start us, length us, event | category | flops | bytes accessed | tf_op | source)
XLA Modules:
  0.0 95.2 jit_solution(17925032725036216845)
XLA Ops:
  0.7 2.6 %pack.1 = bf16[8,96,256]{2,1,0:T(8,128)(2,1)} custom-call(s32[4,4]{1,0:T(4,128)} %seams_ref.3, bf16[4,64,256]{2,1,0:T(8,128)(2,1)} %bitcast.16, bf16[4,64,256]{2,1,0:T(8,128)(2,1)} %bitcast.19), custom_call_target="tpu_custom_call" | custom-call | bytes 1048576 | tf_op jit(solution)/shard_map/pack/pallas_call | solution.py:389
  3.3 0.0 copy-start.1
  3.3 0.0 copy-start.3
  3.3 0.0 copy-start.4
  3.3 0.0 copy-start.5
  3.3 0.0 copy-start.6
  3.3 0.1 pad_add_fusion.flags_ref
  3.4 14.9 %all_to_all.20.table_ref = bf16[8,96,256]{2,1,0:T(8,128)(2,1)S(1)} all-to-all(bf16[8,96,256]{2,1,0:T(8,128)(2,1)} %pack.1), channel_id=1, replica_groups=mesh['xh'=2,'y'=4,'xl'=2,'z'=16,'c'=2] {'xh','y'}, dimensions={0} | all-to-all | bytes 786432 | tf_op jit(solution)/shard_map/all_to_all | solution.py:440
  18.4 0.1 copy.11
  18.5 1.4 %pick.1 = bf16[8,64,256]{2,1,0:T(8,128)(2,1)} custom-call(s32[32]{0:T(128)S(1)} %fusion.want_ref, bf16[8,96,256]{2,1,0:T(8,128)(2,1)S(1)} %all_to_all.20.table_ref), custom_call_target="tpu_custom_call" | custom-call | bytes 1048576 | tf_op jit(solution)/shard_map/pick/pallas_call | solution.py:389
  19.9 6.2 %all-to-all-start.1 = ((bf16[8,64,256]{2,1,0:T(8,128)(2,1)}), bf16[8,64,256]{2,1,0:T(8,128)(2,1)S(1)}, u32[]{:S(2)}, u32[]{:S(2)}) async-start(bf16[8,64,256]{2,1,0:T(8,128)(2,1)} %pick.1), calls=%async_computation.1 | async-start | bytes 524288 | tf_op jit(solution)/shard_map/all_to_all | solution.py:455
  26.1 0.0 copy-start.2
  26.1 0.0 copy-done.1
  26.1 0.0 copy-done.3
  26.1 0.0 copy-done.4
  26.1 0.0 copy-done.5
  26.1 0.0 copy-done.6
  26.1 1.1 %border.1 = (bf16[544,256]{1,0:T(8,128)(2,1)S(1)}, bf16[32,256]{1,0:T(8,128)(2,1)S(1)}, bf16[400,256]{1,0:T(8,128)(2,1)S(1)}, bf16[256,128]{1,0:T(8,128)(2,1)S(1)}) custom-call(s32[4]{0:T(128)S(1)} %pad_add_fusion.flags_ref, s32[4,4]{1,0:T(4,128)S(1)} %copy-done.5, s32[4,4]{1,0:T(4,128)S(1)} %copy-done.6, bf16[8,96,256]{2,1,0:T(8,128)(2,1)S(1)} %all_to_all.20.table_ref, ...), custom_call_target="tpu_custom_call" | custom-call | bytes 1048576 | tf_op jit(solution)/shard_map/border/pallas_call | solution.py:389
  27.2 1.9 %collective-permute-start = (bf16[400,256]{1,0:T(8,128)(2,1)S(1)}, bf16[400,256]{1,0:T(8,128)(2,1)S(1)}, u32[]{:S(2)}, u32[]{:S(2)}) collective-permute-start(bf16[400,256]{1,0:T(8,128)(2,1)S(1)} %get-tuple-element.34), channel_id=1, source_target_pairs={{0,1},{1,0},{2,3},{3,2},{4,5},{5,4},{6,7},{7,6},{8,9},{9,8},{10,11... | collective-permute-start | bytes 614408 | tf_op jit(solution)/shard_map/ppermute | solution.py:438
  29.1 1.4 %collective-permute-done.part_ref = bf16[400,256]{1,0:T(8,128)(2,1)S(1)} collective-permute-done((bf16[400,256]{1,0:T(8,128)(2,1)S(1)}, bf16[400,256]{1,0:T(8,128)(2,1)S(1)}, u32[]{:S(2)}, u32[]{:S(2)}) %collective-permute-start) | collective-permute-done | bytes 204832 | tf_op jit(solution)/shard_map/ppermute | solution.py:438
  30.6 1.3 %all-to-all-done.1.pieces_ref = bf16[8,64,256]{2,1,0:T(8,128)(2,1)S(1)} async-done(((bf16[8,64,256]{2,1,0:T(8,128)(2,1)}), bf16[8,64,256]{2,1,0:T(8,128)(2,1)S(1)}, u32[]{:S(2)}, u32[]{:S(2)}) %all-to-all-start.1) | async-done | bytes 262176 | tf_op jit(solution)/shard_map/all_to_all | solution.py:455
  31.9 0.6 send.1
  32.5 10.1 %collective-permute-start.1 = (bf16[544,256]{1,0:T(8,128)(2,1)S(1)}, bf16[544,256]{1,0:T(8,128)(2,1)S(1)}, u32[]{:S(2)}, u32[]{:S(2)}) collective-permute-start(bf16[544,256]{1,0:T(8,128)(2,1)S(1)} %get-tuple-element.36), channel_id=1, source_target_pairs={{63,0},{2,1},{1,2},{4,3},{3,4},{6,5},{5,6},{8,7},{7,8},{10,9},{9,1... | collective-permute-start | bytes 835592 | tf_op jit(solution)/shard_map/ppermute | solution.py:481
  42.6 1.9 %collective-permute-start.2 = (bf16[272,256]{1,0:T(8,128)(2,1)S(1)}, bf16[272,256]{1,0:T(8,128)(2,1)S(1)}, u32[]{:S(2)}, u32[]{:S(2)}) collective-permute-start(bf16[272,256]{1,0:T(8,128)(2,1)S(1)} %get-tuple-element.37), channel_id=1, source_target_pairs={{62,0},{3,1},{0,2},{5,3},{2,4},{7,5},{4,6},{9,7},{6,8},{11,9},{8,1... | collective-permute-start | bytes 417800 | tf_op jit(solution)/shard_map/ppermute | solution.py:482
  44.5 0.8 copies.1.x_ref
  45.3 0.0 copy-done.2
  45.3 1.4 %near_half.1 = (f32[768,256]{1,0:T(8,128)S(1)}, f32[384,256]{1,0:T(8,128)S(1)}) custom-call(s32[4]{0:T(128)S(1)} %pad_add_fusion.flags_ref, bf16[544,256]{1,0:T(8,128)(2,1)S(1)} %get-tuple-element.31.own_ref, bf16[400,256]{1,0:T(8,128)(2,1)S(1)} %collective-permute-done.part_ref, bf16[3,3,256,256]{3,2,1,0:T(8,128)(2,1)S(1)} %copy-done.2), custom_call_target="tpu_custom_call" | custom-call | flops 452984832 | bytes 2097152 | tf_op jit(solution)/shard_map/near_half/pallas_call | solution.py:389
  46.6 5.0 %collective-permute-done.2.far_ref = bf16[272,256]{1,0:T(8,128)(2,1)S(1)} collective-permute-done((bf16[272,256]{1,0:T(8,128)(2,1)S(1)}, bf16[272,256]{1,0:T(8,128)(2,1)S(1)}, u32[]{:S(2)}, u32[]{:S(2)}) %collective-permute-start.2) | collective-permute-done | bytes 139296 | tf_op jit(solution)/shard_map/ppermute | solution.py:482
  51.6 0.0 collective-permute-done.1.near_ref
  51.6 1.4 %grad_pre.1.pre_ref = bf16[768,256]{1,0:T(8,128)(2,1)S(1)} custom-call(s32[4]{0:T(128)S(1)} %pad_add_fusion.flags_ref, bf16[544,256]{1,0:T(8,128)(2,1)S(1)} %collective-permute-done.1.near_ref, bf16[272,256]{1,0:T(8,128)(2,1)S(1)} %collective-permute-done.2.far_ref, f32[768,256]{1,0:T(8,128)S(1)} %get-tuple-element.44.hidden_ref, ...), custom_call_target="tpu_custom_call" | custom-call | flops 452984832 | bytes 4194304 | tf_op jit(solution)/shard_map/grad_pre/pallas_call | solution.py:389
  53.0 1.9 %collective-permute-start.3 = (bf16[768,256]{1,0:T(8,128)(2,1)S(1)}, bf16[768,256]{1,0:T(8,128)(2,1)S(1)}, u32[]{:S(2)}, u32[]{:S(2)}) collective-permute-start(bf16[768,256]{1,0:T(8,128)(2,1)S(1)} %grad_pre.1.pre_ref), channel_id=1, source_target_pairs={{0,1},{1,0},{2,3},{3,2},{4,5},{5,4},{6,7},{7,6},{8,9},{9,8},{10,11... | collective-permute-start | bytes 1179656 | tf_op jit(solution)/shard_map/ppermute | solution.py:438
  55.0 1.2 %first_half.1 = (bf16[16,48,128]{2,1,0:T(8,128)(2,1)S(1)}, f32[256,384]{1,0:T(8,128)S(1)}) custom-call(s32[4]{0:T(128)S(1)} %pad_add_fusion.flags_ref, bf16[768,384]{1,0:T(8,128)(2,1)S(1)} %copies.1.x_ref, bf16[768,256]{1,0:T(8,128)(2,1)S(1)} %grad_pre.1.pre_ref), custom_call_target="tpu_custom_call" | custom-call | bytes 1048576 | tf_op jit(solution)/shard_map/first_half/pallas_call | solution.py:389
  56.1 0.5 collective-permute-done.3.swapped_ref
  56.7 1.2 %grad_first.1 = bf16[16,144,128]{2,1,0:T(8,128)(2,1)S(1)} custom-call(s32[4]{0:T(128)S(1)} %pad_add_fusion.flags_ref, bf16[768,384]{1,0:T(8,128)(2,1)S(1)} %copies.1.x_ref, bf16[768,256]{1,0:T(8,128)(2,1)S(1)} %collective-permute-done.3.swapped_ref, bf16[16,48,128]{2,1,0:T(8,128)(2,1)S(1)} %get-tuple-element.50.done_ref, ...), custom_call_target="tpu_custom_call" | custom-call | flops 226492416 | bytes 1048576 | tf_op jit(solution)/shard_map/grad_first/pallas_call | solution.py:389
  57.8 0.0 copy-start
  57.9 18.1 %all_to_all.21.got_ref = bf16[16,144,128]{2,1,0:T(8,128)(2,1)S(1)} all-to-all(bf16[16,144,128]{2,1,0:T(8,128)(2,1)S(1)} %grad_first.1), channel_id=1, replica_groups=mesh['xh'=2,'y'=4,'xl'=2,'z'=16,'c'=2] {'xh','y','xl'}, dimensions={0} | all-to-all | bytes 1179648 | tf_op jit(solution)/shard_map/all_to_all | solution.py:548
  76.0 0.8 first_sum.1
  76.8 4.9 %all-to-all-start.3 = ((bf16[16,8,144]{2,1,0:T(8,128)(2,1)}), bf16[16,8,144]{2,1,0:T(8,128)(2,1)S(1)}, u32[]{:S(2)}, u32[]{:S(2)}) async-start(bf16[16,8,144]{2,1,0:T(8,128)(2,1)} %first_sum.1), calls=%async_computation.3 | async-start | bytes 131072 | tf_op jit(solution)/shard_map/all_to_all | solution.py:555
  81.7 0.0 copy-done
  81.7 1.9 %grad_input.1 = bf16[4,64,256]{2,1,0:T(8,128)(2,1)} custom-call(s32[4]{0:T(128)S(1)} %pad_add_fusion.flags_ref, bf16[768,256]{1,0:T(8,128)(2,1)S(1)} %grad_pre.1.pre_ref, bf16[768,256]{1,0:T(8,128)(2,1)S(1)} %collective-permute-done.3.swapped_ref, bf16[4,64,256]{2,1,0:T(8,128)(2,1)S(1)} %bitcast.18, bf16[3,3,256,256]{3,2,1,0:T(8,128)(2,1)S(1)} %copy-done), custom_call_target="tpu_custom_call" | custom-call | flops 452984832 | bytes 2097152 | tf_op jit(solution)/shard_map/grad_input/pallas_call | solution.py:389
  83.6 10.9 %all-to-all-done.3.got_ref = bf16[16,8,144]{2,1,0:T(8,128)(2,1)S(1)} async-done(((bf16[16,8,144]{2,1,0:T(8,128)(2,1)}), bf16[16,8,144]{2,1,0:T(8,128)(2,1)S(1)}, u32[]{:S(2)}, u32[]{:S(2)}) %all-to-all-start.3) | async-done | bytes 36896 | tf_op jit(solution)/shard_map/all_to_all | solution.py:555
  94.5 0.7 second_sum.1
  (4 shorter events, 0.0 us)
Async XLA Ops:
  3.3 22.8 %copy-start.1 = (bf16[1,4,1,64,256]{4,3,2,1,0:T(8,128)(2,1)S(1)}, bf16[1,4,1,64,256]{4,3,2,1,0:T(8,128)(2,1)}, u32[]{:S(2)}) copy-start(bf16[1,4,1,64,256]{4,3,2,1,0:T(8,128)(2,1)} %param.9) | copy-start | bytes 393220
  3.3 22.8 %copy-start.3 = (bf16[1,4,1,64,256]{4,3,2,1,0:T(8,128)(2,1)S(1)}, bf16[1,4,1,64,256]{4,3,2,1,0:T(8,128)(2,1)}, u32[]{:S(2)}) copy-start(bf16[1,4,1,64,256]{4,3,2,1,0:T(8,128)(2,1)} %param.8) | copy-start | bytes 393220
  3.3 22.8 %copy-start.4 = (bf16[1,4,1,64,256]{4,3,2,1,0:T(8,128)(2,1)S(1)}, bf16[1,4,1,64,256]{4,3,2,1,0:T(8,128)(2,1)}, u32[]{:S(2)}) copy-start(bf16[1,4,1,64,256]{4,3,2,1,0:T(8,128)(2,1)} %param.7) | copy-start | bytes 393220
  3.3 22.8 %copy-start.5 = (s32[4,4]{1,0:T(4,128)S(1)}, s32[4,4]{1,0:T(4,128)}, u32[]{:S(2)}) copy-start(s32[4,4]{1,0:T(4,128)} %seams_ref.3) | copy-start | bytes 196
  3.3 22.8 %copy-start.6 = (s32[4,4]{1,0:T(4,128)S(1)}, s32[4,4]{1,0:T(4,128)}, u32[]{:S(2)}) copy-start(s32[4,4]{1,0:T(4,128)} %corners_ref.1) | copy-start | bytes 196
  19.9 12.0 %all-to-all-start.1 = ((bf16[8,64,256]{2,1,0:T(8,128)(2,1)}), bf16[8,64,256]{2,1,0:T(8,128)(2,1)S(1)}, u32[]{:S(2)}, u32[]{:S(2)}) async-start(bf16[8,64,256]{2,1,0:T(8,128)(2,1)} %pick.1), calls=%async_computation.1 | async-start | bytes 524288 | tf_op jit(solution)/shard_map/all_to_all | solution.py:455
  26.1 19.2 %copy-start.2 = (bf16[3,3,256,256]{3,2,1,0:T(8,128)(2,1)S(1)}, bf16[3,3,256,256]{3,2,1,0:T(8,128)(2,1)}, u32[]{:S(2)}) copy-start(bf16[3,3,256,256]{3,2,1,0:T(8,128)(2,1)} %weight_ref.4) | copy-start | bytes 3538948
  27.2 3.3 %collective-permute-start = (bf16[400,256]{1,0:T(8,128)(2,1)S(1)}, bf16[400,256]{1,0:T(8,128)(2,1)S(1)}, u32[]{:S(2)}, u32[]{:S(2)}) collective-permute-start(bf16[400,256]{1,0:T(8,128)(2,1)S(1)} %get-tuple-element.34), channel_id=1, source_target_pairs={{0,1},{1,0},{2,3},{3,2},{4,5},{5,4},{6,7},{7,6},{8,9},{9,8},{10,11... | collective-permute-start | bytes 614408 | tf_op jit(solution)/shard_map/ppermute | solution.py:438
  32.5 19.2 %collective-permute-start.1 = (bf16[544,256]{1,0:T(8,128)(2,1)S(1)}, bf16[544,256]{1,0:T(8,128)(2,1)S(1)}, u32[]{:S(2)}, u32[]{:S(2)}) collective-permute-start(bf16[544,256]{1,0:T(8,128)(2,1)S(1)} %get-tuple-element.36), channel_id=1, source_target_pairs={{63,0},{2,1},{1,2},{4,3},{3,4},{6,5},{5,6},{8,7},{7,8},{10,9},{9,1... | collective-permute-start | bytes 835592 | tf_op jit(solution)/shard_map/ppermute | solution.py:481
  42.6 9.1 %collective-permute-start.2 = (bf16[272,256]{1,0:T(8,128)(2,1)S(1)}, bf16[272,256]{1,0:T(8,128)(2,1)S(1)}, u32[]{:S(2)}, u32[]{:S(2)}) collective-permute-start(bf16[272,256]{1,0:T(8,128)(2,1)S(1)} %get-tuple-element.37), channel_id=1, source_target_pairs={{62,0},{3,1},{0,2},{5,3},{2,4},{7,5},{4,6},{9,7},{6,8},{11,9},{8,1... | collective-permute-start | bytes 417800 | tf_op jit(solution)/shard_map/ppermute | solution.py:482
  53.0 3.6 %collective-permute-start.3 = (bf16[768,256]{1,0:T(8,128)(2,1)S(1)}, bf16[768,256]{1,0:T(8,128)(2,1)S(1)}, u32[]{:S(2)}, u32[]{:S(2)}) collective-permute-start(bf16[768,256]{1,0:T(8,128)(2,1)S(1)} %grad_pre.1.pre_ref), channel_id=1, source_target_pairs={{0,1},{1,0},{2,3},{3,2},{4,5},{5,4},{6,7},{7,6},{8,9},{9,8},{10,11... | collective-permute-start | bytes 1179656 | tf_op jit(solution)/shard_map/ppermute | solution.py:438
  57.8 23.8 %copy-start = (bf16[3,3,256,256]{3,2,1,0:T(8,128)(2,1)S(1)}, bf16[3,3,256,256]{3,2,1,0:T(8,128)(2,1)}, u32[]{:S(2)}) copy-start(bf16[3,3,256,256]{3,2,1,0:T(8,128)(2,1)} %weight_ref.5) | copy-start | bytes 3538948
  76.8 17.7 %all-to-all-start.3 = ((bf16[16,8,144]{2,1,0:T(8,128)(2,1)}), bf16[16,8,144]{2,1,0:T(8,128)(2,1)S(1)}, u32[]{:S(2)}, u32[]{:S(2)}) async-start(bf16[16,8,144]{2,1,0:T(8,128)(2,1)} %first_sum.1), calls=%async_computation.3 | async-start | bytes 131072 | tf_op jit(solution)/shard_map/all_to_all | solution.py:555

commit v13 on v12

--- a/solution.py
+++ b/solution.py
@@ -412,7 +412,7 @@
     top = tile >= ntile // 2
     near_wraps = (tile == 0) | (tile == ntile - 1)
     far_wraps = (tile == 1) | (tile == ntile - 2)
-    flags = jnp.stack([core, *(flag.astype(jnp.int32) for flag in (near_wraps, far_wraps, ~top))])
+    marks = [core, *(flag.astype(jnp.int32) for flag in (near_wraps, far_wraps, ~top))]
 
     px_blocks = 4
     ch_blocks = nface // px_blocks
@@ -436,8 +436,9 @@
         out_hbm=True,
     )
     swap = lambda a: lax.ppermute(a, "c", [(0, 1), (1, 0)])
-    sent, flags, top = lax.optimization_barrier((sent, flags, top))
-    table = lax.all_to_all(sent, FACE, 0, 0, tiled=True)
+    sent, marks, top = lax.optimization_barrier((sent, marks, top))
+    table, marks = lax.optimization_barrier((lax.all_to_all(sent, FACE, 0, 0, tiled=True), marks))
+    flags = jnp.stack(marks)
 
     cells = table[:, local * count :].reshape(faces, CELLS, channels)
     all_seams = cells[:, SEAM_AT, :4].astype(jnp.int32)

time: 96.5 us -> 96.5 us (level)
  no operation moved by 1% of the time
where the time goes in v13:
time: 96.5 us; the launch traced here: 95.1 us
  blocking collectives  33 us (34%)
  starting transfers between devices  27 us (28%)
  waiting for transfers between devices  19.1 us (20%)
  Pallas kernels  14.9 us (15%)
    all_to_all x1, blocking collectives, on_device(): got = lax.all_to_all(parts, FACE + ('xl',), 0, 0, tiled=True)  18.1 us
    all_to_all x1, blocking collectives, on_device(): lax.all_to_all(sent, FACE, 0, 0, tiled=True)  14.9 us
    pallas_call x12, Pallas kernels, kernel(): pl.pallas_call(body, out_shape=out_shape, in_specs=[pl.BlockSpec(memory_s...  14.9 us
    all_to_all x1, waiting for transfers between devices, on_device(): got = lax.all_to_all(total, 'z', 0, 0, tiled=True)  10.9 us
    ppermute x1, starting transfers between devices, on_device(): near = lax.ppermute(near, TILE, pairs(1))  10.2 us
    all_to_all x1, starting transfers between devices, on_device(): wrapped = lax.all_to_all(picked, FACE, 0, 0, tiled=True)  6.19 us
    ppermute x1, waiting for transfers between devices, on_device(): far = lax.ppermute(far, TILE, pairs(2))  4.97 us
    all_to_all x1, starting transfers between devices, on_device(): got = lax.all_to_all(total, 'z', 0, 0, tiled=True)  4.9 us
  transfers between devices with their start and end apart: 6, of which 5 were waited for; matrix products, arithmetic and copies ran while one was open for 0% of the time, Pallas kernels for 7%

profile of v13, /device:TPU:6, one launch (start us, length us, event | category | flops | bytes accessed | tf_op | source)
XLA Modules:
  0.0 95.1 jit_solution(12090234370390166763)
XLA Ops:
  0.7 2.6 %pack.1 = bf16[8,96,256]{2,1,0:T(8,128)(2,1)} custom-call(s32[4,4]{1,0:T(4,128)} %seams_ref.3, bf16[4,64,256]{2,1,0:T(8,128)(2,1)} %bitcast.16, bf16[4,64,256]{2,1,0:T(8,128)(2,1)} %bitcast.19), custom_call_target="tpu_custom_call" | custom-call | bytes 1048576 | tf_op jit(solution)/shard_map/pack/pallas_call | solution.py:389
  3.3 0.0 copy-start.1
  3.3 0.0 copy-start.3
  3.3 0.0 copy-start.4
  3.3 0.0 copy-start.5
  3.3 0.0 copy-start.6
  3.3 14.9 %all_to_all.20.table_ref = bf16[8,96,256]{2,1,0:T(8,128)(2,1)S(1)} all-to-all(bf16[8,96,256]{2,1,0:T(8,128)(2,1)} %pack.1), channel_id=1, replica_groups=mesh['xh'=2,'y'=4,'xl'=2,'z'=16,'c'=2] {'xh','y'}, dimensions={0} | all-to-all | bytes 786432 | tf_op jit(solution)/shard_map/all_to_all | solution.py:440
  18.3 0.1 copy.11
  18.4 1.4 %pick.1 = bf16[8,64,256]{2,1,0:T(8,128)(2,1)} custom-call(s32[32]{0:T(128)S(1)} %fusion.want_ref, bf16[8,96,256]{2,1,0:T(8,128)(2,1)S(1)} %all_to_all.20.table_ref), custom_call_target="tpu_custom_call" | custom-call | bytes 1048576 | tf_op jit(solution)/shard_map/pick/pallas_call | solution.py:389
  19.8 6.2 %all-to-all-start.1 = ((bf16[8,64,256]{2,1,0:T(8,128)(2,1)}), bf16[8,64,256]{2,1,0:T(8,128)(2,1)S(1)}, u32[]{:S(2)}, u32[]{:S(2)}) async-start(bf16[8,64,256]{2,1,0:T(8,128)(2,1)} %pick.1), calls=%async_computation.1 | async-start | bytes 524288 | tf_op jit(solution)/shard_map/all_to_all | solution.py:456
  26.0 0.0 copy-start.2
  26.0 0.1 pad_add_fusion.flags_ref
  26.1 0.0 copy-done.1
  26.1 0.0 copy-done.3
  26.1 0.0 copy-done.4
  26.1 0.0 copy-done.5
  26.1 0.0 copy-done.6
  26.1 1.1 %border.1 = (bf16[544,256]{1,0:T(8,128)(2,1)S(1)}, bf16[32,256]{1,0:T(8,128)(2,1)S(1)}, bf16[400,256]{1,0:T(8,128)(2,1)S(1)}, bf16[256,128]{1,0:T(8,128)(2,1)S(1)}) custom-call(s32[4]{0:T(128)S(1)} %pad_add_fusion.flags_ref, s32[4,4]{1,0:T(4,128)S(1)} %copy-done.5, s32[4,4]{1,0:T(4,128)S(1)} %copy-done.6, bf16[8,96,256]{2,1,0:T(8,128)(2,1)S(1)} %all_to_all.20.table_ref, ...), custom_call_target="tpu_custom_call" | custom-call | bytes 1048576 | tf_op jit(solution)/shard_map/border/pallas_call | solution.py:389
  27.2 1.9 %collective-permute-start = (bf16[400,256]{1,0:T(8,128)(2,1)S(1)}, bf16[400,256]{1,0:T(8,128)(2,1)S(1)}, u32[]{:S(2)}, u32[]{:S(2)}) collective-permute-start(bf16[400,256]{1,0:T(8,128)(2,1)S(1)} %get-tuple-element.50), channel_id=1, source_target_pairs={{0,1},{1,0},{2,3},{3,2},{4,5},{5,4},{6,7},{7,6},{8,9},{9,8},{10,11... | collective-permute-start | bytes 614408 | tf_op jit(solution)/shard_map/ppermute | solution.py:438
  29.1 1.4 %collective-permute-done.part_ref = bf16[400,256]{1,0:T(8,128)(2,1)S(1)} collective-permute-done((bf16[400,256]{1,0:T(8,128)(2,1)S(1)}, bf16[400,256]{1,0:T(8,128)(2,1)S(1)}, u32[]{:S(2)}, u32[]{:S(2)}) %collective-permute-start) | collective-permute-done | bytes 204832 | tf_op jit(solution)/shard_map/ppermute | solution.py:438
  30.6 1.3 %all-to-all-done.1.pieces_ref = bf16[8,64,256]{2,1,0:T(8,128)(2,1)S(1)} async-done(((bf16[8,64,256]{2,1,0:T(8,128)(2,1)}), bf16[8,64,256]{2,1,0:T(8,128)(2,1)S(1)}, u32[]{:S(2)}, u32[]{:S(2)}) %all-to-all-start.1) | async-done | bytes 262176 | tf_op jit(solution)/shard_map/all_to_all | solution.py:456
  31.8 0.6 send.1
  32.4 10.2 %collective-permute-start.1 = (bf16[544,256]{1,0:T(8,128)(2,1)S(1)}, bf16[544,256]{1,0:T(8,128)(2,1)S(1)}, u32[]{:S(2)}, u32[]{:S(2)}) collective-permute-start(bf16[544,256]{1,0:T(8,128)(2,1)S(1)} %get-tuple-element.52), channel_id=1, source_target_pairs={{63,0},{2,1},{1,2},{4,3},{3,4},{6,5},{5,6},{8,7},{7,8},{10,9},{9,1... | collective-permute-start | bytes 835592 | tf_op jit(solution)/shard_map/ppermute | solution.py:482
  42.6 1.9 %collective-permute-start.2 = (bf16[272,256]{1,0:T(8,128)(2,1)S(1)}, bf16[272,256]{1,0:T(8,128)(2,1)S(1)}, u32[]{:S(2)}, u32[]{:S(2)}) collective-permute-start(bf16[272,256]{1,0:T(8,128)(2,1)S(1)} %get-tuple-element.53), channel_id=1, source_target_pairs={{62,0},{3,1},{0,2},{5,3},{2,4},{7,5},{4,6},{9,7},{6,8},{11,9},{8,1... | collective-permute-start | bytes 417800 | tf_op jit(solution)/shard_map/ppermute | solution.py:483
  44.5 0.8 copies.1.x_ref
  45.3 0.0 copy-done.2
  45.3 1.4 %near_half.1 = (f32[768,256]{1,0:T(8,128)S(1)}, f32[384,256]{1,0:T(8,128)S(1)}) custom-call(s32[4]{0:T(128)S(1)} %pad_add_fusion.flags_ref, bf16[544,256]{1,0:T(8,128)(2,1)S(1)} %get-tuple-element.47.own_ref, bf16[400,256]{1,0:T(8,128)(2,1)S(1)} %collective-permute-done.part_ref, bf16[3,3,256,256]{3,2,1,0:T(8,128)(2,1)S(1)} %copy-done.2), custom_call_target="tpu_custom_call" | custom-call | flops 452984832 | bytes 2097152 | tf_op jit(solution)/shard_map/near_half/pallas_call | solution.py:389
  46.7 5.0 %collective-permute-done.2.far_ref = bf16[272,256]{1,0:T(8,128)(2,1)S(1)} collective-permute-done((bf16[272,256]{1,0:T(8,128)(2,1)S(1)}, bf16[272,256]{1,0:T(8,128)(2,1)S(1)}, u32[]{:S(2)}, u32[]{:S(2)}) %collective-permute-start.2) | collective-permute-done | bytes 139296 | tf_op jit(solution)/shard_map/ppermute | solution.py:483
  51.6 0.0 collective-permute-done.1.near_ref
  51.6 1.4 %grad_pre.1.pre_ref = bf16[768,256]{1,0:T(8,128)(2,1)S(1)} custom-call(s32[4]{0:T(128)S(1)} %pad_add_fusion.flags_ref, bf16[544,256]{1,0:T(8,128)(2,1)S(1)} %collective-permute-done.1.near_ref, bf16[272,256]{1,0:T(8,128)(2,1)S(1)} %collective-permute-done.2.far_ref, f32[768,256]{1,0:T(8,128)S(1)} %get-tuple-element.60.hidden_ref, ...), custom_call_target="tpu_custom_call" | custom-call | flops 452984832 | bytes 4194304 | tf_op jit(solution)/shard_map/grad_pre/pallas_call | solution.py:389
  53.0 1.9 %collective-permute-start.3 = (bf16[768,256]{1,0:T(8,128)(2,1)S(1)}, bf16[768,256]{1,0:T(8,128)(2,1)S(1)}, u32[]{:S(2)}, u32[]{:S(2)}) collective-permute-start(bf16[768,256]{1,0:T(8,128)(2,1)S(1)} %grad_pre.1.pre_ref), channel_id=1, source_target_pairs={{0,1},{1,0},{2,3},{3,2},{4,5},{5,4},{6,7},{7,6},{8,9},{9,8},{10,11... | collective-permute-start | bytes 1179656 | tf_op jit(solution)/shard_map/ppermute | solution.py:438
  55.0 1.1 %first_half.1 = (bf16[16,48,128]{2,1,0:T(8,128)(2,1)S(1)}, f32[256,384]{1,0:T(8,128)S(1)}) custom-call(s32[4]{0:T(128)S(1)} %pad_add_fusion.flags_ref, bf16[768,384]{1,0:T(8,128)(2,1)S(1)} %copies.1.x_ref, bf16[768,256]{1,0:T(8,128)(2,1)S(1)} %grad_pre.1.pre_ref), custom_call_target="tpu_custom_call" | custom-call | bytes 1048576 | tf_op jit(solution)/shard_map/first_half/pallas_call | solution.py:389
  56.1 0.5 collective-permute-done.3.swapped_ref
  56.6 1.2 %grad_first.1 = bf16[16,144,128]{2,1,0:T(8,128)(2,1)S(1)} custom-call(s32[4]{0:T(128)S(1)} %pad_add_fusion.flags_ref, bf16[768,384]{1,0:T(8,128)(2,1)S(1)} %copies.1.x_ref, bf16[768,256]{1,0:T(8,128)(2,1)S(1)} %collective-permute-done.3.swapped_ref, bf16[16,48,128]{2,1,0:T(8,128)(2,1)S(1)} %get-tuple-element.66.done_ref, ...), custom_call_target="tpu_custom_call" | custom-call | flops 226492416 | bytes 1048576 | tf_op jit(solution)/shard_map/grad_first/pallas_call | solution.py:389
  57.8 0.0 copy-start
  57.8 18.1 %all_to_all.21.got_ref = bf16[16,144,128]{2,1,0:T(8,128)(2,1)S(1)} all-to-all(bf16[16,144,128]{2,1,0:T(8,128)(2,1)S(1)} %grad_first.1), channel_id=1, replica_groups=mesh['xh'=2,'y'=4,'xl'=2,'z'=16,'c'=2] {'xh','y','xl'}, dimensions={0} | all-to-all | bytes 1179648 | tf_op jit(solution)/shard_map/all_to_all | solution.py:549
  76.0 0.8 first_sum.1
  76.7 4.9 %all-to-all-start.3 = ((bf16[16,8,144]{2,1,0:T(8,128)(2,1)}), bf16[16,8,144]{2,1,0:T(8,128)(2,1)S(1)}, u32[]{:S(2)}, u32[]{:S(2)}) async-start(bf16[16,8,144]{2,1,0:T(8,128)(2,1)} %first_sum.1), calls=%async_computation.3 | async-start | bytes 131072 | tf_op jit(solution)/shard_map/all_to_all | solution.py:556
  81.7 0.0 copy-done
  81.7 1.9 %grad_input.1 = bf16[4,64,256]{2,1,0:T(8,128)(2,1)} custom-call(s32[4]{0:T(128)S(1)} %pad_add_fusion.flags_ref, bf16[768,256]{1,0:T(8,128)(2,1)S(1)} %grad_pre.1.pre_ref, bf16[768,256]{1,0:T(8,128)(2,1)S(1)} %collective-permute-done.3.swapped_ref, bf16[4,64,256]{2,1,0:T(8,128)(2,1)S(1)} %bitcast.18, bf16[3,3,256,256]{3,2,1,0:T(8,128)(2,1)S(1)} %copy-done), custom_call_target="tpu_custom_call" | custom-call | flops 452984832 | bytes 2097152 | tf_op jit(solution)/shard_map/grad_input/pallas_call | solution.py:389
  83.5 10.9 %all-to-all-done.3.got_ref = bf16[16,8,144]{2,1,0:T(8,128)(2,1)S(1)} async-done(((bf16[16,8,144]{2,1,0:T(8,128)(2,1)}), bf16[16,8,144]{2,1,0:T(8,128)(2,1)S(1)}, u32[]{:S(2)}, u32[]{:S(2)}) %all-to-all-start.3) | async-done | bytes 36896 | tf_op jit(solution)/shard_map/all_to_all | solution.py:556
  94.4 0.7 second_sum.1
  (4 shorter events, 0.0 us)
Async XLA Ops:
  3.3 22.8 %copy-start.1 = (bf16[1,4,1,64,256]{4,3,2,1,0:T(8,128)(2,1)S(1)}, bf16[1,4,1,64,256]{4,3,2,1,0:T(8,128)(2,1)}, u32[]{:S(2)}) copy-start(bf16[1,4,1,64,256]{4,3,2,1,0:T(8,128)(2,1)} %param.9) | copy-start | bytes 393220
  3.3 22.8 %copy-start.3 = (bf16[1,4,1,64,256]{4,3,2,1,0:T(8,128)(2,1)S(1)}, bf16[1,4,1,64,256]{4,3,2,1,0:T(8,128)(2,1)}, u32[]{:S(2)}) copy-start(bf16[1,4,1,64,256]{4,3,2,1,0:T(8,128)(2,1)} %param.8) | copy-start | bytes 393220
  3.3 22.8 %copy-start.4 = (bf16[1,4,1,64,256]{4,3,2,1,0:T(8,128)(2,1)S(1)}, bf16[1,4,1,64,256]{4,3,2,1,0:T(8,128)(2,1)}, u32[]{:S(2)}) copy-start(bf16[1,4,1,64,256]{4,3,2,1,0:T(8,128)(2,1)} %param.7) | copy-start | bytes 393220
  3.3 22.8 %copy-start.5 = (s32[4,4]{1,0:T(4,128)S(1)}, s32[4,4]{1,0:T(4,128)}, u32[]{:S(2)}) copy-start(s32[4,4]{1,0:T(4,128)} %seams_ref.3) | copy-start | bytes 196
  3.3 22.8 %copy-start.6 = (s32[4,4]{1,0:T(4,128)S(1)}, s32[4,4]{1,0:T(4,128)}, u32[]{:S(2)}) copy-start(s32[4,4]{1,0:T(4,128)} %corners_ref.1) | copy-start | bytes 196
  19.8 12.0 %all-to-all-start.1 = ((bf16[8,64,256]{2,1,0:T(8,128)(2,1)}), bf16[8,64,256]{2,1,0:T(8,128)(2,1)S(1)}, u32[]{:S(2)}, u32[]{:S(2)}) async-start(bf16[8,64,256]{2,1,0:T(8,128)(2,1)} %pick.1), calls=%async_computation.1 | async-start | bytes 524288 | tf_op jit(solution)/shard_map/all_to_all | solution.py:456
  26.0 19.3 %copy-start.2 = (bf16[3,3,256,256]{3,2,1,0:T(8,128)(2,1)S(1)}, bf16[3,3,256,256]{3,2,1,0:T(8,128)(2,1)}, u32[]{:S(2)}) copy-start(bf16[3,3,256,256]{3,2,1,0:T(8,128)(2,1)} %weight_ref.4) | copy-start | bytes 3538948
  27.2 3.3 %collective-permute-start = (bf16[400,256]{1,0:T(8,128)(2,1)S(1)}, bf16[400,256]{1,0:T(8,128)(2,1)S(1)}, u32[]{:S(2)}, u32[]{:S(2)}) collective-permute-start(bf16[400,256]{1,0:T(8,128)(2,1)S(1)} %get-tuple-element.50), channel_id=1, source_target_pairs={{0,1},{1,0},{2,3},{3,2},{4,5},{5,4},{6,7},{7,6},{8,9},{9,8},{10,11... | collective-permute-start | bytes 614408 | tf_op jit(solution)/shard_map/ppermute | solution.py:438
  32.4 19.2 %collective-permute-start.1 = (bf16[544,256]{1,0:T(8,128)(2,1)S(1)}, bf16[544,256]{1,0:T(8,128)(2,1)S(1)}, u32[]{:S(2)}, u32[]{:S(2)}) collective-permute-start(bf16[544,256]{1,0:T(8,128)(2,1)S(1)} %get-tuple-element.52), channel_id=1, source_target_pairs={{63,0},{2,1},{1,2},{4,3},{3,4},{6,5},{5,6},{8,7},{7,8},{10,9},{9,1... | collective-permute-start | bytes 835592 | tf_op jit(solution)/shard_map/ppermute | solution.py:482
  42.6 9.1 %collective-permute-start.2 = (bf16[272,256]{1,0:T(8,128)(2,1)S(1)}, bf16[272,256]{1,0:T(8,128)(2,1)S(1)}, u32[]{:S(2)}, u32[]{:S(2)}) collective-permute-start(bf16[272,256]{1,0:T(8,128)(2,1)S(1)} %get-tuple-element.53), channel_id=1, source_target_pairs={{62,0},{3,1},{0,2},{5,3},{2,4},{7,5},{4,6},{9,7},{6,8},{11,9},{8,1... | collective-permute-start | bytes 417800 | tf_op jit(solution)/shard_map/ppermute | solution.py:483
  53.0 3.6 %collective-permute-start.3 = (bf16[768,256]{1,0:T(8,128)(2,1)S(1)}, bf16[768,256]{1,0:T(8,128)(2,1)S(1)}, u32[]{:S(2)}, u32[]{:S(2)}) collective-permute-start(bf16[768,256]{1,0:T(8,128)(2,1)S(1)} %grad_pre.1.pre_ref), channel_id=1, source_target_pairs={{0,1},{1,0},{2,3},{3,2},{4,5},{5,4},{6,7},{7,6},{8,9},{9,8},{10,11... | collective-permute-start | bytes 1179656 | tf_op jit(solution)/shard_map/ppermute | solution.py:438
  57.8 23.8 %copy-start = (bf16[3,3,256,256]{3,2,1,0:T(8,128)(2,1)S(1)}, bf16[3,3,256,256]{3,2,1,0:T(8,128)(2,1)}, u32[]{:S(2)}) copy-start(bf16[3,3,256,256]{3,2,1,0:T(8,128)(2,1)} %weight_ref.5) | copy-start | bytes 3538948
  76.7 17.7 %all-to-all-start.3 = ((bf16[16,8,144]{2,1,0:T(8,128)(2,1)}), bf16[16,8,144]{2,1,0:T(8,128)(2,1)S(1)}, u32[]{:S(2)}, u32[]{:S(2)}) async-start(bf16[16,8,144]{2,1,0:T(8,128)(2,1)} %first_sum.1), calls=%async_computation.3 | async-start | bytes 131072 | tf_op jit(solution)/shard_map/all_to_all | solution.py:556
